TPU v7x, 32 devices: a whole 2x2x4 slice. The times are simulated.
32 devices in a mesh: section: 4 (over x, core), row: 4 (over z), dp: 2 (over y).
Axes of the slice: x: 2, y: 2, z: 4, core: 2. Of those that a mesh axis runs over, the one named last changes fastest.
Arguments:
- inputs: bfloat16 [4, 2, 16, 48, 352], P(None, 'dp', 'row'), may hold values from -8 to 8
- depth_kernel: bfloat16 [4, 7, 7, 352], P('section'), may hold values from -0.875 to 0.875
- depth_bias: bfloat16 [4, 352], P('section'), may hold values from -3 to 3
- norm_gain: bfloat16 [4, 352], P('section'), may hold values from 0.099609375 to 1.8984375
- norm_bias: bfloat16 [4, 352], P('section'), may hold values from -3 to 3
- proj_in: bfloat16 [4, 352, 1408], P('section', None, 'dp'), may hold values from -0.3125 to 0.3125
- bias_in: bfloat16 [4, 1408], P('section'), may hold values from -3 to 3
- grn_gamma: bfloat16 [4, 1408], P('section'), may hold values from -3 to 3
- grn_beta: bfloat16 [4, 1408], P('section'), may hold values from -2 to 2
- proj_out: bfloat16 [4, 1408, 352], P('section', 'dp'), may hold values from -0.15625 to 0.15625
- bias_out: bfloat16 [4, 352], P('section'), may hold values from -3 to 3
Outputs:
- saved: bfloat16 [4, 4, 2, 16, 48, 352], P('section', None, 'dp', 'row')
All inputs are finite; a program needn't handle non-finite values.
Results may differ from a plain program's by a relative error of at most 0.015.
Values may be sent and summed in bfloat16 or wider, within the bound.
No kernel may reach another device: no remote copies, remote signals or barrier semaphores. Data moves between devices by JAX's collectives and lax.ppermute only.
A program may use at most 64 MiB of HBM per device.

v0:
```python
import functools

import jax
import jax.numpy as jnp
from jax import lax
from jax.experimental import pallas as pl
from jax.experimental.pallas import tpu as pltpu
from jax.sharding import PartitionSpec as P

EPS_NORM = 1e-06
EPS_GRN = 1e-06
LANES = 128
VMEM_BYTES = 40 * 1024 * 1024
REACH = 3
CHUNK = 4


def fill_columns(xp, xs, x, channels):
    height, reach_cols, blocks, lanes = xs.shape
    stride = reach_cols - 2 * REACH
    width = stride * blocks
    groups = lanes // LANES
    xp[...] = jnp.zeros(xp.shape, jnp.float32)

    def rows(n, carry):
        for k in range(2):
            r = 2 * n + k
            row = x[r].astype(jnp.float32)
            for g in range(groups):
                at = slice(g * LANES, (g + 1) * LANES)
                own = row[:, g * LANES : min((g + 1) * LANES, channels)]
                xp[k * groups + g, 8 : 8 + width, 0 : own.shape[1]] = own
                for q in range(reach_cols):
                    near = pl.ds(8 - REACH + q, blocks, stride=stride)
                    xs[r, q, :, at] = xp[k * groups + g, near, :]
        return carry

    lax.fori_loop(0, height // 2, rows, 0)


def conv(xs, taps, cvec, cq):
    rows = xs.shape[0]
    height, stride, blocks, lanes = cq.shape
    span = 2 * REACH + 1
    above = (height - rows) // 2

    def group(g, carry):
        at = pl.ds(pl.multiple_of(g * LANES, LANES), LANES)

        def column(q, carry):
            bias = jnp.broadcast_to(cvec[0:1, at], (blocks, LANES))
            acc = [None if above else bias] * height
            for j in range(span):
                kern = [
                    jnp.broadcast_to(taps[i * span + j : i * span + j + 1, at], (blocks, LANES))
                    for i in range(span)
                ]
                for r in range(rows):
                    x_row = xs[r, q + j, :, at]
                    for i in range(span):
                        h = r + above + REACH - i
                        if 0 <= h < height:
                            term = kern[i] * x_row
                            acc[h] = term if acc[h] is None else acc[h] + term
            for h in range(height):
                cq[h, q, :, at] = acc[h]
            return carry

        return lax.fori_loop(0, stride, column, carry)

    lax.fori_loop(0, lanes // LANES, group, 0)


def norm(cq, cvec, xp, flat, skip=0):
    padded, stride, blocks, lanes = cq.shape
    height = padded - 2 * skip
    channels = flat.shape[1]
    width = stride * blocks
    groups = lanes // LANES
    inside = lax.broadcasted_iota(jnp.int32, (blocks, lanes), 1) < channels

    def rows(n, carry):
        for k in range(2):
            h = 2 * n + k
            for q in range(stride):
                v = cq[h + skip, q]
                mean = jnp.sum(v, axis=-1, keepdims=True) * (1.0 / channels)
                c = jnp.where(inside, v - mean, 0.0)
                var = jnp.sum(c * c, axis=-1, keepdims=True) * (1.0 / channels)
                c = c * lax.rsqrt(var + EPS_NORM) * cvec[1:2, :] + cvec[2:3, :]
                for g in range(groups):
                    at = slice(g * LANES, (g + 1) * LANES)
                    xp[k * groups + g, pl.ds(q, blocks, stride=stride), :] = c[:, at]
            at_cell = pl.ds(pl.multiple_of(h * width, width), width)
            for g in range(groups):
                at = slice(g * LANES, min((g + 1) * LANES, channels))
                flat[at_cell, at] = xp[k * groups + g, 0:width, 0 : at.stop - at.start].astype(
                    jnp.bfloat16
                )
        return carry

    lax.fori_loop(0, height // 2, rows, 0)


def conv_norm(x, taps, cvec, flat, xp, xs, cq):
    fill_columns(xp, xs, x, x.shape[2])
    conv(xs, taps, cvec, cq)
    norm(cq, cvec, xp, flat)


def conv_scratch(rows, out_rows, width, lanes):
    return [
        pltpu.VMEM((2 * lanes // LANES, width + 16, LANES), jnp.float32),
        pltpu.VMEM((rows, width // 8 + 2 * REACH, 8, lanes), jnp.float32),
        pltpu.VMEM((out_rows, width // 8, 8, lanes), jnp.float32),
    ]


def gelu(v):
    return 0.5 * v * (1.0 + lax.erf(v * (0.5**0.5)))


def mlp(x, flat, ins, outs, cvec, fvec, acts, ssq, out):
    height, width, channels = x.shape
    half = ins[0].shape[1]
    step = 2 * LANES

    def units(w_in, act, which, start, count):
        raised = jnp.dot(
            flat[...], w_in[:, pl.ds(start, count)], preferred_element_type=jnp.float32
        )
        active = gelu(raised + fvec[which, 0:1, pl.ds(start, count)]).astype(jnp.bfloat16)
        act[:, pl.ds(start, count)] = active
        wide = active.astype(jnp.float32)
        ssq[which, :, pl.ds(start, count)] = jnp.sum(
            (wide * wide).reshape(height * width // 8, 8, count), axis=0
        )

    whole = half // step
    for which in range(2):

        def full(n, carry):
            units(ins[which], acts[which], which, pl.multiple_of(n * step, step), step)
            return carry

        lax.fori_loop(0, whole, full, 0)
        if half % step:
            units(ins[which], acts[which], which, whole * step, half % step)

    magnitude = jnp.sqrt(jnp.sum(ssq[...], axis=1, keepdims=True))
    total = jnp.sum(jnp.sum(magnitude, axis=2, keepdims=True), axis=0, keepdims=True)
    ratio = magnitude / (total * (0.5 / half) + EPS_GRN)
    scale = fvec[:, 1:2, :] * ratio + 1.0
    shift = fvec[:, 2:3, :]
    rows = CHUNK * width

    def lower(n, carry):
        update = cvec[3:4, 0:channels]
        for which in range(2):
            a = acts[which][pl.ds(pl.multiple_of(n * rows, rows), rows), :].astype(jnp.float32)
            hidden = (a * scale[which] + shift[which]).astype(jnp.bfloat16)
            update = update + jnp.dot(
                hidden, outs[which][...], preferred_element_type=jnp.float32
            )
        at = pl.ds(n * CHUNK, CHUNK)
        out[at] = (
            x[at].astype(jnp.float32) + update.reshape(CHUNK, width, channels)
        ).astype(jnp.bfloat16)
        return carry

    lax.fori_loop(0, height // CHUNK, lower, 0)


def pick_kernel(pos, inputs, *refs):
    outs, sems = refs[:-1], refs[-1]
    copies = [
        pltpu.make_async_copy(inputs.at[pos[n], 0], out, sems.at[n]) for n, out in enumerate(outs)
    ]
    for copy in copies:
        copy.start()
    for copy in copies:
        copy.wait()


def piece_kernel(piece, taps, cvec, part, xp, xs):
    fill_columns(xp, xs, piece, piece.shape[2])
    conv(xs, taps, cvec, part)


def last_piece_kernel(pos, *refs, count):
    pieces, parts = refs[:count], refs[count : 2 * count - 1]
    taps, cvec, x, flat, xp, xs, own, cq = refs[2 * count - 1 :]
    rows = pieces[0].shape[0]
    height, stride, blocks, lanes = cq.shape
    cq[...] = jnp.broadcast_to(cvec[0:1, :].reshape(1, 1, 1, lanes), cq.shape)
    fill_columns(xp, xs, pieces[-1], x.shape[2])
    conv(xs, taps, cvec, own)
    for piece, part, p in zip(pieces, (*parts, own), range(count)):
        at = pos[p] * rows
        x[pl.ds(at, rows)] = piece[...]
        cq[pl.ds(at, rows + 2 * REACH)] += part[...]
    norm(cq, cvec, xp, flat, REACH)


def conv_kernel(section, x, taps, cvec, flat, xp, xs, cq, *, tick):
    @pl.when(section[0] == tick)
    def _():
        conv_norm(x, taps, cvec, flat, xp, xs, cq)


def mlp_kernel(section, *refs, tick):
    ins, outs = (refs[0], refs[1]), (refs[2], refs[3])
    x, flat, cvec, fvec, prev, out, act_a, act_b, ssq = refs[4:]

    @pl.when(jnp.logical_or(tick == 0, section[0] == tick))
    def _():
        mlp(x, flat, ins, outs, cvec, fvec, (act_a, act_b), ssq, out)

    @pl.when(jnp.logical_and(tick != 0, section[0] != tick))
    def _():
        out[...] = prev[...]


def block_kernel(section, x, taps, cvec, fvec, *refs, tick):
    ins, outs = (refs[0], refs[1]), (refs[2], refs[3])
    prev, out, xp, xs, cq, flat, act_a, act_b, ssq = refs[4:]

    @pl.when(section[0] == tick)
    def _():
        conv_norm(x, taps, cvec, flat, xp, xs, cq)
        mlp(x, flat, ins, outs, cvec, fvec, (act_a, act_b), ssq, out)

    @pl.when(section[0] != tick)
    def _():
        out[...] = prev[...]


SMEM = pl.BlockSpec(memory_space=pltpu.SMEM)
VMEM = pl.BlockSpec(memory_space=pltpu.VMEM)


def block_cost(cells, channels, hidden_units):
    return pl.CostEstimate(
        flops=4 * cells * channels * hidden_units,
        bytes_accessed=4 * channels * hidden_units + 4 * cells * channels,
        transcendentals=cells * hidden_units,
    )


def mlp_scratch(cells, half):
    return [
        pltpu.VMEM((cells, half), jnp.bfloat16),
        pltpu.VMEM((cells, half), jnp.bfloat16),
        pltpu.VMEM((2, 8, half), jnp.float32),
    ]


def kernel_params():
    return pltpu.CompilerParams(vmem_limit_bytes=VMEM_BYTES)


def run_pick(pos, inputs):
    count = pos.shape[0]
    return pl.pallas_call(
        pick_kernel,
        out_shape=(jax.ShapeDtypeStruct(inputs.shape[2:], inputs.dtype),) * count,
        in_specs=[SMEM, pl.BlockSpec(memory_space=pl.ANY)],
        out_specs=(VMEM,) * count,
        scratch_shapes=[pltpu.SemaphoreType.DMA((count,))],
        compiler_params=kernel_params(),
        name="pick_rows",
    )(pos, inputs)


def run_piece(piece, taps, cvec):
    rows, width, _ = piece.shape
    lanes = taps.shape[1]
    out_rows = rows + 2 * REACH
    return pl.pallas_call(
        piece_kernel,
        out_shape=jax.ShapeDtypeStruct((out_rows, width // 8, 8, lanes), jnp.float32),
        in_specs=[VMEM] * 3,
        out_specs=VMEM,
        scratch_shapes=conv_scratch(rows, out_rows, width, lanes)[:2],
        compiler_params=kernel_params(),
        name="conv_piece",
    )(piece, taps, cvec)


def run_last_piece(pos, pieces, parts, taps, cvec):
    rows, width, channels = pieces[0].shape
    lanes = taps.shape[1]
    height = rows * len(pieces)
    scratch = conv_scratch(rows, rows + 2 * REACH, width, lanes)
    return pl.pallas_call(
        functools.partial(last_piece_kernel, count=len(pieces)),
        out_shape=(
            jax.ShapeDtypeStruct((height, width, channels), jnp.bfloat16),
            jax.ShapeDtypeStruct((height * width, channels), jnp.bfloat16),
        ),
        in_specs=[SMEM] + [VMEM] * (len(pieces) + len(parts) + 2),
        out_specs=(VMEM, VMEM),
        scratch_shapes=scratch + [conv_scratch(1, height + 2 * REACH, width, lanes)[2]],
        compiler_params=kernel_params(),
        name="last_piece",
    )(pos, *pieces, *parts, taps, cvec)


def run_conv(section, x, taps, cvec, tick):
    height, width, channels = x.shape
    lanes = taps.shape[1]
    return pl.pallas_call(
        functools.partial(conv_kernel, tick=tick),
        out_shape=jax.ShapeDtypeStruct((height * width, channels), jnp.bfloat16),
        in_specs=[SMEM] + [VMEM] * 3,
        out_specs=VMEM,
        scratch_shapes=conv_scratch(height, height, width, lanes),
        compiler_params=kernel_params(),
        name="conv",
    )(section, x, taps, cvec)


def run_mlp(section, x, flat, cvec, fvec, weights, prev, tick):
    height, width, channels = x.shape
    half = weights[0].shape[1]
    return pl.pallas_call(
        functools.partial(mlp_kernel, tick=tick),
        out_shape=jax.ShapeDtypeStruct(x.shape, jnp.bfloat16),
        in_specs=[SMEM] + [VMEM] * 9,
        out_specs=VMEM,
        scratch_shapes=mlp_scratch(height * width, half),
        compiler_params=kernel_params(),
        cost_estimate=block_cost(height * width, channels, 2 * half),
        name="mlp",
    )(section, *weights, x, flat, cvec, fvec, prev)


def run_block(section, x, taps, cvec, fvec, weights, prev, tick):
    height, width, channels = x.shape
    lanes = taps.shape[1]
    half = weights[0].shape[1]
    return pl.pallas_call(
        functools.partial(block_kernel, tick=tick),
        out_shape=jax.ShapeDtypeStruct(x.shape, jnp.bfloat16),
        in_specs=[SMEM] + [VMEM] * 9,
        out_specs=VMEM,
        scratch_shapes=conv_scratch(height, height, width, lanes)
        + [pltpu.VMEM((height * width, channels), jnp.bfloat16)]
        + mlp_scratch(height * width, half),
        compiler_params=kernel_params(),
        cost_estimate=block_cost(height * width, channels, 2 * half),
        name="block",
    )(section, x, taps, cvec, fvec, *weights, prev)


def swap_pairs(sections, size, by):
    return [(s * size + p, s * size + (p ^ by)) for s in sections for p in range(size)]


def image_plan(
    inputs,
    depth_kernel,
    depth_bias,
    norm_gain,
    norm_bias,
    proj_in,
    bias_in,
    grn_gamma,
    grn_beta,
    proj_out,
    bias_out,
):
    sections = lax.axis_size("section")
    rows_axis = lax.axis_size("row")
    section = lax.axis_index("section")
    me = lax.axis_index("row")
    part = lax.axis_index("dp")
    _, _, local_rows, width, channels = inputs.shape
    height = local_rows * rows_axis
    lanes = -(-channels // LANES) * LANES
    extra = lanes - channels
    half = proj_in.shape[2]

    def rows_from_helper(x, by):
        pairs = [(rows_axis + (p ^ by), p) for p in range(rows_axis)]
        return lax.ppermute(x, ("section", "row"), pairs)

    def part_swap(x, which):
        return lax.ppermute(x, ("section", "dp"), swap_pairs(which, 2, 1))

    even = range(0, sections, 2)
    odd = range(1, sections, 2)
    w_in, w_out = proj_in[0], proj_out[0]
    order = (0, 2, 3, 1)
    pos = jnp.stack([me ^ by for by in order]).astype(jnp.int32)
    pieces = run_pick(pos, inputs)
    pieces = [pieces[0]] + [rows_from_helper(p, by) for p, by in zip(pieces[1:], order[1:])]
    even_in = part_swap(w_in, even)
    even_out = part_swap(w_out, even)

    fvec = jnp.concatenate([bias_in, grn_gamma, grn_beta], axis=0).astype(jnp.float32)
    fvec = fvec.reshape(3, 2, half).transpose(1, 0, 2)
    fvec = jnp.where(part == 0, fvec, fvec[::-1])
    cvec = jnp.concatenate([depth_bias, norm_gain, norm_bias, bias_out], axis=0)
    cvec = jnp.pad(cvec.astype(jnp.float32), ((0, 0), (0, extra)))
    taps = depth_kernel[0].reshape(-1, channels).astype(jnp.float32)
    taps = jnp.pad(taps, ((0, 0), (0, extra)))
    at = section.astype(jnp.int32).reshape(1)

    parts = [run_piece(p, taps, cvec) for p in pieces[:-1]]
    x, flat = run_last_piece(pos, pieces, parts, taps, cvec)
    weights = [(w_in, even_in, w_out, even_out)]
    result = run_mlp(at, x, flat, cvec, fvec, weights[0], x, 0)
    for tick in range(1, sections):
        arriving = lax.ppermute(result, "section", [(tick - 1, tick)])
        if tick == 1:
            late_in, late_out, result = lax.optimization_barrier((w_in, w_out, result))
            weights.append(
                (w_in, part_swap(late_in, odd), w_out, part_swap(late_out, odd))
            )
            flat = run_conv(at, arriving, taps, cvec, tick)
            result = run_mlp(at, arriving, flat, cvec, fvec, weights[1], result, tick)
        else:
            result = run_block(
                at, arriving, taps, cvec, fvec, weights[tick % 2], result, tick
            )

    def rows_of(p):
        return lax.dynamic_slice_in_dim(result, p * local_rows, local_rows, axis=0)

    saved = jnp.zeros((rows_axis, local_rows, width, channels), jnp.bfloat16)
    saved = lax.dynamic_update_index_in_dim(saved, rows_of(me), me, 0)
    for by in (2, 3, 1):
        got = lax.ppermute(rows_of(me ^ by), "row", [(p, p ^ by) for p in range(rows_axis)])
        saved = lax.dynamic_update_index_in_dim(saved, got, me ^ by, 0)
    return saved[None, :, None]


def extended(cells, sides, width):
    for axis, dim in sides:
        count = lax.axis_size(axis)
        ends = count - 1
        head = lax.slice_in_dim(cells, 0, width, axis=dim)
        tail = lax.slice_in_dim(cells, cells.shape[dim] - width, cells.shape[dim], axis=dim)
        cells = jnp.concatenate(
            [
                lax.ppermute(tail, axis, [(i, (i + 1) % count) for i in range(ends)]),
                cells,
                lax.ppermute(head, axis, [((i + 1) % count, i) for i in range(ends)]),
            ],
            axis=dim,
        )
    return cells


def depthwise(padded, kernel, bias_term):
    channels = padded.shape[-1]
    conv_out = lax.conv_general_dilated(
        padded.astype(jnp.float32),
        kernel.astype(jnp.float32)[:, :, None, :],
        (1, 1),
        "VALID",
        dimension_numbers=("NHWC", "HWIO", "NHWC"),
        feature_group_count=channels,
        precision=lax.Precision.HIGHEST,
    )
    return conv_out + bias_term.astype(jnp.float32)


def conv_block(current, params):
    (
        depth_kernel,
        depth_bias,
        norm_gain,
        norm_bias,
        proj_in,
        bias_in,
        grn_gamma,
        grn_beta,
        proj_out,
        bias_out,
    ) = params
    num_items, num_rows, num_cols, channels = current.shape
    padded = extended(current, (("row", 1),), REACH)
    padded = jnp.pad(padded, ((0, 0), (0, 0), (REACH, REACH), (0, 0)))
    conv_out = depthwise(padded, depth_kernel, depth_bias)
    center = conv_out - jnp.mean(conv_out, axis=-1, keepdims=True)
    spread = jnp.mean(center * center, axis=-1, keepdims=True)
    normed = (
        center * lax.rsqrt(spread + EPS_NORM) * norm_gain.astype(jnp.float32)
        + norm_bias.astype(jnp.float32)
    ).astype(jnp.bfloat16)
    flat_rows = normed.reshape(num_items * num_rows * num_cols, channels)
    raised = jnp.dot(flat_rows, proj_in, preferred_element_type=jnp.float32) + bias_in.astype(
        jnp.float32
    )
    active = jax.nn.gelu(raised, approximate=False).astype(jnp.bfloat16)
    grouped = active.reshape(num_items, num_rows * num_cols, -1).astype(jnp.float32)
    local_sq = jnp.sum(grouped * grouped, axis=1)
    total_sq = lax.psum(local_sq, "row")
    magnitude = jnp.sqrt(total_sq)
    grn_ratio = magnitude / (jnp.mean(magnitude, axis=-1, keepdims=True) + EPS_GRN)
    hidden = (
        grn_gamma.astype(jnp.float32) * grouped * grn_ratio[:, None, :]
        + grn_beta.astype(jnp.float32)
        + grouped
    ).astype(jnp.bfloat16)
    update = jnp.dot(
        hidden.reshape(num_items * num_rows * num_cols, -1),
        proj_out,
        preferred_element_type=jnp.float32,
    ) + bias_out.astype(jnp.float32)
    return (
        current.astype(jnp.float32) + update.reshape(num_items, num_rows, num_cols, channels)
    ).astype(jnp.bfloat16)


def rows_plan(inputs, *weights):
    (
        depth_kernel,
        depth_bias,
        norm_gain,
        norm_bias,
        proj_in,
        bias_in,
        grn_gamma,
        grn_beta,
        proj_out,
        bias_out,
    ) = weights
    proj_in = lax.all_gather(proj_in, "dp", axis=2, tiled=True)
    proj_out = lax.all_gather(proj_out, "dp", axis=1, tiled=True)
    own_params = tuple(
        w[0]
        for w in (
            depth_kernel,
            depth_bias,
            norm_gain,
            norm_bias,
            proj_in,
            bias_in,
            grn_gamma,
            grn_beta,
            proj_out,
            bias_out,
        )
    )
    sections = lax.axis_size("section")
    section_index = lax.axis_index("section")
    num_micro = inputs.shape[0]
    num_ticks = num_micro + sections - 1
    arriving = jnp.zeros_like(inputs[0])
    saved = jnp.zeros_like(inputs)
    for tick_index in range(num_ticks):
        fresh_input = inputs[min(tick_index, num_micro - 1)]
        current = jnp.where(section_index == 0, fresh_input, arriving)
        produced = conv_block(current, own_params)
        slot_index = tick_index - section_index
        is_valid = jnp.logical_and(slot_index >= 0, slot_index < num_micro)
        safe_slot = jnp.clip(slot_index, 0, num_micro - 1)
        previous = lax.dynamic_index_in_dim(saved, safe_slot, 0, keepdims=False)
        saved = lax.dynamic_update_index_in_dim(
            saved, jnp.where(is_valid, produced, previous), safe_slot, 0
        )
        if tick_index + 1 < num_ticks:
            arriving = lax.ppermute(
                produced, "section", [(i, i + 1) for i in range(sections - 1)]
            )
    return saved[None]


def on_device(inputs, *weights):
    num_micro, images, local_rows, width, _ = inputs.shape
    one_image_each = (
        images == 1
        and lax.axis_size("row") == num_micro == 4
        and lax.axis_size("dp") == 2
        and lax.axis_size("section") > 1
        and local_rows % 4 == 0
        and width % 16 == 0
    )
    plan = image_plan if one_image_each else rows_plan
    return plan(inputs, *weights)


def solution(mesh):
    return jax.shard_map(
        on_device,
        mesh=mesh,
        in_specs=(
            P(None, "dp", "row", None, None),
            P("section", None, None, None),
            P("section", None),
            P("section", None),
            P("section", None),
            P("section", None, "dp"),
            P("section", None),
            P("section", None),
            P("section", None),
            P("section", "dp", None),
            P("section", None),
        ),
        out_specs=P("section", None, "dp", "row", None, None),
        check_vma=False,
    )
```

profile of v0, /device:TPU:7, one launch (start us, length us, event | category | flops | bytes accessed | tf_op | source)
XLA Modules:
  0.0 95.4 jit_solution(11933682518683654340)
XLA Ops:
  0.1 1.1 %copy-done = bf16[4,1,4,48,352]{4,3,2,1,0:T(8,128)(2,1)S(1)} copy-done((bf16[4,1,4,48,352]{4,3,2,1,0:T(8,128)(2,1)S(1)}, bf16[4,1,4,48,352]{4,3,2,1,0:T(8,128)(2,1)}, u32[]{:S(2)}) %copy-start) | copy-done | bytes 540696
  1.1 1.3 %pick_rows.1 = (bf16[4,48,352]{2,1,0:T(8,128)(2,1)S(1)}, bf16[4,48,352]{2,1,0:T(8,128)(2,1)S(1)}, bf16[4,48,352]{2,1,0:T(8,128)(2,1)S(1)}, bf16[4,48,352]{2,1,0:T(8,128)(2,1)S(1)}) custom-call(s32[4]{0:T(128)S(1)} %pad_add_fusion.pos, bf16[4,1,4,48,352]{4,3,2,1,0:T(8,128)(2,1)S(1)} %copy-done), custom_call_target="tpu_custom_call" | custom-call | tf_op jit(solution)/shard_map/pick_rows/pallas_call | solution.py:264
  3.9 0.8 collective-permute-start.4
  4.7 0.7 collective-permute-start
  5.4 0.7 collective-permute-start.1
  8.5 1.2 %conv_piece.3.refs_4_ = f32[10,6,8,384]{3,2,1,0:T(8,128)S(1)} custom-call(bf16[4,48,352]{2,1,0:T(8,128)(2,1)S(1)} %get-tuple-element.14.piece.refs_0_, f32[49,384]{1,0:T(8,128)S(1)} %pad_convert_fusion.taps.refs_7_, f32[4,384]{1,0:T(4,128)S(1)} %fusion.7.cvec.refs_8_.refs_6_), custom_call_target="tpu_custom_call" | custom-call | tf_op jit(solution)/shard_map/conv_piece/pallas_call | solution.py:279
  9.7 1.2 %conv_piece.4.refs_5_ = f32[10,6,8,384]{3,2,1,0:T(8,128)S(1)} custom-call(bf16[4,48,352]{2,1,0:T(8,128)(2,1)S(1)} %collective-permute-done.2.piece.refs_1_, f32[49,384]{1,0:T(8,128)S(1)} %pad_convert_fusion.taps.refs_7_, f32[4,384]{1,0:T(4,128)S(1)} %fusion.7.cvec.refs_8_.refs_6_), custom_call_target="tpu_custom_call" | custom-call | tf_op jit(solution)/shard_map/conv_piece/pallas_call | solution.py:279
  10.9 1.2 %conv_piece.5.refs_6_ = f32[10,6,8,384]{3,2,1,0:T(8,128)S(1)} custom-call(bf16[4,48,352]{2,1,0:T(8,128)(2,1)S(1)} %collective-permute-done.3.piece.refs_2_, f32[49,384]{1,0:T(8,128)S(1)} %pad_convert_fusion.taps.refs_7_, f32[4,384]{1,0:T(4,128)S(1)} %fusion.7.cvec.refs_8_.refs_6_), custom_call_target="tpu_custom_call" | custom-call | tf_op jit(solution)/shard_map/conv_piece/pallas_call | solution.py:279
  12.1 3.8 %last_piece.1 = (bf16[16,48,352]{2,1,0:T(8,128)(2,1)S(1)}, bf16[768,352]{1,0:T(8,128)(2,1)S(1)}) custom-call(s32[4]{0:T(128)S(1)} %pad_add_fusion.pos, bf16[4,48,352]{2,1,0:T(8,128)(2,1)S(1)} %get-tuple-element.14.piece.refs_0_, bf16[4,48,352]{2,1,0:T(8,128)(2,1)S(1)} %collective-permute-done.2.piece.refs_1_, ...), custom_call_target="tpu_custom_call" | custom-call | tf_op jit(solution)/shard_map/last_piece/pallas_call | solution.py:295
  15.9 4.8 %mlp.2.refs_8_ = bf16[16,48,352]{2,1,0:T(8,128)(2,1)S(1)} custom-call(s32[1]{0:T(128)} %bitcast.section, bf16[352,704]{1,0:T(8,128)(2,1)S(1)} %bitcast.18, bf16[352,704]{1,0:T(8,128)(2,1)S(1)} %collective-permute-done.refs_1_, bf16[704,352]{1,0:T(8,128)(2,1)S(1)} %bitcast.24, bf16[704,352]{1,0:T(8,128)(2,1)S(1)} %collective-permute-done.1.refs_3_, ...), custom_call_target="tpu_custom_call" | custom-call | flops 1522532352 | bytes 3063808 | tf_op jit(solution)/shard_map/mlp/pallas_call | solution.py:326
  20.7 0.7 collective-permute-start.7
  21.4 2.1 %collective-permute-start.5 = (bf16[352,704]{1,0:T(8,128)(2,1)S(1)}, bf16[352,704]{1,0:T(8,128)(2,1)S(1)}, u32[]{:S(2)}, u32[]{:S(2)}) collective-permute-start(bf16[352,704]{1,0:T(8,128)(2,1)S(1)} %bitcast.19), channel_id=1, source_target_pairs={{8,9},{9,8},{24,25},{25,24},{10,11},{11,10},{26,27},{27,26},{12,13... | collective-permute-start | bytes 1486856 | tf_op jit(solution)/shard_map/ppermute | solution.py:389
  23.5 3.1 %collective-permute-start.6 = (bf16[704,352]{1,0:T(8,128)(2,1)S(1)}, bf16[704,352]{1,0:T(8,128)(2,1)S(1)}, u32[]{:S(2)}, u32[]{:S(2)}) collective-permute-start(bf16[704,352]{1,0:T(8,128)(2,1)S(1)} %bitcast.25), channel_id=1, source_target_pairs={{8,9},{9,8},{24,25},{25,24},{10,11},{11,10},{26,27},{27,26},{12,13... | collective-permute-start | bytes 1486856 | tf_op jit(solution)/shard_map/ppermute | solution.py:389
  26.7 4.8 %collective-permute-done.5.refs_1_ = bf16[352,704]{1,0:T(8,128)(2,1)S(1)} collective-permute-done((bf16[352,704]{1,0:T(8,128)(2,1)S(1)}, bf16[352,704]{1,0:T(8,128)(2,1)S(1)}, u32[]{:S(2)}, u32[]{:S(2)}) %collective-permute-start.5) | collective-permute-done | bytes 495648 | tf_op jit(solution)/shard_map/ppermute | solution.py:389
  31.5 5.8 %collective-permute-done.6.refs_3_ = bf16[704,352]{1,0:T(8,128)(2,1)S(1)} collective-permute-done((bf16[704,352]{1,0:T(8,128)(2,1)S(1)}, bf16[704,352]{1,0:T(8,128)(2,1)S(1)}, u32[]{:S(2)}, u32[]{:S(2)}) %collective-permute-start.6) | collective-permute-done | bytes 495648 | tf_op jit(solution)/shard_map/ppermute | solution.py:389
  37.4 0.7 copy-done.5
  38.9 1.3 %collective-permute-start.9 = (bf16[16,48,352]{2,1,0:T(8,128)(2,1)S(1)}, bf16[16,48,352]{2,1,0:T(8,128)(2,1)S(1)}, u32[]{:S(2)}, u32[]{:S(2)}) collective-permute-start(bf16[16,48,352]{2,1,0:T(8,128)(2,1)S(1)} %block.2.refs_4_), channel_id=1, source_target_pairs={{16,24},{17,25},{18,26},{19,27},{20,28},{21,29},{22,30},{23,31}} | collective-permute-start | bytes 1622024 | tf_op jit(solution)/shard_map/ppermute | solution.py:415
  40.2 32.2 %collective-permute-done.9.x = bf16[16,48,352]{2,1,0:T(8,128)(2,1)S(1)} collective-permute-done((bf16[16,48,352]{2,1,0:T(8,128)(2,1)S(1)}, bf16[16,48,352]{2,1,0:T(8,128)(2,1)S(1)}, u32[]{:S(2)}, u32[]{:S(2)}) %collective-permute-start.9) | collective-permute-done | bytes 540704 | tf_op jit(solution)/shard_map/ppermute | solution.py:415
  72.4 1.0 %copy-done.4 = bf16[352,704]{1,0:T(8,128)(2,1)S(1)} copy-done((bf16[352,704]{1,0:T(8,128)(2,1)S(1)}, bf16[352,704]{1,0:T(8,128)(2,1)}, u32[]{:S(2)}) %copy-start.4) | copy-done | bytes 495640
  73.4 1.0 %copy-done.6 = bf16[704,352]{1,0:T(8,128)(2,1)S(1)} copy-done((bf16[704,352]{1,0:T(8,128)(2,1)S(1)}, bf16[704,352]{1,0:T(8,128)(2,1)}, u32[]{:S(2)}) %copy-start.6) | copy-done | bytes 495640
  74.5 10.7 %block.3 = bf16[16,48,352]{2,1,0:T(8,128)(2,1)S(1)} custom-call(s32[1]{0:T(128)} %bitcast.section, bf16[16,48,352]{2,1,0:T(8,128)(2,1)S(1)} %collective-permute-done.9.x, f32[49,384]{1,0:T(8,128)S(1)} %pad_convert_fusion.taps.refs_7_, f32[4,384]{1,0:T(4,128)S(1)} %fusion.7.cvec.refs_8_.refs_6_, f32[2,3,704]{2,1,0:T(4,128)S(1)} %reverse_select_fusion.refs_7_.fvec, ...), custom_call_target="tpu_custom_call" | custom-call | flops 1522532352 | bytes 3063808 | tf_op jit(solution)/shard_map/block/pallas_call | solution.py:342
  85.5 2.2 %collective-permute-start.11 = (bf16[4,48,352]{2,1,0:T(8,128)(2,1)S(1)}, bf16[4,48,352]{2,1,0:T(8,128)(2,1)S(1)}, u32[]{:S(2)}, u32[]{:S(2)}) collective-permute-start(bf16[4,48,352]{2,1,0:T(8,128)(2,1)S(1)} %get-tuple-element.24), channel_id=1, source_target_pairs={{0,6},{2,4},{4,2},{6,0},{1,7},{3,5},{5,3},{7,1},{8,14},{10,12},{12... | collective-permute-start | bytes 405512 | tf_op jit(solution)/shard_map/ppermute | solution.py:434
  88.1 5.4 %collective-permute-done.10 = bf16[4,48,352]{2,1,0:T(8,128)(2,1)S(1)} collective-permute-done((bf16[4,48,352]{2,1,0:T(8,128)(2,1)S(1)}, bf16[4,48,352]{2,1,0:T(8,128)(2,1)S(1)}, u32[]{:S(2)}, u32[]{:S(2)}) %collective-permute-start.10) | collective-permute-done | bytes 135200 | tf_op jit(solution)/shard_map/ppermute | solution.py:434
  93.6 1.2 %collective-permute-done.12 = bf16[4,48,352]{2,1,0:T(8,128)(2,1)S(1)} collective-permute-done((bf16[4,48,352]{2,1,0:T(8,128)(2,1)S(1)}, bf16[4,48,352]{2,1,0:T(8,128)(2,1)S(1)}, u32[]{:S(2)}, u32[]{:S(2)}) %collective-permute-start.12) | collective-permute-done | bytes 135200 | tf_op jit(solution)/shard_map/ppermute | solution.py:434
  (62 shorter events, 6.0 us)
Async XLA Ops:
  0.1 1.1 %copy-start = (bf16[4,1,4,48,352]{4,3,2,1,0:T(8,128)(2,1)S(1)}, bf16[4,1,4,48,352]{4,3,2,1,0:T(8,128)(2,1)}, u32[]{:S(2)}) copy-start(bf16[4,1,4,48,352]{4,3,2,1,0:T(8,128)(2,1)} %inputs.1) | copy-start | bytes 1622020
  1.1 3.6 %copy-start.1 = (bf16[1,352,704]{2,1,0:T(8,128)(2,1)S(1)}, bf16[1,352,704]{2,1,0:T(8,128)(2,1)}, u32[]{:S(2)}) copy-start(bf16[1,352,704]{2,1,0:T(8,128)(2,1)} %param.16) | copy-start | bytes 1486852
  1.1 5.0 %copy-start.8 = (bf16[1,7,7,352]{3,2,1,0:T(8,128)(2,1)S(1)}, bf16[1,7,7,352]{3,2,1,0:T(8,128)(2,1)}, u32[]{:S(2)}) copy-start(bf16[1,7,7,352]{3,2,1,0:T(8,128)(2,1)} %param.12) | copy-start | bytes 103492
  2.5 7.2 %collective-permute-start.2 = (bf16[4,48,352]{2,1,0:T(8,128)(2,1)S(1)}, bf16[4,48,352]{2,1,0:T(8,128)(2,1)S(1)}, u32[]{:S(2)}, u32[]{:S(2)}) collective-permute-start(bf16[4,48,352]{2,1,0:T(8,128)(2,1)S(1)} %get-tuple-element.15), channel_id=1, source_target_pairs={{12,0},{14,2},{8,4},{10,6},{13,1},{15,3},{9,5},{11,7}} | collective-permute-start | bytes 405512 | tf_op jit(solution)/shard_map/ppermute | solution.py:386
  3.2 3.0 %copy-start.15 = (bf16[1,352]{1,0:T(2,128)(2,1)S(1)}, bf16[1,352]{1,0:T(2,128)(2,1)}, u32[]{:S(2)}) copy-start(bf16[1,352]{1,0:T(2,128)(2,1)} %param.13) | copy-start | bytes 2116
  3.2 7.7 %collective-permute-start.3 = (bf16[4,48,352]{2,1,0:T(8,128)(2,1)S(1)}, bf16[4,48,352]{2,1,0:T(8,128)(2,1)S(1)}, u32[]{:S(2)}, u32[]{:S(2)}) collective-permute-start(bf16[4,48,352]{2,1,0:T(8,128)(2,1)S(1)} %get-tuple-element.16), channel_id=1, source_target_pairs={{14,0},{12,2},{10,4},{8,6},{15,1},{13,3},{11,5},{9,7}} | collective-permute-start | bytes 405512 | tf_op jit(solution)/shard_map/ppermute | solution.py:386
  3.9 2.3 %copy-start.14 = (bf16[1,352]{1,0:T(2,128)(2,1)S(1)}, bf16[1,352]{1,0:T(2,128)(2,1)}, u32[]{:S(2)}) copy-start(bf16[1,352]{1,0:T(2,128)(2,1)} %param.14) | copy-start | bytes 2116
  3.9 2.3 %copy-start.12 = (bf16[1,352]{1,0:T(2,128)(2,1)S(1)}, bf16[1,352]{1,0:T(2,128)(2,1)}, u32[]{:S(2)}) copy-start(bf16[1,352]{1,0:T(2,128)(2,1)} %param.21) | copy-start | bytes 2116
  3.9 2.3 %copy-start.13 = (bf16[1,352]{1,0:T(2,128)(2,1)S(1)}, bf16[1,352]{1,0:T(2,128)(2,1)}, u32[]{:S(2)}) copy-start(bf16[1,352]{1,0:T(2,128)(2,1)} %param.15) | copy-start | bytes 2116
  3.9 8.2 %collective-permute-start.4 = (bf16[4,48,352]{2,1,0:T(8,128)(2,1)S(1)}, bf16[4,48,352]{2,1,0:T(8,128)(2,1)S(1)}, u32[]{:S(2)}, u32[]{:S(2)}) collective-permute-start(bf16[4,48,352]{2,1,0:T(8,128)(2,1)S(1)} %get-tuple-element.17), channel_id=1, source_target_pairs={{10,0},{8,2},{14,4},{12,6},{11,1},{9,3},{15,5},{13,7}} | collective-permute-start | bytes 405512 | tf_op jit(solution)/shard_map/ppermute | solution.py:386
  4.7 11.2 %collective-permute-start = (bf16[352,704]{1,0:T(8,128)(2,1)S(1)}, bf16[352,704]{1,0:T(8,128)(2,1)S(1)}, u32[]{:S(2)}, u32[]{:S(2)}) collective-permute-start(bf16[352,704]{1,0:T(8,128)(2,1)S(1)} %bitcast.17), channel_id=1, source_target_pairs={{0,1},{1,0},{16,17},{17,16},{2,3},{3,2},{18,19},{19,18},{4,5},{5,4... | collective-permute-start | bytes 1486856 | tf_op jit(solution)/shard_map/ppermute | solution.py:389
  5.4 10.5 %collective-permute-start.1 = (bf16[704,352]{1,0:T(8,128)(2,1)}, bf16[704,352]{1,0:T(8,128)(2,1)S(1)}, u32[]{:S(2)}, u32[]{:S(2)}) collective-permute-start(bf16[704,352]{1,0:T(8,128)(2,1)} %bitcast.23), channel_id=1, source_target_pairs={{0,1},{1,0},{16,17},{17,16},{2,3},{3,2},{18,19},{19,18},{4,5},{5,4... | collective-permute-start | bytes 1486856 | tf_op jit(solution)/shard_map/ppermute | solution.py:389
  12.1 3.8 %copy-start.2 = (bf16[1,704,352]{2,1,0:T(8,128)(2,1)S(1)}, bf16[1,704,352]{2,1,0:T(8,128)(2,1)}, u32[]{:S(2)}) copy-start(bf16[1,704,352]{2,1,0:T(8,128)(2,1)} %param.20) | copy-start | bytes 1486852
  20.7 6.0 %collective-permute-start.7 = (bf16[16,48,352]{2,1,0:T(8,128)(2,1)S(1)}, bf16[16,48,352]{2,1,0:T(8,128)(2,1)S(1)}, u32[]{:S(2)}, u32[]{:S(2)}) collective-permute-start(bf16[16,48,352]{2,1,0:T(8,128)(2,1)S(1)} %mlp.2.refs_8_), channel_id=1, source_target_pairs={{0,8},{1,9},{2,10},{3,11},{4,12},{5,13},{6,14},{7,15}} | collective-permute-start | bytes 1622024 | tf_op jit(solution)/shard_map/ppermute | solution.py:415
  21.4 10.1 %collective-permute-start.5 = (bf16[352,704]{1,0:T(8,128)(2,1)S(1)}, bf16[352,704]{1,0:T(8,128)(2,1)S(1)}, u32[]{:S(2)}, u32[]{:S(2)}) collective-permute-start(bf16[352,704]{1,0:T(8,128)(2,1)S(1)} %bitcast.19), channel_id=1, source_target_pairs={{8,9},{9,8},{24,25},{25,24},{10,11},{11,10},{26,27},{27,26},{12,13... | collective-permute-start | bytes 1486856 | tf_op jit(solution)/shard_map/ppermute | solution.py:389
  23.5 13.8 %collective-permute-start.6 = (bf16[704,352]{1,0:T(8,128)(2,1)S(1)}, bf16[704,352]{1,0:T(8,128)(2,1)S(1)}, u32[]{:S(2)}, u32[]{:S(2)}) collective-permute-start(bf16[704,352]{1,0:T(8,128)(2,1)S(1)} %bitcast.25), channel_id=1, source_target_pairs={{8,9},{9,8},{24,25},{25,24},{10,11},{11,10},{26,27},{27,26},{12,13... | collective-permute-start | bytes 1486856 | tf_op jit(solution)/shard_map/ppermute | solution.py:389
  31.5 5.9 %copy-start.3 = (bf16[352,704]{1,0:T(8,128)(2,1)}, bf16[352,704]{1,0:T(8,128)(2,1)S(1)}, u32[]{:S(2)}) copy-start(bf16[352,704]{1,0:T(8,128)(2,1)S(1)} %collective-permute-done.5.refs_1_) | copy-start | bytes 1486852
  38.1 0.7 collective-permute-start.8
  38.9 33.5 %collective-permute-start.9 = (bf16[16,48,352]{2,1,0:T(8,128)(2,1)S(1)}, bf16[16,48,352]{2,1,0:T(8,128)(2,1)S(1)}, u32[]{:S(2)}, u32[]{:S(2)}) collective-permute-start(bf16[16,48,352]{2,1,0:T(8,128)(2,1)S(1)} %block.2.refs_4_), channel_id=1, source_target_pairs={{16,24},{17,25},{18,26},{19,27},{20,28},{21,29},{22,30},{23,31}} | collective-permute-start | bytes 1622024 | tf_op jit(solution)/shard_map/ppermute | solution.py:415
  72.4 1.0 %copy-start.4 = (bf16[352,704]{1,0:T(8,128)(2,1)S(1)}, bf16[352,704]{1,0:T(8,128)(2,1)}, u32[]{:S(2)}) copy-start(bf16[352,704]{1,0:T(8,128)(2,1)} %copy-done.3) | copy-start | bytes 1486852
  85.3 8.2 %collective-permute-start.10 = (bf16[4,48,352]{2,1,0:T(8,128)(2,1)S(1)}, bf16[4,48,352]{2,1,0:T(8,128)(2,1)S(1)}, u32[]{:S(2)}, u32[]{:S(2)}) collective-permute-start(bf16[4,48,352]{2,1,0:T(8,128)(2,1)S(1)} %get-tuple-element.25), channel_id=1, source_target_pairs={{0,4},{2,6},{4,0},{6,2},{1,5},{3,7},{5,1},{7,3},{8,12},{10,14},{12... | collective-permute-start | bytes 405512 | tf_op jit(solution)/shard_map/ppermute | solution.py:434
  85.5 8.0 %collective-permute-start.11 = (bf16[4,48,352]{2,1,0:T(8,128)(2,1)S(1)}, bf16[4,48,352]{2,1,0:T(8,128)(2,1)S(1)}, u32[]{:S(2)}, u32[]{:S(2)}) collective-permute-start(bf16[4,48,352]{2,1,0:T(8,128)(2,1)S(1)} %get-tuple-element.24), channel_id=1, source_target_pairs={{0,6},{2,4},{4,2},{6,0},{1,7},{3,5},{5,3},{7,1},{8,14},{10,12},{12... | collective-permute-start | bytes 405512 | tf_op jit(solution)/shard_map/ppermute | solution.py:434
  87.7 7.0 %collective-permute-start.12 = (bf16[4,48,352]{2,1,0:T(8,128)(2,1)S(1)}, bf16[4,48,352]{2,1,0:T(8,128)(2,1)S(1)}, u32[]{:S(2)}, u32[]{:S(2)}) collective-permute-start(bf16[4,48,352]{2,1,0:T(8,128)(2,1)S(1)} %get-tuple-element.23), channel_id=1, source_target_pairs={{0,2},{2,0},{4,6},{6,4},{1,3},{3,1},{5,7},{7,5},{8,10},{10,8},{12,... | collective-permute-start | bytes 405512 | tf_op jit(solution)/shard_map/ppermute | solution.py:434
  93.6 1.2 %copy-start.7 = (bf16[1,4,1,4,48,352]{5,4,3,2,1,0:T(8,128)(2,1)}, bf16[1,4,1,4,48,352]{5,4,3,2,1,0:T(8,128)(2,1)S(1)}, u32[]{:S(2)}) copy-start(bf16[1,4,1,4,48,352]{5,4,3,2,1,0:T(8,128)(2,1)S(1)} %bitcast_dynamic-update-slice_fusion.1) | copy-start | bytes 1622020
  (5 other events, 3.9 us)
where the time goes:
time: 96.1 us; the launch traced here: 95.4 us
  waiting for transfers between devices  49.3 us (51%)
  Pallas kernels  24.2 us (25%)
  starting transfers between devices  14.2 us (15%)
  local copies, waits for them, and re-layouts  7 us (7%)
    ppermute x3, waiting for transfers between devices, image_plan(): arriving = lax.ppermute(result, 'section', [(tick - 1, tick)])  32.2 us
    pallas_call x2, Pallas kernels, run_block(): pl.pallas_call(functools.partial(block_kernel, tick=tick), out_shape=jax....  10.8 us
    ppermute x4, waiting for transfers between devices, part_swap(): return lax.ppermute(x, ('section', 'dp'), swap_pairs(which, 2, 1))  10.6 us
    ppermute x4, starting transfers between devices, part_swap(): return lax.ppermute(x, ('section', 'dp'), swap_pairs(which, 2, 1))  6.67 us
    ppermute x3, waiting for transfers between devices, image_plan(): lax.ppermute(rows_of(me ^ by), 'row', [(p, p ^ by) for p in range(rows_ax...  6.58 us
    unnamed x32, local copies, waits for them, and re-layouts  5.83 us
    pallas_call x2, Pallas kernels, run_mlp(): pl.pallas_call(functools.partial(mlp_kernel, tick=tick), out_shape=jax.Sh...  4.8 us
    pallas_call x1, Pallas kernels, run_last_piece(): pl.pallas_call(functools.partial(last_piece_kernel, count=len(pieces)), o...  3.77 us
  transfers between devices with their start and end apart: 13, of which 5 were waited for; matrix products, arithmetic and copies ran while one was open for 1% of the time, Pallas kernels for 8%

commit v1 on v0

--- a/solution.py
+++ b/solution.py
@@ -10,9 +10,11 @@
 EPS_NORM = 1e-06
 EPS_GRN = 1e-06
 LANES = 128
-VMEM_BYTES = 40 * 1024 * 1024
+VMEM_BYTES = 20 * 1024 * 1024
+PREPARE_VMEM_BYTES = 60 * 1024 * 1024
 REACH = 3
 CHUNK = 4
+NORM_ROWS = 4
 
 
 def fill_columns(xp, xs, x, channels):
@@ -80,8 +82,8 @@
     inside = lax.broadcasted_iota(jnp.int32, (blocks, lanes), 1) < channels
 
     def rows(n, carry):
-        for k in range(2):
-            h = 2 * n + k
+        for k in range(NORM_ROWS):
+            h = NORM_ROWS * n + k
             for q in range(stride):
                 v = cq[h + skip, q]
                 mean = jnp.sum(v, axis=-1, keepdims=True) * (1.0 / channels)
@@ -99,7 +101,7 @@
                 )
         return carry
 
-    lax.fori_loop(0, height // 2, rows, 0)
+    lax.fori_loop(0, height // NORM_ROWS, rows, 0)
 
 
 def conv_norm(x, taps, cvec, flat, xp, xs, cq):
@@ -110,7 +112,7 @@
 
 def conv_scratch(rows, out_rows, width, lanes):
     return [
-        pltpu.VMEM((2 * lanes // LANES, width + 16, LANES), jnp.float32),
+        pltpu.VMEM((NORM_ROWS * lanes // LANES, width + 16, LANES), jnp.float32),
         pltpu.VMEM((rows, width // 8 + 2 * REACH, 8, lanes), jnp.float32),
         pltpu.VMEM((out_rows, width // 8, 8, lanes), jnp.float32),
     ]
@@ -171,15 +173,33 @@
     lax.fori_loop(0, height // CHUNK, lower, 0)
 
 
-def pick_kernel(pos, inputs, *refs):
-    outs, sems = refs[:-1], refs[-1]
-    copies = [
-        pltpu.make_async_copy(inputs.at[pos[n], 0], out, sems.at[n]) for n, out in enumerate(outs)
-    ]
+def prepare_kernel(index, inputs, kernel, *refs):
+    vectors, refs = refs[:7], refs[7:]
+    count = len(refs) - 12
+    pieces, (taps, cvec, fvec) = refs[:count], refs[count : count + 3]
+    held, staged, sems = refs[count + 3], refs[count + 4 : -1], refs[-1]
+    moves = [(kernel, held), *zip(vectors, staged)]
+    moves += [(inputs.at[index[n], 0], piece) for n, piece in enumerate(pieces)]
+    copies = [pltpu.make_async_copy(a, b, sems.at[n]) for n, (a, b) in enumerate(moves)]
     for copy in copies:
         copy.start()
+    taps[...] = jnp.zeros(taps.shape, jnp.float32)
+    cvec[...] = jnp.zeros(cvec.shape, jnp.float32)
     for copy in copies:
         copy.wait()
+    channels = kernel.shape[3]
+    span = kernel.shape[1]
+    half = fvec.shape[2]
+    for i in range(span):
+        taps[i * span : (i + 1) * span, 0:channels] = held[0, i].astype(jnp.float32)
+    for n in range(4):
+        cvec[n : n + 1, 0:channels] = staged[n][...].astype(jnp.float32)
+    first = index[count] == 0
+    for n in range(3):
+        v = staged[4 + n][...].astype(jnp.float32)
+        low, high = v[:, 0:half], v[:, half:]
+        fvec[0, n : n + 1, :] = jnp.where(first, low, high)
+        fvec[1, n : n + 1, :] = jnp.where(first, high, low)
 
 
 def piece_kernel(piece, taps, cvec, part, xp, xs):
@@ -187,7 +207,7 @@
     conv(xs, taps, cvec, part)
 
 
-def last_piece_kernel(pos, *refs, count):
+def last_piece_kernel(index, *refs, count):
     pieces, parts = refs[:count], refs[count : 2 * count - 1]
     taps, cvec, x, flat, xp, xs, own, cq = refs[2 * count - 1 :]
     rows = pieces[0].shape[0]
@@ -196,7 +216,7 @@
     fill_columns(xp, xs, pieces[-1], x.shape[2])
     conv(xs, taps, cvec, own)
     for piece, part, p in zip(pieces, (*parts, own), range(count)):
-        at = pos[p] * rows
+        at = index[p] * rows
         x[pl.ds(at, rows)] = piece[...]
         cq[pl.ds(at, rows + 2 * REACH)] += part[...]
     norm(cq, cvec, xp, flat, REACH)
@@ -212,11 +232,11 @@
     ins, outs = (refs[0], refs[1]), (refs[2], refs[3])
     x, flat, cvec, fvec, prev, out, act_a, act_b, ssq = refs[4:]
 
-    @pl.when(jnp.logical_or(tick == 0, section[0] == tick))
+    @pl.when(section[0] == tick)
     def _():
         mlp(x, flat, ins, outs, cvec, fvec, (act_a, act_b), ssq, out)
 
-    @pl.when(jnp.logical_and(tick != 0, section[0] != tick))
+    @pl.when(section[0] != tick)
     def _():
         out[...] = prev[...]
 
@@ -237,6 +257,7 @@
 
 SMEM = pl.BlockSpec(memory_space=pltpu.SMEM)
 VMEM = pl.BlockSpec(memory_space=pltpu.VMEM)
+HBM = pl.BlockSpec(memory_space=pltpu.HBM)
 
 
 def block_cost(cells, channels, hidden_units):
@@ -259,17 +280,25 @@
     return pltpu.CompilerParams(vmem_limit_bytes=VMEM_BYTES)
 
 
-def run_pick(pos, inputs):
-    count = pos.shape[0]
+def run_prepare(index, inputs, kernel, vectors, lanes):
+    count = index.shape[0] - 1
+    half = vectors[-1].shape[1] // 2
+    held = (kernel, *vectors)
     return pl.pallas_call(
-        pick_kernel,
-        out_shape=(jax.ShapeDtypeStruct(inputs.shape[2:], inputs.dtype),) * count,
-        in_specs=[SMEM, pl.BlockSpec(memory_space=pl.ANY)],
-        out_specs=(VMEM,) * count,
-        scratch_shapes=[pltpu.SemaphoreType.DMA((count,))],
-        compiler_params=kernel_params(),
-        name="pick_rows",
-    )(pos, inputs)
+        prepare_kernel,
+        out_shape=(jax.ShapeDtypeStruct(inputs.shape[2:], inputs.dtype),) * count
+        + (
+            jax.ShapeDtypeStruct((kernel.shape[1] * kernel.shape[2], lanes), jnp.float32),
+            jax.ShapeDtypeStruct((4, lanes), jnp.float32),
+            jax.ShapeDtypeStruct((2, 3, half), jnp.float32),
+        ),
+        in_specs=[SMEM] + [HBM] * (len(held) + 1),
+        out_specs=(VMEM,) * (count + 3),
+        scratch_shapes=[pltpu.VMEM(v.shape, v.dtype) for v in held]
+        + [pltpu.SemaphoreType.DMA((len(held) + count,))],
+        compiler_params=pltpu.CompilerParams(vmem_limit_bytes=PREPARE_VMEM_BYTES),
+        name="prepare",
+    )(index, inputs, *held)
 
 
 def run_piece(piece, taps, cvec):
@@ -287,7 +316,7 @@
     )(piece, taps, cvec)
 
 
-def run_last_piece(pos, pieces, parts, taps, cvec):
+def run_last_piece(index, pieces, parts, taps, cvec):
     rows, width, channels = pieces[0].shape
     lanes = taps.shape[1]
     height = rows * len(pieces)
@@ -303,7 +332,7 @@
         scratch_shapes=scratch + [conv_scratch(1, height + 2 * REACH, width, lanes)[2]],
         compiler_params=kernel_params(),
         name="last_piece",
-    )(pos, *pieces, *parts, taps, cvec)
+    )(index, *pieces, *parts, taps, cvec)
 
 
 def run_conv(section, x, taps, cvec, tick):
@@ -378,8 +407,6 @@
     _, _, local_rows, width, channels = inputs.shape
     height = local_rows * rows_axis
     lanes = -(-channels // LANES) * LANES
-    extra = lanes - channels
-    half = proj_in.shape[2]
 
     def rows_from_helper(x, by):
         pairs = [(rows_axis + (p ^ by), p) for p in range(rows_axis)]
@@ -392,23 +419,17 @@
     odd = range(1, sections, 2)
     w_in, w_out = proj_in[0], proj_out[0]
     order = (0, 2, 3, 1)
-    pos = jnp.stack([me ^ by for by in order]).astype(jnp.int32)
-    pieces = run_pick(pos, inputs)
+    vectors = (depth_bias, norm_gain, norm_bias, bias_out, bias_in, grn_gamma, grn_beta)
+    index = jnp.stack([me ^ by for by in order] + [part]).astype(jnp.int32)
+    *pieces, taps, cvec, fvec = run_prepare(index, inputs, depth_kernel, vectors, lanes)
     pieces = [pieces[0]] + [rows_from_helper(p, by) for p, by in zip(pieces[1:], order[1:])]
     even_in = part_swap(w_in, even)
     even_out = part_swap(w_out, even)
 
-    fvec = jnp.concatenate([bias_in, grn_gamma, grn_beta], axis=0).astype(jnp.float32)
-    fvec = fvec.reshape(3, 2, half).transpose(1, 0, 2)
-    fvec = jnp.where(part == 0, fvec, fvec[::-1])
-    cvec = jnp.concatenate([depth_bias, norm_gain, norm_bias, bias_out], axis=0)
-    cvec = jnp.pad(cvec.astype(jnp.float32), ((0, 0), (0, extra)))
-    taps = depth_kernel[0].reshape(-1, channels).astype(jnp.float32)
-    taps = jnp.pad(taps, ((0, 0), (0, extra)))
     at = section.astype(jnp.int32).reshape(1)
 
     parts = [run_piece(p, taps, cvec) for p in pieces[:-1]]
-    x, flat = run_last_piece(pos, pieces, parts, taps, cvec)
+    x, flat = run_last_piece(index, pieces, parts, taps, cvec)
     weights = [(w_in, even_in, w_out, even_out)]
     result = run_mlp(at, x, flat, cvec, fvec, weights[0], x, 0)
     for tick in range(1, sections):

time: 96.1 us -> 95.6 us (level)
  Pallas kernels: 24.2 us -> 19.7 us
  waiting for transfers between devices: 49.3 us -> 53.8 us
    pallas_call x2, Pallas kernels: 4.8 us -> 0.12 us  [run_mlp(): pl.pallas_call(functools.partial(mlp_kernel, tick=tick), out_shape=jax.Sh...]
    ppermute x3, waiting for transfers between devices: 32.2 us -> 36.7 us  [image_plan(): arriving = lax.ppermute(result, 'section', [(tick - 1, tick)])]
    pallas_call x1, Pallas kernels: 1.35 us -> 2.87 us  [run_prepare(): pl.pallas_call(prepare_kernel, out_shape=(jax.ShapeDtypeStruct(inputs.sha...]
    unnamed x32 -> x28, local copies, waits for them, and re-layouts: 5.83 us -> 5.55 us
  transfers between devices with their start and end apart: 13 -> 13, of which waited for: 5 -> 5; matrix products, arithmetic and copies ran while one was open for 1% -> 1% of each run, Pallas kernels for 8% -> 10%
where the time goes in v1:
time: 95.6 us; the launch traced here: 95.1 us
  waiting for transfers between devices  53.8 us (56%)
  Pallas kernels  19.7 us (21%)
  starting transfers between devices  14 us (15%)
  local copies, waits for them, and re-layouts  7.08 us (7%)
    ppermute x3, waiting for transfers between devices, image_plan(): arriving = lax.ppermute(result, 'section', [(tick - 1, tick)])  36.7 us
    ppermute x4, waiting for transfers between devices, part_swap(): return lax.ppermute(x, ('section', 'dp'), swap_pairs(which, 2, 1))  10.6 us
    pallas_call x2, Pallas kernels, run_block(): pl.pallas_call(functools.partial(block_kernel, tick=tick), out_shape=jax....  10.1 us
    ppermute x4, starting transfers between devices, part_swap(): return lax.ppermute(x, ('section', 'dp'), swap_pairs(which, 2, 1))  6.66 us
    ppermute x3, waiting for transfers between devices, image_plan(): lax.ppermute(rows_of(me ^ by), 'row', [(p, p ^ by) for p in range(rows_ax...  6.51 us
    unnamed x28, local copies, waits for them, and re-layouts  5.55 us
    pallas_call x3, Pallas kernels, run_piece(): pl.pallas_call(piece_kernel, out_shape=jax.ShapeDtypeStruct((out_rows, wi...  3.49 us
    pallas_call x1, Pallas kernels, run_last_piece(): pl.pallas_call(functools.partial(last_piece_kernel, count=len(pieces)), o...  3.09 us
  transfers between devices with their start and end apart: 13, of which 5 were waited for; matrix products, arithmetic and copies ran while one was open for 1% of the time, Pallas kernels for 10%

profile of v1, /device:TPU:7, one launch (start us, length us, event | category | flops | bytes accessed | tf_op | source)
XLA Modules:
  0.0 95.1 jit_solution(15715902996130830077)
XLA Ops:
  0.7 0.7 collective-permute-start.1
  2.1 2.9 %prepare.1 = (bf16[4,48,352]{2,1,0:T(8,128)(2,1)}, bf16[4,48,352]{2,1,0:T(8,128)(2,1)}, bf16[4,48,352]{2,1,0:T(8,128)(2,1)}, bf16[4,48,352]{2,1,0:T(8,128)(2,1)}...) custom-call(s32[5]{0:T(128)} %stack.23.index, bf16[4,1,4,48,352]{4,3,2,1,0:T(8,128)(2,1)} %inputs.1, ...), custom_call_target="tpu_custom_call" | custom-call | tf_op jit(solution)/shard_map/prepare/pallas_call | solution.py:287
  7.0 0.9 copy-done
  7.9 0.9 copy-done.2
  8.8 1.2 %conv_piece.3.refs_4_ = f32[10,6,8,384]{3,2,1,0:T(8,128)S(1)} custom-call(bf16[4,48,352]{2,1,0:T(8,128)(2,1)S(1)} %copy-done.2, f32[49,384]{1,0:T(8,128)S(1)} %copy-done, f32[4,384]{1,0:T(4,128)S(1)} %copy-done.4), custom_call_target="tpu_custom_call" | custom-call | tf_op jit(solution)/shard_map/conv_piece/pallas_call | solution.py:308
  10.0 1.2 %conv_piece.4.refs_5_ = f32[10,6,8,384]{3,2,1,0:T(8,128)S(1)} custom-call(bf16[4,48,352]{2,1,0:T(8,128)(2,1)S(1)} %collective-permute-done.2.piece.refs_1_, f32[49,384]{1,0:T(8,128)S(1)} %copy-done.1, f32[4,384]{1,0:T(4,128)S(1)} %copy-done.4), custom_call_target="tpu_custom_call" | custom-call | tf_op jit(solution)/shard_map/conv_piece/pallas_call | solution.py:308
  11.2 1.2 %conv_piece.5.refs_6_ = f32[10,6,8,384]{3,2,1,0:T(8,128)S(1)} custom-call(bf16[4,48,352]{2,1,0:T(8,128)(2,1)S(1)} %collective-permute-done.3.piece.refs_2_, f32[49,384]{1,0:T(8,128)S(1)} %copy-done.1, f32[4,384]{1,0:T(4,128)S(1)} %copy-done.4), custom_call_target="tpu_custom_call" | custom-call | tf_op jit(solution)/shard_map/conv_piece/pallas_call | solution.py:308
  12.4 3.1 %last_piece.1 = (bf16[16,48,352]{2,1,0:T(8,128)(2,1)S(1)}, bf16[768,352]{1,0:T(8,128)(2,1)S(1)}) custom-call(s32[5]{0:T(128)S(1)} %copy-done.5, bf16[4,48,352]{2,1,0:T(8,128)(2,1)S(1)} %copy-done.3, bf16[4,48,352]{2,1,0:T(8,128)(2,1)S(1)} %collective-permute-done.2.piece.refs_1_, bf16[4,48,352]{2,1,0:T(8,128)(2,1)S(1)} %collective-permute-done.3.piece.refs_2_, ...), custom_call_target="tpu_custom_call" | custom-call | tf_op jit(solution)/shard_map/last_piece/pallas_call | solution.py:324
  15.7 0.7 collective-permute-start.7
  16.4 2.1 %collective-permute-start.5 = (bf16[352,704]{1,0:T(8,128)(2,1)S(1)}, bf16[352,704]{1,0:T(8,128)(2,1)S(1)}, u32[]{:S(2)}, u32[]{:S(2)}) collective-permute-start(bf16[352,704]{1,0:T(8,128)(2,1)S(1)} %bitcast.18), channel_id=1, source_target_pairs={{8,9},{9,8},{24,25},{25,24},{10,11},{11,10},{26,27},{27,26},{12,13... | collective-permute-start | bytes 1486856 | tf_op jit(solution)/shard_map/ppermute | solution.py:416
  18.5 3.1 %collective-permute-start.6 = (bf16[704,352]{1,0:T(8,128)(2,1)S(1)}, bf16[704,352]{1,0:T(8,128)(2,1)S(1)}, u32[]{:S(2)}, u32[]{:S(2)}) collective-permute-start(bf16[704,352]{1,0:T(8,128)(2,1)S(1)} %bitcast.24), channel_id=1, source_target_pairs={{8,9},{9,8},{24,25},{25,24},{10,11},{11,10},{26,27},{27,26},{12,13... | collective-permute-start | bytes 1486856 | tf_op jit(solution)/shard_map/ppermute | solution.py:416
  21.7 4.8 %collective-permute-done.5.refs_1_ = bf16[352,704]{1,0:T(8,128)(2,1)S(1)} collective-permute-done((bf16[352,704]{1,0:T(8,128)(2,1)S(1)}, bf16[352,704]{1,0:T(8,128)(2,1)S(1)}, u32[]{:S(2)}, u32[]{:S(2)}) %collective-permute-start.5) | collective-permute-done | bytes 495648 | tf_op jit(solution)/shard_map/ppermute | solution.py:416
  26.5 5.8 %collective-permute-done.6.refs_3_ = bf16[704,352]{1,0:T(8,128)(2,1)S(1)} collective-permute-done((bf16[704,352]{1,0:T(8,128)(2,1)S(1)}, bf16[704,352]{1,0:T(8,128)(2,1)S(1)}, u32[]{:S(2)}, u32[]{:S(2)}) %collective-permute-start.6) | collective-permute-done | bytes 495648 | tf_op jit(solution)/shard_map/ppermute | solution.py:416
  32.3 0.8 copy-done.8
  33.1 0.8 copy-done.10
  33.9 0.7 collective-permute-start.8
  34.7 1.3 %collective-permute-start.9 = (bf16[16,48,352]{2,1,0:T(8,128)(2,1)S(1)}, bf16[16,48,352]{2,1,0:T(8,128)(2,1)S(1)}, u32[]{:S(2)}, u32[]{:S(2)}) collective-permute-start(bf16[16,48,352]{2,1,0:T(8,128)(2,1)S(1)} %block.2.refs_4_), channel_id=1, source_target_pairs={{16,24},{17,25},{18,26},{19,27},{20,28},{21,29},{22,30},{23,31}} | collective-permute-start | bytes 1622024 | tf_op jit(solution)/shard_map/ppermute | solution.py:436
  36.0 36.7 %collective-permute-done.9.x = bf16[16,48,352]{2,1,0:T(8,128)(2,1)S(1)} collective-permute-done((bf16[16,48,352]{2,1,0:T(8,128)(2,1)S(1)}, bf16[16,48,352]{2,1,0:T(8,128)(2,1)S(1)}, u32[]{:S(2)}, u32[]{:S(2)}) %collective-permute-start.9) | collective-permute-done | bytes 540704 | tf_op jit(solution)/shard_map/ppermute | solution.py:436
  72.7 1.0 %copy-done.9 = bf16[352,704]{1,0:T(8,128)(2,1)S(1)} copy-done((bf16[352,704]{1,0:T(8,128)(2,1)S(1)}, bf16[352,704]{1,0:T(8,128)(2,1)}, u32[]{:S(2)}) %copy-start.9) | copy-done | bytes 495640
  73.8 1.0 %copy-done.11 = bf16[704,352]{1,0:T(8,128)(2,1)S(1)} copy-done((bf16[704,352]{1,0:T(8,128)(2,1)S(1)}, bf16[704,352]{1,0:T(8,128)(2,1)}, u32[]{:S(2)}) %copy-start.11) | copy-done | bytes 495640
  74.8 10.1 %block.3 = bf16[16,48,352]{2,1,0:T(8,128)(2,1)S(1)} custom-call(s32[1]{0:T(128)} %bitcast.section, bf16[16,48,352]{2,1,0:T(8,128)(2,1)S(1)} %collective-permute-done.9.x, f32[49,384]{1,0:T(8,128)S(1)} %copy-done.1, f32[4,384]{1,0:T(4,128)S(1)} %copy-done.4, f32[2,3,704]{2,1,0:T(4,128)S(1)} %copy-done.12, bf16[352,704]{1,0:T(8,128)(2,1)S(1)} %bitcast.21, ...), custom_call_target="tpu_custom_call" | custom-call | flops 1522532352 | bytes 3063808 | tf_op jit(solution)/shard_map/block/pallas_call | solution.py:371
  85.1 2.2 %collective-permute-start.11 = (bf16[4,48,352]{2,1,0:T(8,128)(2,1)S(1)}, bf16[4,48,352]{2,1,0:T(8,128)(2,1)S(1)}, u32[]{:S(2)}, u32[]{:S(2)}) collective-permute-start(bf16[4,48,352]{2,1,0:T(8,128)(2,1)S(1)} %get-tuple-element.30), channel_id=1, source_target_pairs={{0,6},{2,4},{4,2},{6,0},{1,7},{3,5},{5,3},{7,1},{8,14},{10,12},{12... | collective-permute-start | bytes 405512 | tf_op jit(solution)/shard_map/ppermute | solution.py:455
  87.8 5.3 %collective-permute-done.10 = bf16[4,48,352]{2,1,0:T(8,128)(2,1)S(1)} collective-permute-done((bf16[4,48,352]{2,1,0:T(8,128)(2,1)S(1)}, bf16[4,48,352]{2,1,0:T(8,128)(2,1)S(1)}, u32[]{:S(2)}, u32[]{:S(2)}) %collective-permute-start.10) | collective-permute-done | bytes 135200 | tf_op jit(solution)/shard_map/ppermute | solution.py:455
  93.2 1.2 %collective-permute-done.12 = bf16[4,48,352]{2,1,0:T(8,128)(2,1)S(1)} collective-permute-done((bf16[4,48,352]{2,1,0:T(8,128)(2,1)S(1)}, bf16[4,48,352]{2,1,0:T(8,128)(2,1)S(1)}, u32[]{:S(2)}, u32[]{:S(2)}) %collective-permute-start.12) | collective-permute-done | bytes 135200 | tf_op jit(solution)/shard_map/ppermute | solution.py:455
  (47 shorter events, 4.9 us)
Async XLA Ops:
  0.0 15.5 %collective-permute-start = (bf16[352,704]{1,0:T(8,128)(2,1)}, bf16[352,704]{1,0:T(8,128)(2,1)S(1)}, u32[]{:S(2)}, u32[]{:S(2)}) collective-permute-start(bf16[352,704]{1,0:T(8,128)(2,1)} %bitcast.16), channel_id=1, source_target_pairs={{0,1},{1,0},{16,17},{17,16},{2,3},{3,2},{18,19},{19,18},{4,5},{5,4... | collective-permute-start | bytes 1486856 | tf_op jit(solution)/shard_map/ppermute | solution.py:416
  0.7 14.9 %collective-permute-start.1 = (bf16[704,352]{1,0:T(8,128)(2,1)}, bf16[704,352]{1,0:T(8,128)(2,1)S(1)}, u32[]{:S(2)}, u32[]{:S(2)}) collective-permute-start(bf16[704,352]{1,0:T(8,128)(2,1)} %bitcast.22), channel_id=1, source_target_pairs={{0,1},{1,0},{16,17},{17,16},{2,3},{3,2},{18,19},{19,18},{4,5},{5,4... | collective-permute-start | bytes 1486856 | tf_op jit(solution)/shard_map/ppermute | solution.py:416
  4.9 5.0 %collective-permute-start.2 = (bf16[4,48,352]{2,1,0:T(8,128)(2,1)}, bf16[4,48,352]{2,1,0:T(8,128)(2,1)S(1)}, u32[]{:S(2)}, u32[]{:S(2)}) collective-permute-start(bf16[4,48,352]{2,1,0:T(8,128)(2,1)} %get-tuple-element.18), channel_id=1, source_target_pairs={{12,0},{14,2},{8,4},{10,6},{13,1},{15,3},{9,5},{11,7}} | collective-permute-start | bytes 405512 | tf_op jit(solution)/shard_map/ppermute | solution.py:413
  5.6 5.6 %collective-permute-start.3 = (bf16[4,48,352]{2,1,0:T(8,128)(2,1)}, bf16[4,48,352]{2,1,0:T(8,128)(2,1)S(1)}, u32[]{:S(2)}, u32[]{:S(2)}) collective-permute-start(bf16[4,48,352]{2,1,0:T(8,128)(2,1)} %get-tuple-element.19), channel_id=1, source_target_pairs={{14,0},{12,2},{10,4},{8,6},{15,1},{13,3},{11,5},{9,7}} | collective-permute-start | bytes 405512 | tf_op jit(solution)/shard_map/ppermute | solution.py:413
  6.3 6.1 %collective-permute-start.4 = (bf16[4,48,352]{2,1,0:T(8,128)(2,1)}, bf16[4,48,352]{2,1,0:T(8,128)(2,1)S(1)}, u32[]{:S(2)}, u32[]{:S(2)}) collective-permute-start(bf16[4,48,352]{2,1,0:T(8,128)(2,1)} %get-tuple-element.20), channel_id=1, source_target_pairs={{10,0},{8,2},{14,4},{12,6},{11,1},{9,3},{15,5},{13,7}} | collective-permute-start | bytes 405512 | tf_op jit(solution)/shard_map/ppermute | solution.py:413
  7.0 0.9 copy-start
  7.9 0.9 copy-start.2
  8.8 1.2 %copy-start.1 = (f32[49,384]{1,0:T(8,128)S(1)}, f32[49,384]{1,0:T(8,128)}, u32[]{:S(2)}) copy-start(f32[49,384]{1,0:T(8,128)} %get-tuple-element.21.taps.refs_7_) | copy-start | bytes 225796
  11.2 1.3 %copy-start.3 = (bf16[4,48,352]{2,1,0:T(8,128)(2,1)S(1)}, bf16[4,48,352]{2,1,0:T(8,128)(2,1)}, u32[]{:S(2)}) copy-start(bf16[4,48,352]{2,1,0:T(8,128)(2,1)} %get-tuple-element.17.piece.refs_0_) | copy-start | bytes 405508
  11.2 1.2 %copy-start.5 = (s32[5]{0:T(128)S(1)}, s32[5]{0:T(128)}, u32[]{:S(2)}) copy-start(s32[5]{0:T(128)} %stack.23.index) | copy-start | bytes 64
  12.4 3.2 %copy-start.6 = (bf16[1,352,704]{2,1,0:T(8,128)(2,1)S(1)}, bf16[1,352,704]{2,1,0:T(8,128)(2,1)}, u32[]{:S(2)}) copy-start(bf16[1,352,704]{2,1,0:T(8,128)(2,1)} %param.16) | copy-start | bytes 1486852
  12.4 3.2 %copy-start.7 = (bf16[1,704,352]{2,1,0:T(8,128)(2,1)S(1)}, bf16[1,704,352]{2,1,0:T(8,128)(2,1)}, u32[]{:S(2)}) copy-start(bf16[1,704,352]{2,1,0:T(8,128)(2,1)} %param.20) | copy-start | bytes 1486852
  12.4 3.2 %copy-start.12 = (f32[2,3,704]{2,1,0:T(4,128)S(1)}, f32[2,3,704]{2,1,0:T(4,128)}, u32[]{:S(2)}) copy-start(f32[2,3,704]{2,1,0:T(4,128)} %get-tuple-element.25.refs_7_.fvec) | copy-start | bytes 50692
  15.7 6.0 %collective-permute-start.7 = (bf16[16,48,352]{2,1,0:T(8,128)(2,1)S(1)}, bf16[16,48,352]{2,1,0:T(8,128)(2,1)S(1)}, u32[]{:S(2)}, u32[]{:S(2)}) collective-permute-start(bf16[16,48,352]{2,1,0:T(8,128)(2,1)S(1)} %mlp.2.refs_8_), channel_id=1, source_target_pairs={{0,8},{1,9},{2,10},{3,11},{4,12},{5,13},{6,14},{7,15}} | collective-permute-start | bytes 1622024 | tf_op jit(solution)/shard_map/ppermute | solution.py:436
  16.4 10.1 %collective-permute-start.5 = (bf16[352,704]{1,0:T(8,128)(2,1)S(1)}, bf16[352,704]{1,0:T(8,128)(2,1)S(1)}, u32[]{:S(2)}, u32[]{:S(2)}) collective-permute-start(bf16[352,704]{1,0:T(8,128)(2,1)S(1)} %bitcast.18), channel_id=1, source_target_pairs={{8,9},{9,8},{24,25},{25,24},{10,11},{11,10},{26,27},{27,26},{12,13... | collective-permute-start | bytes 1486856 | tf_op jit(solution)/shard_map/ppermute | solution.py:416
  18.5 13.8 %collective-permute-start.6 = (bf16[704,352]{1,0:T(8,128)(2,1)S(1)}, bf16[704,352]{1,0:T(8,128)(2,1)S(1)}, u32[]{:S(2)}, u32[]{:S(2)}) collective-permute-start(bf16[704,352]{1,0:T(8,128)(2,1)S(1)} %bitcast.24), channel_id=1, source_target_pairs={{8,9},{9,8},{24,25},{25,24},{10,11},{11,10},{26,27},{27,26},{12,13... | collective-permute-start | bytes 1486856 | tf_op jit(solution)/shard_map/ppermute | solution.py:416
  33.9 0.7 collective-permute-start.8
  34.7 38.0 %collective-permute-start.9 = (bf16[16,48,352]{2,1,0:T(8,128)(2,1)S(1)}, bf16[16,48,352]{2,1,0:T(8,128)(2,1)S(1)}, u32[]{:S(2)}, u32[]{:S(2)}) collective-permute-start(bf16[16,48,352]{2,1,0:T(8,128)(2,1)S(1)} %block.2.refs_4_), channel_id=1, source_target_pairs={{16,24},{17,25},{18,26},{19,27},{20,28},{21,29},{22,30},{23,31}} | collective-permute-start | bytes 1622024 | tf_op jit(solution)/shard_map/ppermute | solution.py:436
  72.7 1.0 %copy-start.9 = (bf16[352,704]{1,0:T(8,128)(2,1)S(1)}, bf16[352,704]{1,0:T(8,128)(2,1)}, u32[]{:S(2)}) copy-start(bf16[352,704]{1,0:T(8,128)(2,1)} %copy-done.8) | copy-start | bytes 1486852
  73.8 1.0 %copy-start.11 = (bf16[704,352]{1,0:T(8,128)(2,1)S(1)}, bf16[704,352]{1,0:T(8,128)(2,1)}, u32[]{:S(2)}) copy-start(bf16[704,352]{1,0:T(8,128)(2,1)} %copy-done.10) | copy-start | bytes 1486852
  85.0 8.1 %collective-permute-start.10 = (bf16[4,48,352]{2,1,0:T(8,128)(2,1)S(1)}, bf16[4,48,352]{2,1,0:T(8,128)(2,1)S(1)}, u32[]{:S(2)}, u32[]{:S(2)}) collective-permute-start(bf16[4,48,352]{2,1,0:T(8,128)(2,1)S(1)} %get-tuple-element.31), channel_id=1, source_target_pairs={{0,4},{2,6},{4,0},{6,2},{1,5},{3,7},{5,1},{7,3},{8,12},{10,14},{12... | collective-permute-start | bytes 405512 | tf_op jit(solution)/shard_map/ppermute | solution.py:455
  85.1 8.1 %collective-permute-start.11 = (bf16[4,48,352]{2,1,0:T(8,128)(2,1)S(1)}, bf16[4,48,352]{2,1,0:T(8,128)(2,1)S(1)}, u32[]{:S(2)}, u32[]{:S(2)}) collective-permute-start(bf16[4,48,352]{2,1,0:T(8,128)(2,1)S(1)} %get-tuple-element.30), channel_id=1, source_target_pairs={{0,6},{2,4},{4,2},{6,0},{1,7},{3,5},{5,3},{7,1},{8,14},{10,12},{12... | collective-permute-start | bytes 405512 | tf_op jit(solution)/shard_map/ppermute | solution.py:455
  87.3 7.1 %collective-permute-start.12 = (bf16[4,48,352]{2,1,0:T(8,128)(2,1)S(1)}, bf16[4,48,352]{2,1,0:T(8,128)(2,1)S(1)}, u32[]{:S(2)}, u32[]{:S(2)}) collective-permute-start(bf16[4,48,352]{2,1,0:T(8,128)(2,1)S(1)} %get-tuple-element.29), channel_id=1, source_target_pairs={{0,2},{2,0},{4,6},{6,4},{1,3},{3,1},{5,7},{7,5},{8,10},{10,8},{12,... | collective-permute-start | bytes 405512 | tf_op jit(solution)/shard_map/ppermute | solution.py:455
  93.2 1.2 %copy-start.13 = (bf16[1,4,1,4,48,352]{5,4,3,2,1,0:T(8,128)(2,1)}, bf16[1,4,1,4,48,352]{5,4,3,2,1,0:T(8,128)(2,1)S(1)}, u32[]{:S(2)}) copy-start(bf16[1,4,1,4,48,352]{5,4,3,2,1,0:T(8,128)(2,1)S(1)} %bitcast_dynamic-update-slice_fusion.1) | copy-start | bytes 1622020
  (3 other events, 2.3 us)

commit v2 on v1

v2 whole, which is shorter than its diff:
```python
import functools

import jax
import jax.numpy as jnp
from jax import lax
from jax.experimental import pallas as pl
from jax.experimental.pallas import tpu as pltpu
from jax.sharding import PartitionSpec as P

EPS_NORM = 1e-06
EPS_GRN = 1e-06
LANES = 128
VMEM_BYTES = 20 * 1024 * 1024
REACH = 3
CHUNK = 4
NORM_ROWS = 4


def fill_columns(xp, xs, x, channels):
    height, reach_cols, blocks, lanes = xs.shape
    stride = reach_cols - 2 * REACH
    width = stride * blocks
    groups = lanes // LANES
    xp[...] = jnp.zeros(xp.shape, jnp.float32)

    def rows(n, carry):
        for k in range(2):
            r = 2 * n + k
            row = x[r].astype(jnp.float32)
            for g in range(groups):
                at = slice(g * LANES, (g + 1) * LANES)
                own = row[:, g * LANES : min((g + 1) * LANES, channels)]
                xp[k * groups + g, 8 : 8 + width, 0 : own.shape[1]] = own
                for q in range(reach_cols):
                    near = pl.ds(8 - REACH + q, blocks, stride=stride)
                    xs[r, q, :, at] = xp[k * groups + g, near, :]
        return carry

    lax.fori_loop(0, height // 2, rows, 0)


def conv(xs, taps, cvec, cq):
    rows = xs.shape[0]
    height, stride, blocks, lanes = cq.shape
    span = 2 * REACH + 1
    above = (height - rows) // 2

    def group(g, carry):
        at = pl.ds(pl.multiple_of(g * LANES, LANES), LANES)

        def column(q, carry):
            bias = jnp.broadcast_to(cvec[0:1, at], (blocks, LANES))
            acc = [None if above else bias] * height
            for j in range(span):
                kern = [
                    jnp.broadcast_to(taps[i * span + j : i * span + j + 1, at], (blocks, LANES))
                    for i in range(span)
                ]
                for r in range(rows):
                    x_row = xs[r, q + j, :, at]
                    for i in range(span):
                        h = r + above + REACH - i
                        if 0 <= h < height:
                            term = kern[i] * x_row
                            acc[h] = term if acc[h] is None else acc[h] + term
            for h in range(height):
                cq[h, q, :, at] = acc[h]
            return carry

        return lax.fori_loop(0, stride, column, carry)

    lax.fori_loop(0, lanes // LANES, group, 0)


def norm(cq, cvec, xp, flat, skip=0):
    padded, stride, blocks, lanes = cq.shape
    height = padded - 2 * skip
    channels = flat.shape[1]
    width = stride * blocks
    groups = lanes // LANES
    inside = lax.broadcasted_iota(jnp.int32, (blocks, lanes), 1) < channels

    def rows(n, carry):
        for k in range(NORM_ROWS):
            h = NORM_ROWS * n + k
            for q in range(stride):
                v = cq[h + skip, q]
                mean = jnp.sum(v, axis=-1, keepdims=True) * (1.0 / channels)
                c = jnp.where(inside, v - mean, 0.0)
                var = jnp.sum(c * c, axis=-1, keepdims=True) * (1.0 / channels)
                c = c * lax.rsqrt(var + EPS_NORM) * cvec[1:2, :] + cvec[2:3, :]
                for g in range(groups):
                    at = slice(g * LANES, (g + 1) * LANES)
                    xp[k * groups + g, pl.ds(q, blocks, stride=stride), :] = c[:, at]
            at_cell = pl.ds(pl.multiple_of(h * width, width), width)
            for g in range(groups):
                at = slice(g * LANES, min((g + 1) * LANES, channels))
                flat[at_cell, at] = xp[k * groups + g, 0:width, 0 : at.stop - at.start].astype(
                    jnp.bfloat16
                )
        return carry

    lax.fori_loop(0, height // NORM_ROWS, rows, 0)


def conv_norm(x, taps, cvec, flat, xp, xs, cq):
    fill_columns(xp, xs, x, x.shape[2])
    conv(xs, taps, cvec, cq)
    norm(cq, cvec, xp, flat)


def conv_scratch(rows, out_rows, width, lanes):
    return [
        pltpu.VMEM((NORM_ROWS * lanes // LANES, width + 16, LANES), jnp.float32),
        pltpu.VMEM((rows, width // 8 + 2 * REACH, 8, lanes), jnp.float32),
        pltpu.VMEM((out_rows, width // 8, 8, lanes), jnp.float32),
    ]


def gelu(v):
    return 0.5 * v * (1.0 + lax.erf(v * (0.5**0.5)))


def up(flat, w_in, bias, act, ssq):
    cells = flat.shape[0]
    half = w_in.shape[1]
    step = 2 * LANES

    def units(start, count):
        raised = jnp.dot(
            flat[...], w_in[:, pl.ds(start, count)], preferred_element_type=jnp.float32
        )
        active = gelu(raised + bias[0:1, pl.ds(start, count)]).astype(jnp.bfloat16)
        act[:, pl.ds(start, count)] = active
        wide = active.astype(jnp.float32)
        ssq[:, pl.ds(start, count)] = jnp.sum((wide * wide).reshape(cells // 8, 8, count), axis=0)

    def full(n, carry):
        units(pl.multiple_of(n * step, step), step)
        return carry

    whole = half // step
    lax.fori_loop(0, whole, full, 0)
    if half % step:
        units(whole * step, half % step)


def norm_scale(ssqs, fvec, scale):
    half = fvec.shape[2]
    magnitude = [jnp.sqrt(jnp.sum(ssq[...], axis=0, keepdims=True)) for ssq in ssqs]
    mean = jnp.sum(magnitude[0] + magnitude[1], axis=1, keepdims=True) * (0.5 / half)
    for which in range(2):
        ratio = magnitude[which] / (mean + EPS_GRN)
        scale[which] = fvec[which, 1:2, :] * ratio + 1.0


def down(x_rows, first_row, acts, outs, scale, fvec, cvec):
    _, width, channels = x_rows.shape
    cells = CHUNK * width
    at = pl.ds(pl.multiple_of(first_row * width, cells), cells)
    update = cvec[3:4, 0:channels]
    for which in range(2):
        a = acts[which][at, :].astype(jnp.float32)
        hidden = (a * scale[which] + fvec[which, 2:3, :]).astype(jnp.bfloat16)
        update = update + jnp.dot(hidden, outs[which][...], preferred_element_type=jnp.float32)
    return (x_rows.astype(jnp.float32) + update.reshape(CHUNK, width, channels)).astype(
        jnp.bfloat16
    )


def down_all(x, acts, outs, scale, fvec, cvec, out):
    def rows(n, carry):
        at = pl.ds(n * CHUNK, CHUNK)
        out[at] = down(x[at], n * CHUNK, acts, outs, scale, fvec, cvec)
        return carry

    lax.fori_loop(0, x.shape[0] // CHUNK, rows, 0)


def prepare_kernel(part, kernel, *refs):
    vectors, (taps, cvec, fvec), (held, *staged), sems = refs[:7], refs[7:10], refs[10:-1], refs[-1]
    moves = [(kernel, held), *zip(vectors, staged)]
    copies = [pltpu.make_async_copy(a, b, sems.at[n]) for n, (a, b) in enumerate(moves)]
    for copy in copies:
        copy.start()
    taps[...] = jnp.zeros(taps.shape, jnp.float32)
    cvec[...] = jnp.zeros(cvec.shape, jnp.float32)
    for copy in copies:
        copy.wait()
    channels = kernel.shape[3]
    span = kernel.shape[1]
    half = fvec.shape[2]
    for i in range(span):
        taps[i * span : (i + 1) * span, 0:channels] = held[0, i].astype(jnp.float32)
    for n in range(4):
        cvec[n : n + 1, 0:channels] = staged[n][...].astype(jnp.float32)
    first = part[0] == 0
    for n in range(3):
        v = staged[4 + n][...].astype(jnp.float32)
        low, high = v[:, 0:half], v[:, half:]
        fvec[0, n : n + 1, :] = jnp.where(first, low, high)
        fvec[1, n : n + 1, :] = jnp.where(first, high, low)


def piece_kernel(section, piece, taps, cvec, part, xp, xs, *, tick):
    @pl.when(jnp.logical_or(tick == 0, section[0] == tick))
    def _():
        fill_columns(xp, xs, piece, piece.shape[2])
        conv(xs, taps, cvec, part)


def last_piece_kernel(section, index, *refs, count, tick):
    pieces, parts = refs[:count], refs[count : 2 * count - 1]
    taps, cvec, x, flat, xp, xs, own, cq = refs[2 * count - 1 :]
    rows = pieces[0].shape[0]

    @pl.when(jnp.logical_or(tick == 0, section[0] == tick))
    def _():
        cq[...] = jnp.broadcast_to(cvec[0:1, :].reshape(1, 1, 1, cq.shape[3]), cq.shape)
        fill_columns(xp, xs, pieces[-1], x.shape[2])
        conv(xs, taps, cvec, own)
        for n, (piece, part) in enumerate(zip(pieces, (*parts, own))):
            at = index[n] * rows
            x[pl.ds(at, rows)] = piece[...]
            cq[pl.ds(at, rows + 2 * REACH)] += part[...]
        norm(cq, cvec, xp, flat, REACH)


def conv_kernel(section, x, taps, cvec, flat, xp, xs, cq, *, tick):
    @pl.when(section[0] == tick)
    def _():
        conv_norm(x, taps, cvec, flat, xp, xs, cq)


def up_first_kernel(section, flat, w_in, fvec, act, ssq, *, tick):
    @pl.when(section[0] == tick)
    def _():
        up(flat, w_in, fvec.at[0], act, ssq)


def up_second_kernel(section, flat, w_in, fvec, other, act, scale, ssq, *, tick):
    @pl.when(section[0] == tick)
    def _():
        up(flat, w_in, fvec.at[1], act, ssq)
        norm_scale((other, ssq), fvec, scale)


def first_down_kernel(section, x, act_a, act_b, out_a, out_b, scale, fvec, cvec, out):
    @pl.when(section[0] == 0)
    def _():
        down_all(x, (act_a, act_b), (out_a, out_b), scale, fvec, cvec, out)


def down_piece_kernel(
    section, index, x, act_a, act_b, out_a, out_b, scale, fvec, cvec, prev, out, *, tick, n
):
    first_row = index[n] * CHUNK
    at = pl.ds(first_row, CHUNK)

    @pl.when(section[0] == tick)
    def _():
        out[...] = down(x[at], first_row, (act_a, act_b), (out_a, out_b), scale, fvec, cvec)

    @pl.when(section[0] != tick)
    def _():
        out[...] = prev[at]


def mlp_kernel(section, x, flat, in_a, in_b, out_a, out_b, fvec, cvec, *refs, tick):
    *pieces, prev, out, act_a, act_b, ssq_a, ssq_b, scale = refs

    @pl.when(section[0] == tick)
    def _():
        up(flat, in_a, fvec.at[0], act_a, ssq_a)
        up(flat, in_b, fvec.at[1], act_b, ssq_b)
        norm_scale((ssq_a, ssq_b), fvec, scale)
        down_all(x, (act_a, act_b), (out_a, out_b), scale, fvec, cvec, out)

    @pl.when(section[0] == tick - 1)
    def _():
        for n, piece in enumerate(pieces):
            out[n * CHUNK : (n + 1) * CHUNK] = piece[...]

    @pl.when(section[0] < tick - 1)
    def _():
        out[...] = prev[...]


def conv_up_kernel(section, x, taps, cvec, in_a, in_b, fvec, *refs, tick):
    act_a, act_b, scale, xp, xs, cq, flat, ssq_a, ssq_b = refs

    @pl.when(section[0] == tick)
    def _():
        conv_norm(x, taps, cvec, flat, xp, xs, cq)
        up(flat, in_a, fvec.at[0], act_a, ssq_a)
        up(flat, in_b, fvec.at[1], act_b, ssq_b)
        norm_scale((ssq_a, ssq_b), fvec, scale)


def place_kernel(index, *refs):
    *pieces, saved, sems = refs
    copies = [
        pltpu.make_async_copy(piece, saved.at[0, index[n], 0], sems.at[n])
        for n, piece in enumerate(pieces)
    ]
    for copy in copies:
        copy.start()
    for copy in copies:
        copy.wait()


SMEM = pl.BlockSpec(memory_space=pltpu.SMEM)
VMEM = pl.BlockSpec(memory_space=pltpu.VMEM)
HBM = pl.BlockSpec(memory_space=pltpu.HBM)


def call(kernel, name, args, out, specs=None, out_specs=None, scratch=(), flops=0, **static):
    if specs is None:
        specs = [SMEM if a.dtype == jnp.int32 else VMEM for a in args]
    if out_specs is None:
        out_specs = jax.tree.map(lambda _: VMEM, out)
    moved = sum(a.size * a.dtype.itemsize for a in args)
    return pl.pallas_call(
        functools.partial(kernel, **static),
        out_shape=out,
        in_specs=specs,
        out_specs=out_specs,
        scratch_shapes=list(scratch),
        compiler_params=pltpu.CompilerParams(vmem_limit_bytes=VMEM_BYTES),
        cost_estimate=pl.CostEstimate(flops=flops, bytes_accessed=moved, transcendentals=0),
        name=name,
    )(*args)


def shape(*dims, dtype=jnp.float32):
    return jax.ShapeDtypeStruct(dims, dtype)


def ssq_scratch(half):
    return pltpu.VMEM((8, half), jnp.float32)


def image_plan(
    inputs,
    depth_kernel,
    depth_bias,
    norm_gain,
    norm_bias,
    proj_in,
    bias_in,
    grn_gamma,
    grn_beta,
    proj_out,
    bias_out,
):
    sections = lax.axis_size("section")
    count = lax.axis_size("row")
    me = lax.axis_index("row").astype(jnp.int32)
    section = lax.axis_index("section").astype(jnp.int32).reshape(1)
    part = lax.axis_index("dp").astype(jnp.int32).reshape(1)
    _, _, rows, width, channels = inputs.shape
    height = rows * count
    cells = height * width
    lanes = -(-channels // LANES) * LANES
    half = proj_in.shape[2]
    span = depth_kernel.shape[1]
    order = (0, 2, 3, 1)
    index = jnp.stack([me ^ by for by in order])
    in_order = jnp.arange(count, dtype=jnp.int32)
    bf16 = jnp.bfloat16
    whole = shape(height, width, channels, dtype=bf16)
    flat_shape = shape(cells, channels, dtype=bf16)
    piece_shape = shape(rows, width, channels, dtype=bf16)
    act_shape = shape(cells, half, dtype=bf16)
    scale_shape = shape(2, 1, half)
    matmul = 2 * cells * channels * half

    pieces = []
    for by in order:
        piece = lax.dynamic_index_in_dim(inputs, me ^ by, 0, keepdims=False)[0]
        if by:
            pairs = [(count + (p ^ by), p) for p in range(count)]
            piece = lax.ppermute(piece, ("section", "row"), pairs)
        pieces.append(piece)

    def other_half(x, which):
        pairs = [(2 * s + p, 2 * s + 1 - p) for s in which for p in range(2)]
        return lax.ppermute(x, ("section", "dp"), pairs)

    w_in, w_out = proj_in[0], proj_out[0]
    even = range(0, sections, 2)
    odd = range(1, sections, 2)
    other_in = other_half(w_in, even)
    other_out = other_half(w_out, even)

    held = (
        depth_kernel, depth_bias, norm_gain, norm_bias, bias_out, bias_in, grn_gamma, grn_beta
    )
    taps, cvec, fvec = call(
        prepare_kernel,
        "prepare",
        (part, *held),
        (shape(span * span, lanes), shape(4, lanes), shape(2, 3, half)),
        specs=[SMEM] + [HBM] * len(held),
        scratch=[pltpu.VMEM(v.shape, v.dtype) for v in held]
        + [pltpu.SemaphoreType.DMA((len(held),))],
    )

    def conv_pieces(pieces, at, tick):
        out_rows = rows + 2 * REACH
        scratch = conv_scratch(rows, out_rows, width, lanes)
        parts = []
        for piece in pieces[:-1]:
            if parts:
                piece, parts[-1] = lax.optimization_barrier((piece, parts[-1]))
            part = call(
                piece_kernel,
                "conv_piece",
                (section, piece, taps, cvec),
                shape(out_rows, width // 8, 8, lanes),
                scratch=scratch[:2],
                tick=tick,
            )
            parts.append(part)
        return call(
            last_piece_kernel,
            "last_piece",
            (section, at, *pieces, *parts, taps, cvec),
            (whole, flat_shape),
            scratch=scratch + [conv_scratch(1, height + 2 * REACH, width, lanes)[2]],
            count=count,
            tick=tick,
        )

    def up_halves(flat, other_in, tick):
        act_a, ssq = call(
            up_first_kernel,
            "up_own",
            (section, flat, w_in, fvec),
            (act_shape, shape(8, half)),
            flops=matmul,
            tick=tick,
        )
        act_b, scale = call(
            up_second_kernel,
            "up_other",
            (section, flat, other_in, fvec, ssq),
            (act_shape, scale_shape),
            scratch=[ssq_scratch(half)],
            flops=matmul,
            tick=tick,
        )
        return act_a, act_b, scale

    def down_piece(x, acts, other_out, prev, at, tick, n):
        act_a, act_b, scale = acts
        return call(
            down_piece_kernel,
            "down_piece",
            (section, at, x, act_a, act_b, w_out, other_out, scale, fvec, cvec, prev),
            piece_shape,
            flops=2 * matmul // count,
            tick=tick,
            n=n,
        )

    def pass_on(x, tick):
        return lax.ppermute(x, "section", [(tick - 1, tick)])

    x, flat = conv_pieces(pieces, index, 0)
    act_a, act_b, scale = up_halves(flat, other_in, 0)
    result = call(
        first_down_kernel,
        "down",
        (section, x, act_a, act_b, w_out, other_out, scale, fvec, cvec),
        whole,
        flops=2 * matmul,
    )
    x = pass_on(result, 1)
    late_in, late_out, result = lax.optimization_barrier((w_in, w_out, result))
    odd_in = other_half(late_in, odd)
    odd_out = other_half(late_out, odd)
    flat = call(
        conv_kernel,
        "conv",
        (section, x, taps, cvec),
        flat_shape,
        scratch=conv_scratch(height, height, width, lanes),
        tick=1,
    )
    acts = up_halves(flat, odd_in, 1)
    kept = [down_piece(x, acts, odd_out, result, in_order, 1, n) for n in range(count)]
    x, flat = conv_pieces([pass_on(piece, 2) for piece in kept], in_order, 2)
    result = call(
        mlp_kernel,
        "mlp",
        (section, x, flat, w_in, other_in, w_out, other_out, fvec, cvec, *kept, result),
        whole,
        scratch=[pltpu.VMEM((cells, half), bf16)] * 2
        + [ssq_scratch(half)] * 2
        + [pltpu.VMEM((2, 1, half), jnp.float32)],
        flops=4 * matmul,
        tick=2,
    )
    x = pass_on(result, 3)
    acts = call(
        conv_up_kernel,
        "conv_up",
        (section, x, taps, cvec, w_in, odd_in, fvec),
        (act_shape, act_shape, scale_shape),
        scratch=conv_scratch(height, height, width, lanes)
        + [pltpu.VMEM((cells, channels), bf16)]
        + [ssq_scratch(half)] * 2,
        flops=2 * matmul,
        tick=3,
    )
    done = []
    for n in (1, 2, 3, 0):
        piece = down_piece(x, acts, odd_out, result, index, 3, n)
        if n:
            piece = lax.ppermute(piece, "row", [(p, p ^ order[n]) for p in range(count)])
        done.append(piece)
    return call(
        place_kernel,
        "place",
        (index, done[3], *done[:3]),
        shape(1, count, 1, rows, width, channels, dtype=bf16),
        out_specs=HBM,
        scratch=[pltpu.SemaphoreType.DMA((count,))],
    )


def extended(cells, sides, width):
    for axis, dim in sides:
        count = lax.axis_size(axis)
        ends = count - 1
        head = lax.slice_in_dim(cells, 0, width, axis=dim)
        tail = lax.slice_in_dim(cells, cells.shape[dim] - width, cells.shape[dim], axis=dim)
        cells = jnp.concatenate(
            [
                lax.ppermute(tail, axis, [(i, (i + 1) % count) for i in range(ends)]),
                cells,
                lax.ppermute(head, axis, [((i + 1) % count, i) for i in range(ends)]),
            ],
            axis=dim,
        )
    return cells


def depthwise(padded, kernel, bias_term):
    channels = padded.shape[-1]
    conv_out = lax.conv_general_dilated(
        padded.astype(jnp.float32),
        kernel.astype(jnp.float32)[:, :, None, :],
        (1, 1),
        "VALID",
        dimension_numbers=("NHWC", "HWIO", "NHWC"),
        feature_group_count=channels,
        precision=lax.Precision.HIGHEST,
    )
    return conv_out + bias_term.astype(jnp.float32)


def conv_block(current, params):
    (
        depth_kernel,
        depth_bias,
        norm_gain,
        norm_bias,
        proj_in,
        bias_in,
        grn_gamma,
        grn_beta,
        proj_out,
        bias_out,
    ) = params
    num_items, num_rows, num_cols, channels = current.shape
    padded = extended(current, (("row", 1),), REACH)
    padded = jnp.pad(padded, ((0, 0), (0, 0), (REACH, REACH), (0, 0)))
    conv_out = depthwise(padded, depth_kernel, depth_bias)
    center = conv_out - jnp.mean(conv_out, axis=-1, keepdims=True)
    spread = jnp.mean(center * center, axis=-1, keepdims=True)
    normed = (
        center * lax.rsqrt(spread + EPS_NORM) * norm_gain.astype(jnp.float32)
        + norm_bias.astype(jnp.float32)
    ).astype(jnp.bfloat16)
    flat_rows = normed.reshape(num_items * num_rows * num_cols, channels)
    raised = jnp.dot(flat_rows, proj_in, preferred_element_type=jnp.float32) + bias_in.astype(
        jnp.float32
    )
    active = jax.nn.gelu(raised, approximate=False).astype(jnp.bfloat16)
    grouped = active.reshape(num_items, num_rows * num_cols, -1).astype(jnp.float32)
    local_sq = jnp.sum(grouped * grouped, axis=1)
    total_sq = lax.psum(local_sq, "row")
    magnitude = jnp.sqrt(total_sq)
    grn_ratio = magnitude / (jnp.mean(magnitude, axis=-1, keepdims=True) + EPS_GRN)
    hidden = (
        grn_gamma.astype(jnp.float32) * grouped * grn_ratio[:, None, :]
        + grn_beta.astype(jnp.float32)
        + grouped
    ).astype(jnp.bfloat16)
    update = jnp.dot(
        hidden.reshape(num_items * num_rows * num_cols, -1),
        proj_out,
        preferred_element_type=jnp.float32,
    ) + bias_out.astype(jnp.float32)
    return (
        current.astype(jnp.float32) + update.reshape(num_items, num_rows, num_cols, channels)
    ).astype(jnp.bfloat16)


def rows_plan(inputs, *weights):
    (
        depth_kernel,
        depth_bias,
        norm_gain,
        norm_bias,
        proj_in,
        bias_in,
        grn_gamma,
        grn_beta,
        proj_out,
        bias_out,
    ) = weights
    proj_in = lax.all_gather(proj_in, "dp", axis=2, tiled=True)
    proj_out = lax.all_gather(proj_out, "dp", axis=1, tiled=True)
    own_params = tuple(
        w[0]
        for w in (
            depth_kernel,
            depth_bias,
            norm_gain,
            norm_bias,
            proj_in,
            bias_in,
            grn_gamma,
            grn_beta,
            proj_out,
            bias_out,
        )
    )
    sections = lax.axis_size("section")
    section_index = lax.axis_index("section")
    num_micro = inputs.shape[0]
    num_ticks = num_micro + sections - 1
    arriving = jnp.zeros_like(inputs[0])
    saved = jnp.zeros_like(inputs)
    for tick_index in range(num_ticks):
        fresh_input = inputs[min(tick_index, num_micro - 1)]
        current = jnp.where(section_index == 0, fresh_input, arriving)
        produced = conv_block(current, own_params)
        slot_index = tick_index - section_index
        is_valid = jnp.logical_and(slot_index >= 0, slot_index < num_micro)
        safe_slot = jnp.clip(slot_index, 0, num_micro - 1)
        previous = lax.dynamic_index_in_dim(saved, safe_slot, 0, keepdims=False)
        saved = lax.dynamic_update_index_in_dim(
            saved, jnp.where(is_valid, produced, previous), safe_slot, 0
        )
        if tick_index + 1 < num_ticks:
            arriving = lax.ppermute(
                produced, "section", [(i, i + 1) for i in range(sections - 1)]
            )
    return saved[None]


def on_device(inputs, *weights):
    num_micro, images, local_rows, width, _ = inputs.shape
    one_image_each = (
        images == 1
        and lax.axis_size("row") == num_micro == 4
        and lax.axis_size("dp") == 2
        and lax.axis_size("section") == 4
        and local_rows % 4 == 0
        and width % 16 == 0
    )
    plan = image_plan if one_image_each else rows_plan
    return plan(inputs, *weights)


def solution(mesh):
    return jax.shard_map(
        on_device,
        mesh=mesh,
        in_specs=(
            P(None, "dp", "row", None, None),
            P("section", None, None, None),
            P("section", None),
            P("section", None),
            P("section", None),
            P("section", None, "dp"),
            P("section", None),
            P("section", None),
            P("section", None),
            P("section", "dp", None),
            P("section", None),
        ),
        out_specs=P("section", None, "dp", "row", None, None),
        check_vma=False,
    )
```

time: 95.6 us -> 86.1 us (0.901)
  waiting for transfers between devices: 53.8 us -> 41.6 us
  local copies, waits for them, and re-layouts: 7.08 us -> 2.23 us
  Pallas kernels: 19.7 us -> 23.7 us
  starting transfers between devices: 14 us -> 17.4 us
    ppermute x13 -> x16, waiting for transfers between devices: 53.8 us -> 41.6 us  [the longest x6 27.9 us: pass_on(): return lax.ppermute(x, 'section', [(tick - 1, tick)])]
    unnamed x28 -> x20, local copies, waits for them, and re-layouts: 5.55 us -> 1.02 us
    pallas_call x10 -> x26, Pallas kernels: 19.7 us -> 23.7 us  [call(): pl.pallas_call(functools.partial(kernel, **static), out_shape=out, in_spe...]
    ppermute x13 -> x16, starting transfers between devices: 14 us -> 17.4 us  [the longest x4 6.8 us: other_half(): return lax.ppermute(x, ('section', 'dp'), pairs)]
    squeeze x0 -> x1, local copies, waits for them, and re-layouts: none -> 1.19 us  [image_plan(): piece = lax.dynamic_index_in_dim(inputs, me ^ by, 0, keepdims=False)[0]]
  transfers between devices with their start and end apart: 13 -> 16, of which waited for: 5 -> 5; matrix products, arithmetic and copies ran while one was open for 1% -> 1% of each run, Pallas kernels for 10% -> 14%
where the time goes in v2:
time: 86.1 us; the launch traced here: 85.7 us
  waiting for transfers between devices  41.6 us (48%)
  Pallas kernels  23.7 us (28%)
  starting transfers between devices  17.4 us (20%)
  local copies, waits for them, and re-layouts  2.23 us (3%)
    ppermute x6, waiting for transfers between devices, pass_on(): return lax.ppermute(x, 'section', [(tick - 1, tick)])  27.9 us
    pallas_call x26, Pallas kernels, call(): pl.pallas_call(functools.partial(kernel, **static), out_shape=out, in_spe...  23.7 us
    ppermute x4, waiting for transfers between devices, other_half(): return lax.ppermute(x, ('section', 'dp'), pairs)  10.6 us
    ppermute x4, starting transfers between devices, other_half(): return lax.ppermute(x, ('section', 'dp'), pairs)  6.8 us
    ppermute x6, starting transfers between devices, pass_on(): return lax.ppermute(x, 'section', [(tick - 1, tick)])  4.66 us
    ppermute x3, starting transfers between devices, image_plan(): lax.ppermute(piece, 'row', [(p, p ^ order[n]) for p in range(count)])  3.89 us
    ppermute x3, waiting for transfers between devices, image_plan(): lax.ppermute(piece, 'row', [(p, p ^ order[n]) for p in range(count)])  3.12 us
    ppermute x3, starting transfers between devices, image_plan(): piece = lax.ppermute(piece, ('section', 'row'), pairs)  2.01 us
  transfers between devices with their start and end apart: 16, of which 5 were waited for; matrix products, arithmetic and copies ran while one was open for 1% of the time, Pallas kernels for 14%

profile of v2, /device:TPU:7, one launch (start us, length us, event | category | flops | bytes accessed | tf_op | source)
XLA Modules:
  0.0 85.7 jit_solution(7198330794237206121)
XLA Ops:
  0.1 0.8 collective-permute-start.3
  0.9 0.7 collective-permute-start.4
  1.6 1.2 %dynamic-slice_bitcast_fusion = (bf16[4,48,352]{2,1,0:T(8,128)(2,1)S(1)}, bf16[4,48,352]{2,1,0:T(8,128)(2,1)S(1)}, bf16[4,48,352]{2,1,0:T(8,128)(2,1)S(1)}, bf16[4,48,352]{2,1,0:T(8,128)(2,1)S(1)}) fusion(bf16[4,1,4,48,352]{4,3,2,1,0:T(8,128)(2,1)} %param.11, s32[]{:T(128)S(6)} %select_n.16, s32[]{:T(128)S(6)} %select_n.14, s32[]{:T(128)S(6)} %select_n.13, ...), kind=kLoop, calls=%fused_computation | loop fusion | bytes 1081360 | tf_op jit(solution)/shard_map/squeeze | solution.py:380
  5.2 1.2 %conv_piece.6.refs_4_ = f32[10,6,8,384]{3,2,1,0:T(8,128)S(1)} custom-call(s32[1]{0:T(128)} %bitcast.4.section, bf16[4,48,352]{2,1,0:T(8,128)(2,1)S(1)} %get-tuple-element.65.piece.refs_0_, f32[49,384]{1,0:T(8,128)S(1)} %get-tuple-element.34.taps.refs_7_, f32[4,384]{1,0:T(4,128)S(1)} %get-tuple-element.35.cvec.refs_8_), custom_call_target="tpu_custom_call" | custom-call | bytes 216580 | tf_op jit(solution)/shard_map/conv_piece/pallas_call | solution.py:323
  6.5 1.2 %conv_piece.7.refs_5_ = f32[10,6,8,384]{3,2,1,0:T(8,128)S(1)} custom-call(s32[1]{0:T(128)} %bitcast.4.section, bf16[4,48,352]{2,1,0:T(8,128)(2,1)S(1)} %collective-permute-done.piece.refs_1_, f32[49,384]{1,0:T(8,128)S(1)} %get-tuple-element.34.taps.refs_7_, f32[4,384]{1,0:T(4,128)S(1)} %get-tuple-element.35.cvec.refs_8_), custom_call_target="tpu_custom_call" | custom-call | bytes 216580 | tf_op jit(solution)/shard_map/conv_piece/pallas_call | solution.py:323
  7.7 1.2 %conv_piece.8.refs_6_ = f32[10,6,8,384]{3,2,1,0:T(8,128)S(1)} custom-call(s32[1]{0:T(128)} %bitcast.4.section, bf16[4,48,352]{2,1,0:T(8,128)(2,1)S(1)} %collective-permute-done.1.piece.refs_2_, f32[49,384]{1,0:T(8,128)S(1)} %get-tuple-element.34.taps.refs_7_, f32[4,384]{1,0:T(4,128)S(1)} %get-tuple-element.35.cvec.refs_8_), custom_call_target="tpu_custom_call" | custom-call | bytes 216580 | tf_op jit(solution)/shard_map/conv_piece/pallas_call | solution.py:323
  8.9 3.1 %last_piece.2 = (bf16[16,48,352]{2,1,0:T(8,128)(2,1)S(1)}, bf16[768,352]{1,0:T(8,128)(2,1)S(1)}) custom-call(s32[1]{0:T(128)} %bitcast.4.section, s32[4]{0:T(128)S(1)} %pad_add_fusion.index, bf16[4,48,352]{2,1,0:T(8,128)(2,1)S(1)} %get-tuple-element.65.piece.refs_0_, bf16[4,48,352]{2,1,0:T(8,128)(2,1)S(1)} %collective-permute-done.piece.refs_1_, ...), custom_call_target="tpu_custom_call" | custom-call | bytes 2833940 | tf_op jit(solution)/shard_map/last_piece/pallas_call | solution.py:323
  12.1 1.0 %copy-done = bf16[1,704,352]{2,1,0:T(8,128)(2,1)S(1)} copy-done((bf16[1,704,352]{2,1,0:T(8,128)(2,1)S(1)}, bf16[1,704,352]{2,1,0:T(8,128)(2,1)}, u32[]{:S(2)}) %copy-start) | copy-done | bytes 495640
  13.7 2.1 %collective-permute-start.6 = (bf16[352,704]{1,0:T(8,128)(2,1)S(1)}, bf16[352,704]{1,0:T(8,128)(2,1)S(1)}, u32[]{:S(2)}, u32[]{:S(2)}) collective-permute-start(bf16[352,704]{1,0:T(8,128)(2,1)S(1)} %bitcast.30), channel_id=1, source_target_pairs={{8,9},{9,8},{24,25},{25,24},{10,11},{11,10},{26,27},{27,26},{12,13... | collective-permute-start | bytes 1486856 | tf_op jit(solution)/shard_map/ppermute | solution.py:388
  15.9 3.1 %collective-permute-start.7 = (bf16[704,352]{1,0:T(8,128)(2,1)S(1)}, bf16[704,352]{1,0:T(8,128)(2,1)S(1)}, u32[]{:S(2)}, u32[]{:S(2)}) collective-permute-start(bf16[704,352]{1,0:T(8,128)(2,1)S(1)} %bitcast.18), channel_id=1, source_target_pairs={{8,9},{9,8},{24,25},{25,24},{10,11},{11,10},{26,27},{27,26},{12,13... | collective-permute-start | bytes 1486856 | tf_op jit(solution)/shard_map/ppermute | solution.py:388
  19.1 4.8 %collective-permute-done.6.w_in.in_b = bf16[352,704]{1,0:T(8,128)(2,1)S(1)} collective-permute-done((bf16[352,704]{1,0:T(8,128)(2,1)S(1)}, bf16[352,704]{1,0:T(8,128)(2,1)S(1)}, u32[]{:S(2)}, u32[]{:S(2)}) %collective-permute-start.6) | collective-permute-done | bytes 495648 | tf_op jit(solution)/shard_map/ppermute | solution.py:388
  23.8 5.8 %collective-permute-done.7.out_b = bf16[704,352]{1,0:T(8,128)(2,1)S(1)} collective-permute-done((bf16[704,352]{1,0:T(8,128)(2,1)S(1)}, bf16[704,352]{1,0:T(8,128)(2,1)S(1)}, u32[]{:S(2)}, u32[]{:S(2)}) %collective-permute-start.7) | collective-permute-done | bytes 495648 | tf_op jit(solution)/shard_map/ppermute | solution.py:388
  35.6 1.3 %collective-permute-start.12 = (bf16[16,48,352]{2,1,0:T(8,128)(2,1)S(1)}, bf16[16,48,352]{2,1,0:T(8,128)(2,1)S(1)}, u32[]{:S(2)}, u32[]{:S(2)}) collective-permute-start(bf16[16,48,352]{2,1,0:T(8,128)(2,1)S(1)} %mlp.1.prev), channel_id=1, source_target_pairs={{16,24},{17,25},{18,26},{19,27},{20,28},{21,29},{22,30},{23,31}} | collective-permute-start | bytes 1622024 | tf_op jit(solution)/shard_map/ppermute | solution.py:468
  36.9 27.9 %collective-permute-done.12.x = bf16[16,48,352]{2,1,0:T(8,128)(2,1)S(1)} collective-permute-done((bf16[16,48,352]{2,1,0:T(8,128)(2,1)S(1)}, bf16[16,48,352]{2,1,0:T(8,128)(2,1)S(1)}, u32[]{:S(2)}, u32[]{:S(2)}) %collective-permute-start.12) | collective-permute-done | bytes 540704 | tf_op jit(solution)/shard_map/ppermute | solution.py:468
  64.8 8.2 %conv_up.1 = (bf16[768,704]{1,0:T(8,128)(2,1)S(1)}, bf16[768,704]{1,0:T(8,128)(2,1)S(1)}, f32[2,1,704]{2,1,0:T(1,128)S(1)}) custom-call(s32[1]{0:T(128)} %bitcast.4.section, bf16[16,48,352]{2,1,0:T(8,128)(2,1)S(1)} %collective-permute-done.12.x, f32[49,384]{1,0:T(8,128)S(1)} %get-tuple-element.34.taps.refs_7_, f32[4,384]{1,0:T(4,128)S(1)} %get-tuple-element.35.cvec.refs_8_, ...), custom_call_target="tpu_custom_call" | custom-call | flops 761266176 | bytes 1630212 | tf_op jit(solution)/shard_map/conv_up/pallas_call | solution.py:323
  73.0 1.0 %down_piece.13 = bf16[4,48,352]{2,1,0:T(8,128)(2,1)S(1)} custom-call(s32[1]{0:T(128)} %bitcast.4.section, s32[4]{0:T(128)S(1)} %pad_add_fusion.index, bf16[16,48,352]{2,1,0:T(8,128)(2,1)S(1)} %collective-permute-done.12.x, bf16[768,704]{1,0:T(8,128)(2,1)S(1)} %get-tuple-element.60.act_a, bf16[768,704]{1,0:T(8,128)(2,1)S(1)} %get-tuple-element.61.act_b, ...), custom_call_target="tpu_custom_call" | custom-call | flops 190316544 | bytes 4263956 | tf_op jit(solution)/shard_map/down_piece/pallas_call | solution.py:323
  74.0 1.6 %collective-permute-start.13 = (bf16[4,48,352]{2,1,0:T(8,128)(2,1)S(1)}, bf16[4,48,352]{2,1,0:T(8,128)(2,1)S(1)}, u32[]{:S(2)}, u32[]{:S(2)}) collective-permute-start(bf16[4,48,352]{2,1,0:T(8,128)(2,1)S(1)} %down_piece.13), channel_id=1, source_target_pairs={{0,4},{2,6},{4,0},{6,2},{1,5},{3,7},{5,1},{7,3},{8,12},{10,14},{12... | collective-permute-start | bytes 405512 | tf_op jit(solution)/shard_map/ppermute | solution.py:521
  75.6 1.0 %down_piece.14 = bf16[4,48,352]{2,1,0:T(8,128)(2,1)S(1)} custom-call(s32[1]{0:T(128)} %bitcast.4.section, s32[4]{0:T(128)S(1)} %pad_add_fusion.index, bf16[16,48,352]{2,1,0:T(8,128)(2,1)S(1)} %collective-permute-done.12.x, bf16[768,704]{1,0:T(8,128)(2,1)S(1)} %get-tuple-element.60.act_a, bf16[768,704]{1,0:T(8,128)(2,1)S(1)} %get-tuple-element.61.act_b, ...), custom_call_target="tpu_custom_call" | custom-call | flops 190316544 | bytes 4263956 | tf_op jit(solution)/shard_map/down_piece/pallas_call | solution.py:323
  76.6 2.2 %collective-permute-start.14 = (bf16[4,48,352]{2,1,0:T(8,128)(2,1)S(1)}, bf16[4,48,352]{2,1,0:T(8,128)(2,1)S(1)}, u32[]{:S(2)}, u32[]{:S(2)}) collective-permute-start(bf16[4,48,352]{2,1,0:T(8,128)(2,1)S(1)} %down_piece.14), channel_id=1, source_target_pairs={{0,6},{2,4},{4,2},{6,0},{1,7},{3,5},{5,3},{7,1},{8,14},{10,12},{12... | collective-permute-start | bytes 405512 | tf_op jit(solution)/shard_map/ppermute | solution.py:521
  78.9 1.0 %down_piece.15 = bf16[4,48,352]{2,1,0:T(8,128)(2,1)S(1)} custom-call(s32[1]{0:T(128)} %bitcast.4.section, s32[4]{0:T(128)S(1)} %pad_add_fusion.index, bf16[16,48,352]{2,1,0:T(8,128)(2,1)S(1)} %collective-permute-done.12.x, bf16[768,704]{1,0:T(8,128)(2,1)S(1)} %get-tuple-element.60.act_a, bf16[768,704]{1,0:T(8,128)(2,1)S(1)} %get-tuple-element.61.act_b, ...), custom_call_target="tpu_custom_call" | custom-call | flops 190316544 | bytes 4263956 | tf_op jit(solution)/shard_map/down_piece/pallas_call | solution.py:323
  80.0 1.0 %down_piece.12.refs_0_ = bf16[4,48,352]{2,1,0:T(8,128)(2,1)S(1)} custom-call(s32[1]{0:T(128)} %bitcast.4.section, s32[4]{0:T(128)S(1)} %pad_add_fusion.index, bf16[16,48,352]{2,1,0:T(8,128)(2,1)S(1)} %collective-permute-done.12.x, bf16[768,704]{1,0:T(8,128)(2,1)S(1)} %get-tuple-element.60.act_a, bf16[768,704]{1,0:T(8,128)(2,1)S(1)} %get-tuple-element.61.act_b, ...), custom_call_target="tpu_custom_call" | custom-call | flops 190316544 | bytes 4263956 | tf_op jit(solution)/shard_map/down_piece/pallas_call | solution.py:323
  81.1 1.6 %collective-permute-done.14.refs_2_ = bf16[4,48,352]{2,1,0:T(8,128)(2,1)S(1)} collective-permute-done((bf16[4,48,352]{2,1,0:T(8,128)(2,1)S(1)}, bf16[4,48,352]{2,1,0:T(8,128)(2,1)S(1)}, u32[]{:S(2)}, u32[]{:S(2)}) %collective-permute-start.14) | collective-permute-done | bytes 135200 | tf_op jit(solution)/shard_map/ppermute | solution.py:521
  82.6 1.6 %collective-permute-done.15.refs_3_ = bf16[4,48,352]{2,1,0:T(8,128)(2,1)S(1)} collective-permute-done((bf16[4,48,352]{2,1,0:T(8,128)(2,1)S(1)}, bf16[4,48,352]{2,1,0:T(8,128)(2,1)S(1)}, u32[]{:S(2)}, u32[]{:S(2)}) %collective-permute-start.15) | collective-permute-done | bytes 135200 | tf_op jit(solution)/shard_map/ppermute | solution.py:521
  84.2 1.4 %place.1 = bf16[1,4,1,4,48,352]{5,4,3,2,1,0:T(8,128)(2,1)} custom-call(s32[4]{0:T(128)S(1)} %pad_add_fusion.index, bf16[4,48,352]{2,1,0:T(8,128)(2,1)S(1)} %down_piece.12.refs_0_, bf16[4,48,352]{2,1,0:T(8,128)(2,1)S(1)} %collective-permute-done.13.refs_1_, bf16[4,48,352]{2,1,0:T(8,128)(2,1)S(1)} %collective-permute-done.14.refs_2_, ...), custom_call_target="tpu_custom_call" | custom-call | bytes 540688 | tf_op jit(solution)/shard_map/place/pallas_call | solution.py:323
  (61 shorter events, 9.0 us)
Async XLA Ops:
  0.0 4.9 %copy-start.8 = (bf16[1,352]{1,0:T(2,128)(2,1)S(1)}, bf16[1,352]{1,0:T(2,128)(2,1)}, u32[]{:S(2)}) copy-start(bf16[1,352]{1,0:T(2,128)(2,1)} %refs_3_.1) | copy-start | bytes 2116
  0.0 4.9 %copy-start.4 = (bf16[1,1408]{1,0:T(2,128)(2,1)S(1)}, bf16[1,1408]{1,0:T(2,128)(2,1)}, u32[]{:S(2)}) copy-start(bf16[1,1408]{1,0:T(2,128)(2,1)} %refs_6_.1) | copy-start | bytes 8452
  0.0 4.9 %copy-start.3 = (bf16[1,1408]{1,0:T(2,128)(2,1)S(1)}, bf16[1,1408]{1,0:T(2,128)(2,1)}, u32[]{:S(2)}) copy-start(bf16[1,1408]{1,0:T(2,128)(2,1)} %refs_5_.1) | copy-start | bytes 8452
  0.0 4.9 %copy-start.2 = (bf16[1,1408]{1,0:T(2,128)(2,1)S(1)}, bf16[1,1408]{1,0:T(2,128)(2,1)}, u32[]{:S(2)}) copy-start(bf16[1,1408]{1,0:T(2,128)(2,1)} %refs_4_.1) | copy-start | bytes 8452
  0.0 4.9 %copy-start.7 = (bf16[1,352]{1,0:T(2,128)(2,1)S(1)}, bf16[1,352]{1,0:T(2,128)(2,1)}, u32[]{:S(2)}) copy-start(bf16[1,352]{1,0:T(2,128)(2,1)} %refs_2_.1) | copy-start | bytes 2116
  0.0 4.9 %copy-start.6 = (bf16[1,352]{1,0:T(2,128)(2,1)S(1)}, bf16[1,352]{1,0:T(2,128)(2,1)}, u32[]{:S(2)}) copy-start(bf16[1,352]{1,0:T(2,128)(2,1)} %refs_1_.1) | copy-start | bytes 2116
  0.0 4.9 %copy-start.5 = (bf16[1,352]{1,0:T(2,128)(2,1)S(1)}, bf16[1,352]{1,0:T(2,128)(2,1)}, u32[]{:S(2)}) copy-start(bf16[1,352]{1,0:T(2,128)(2,1)} %refs_0_.1) | copy-start | bytes 2116
  0.0 4.9 %copy-start.1 = (bf16[1,7,7,352]{3,2,1,0:T(8,128)(2,1)S(1)}, bf16[1,7,7,352]{3,2,1,0:T(8,128)(2,1)}, u32[]{:S(2)}) copy-start(bf16[1,7,7,352]{3,2,1,0:T(8,128)(2,1)} %kernel.1) | copy-start | bytes 103492
  0.1 12.0 %collective-permute-start.3 = (bf16[352,704]{1,0:T(8,128)(2,1)}, bf16[352,704]{1,0:T(8,128)(2,1)S(1)}, u32[]{:S(2)}, u32[]{:S(2)}) collective-permute-start(bf16[352,704]{1,0:T(8,128)(2,1)} %bitcast.28), channel_id=1, source_target_pairs={{0,1},{1,0},{16,17},{17,16},{2,3},{3,2},{18,19},{19,18},{4,5},{5,4... | collective-permute-start | bytes 1486856 | tf_op jit(solution)/shard_map/ppermute | solution.py:388
  0.9 11.2 %collective-permute-start.4 = (bf16[704,352]{1,0:T(8,128)(2,1)}, bf16[704,352]{1,0:T(8,128)(2,1)S(1)}, u32[]{:S(2)}, u32[]{:S(2)}) collective-permute-start(bf16[704,352]{1,0:T(8,128)(2,1)} %bitcast.16), channel_id=1, source_target_pairs={{0,1},{1,0},{16,17},{17,16},{2,3},{3,2},{18,19},{19,18},{4,5},{5,4... | collective-permute-start | bytes 1486856 | tf_op jit(solution)/shard_map/ppermute | solution.py:388
  2.8 3.6 %collective-permute-start = (bf16[4,48,352]{2,1,0:T(8,128)(2,1)S(1)}, bf16[4,48,352]{2,1,0:T(8,128)(2,1)S(1)}, u32[]{:S(2)}, u32[]{:S(2)}) collective-permute-start(bf16[4,48,352]{2,1,0:T(8,128)(2,1)S(1)} %get-tuple-element.64), channel_id=1, source_target_pairs={{12,0},{14,2},{8,4},{10,6},{13,1},{15,3},{9,5},{11,7}} | collective-permute-start | bytes 405512 | tf_op jit(solution)/shard_map/ppermute | solution.py:383
  3.5 4.2 %collective-permute-start.1 = (bf16[4,48,352]{2,1,0:T(8,128)(2,1)S(1)}, bf16[4,48,352]{2,1,0:T(8,128)(2,1)S(1)}, u32[]{:S(2)}, u32[]{:S(2)}) collective-permute-start(bf16[4,48,352]{2,1,0:T(8,128)(2,1)S(1)} %get-tuple-element.66), channel_id=1, source_target_pairs={{14,0},{12,2},{10,4},{8,6},{15,1},{13,3},{11,5},{9,7}} | collective-permute-start | bytes 405512 | tf_op jit(solution)/shard_map/ppermute | solution.py:383
  4.2 4.7 %collective-permute-start.2 = (bf16[4,48,352]{2,1,0:T(8,128)(2,1)S(1)}, bf16[4,48,352]{2,1,0:T(8,128)(2,1)S(1)}, u32[]{:S(2)}, u32[]{:S(2)}) collective-permute-start(bf16[4,48,352]{2,1,0:T(8,128)(2,1)S(1)} %get-tuple-element.63), channel_id=1, source_target_pairs={{10,0},{8,2},{14,4},{12,6},{11,1},{9,3},{15,5},{13,7}} | collective-permute-start | bytes 405512 | tf_op jit(solution)/shard_map/ppermute | solution.py:383
  13.0 6.0 %collective-permute-start.5 = (bf16[16,48,352]{2,1,0:T(8,128)(2,1)S(1)}, bf16[16,48,352]{2,1,0:T(8,128)(2,1)S(1)}, u32[]{:S(2)}, u32[]{:S(2)}) collective-permute-start(bf16[16,48,352]{2,1,0:T(8,128)(2,1)S(1)} %down.1.prev.refs_4_), channel_id=1, source_target_pairs={{0,8},{1,9},{2,10},{3,11},{4,12},{5,13},{6,14},{7,15}} | collective-permute-start | bytes 1622024 | tf_op jit(solution)/shard_map/ppermute | solution.py:468
  13.7 10.1 %collective-permute-start.6 = (bf16[352,704]{1,0:T(8,128)(2,1)S(1)}, bf16[352,704]{1,0:T(8,128)(2,1)S(1)}, u32[]{:S(2)}, u32[]{:S(2)}) collective-permute-start(bf16[352,704]{1,0:T(8,128)(2,1)S(1)} %bitcast.30), channel_id=1, source_target_pairs={{8,9},{9,8},{24,25},{25,24},{10,11},{11,10},{26,27},{27,26},{12,13... | collective-permute-start | bytes 1486856 | tf_op jit(solution)/shard_map/ppermute | solution.py:388
  15.9 13.8 %collective-permute-start.7 = (bf16[704,352]{1,0:T(8,128)(2,1)S(1)}, bf16[704,352]{1,0:T(8,128)(2,1)S(1)}, u32[]{:S(2)}, u32[]{:S(2)}) collective-permute-start(bf16[704,352]{1,0:T(8,128)(2,1)S(1)} %bitcast.18), channel_id=1, source_target_pairs={{8,9},{9,8},{24,25},{25,24},{10,11},{11,10},{26,27},{27,26},{12,13... | collective-permute-start | bytes 1486856 | tf_op jit(solution)/shard_map/ppermute | solution.py:388
  30.2 4.5 %collective-permute-start.8 = (bf16[4,48,352]{2,1,0:T(8,128)(2,1)S(1)}, bf16[4,48,352]{2,1,0:T(8,128)(2,1)S(1)}, u32[]{:S(2)}, u32[]{:S(2)}) collective-permute-start(bf16[4,48,352]{2,1,0:T(8,128)(2,1)S(1)} %down_piece.8.refs_0_), channel_id=1, source_target_pairs={{8,16},{9,17},{10,18},{11,19},{12,20},{13,21},{14,22},{15,23}} | collective-permute-start | bytes 405512 | tf_op jit(solution)/shard_map/ppermute | solution.py:468
  31.5 3.2 %collective-permute-start.9 = (bf16[4,48,352]{2,1,0:T(8,128)(2,1)S(1)}, bf16[4,48,352]{2,1,0:T(8,128)(2,1)S(1)}, u32[]{:S(2)}, u32[]{:S(2)}) collective-permute-start(bf16[4,48,352]{2,1,0:T(8,128)(2,1)S(1)} %down_piece.9.refs_1_), channel_id=1, source_target_pairs={{8,16},{9,17},{10,18},{11,19},{12,20},{13,21},{14,22},{15,23}} | collective-permute-start | bytes 405512 | tf_op jit(solution)/shard_map/ppermute | solution.py:468
  32.8 2.0 %collective-permute-start.10 = (bf16[4,48,352]{2,1,0:T(8,128)(2,1)S(1)}, bf16[4,48,352]{2,1,0:T(8,128)(2,1)S(1)}, u32[]{:S(2)}, u32[]{:S(2)}) collective-permute-start(bf16[4,48,352]{2,1,0:T(8,128)(2,1)S(1)} %down_piece.10.refs_2_), channel_id=1, source_target_pairs={{8,16},{9,17},{10,18},{11,19},{12,20},{13,21},{14,22},{15,23}} | collective-permute-start | bytes 405512 | tf_op jit(solution)/shard_map/ppermute | solution.py:468
  34.0 0.8 collective-permute-start.11
  35.6 29.2 %collective-permute-start.12 = (bf16[16,48,352]{2,1,0:T(8,128)(2,1)S(1)}, bf16[16,48,352]{2,1,0:T(8,128)(2,1)S(1)}, u32[]{:S(2)}, u32[]{:S(2)}) collective-permute-start(bf16[16,48,352]{2,1,0:T(8,128)(2,1)S(1)} %mlp.1.prev), channel_id=1, source_target_pairs={{16,24},{17,25},{18,26},{19,27},{20,28},{21,29},{22,30},{23,31}} | collective-permute-start | bytes 1622024 | tf_op jit(solution)/shard_map/ppermute | solution.py:468
  74.0 7.0 %collective-permute-start.13 = (bf16[4,48,352]{2,1,0:T(8,128)(2,1)S(1)}, bf16[4,48,352]{2,1,0:T(8,128)(2,1)S(1)}, u32[]{:S(2)}, u32[]{:S(2)}) collective-permute-start(bf16[4,48,352]{2,1,0:T(8,128)(2,1)S(1)} %down_piece.13), channel_id=1, source_target_pairs={{0,4},{2,6},{4,0},{6,2},{1,5},{3,7},{5,1},{7,3},{8,12},{10,14},{12... | collective-permute-start | bytes 405512 | tf_op jit(solution)/shard_map/ppermute | solution.py:521
  76.6 6.0 %collective-permute-start.14 = (bf16[4,48,352]{2,1,0:T(8,128)(2,1)S(1)}, bf16[4,48,352]{2,1,0:T(8,128)(2,1)S(1)}, u32[]{:S(2)}, u32[]{:S(2)}) collective-permute-start(bf16[4,48,352]{2,1,0:T(8,128)(2,1)S(1)} %down_piece.14), channel_id=1, source_target_pairs={{0,6},{2,4},{4,2},{6,0},{1,7},{3,5},{5,3},{7,1},{8,14},{10,12},{12... | collective-permute-start | bytes 405512 | tf_op jit(solution)/shard_map/ppermute | solution.py:521
  79.9 4.3 %collective-permute-start.15 = (bf16[4,48,352]{2,1,0:T(8,128)(2,1)S(1)}, bf16[4,48,352]{2,1,0:T(8,128)(2,1)S(1)}, u32[]{:S(2)}, u32[]{:S(2)}) collective-permute-start(bf16[4,48,352]{2,1,0:T(8,128)(2,1)S(1)} %down_piece.15), channel_id=1, source_target_pairs={{0,2},{2,0},{4,6},{6,4},{1,3},{3,1},{5,7},{7,5},{8,10},{10,8},{12,... | collective-permute-start | bytes 405512 | tf_op jit(solution)/shard_map/ppermute | solution.py:521
  (2 other events, 4.2 us)

commit v3 on v2

--- a/solution.py
+++ b/solution.py
@@ -14,6 +14,8 @@
 REACH = 3
 CHUNK = 4
 NORM_ROWS = 4
+IN_ORDER = (0, 1, 2, 3)
+VECTORS = 56
 
 
 def fill_columns(xp, xs, x, channels):
@@ -39,7 +41,7 @@
     lax.fori_loop(0, height // 2, rows, 0)
 
 
-def conv(xs, taps, cvec, cq):
+def conv(xs, cpar, cq):
     rows = xs.shape[0]
     height, stride, blocks, lanes = cq.shape
     span = 2 * REACH + 1
@@ -49,11 +51,11 @@
         at = pl.ds(pl.multiple_of(g * LANES, LANES), LANES)
 
         def column(q, carry):
-            bias = jnp.broadcast_to(cvec[0:1, at], (blocks, LANES))
+            bias = jnp.broadcast_to(cpar[VECTORS : VECTORS + 1, at], (blocks, LANES))
             acc = [None if above else bias] * height
             for j in range(span):
                 kern = [
-                    jnp.broadcast_to(taps[i * span + j : i * span + j + 1, at], (blocks, LANES))
+                    jnp.broadcast_to(cpar[i * span + j : i * span + j + 1, at], (blocks, LANES))
                     for i in range(span)
                 ]
                 for r in range(rows):
@@ -72,10 +74,12 @@
     lax.fori_loop(0, lanes // LANES, group, 0)
 
 
-def norm(cq, cvec, xp, flat, skip=0):
+def norm(cq, cpar, xp, flat, skip=0):
     padded, stride, blocks, lanes = cq.shape
     height = padded - 2 * skip
-    channels = flat.shape[1]
+    gain = cpar[VECTORS + 1 : VECTORS + 2, :]
+    shift = cpar[VECTORS + 2 : VECTORS + 3, :]
+    channels = flat.shape[2]
     width = stride * blocks
     groups = lanes // LANES
     inside = lax.broadcasted_iota(jnp.int32, (blocks, lanes), 1) < channels
@@ -88,14 +92,13 @@
                 mean = jnp.sum(v, axis=-1, keepdims=True) * (1.0 / channels)
                 c = jnp.where(inside, v - mean, 0.0)
                 var = jnp.sum(c * c, axis=-1, keepdims=True) * (1.0 / channels)
-                c = c * lax.rsqrt(var + EPS_NORM) * cvec[1:2, :] + cvec[2:3, :]
+                c = c * lax.rsqrt(var + EPS_NORM) * gain + shift
                 for g in range(groups):
                     at = slice(g * LANES, (g + 1) * LANES)
                     xp[k * groups + g, pl.ds(q, blocks, stride=stride), :] = c[:, at]
-            at_cell = pl.ds(pl.multiple_of(h * width, width), width)
             for g in range(groups):
                 at = slice(g * LANES, min((g + 1) * LANES, channels))
-                flat[at_cell, at] = xp[k * groups + g, 0:width, 0 : at.stop - at.start].astype(
+                flat[h, :, at] = xp[k * groups + g, 0:width, 0 : at.stop - at.start].astype(
                     jnp.bfloat16
                 )
         return carry
@@ -103,10 +106,10 @@
     lax.fori_loop(0, height // NORM_ROWS, rows, 0)
 
 
-def conv_norm(x, taps, cvec, flat, xp, xs, cq):
+def conv_norm(x, cpar, flat, xp, xs, cq):
     fill_columns(xp, xs, x, x.shape[2])
-    conv(xs, taps, cvec, cq)
-    norm(cq, cvec, xp, flat)
+    conv(xs, cpar, cq)
+    norm(cq, cpar, xp, flat)
 
 
 def conv_scratch(rows, out_rows, width, lanes):
@@ -122,13 +125,16 @@
 
 
 def up(flat, w_in, bias, act, ssq):
-    cells = flat.shape[0]
+    height, width, channels = flat.shape
+    cells = height * width
     half = w_in.shape[1]
     step = 2 * LANES
 
     def units(start, count):
         raised = jnp.dot(
-            flat[...], w_in[:, pl.ds(start, count)], preferred_element_type=jnp.float32
+            flat[...].reshape(cells, channels),
+            w_in[:, pl.ds(start, count)],
+            preferred_element_type=jnp.float32,
         )
         active = gelu(raised + bias[0:1, pl.ds(start, count)]).astype(jnp.bfloat16)
         act[:, pl.ds(start, count)] = active
@@ -154,11 +160,11 @@
         scale[which] = fvec[which, 1:2, :] * ratio + 1.0
 
 
-def down(x_rows, first_row, acts, outs, scale, fvec, cvec):
+def down(x_rows, first_row, acts, outs, scale, fvec, cpar):
     _, width, channels = x_rows.shape
     cells = CHUNK * width
     at = pl.ds(pl.multiple_of(first_row * width, cells), cells)
-    update = cvec[3:4, 0:channels]
+    update = cpar[VECTORS + 3 : VECTORS + 4, 0:channels]
     for which in range(2):
         a = acts[which][at, :].astype(jnp.float32)
         hidden = (a * scale[which] + fvec[which, 2:3, :]).astype(jnp.bfloat16)
@@ -178,22 +184,21 @@
 
 
 def prepare_kernel(part, kernel, *refs):
-    vectors, (taps, cvec, fvec), (held, *staged), sems = refs[:7], refs[7:10], refs[10:-1], refs[-1]
+    vectors, (cpar, fvec), (held, *staged), sems = refs[:7], refs[7:9], refs[9:-1], refs[-1]
     moves = [(kernel, held), *zip(vectors, staged)]
     copies = [pltpu.make_async_copy(a, b, sems.at[n]) for n, (a, b) in enumerate(moves)]
     for copy in copies:
         copy.start()
-    taps[...] = jnp.zeros(taps.shape, jnp.float32)
-    cvec[...] = jnp.zeros(cvec.shape, jnp.float32)
+    cpar[...] = jnp.zeros(cpar.shape, jnp.float32)
     for copy in copies:
         copy.wait()
     channels = kernel.shape[3]
     span = kernel.shape[1]
     half = fvec.shape[2]
     for i in range(span):
-        taps[i * span : (i + 1) * span, 0:channels] = held[0, i].astype(jnp.float32)
+        cpar[i * span : (i + 1) * span, 0:channels] = held[0, i].astype(jnp.float32)
     for n in range(4):
-        cvec[n : n + 1, 0:channels] = staged[n][...].astype(jnp.float32)
+        cpar[VECTORS + n : VECTORS + n + 1, 0:channels] = staged[n][...].astype(jnp.float32)
     first = part[0] == 0
     for n in range(3):
         v = staged[4 + n][...].astype(jnp.float32)
@@ -202,34 +207,40 @@
         fvec[1, n : n + 1, :] = jnp.where(first, high, low)
 
 
-def piece_kernel(section, piece, taps, cvec, part, xp, xs, *, tick):
-    @pl.when(jnp.logical_or(tick == 0, section[0] == tick))
+def block_of(me, order, n):
+    return n if order is None else me[0] ^ order[n]
+
+
+def piece_kernel(section, piece, cpar, part, xp, xs, *, on):
+    @pl.when(section[0] == on)
     def _():
         fill_columns(xp, xs, piece, piece.shape[2])
-        conv(xs, taps, cvec, part)
-
-
-def last_piece_kernel(section, index, *refs, count, tick):
+        conv(xs, cpar, part)
+
+
+def last_piece_kernel(section, me, *refs, order, on):
+    count = len(order or IN_ORDER)
     pieces, parts = refs[:count], refs[count : 2 * count - 1]
-    taps, cvec, x, flat, xp, xs, own, cq = refs[2 * count - 1 :]
+    cpar, x, flat, xp, xs, own, cq = refs[2 * count - 1 :]
     rows = pieces[0].shape[0]
 
-    @pl.when(jnp.logical_or(tick == 0, section[0] == tick))
-    def _():
-        cq[...] = jnp.broadcast_to(cvec[0:1, :].reshape(1, 1, 1, cq.shape[3]), cq.shape)
+    @pl.when(section[0] == on)
+    def _():
+        bias = cpar[VECTORS : VECTORS + 1, :].reshape(1, 1, 1, cq.shape[3])
+        cq[...] = jnp.broadcast_to(bias, cq.shape)
         fill_columns(xp, xs, pieces[-1], x.shape[2])
-        conv(xs, taps, cvec, own)
+        conv(xs, cpar, own)
         for n, (piece, part) in enumerate(zip(pieces, (*parts, own))):
-            at = index[n] * rows
+            at = block_of(me, order, n) * rows
             x[pl.ds(at, rows)] = piece[...]
             cq[pl.ds(at, rows + 2 * REACH)] += part[...]
-        norm(cq, cvec, xp, flat, REACH)
-
-
-def conv_kernel(section, x, taps, cvec, flat, xp, xs, cq, *, tick):
+        norm(cq, cpar, xp, flat, REACH)
+
+
+def conv_kernel(section, x, cpar, flat, xp, xs, cq, *, tick):
     @pl.when(section[0] == tick)
     def _():
-        conv_norm(x, taps, cvec, flat, xp, xs, cq)
+        conv_norm(x, cpar, flat, xp, xs, cq)
 
 
 def up_first_kernel(section, flat, w_in, fvec, act, ssq, *, tick):
@@ -245,28 +256,28 @@
         norm_scale((other, ssq), fvec, scale)
 
 
-def first_down_kernel(section, x, act_a, act_b, out_a, out_b, scale, fvec, cvec, out):
+def first_down_kernel(section, x, act_a, act_b, out_a, out_b, scale, fvec, cpar, out):
     @pl.when(section[0] == 0)
     def _():
-        down_all(x, (act_a, act_b), (out_a, out_b), scale, fvec, cvec, out)
+        down_all(x, (act_a, act_b), (out_a, out_b), scale, fvec, cpar, out)
 
 
 def down_piece_kernel(
-    section, index, x, act_a, act_b, out_a, out_b, scale, fvec, cvec, prev, out, *, tick, n
+    section, me, x, act_a, act_b, out_a, out_b, scale, fvec, cpar, prev, out, *, order, tick, n
 ):
-    first_row = index[n] * CHUNK
+    first_row = block_of(me, order, n) * CHUNK
     at = pl.ds(first_row, CHUNK)
 
     @pl.when(section[0] == tick)
     def _():
-        out[...] = down(x[at], first_row, (act_a, act_b), (out_a, out_b), scale, fvec, cvec)
+        out[...] = down(x[at], first_row, (act_a, act_b), (out_a, out_b), scale, fvec, cpar)
 
     @pl.when(section[0] != tick)
     def _():
         out[...] = prev[at]
 
 
-def mlp_kernel(section, x, flat, in_a, in_b, out_a, out_b, fvec, cvec, *refs, tick):
+def mlp_kernel(section, x, flat, in_a, in_b, out_a, out_b, fvec, cpar, *refs, tick):
     *pieces, prev, out, act_a, act_b, ssq_a, ssq_b, scale = refs
 
     @pl.when(section[0] == tick)
@@ -274,7 +285,7 @@
         up(flat, in_a, fvec.at[0], act_a, ssq_a)
         up(flat, in_b, fvec.at[1], act_b, ssq_b)
         norm_scale((ssq_a, ssq_b), fvec, scale)
-        down_all(x, (act_a, act_b), (out_a, out_b), scale, fvec, cvec, out)
+        down_all(x, (act_a, act_b), (out_a, out_b), scale, fvec, cpar, out)
 
     @pl.when(section[0] == tick - 1)
     def _():
@@ -286,21 +297,21 @@
         out[...] = prev[...]
 
 
-def conv_up_kernel(section, x, taps, cvec, in_a, in_b, fvec, *refs, tick):
+def conv_up_kernel(section, x, cpar, in_a, in_b, fvec, *refs, tick):
     act_a, act_b, scale, xp, xs, cq, flat, ssq_a, ssq_b = refs
 
     @pl.when(section[0] == tick)
     def _():
-        conv_norm(x, taps, cvec, flat, xp, xs, cq)
+        conv_norm(x, cpar, flat, xp, xs, cq)
         up(flat, in_a, fvec.at[0], act_a, ssq_a)
         up(flat, in_b, fvec.at[1], act_b, ssq_b)
         norm_scale((ssq_a, ssq_b), fvec, scale)
 
 
-def place_kernel(index, *refs):
+def place_kernel(me, *refs, order):
     *pieces, saved, sems = refs
     copies = [
-        pltpu.make_async_copy(piece, saved.at[0, index[n], 0], sems.at[n])
+        pltpu.make_async_copy(piece, saved.at[0, block_of(me, order, n), 0], sems.at[n])
         for n, piece in enumerate(pieces)
     ]
     for copy in copies:
@@ -357,6 +368,7 @@
     count = lax.axis_size("row")
     me = lax.axis_index("row").astype(jnp.int32)
     section = lax.axis_index("section").astype(jnp.int32).reshape(1)
+    me_ref = me.reshape(1)
     part = lax.axis_index("dp").astype(jnp.int32).reshape(1)
     _, _, rows, width, channels = inputs.shape
     height = rows * count
@@ -365,21 +377,19 @@
     half = proj_in.shape[2]
     span = depth_kernel.shape[1]
     order = (0, 2, 3, 1)
-    index = jnp.stack([me ^ by for by in order])
-    in_order = jnp.arange(count, dtype=jnp.int32)
     bf16 = jnp.bfloat16
     whole = shape(height, width, channels, dtype=bf16)
-    flat_shape = shape(cells, channels, dtype=bf16)
     piece_shape = shape(rows, width, channels, dtype=bf16)
     act_shape = shape(cells, half, dtype=bf16)
     scale_shape = shape(2, 1, half)
     matmul = 2 * cells * channels * half
 
+    helper, source = 1, sections - 1
     pieces = []
     for by in order:
         piece = lax.dynamic_index_in_dim(inputs, me ^ by, 0, keepdims=False)[0]
         if by:
-            pairs = [(count + (p ^ by), p) for p in range(count)]
+            pairs = [(source * count + (p ^ by), helper * count + p) for p in range(count)]
             piece = lax.ppermute(piece, ("section", "row"), pairs)
         pieces.append(piece)
 
@@ -396,17 +406,20 @@
     held = (
         depth_kernel, depth_bias, norm_gain, norm_bias, bias_out, bias_in, grn_gamma, grn_beta
     )
-    taps, cvec, fvec = call(
+    cpar, fvec = call(
         prepare_kernel,
         "prepare",
         (part, *held),
-        (shape(span * span, lanes), shape(4, lanes), shape(2, 3, half)),
+        (shape(VECTORS + 8, lanes), shape(2, 3, half)),
         specs=[SMEM] + [HBM] * len(held),
         scratch=[pltpu.VMEM(v.shape, v.dtype) for v in held]
         + [pltpu.SemaphoreType.DMA((len(held),))],
     )
 
-    def conv_pieces(pieces, at, tick):
+    def send(x, start, end):
+        return lax.ppermute(x, "section", [(start, end)])
+
+    def conv_pieces(pieces, cpar, order, on):
         out_rows = rows + 2 * REACH
         scratch = conv_scratch(rows, out_rows, width, lanes)
         parts = []
@@ -416,24 +429,24 @@
             part = call(
                 piece_kernel,
                 "conv_piece",
-                (section, piece, taps, cvec),
+                (section, piece, cpar),
                 shape(out_rows, width // 8, 8, lanes),
                 scratch=scratch[:2],
-                tick=tick,
+                on=on,
             )
             parts.append(part)
         return call(
             last_piece_kernel,
             "last_piece",
-            (section, at, *pieces, *parts, taps, cvec),
-            (whole, flat_shape),
+            (section, me_ref, *pieces, *parts, cpar),
+            (whole, whole),
             scratch=scratch + [conv_scratch(1, height + 2 * REACH, width, lanes)[2]],
-            count=count,
-            tick=tick,
+            order=order,
+            on=on,
         )
 
-    def up_halves(flat, other_in, tick):
-        act_a, ssq = call(
+    def up_own(flat, tick):
+        return call(
             up_first_kernel,
             "up_own",
             (section, flat, w_in, fvec),
@@ -441,7 +454,9 @@
             flops=matmul,
             tick=tick,
         )
-        act_b, scale = call(
+
+    def up_other(flat, other_in, ssq, tick):
+        return call(
             up_second_kernel,
             "up_other",
             (section, flat, other_in, fvec, ssq),
@@ -450,51 +465,54 @@
             flops=matmul,
             tick=tick,
         )
-        return act_a, act_b, scale
-
-    def down_piece(x, acts, other_out, prev, at, tick, n):
+
+    def down_piece(x, acts, other_out, prev, order, tick, n):
         act_a, act_b, scale = acts
         return call(
             down_piece_kernel,
             "down_piece",
-            (section, at, x, act_a, act_b, w_out, other_out, scale, fvec, cvec, prev),
+            (section, me_ref, x, act_a, act_b, w_out, other_out, scale, fvec, cpar, prev),
             piece_shape,
             flops=2 * matmul // count,
+            order=order,
             tick=tick,
             n=n,
         )
 
-    def pass_on(x, tick):
-        return lax.ppermute(x, "section", [(tick - 1, tick)])
-
-    x, flat = conv_pieces(pieces, index, 0)
-    act_a, act_b, scale = up_halves(flat, other_in, 0)
+    x, flat = conv_pieces(pieces, send(cpar, 0, helper), order, helper)
+    flat, other_in = lax.optimization_barrier((flat, other_in))
+    flat = send(flat, helper, 0)
+    act_a, ssq = up_own(flat, 0)
+    x, other_out, act_a = lax.optimization_barrier((x, other_out, act_a))
+    x = send(x, helper, 0)
+    act_b, scale = up_other(flat, other_in, ssq, 0)
     result = call(
         first_down_kernel,
         "down",
-        (section, x, act_a, act_b, w_out, other_out, scale, fvec, cvec),
+        (section, x, act_a, act_b, w_out, other_out, scale, fvec, cpar),
         whole,
         flops=2 * matmul,
     )
-    x = pass_on(result, 1)
+    x = send(result, 0, 1)
     late_in, late_out, result = lax.optimization_barrier((w_in, w_out, result))
     odd_in = other_half(late_in, odd)
     odd_out = other_half(late_out, odd)
     flat = call(
         conv_kernel,
         "conv",
-        (section, x, taps, cvec),
-        flat_shape,
+        (section, x, cpar),
+        whole,
         scratch=conv_scratch(height, height, width, lanes),
         tick=1,
     )
-    acts = up_halves(flat, odd_in, 1)
-    kept = [down_piece(x, acts, odd_out, result, in_order, 1, n) for n in range(count)]
-    x, flat = conv_pieces([pass_on(piece, 2) for piece in kept], in_order, 2)
+    act_a, ssq = up_own(flat, 1)
+    acts = (act_a, *up_other(flat, odd_in, ssq, 1))
+    kept = [down_piece(x, acts, odd_out, result, None, 1, n) for n in range(count)]
+    x, flat = conv_pieces([send(piece, 1, 2) for piece in kept], cpar, None, 2)
     result = call(
         mlp_kernel,
         "mlp",
-        (section, x, flat, w_in, other_in, w_out, other_out, fvec, cvec, *kept, result),
+        (section, x, flat, w_in, other_in, w_out, other_out, fvec, cpar, *kept, result),
         whole,
         scratch=[pltpu.VMEM((cells, half), bf16)] * 2
         + [ssq_scratch(half)] * 2
@@ -502,31 +520,32 @@
         flops=4 * matmul,
         tick=2,
     )
-    x = pass_on(result, 3)
+    x = send(result, 2, 3)
     acts = call(
         conv_up_kernel,
         "conv_up",
-        (section, x, taps, cvec, w_in, odd_in, fvec),
+        (section, x, cpar, w_in, odd_in, fvec),
         (act_shape, act_shape, scale_shape),
         scratch=conv_scratch(height, height, width, lanes)
-        + [pltpu.VMEM((cells, channels), bf16)]
+        + [pltpu.VMEM((height, width, channels), bf16)]
         + [ssq_scratch(half)] * 2,
         flops=2 * matmul,
         tick=3,
     )
     done = []
     for n in (1, 2, 3, 0):
-        piece = down_piece(x, acts, odd_out, result, index, 3, n)
+        piece = down_piece(x, acts, odd_out, result, order, 3, n)
         if n:
             piece = lax.ppermute(piece, "row", [(p, p ^ order[n]) for p in range(count)])
         done.append(piece)
     return call(
         place_kernel,
         "place",
-        (index, done[3], *done[:3]),
+        (me_ref, done[3], *done[:3]),
         shape(1, count, 1, rows, width, channels, dtype=bf16),
         out_specs=HBM,
         scratch=[pltpu.SemaphoreType.DMA((count,))],
+        order=order,
     )
 
 

time: 86.1 us -> 87 us (1.010)
  Pallas kernels: 23.7 us -> 11.6 us
  starting transfers between devices: 17.4 us -> 25.3 us
  waiting for transfers between devices: 41.6 us -> 47.6 us
    pallas_call x26, Pallas kernels: 23.7 us -> 11.6 us  [call(): pl.pallas_call(functools.partial(kernel, **static), out_shape=out, in_spe...]
    ppermute x3, starting transfers between devices: 2.01 us -> 7.8 us  [image_plan(): piece = lax.ppermute(piece, ('section', 'row'), pairs)]
    ppermute x4, waiting for transfers between devices: 10.6 us -> 13.7 us  [other_half(): return lax.ppermute(x, ('section', 'dp'), pairs)]
    ppermute x6 -> x9, starting transfers between devices: 4.66 us -> 6.86 us  [send(): return lax.ppermute(x, 'section', [(start, end)])]
    ppermute x3, waiting for transfers between devices: 0.01 us -> 1.85 us  [image_plan(): piece = lax.ppermute(piece, ('section', 'row'), pairs)]
    ppermute x3, waiting for transfers between devices: 3.12 us -> 4.82 us  [image_plan(): lax.ppermute(piece, 'row', [(p, p ^ order[n]) for p in range(count)])]
    ppermute x6 -> x9, waiting for transfers between devices: 27.9 us -> 27.2 us  [send(): return lax.ppermute(x, 'section', [(start, end)])]
  transfers between devices with their start and end apart: 16 -> 19, of which waited for: 5 -> 7; matrix products, arithmetic and copies ran while one was open for 1% -> 1% of each run, Pallas kernels for 14% -> 2%
where the time goes in v3:
time: 87 us; the launch traced here: 86.6 us
  waiting for transfers between devices  47.6 us (55%)
  starting transfers between devices  25.3 us (29%)
  Pallas kernels  11.6 us (13%)
  local copies, waits for them, and re-layouts  1.44 us (2%)
    ppermute x9, waiting for transfers between devices, send(): return lax.ppermute(x, 'section', [(start, end)])  27.2 us
    ppermute x4, waiting for transfers between devices, other_half(): return lax.ppermute(x, ('section', 'dp'), pairs)  13.7 us
    pallas_call x26, Pallas kernels, call(): pl.pallas_call(functools.partial(kernel, **static), out_shape=out, in_spe...  11.6 us
    ppermute x3, starting transfers between devices, image_plan(): piece = lax.ppermute(piece, ('section', 'row'), pairs)  7.8 us
    ppermute x9, starting transfers between devices, send(): return lax.ppermute(x, 'section', [(start, end)])  6.86 us
    ppermute x4, starting transfers between devices, other_half(): return lax.ppermute(x, ('section', 'dp'), pairs)  6.79 us
    ppermute x3, waiting for transfers between devices, image_plan(): lax.ppermute(piece, 'row', [(p, p ^ order[n]) for p in range(count)])  4.82 us
    ppermute x3, starting transfers between devices, image_plan(): lax.ppermute(piece, 'row', [(p, p ^ order[n]) for p in range(count)])  3.83 us
  transfers between devices with their start and end apart: 19, of which 7 were waited for; matrix products, arithmetic and copies ran while one was open for 1% of the time, Pallas kernels for 2%

profile of v3, /device:TPU:7, one launch (start us, length us, event | category | flops | bytes accessed | tf_op | source)
XLA Modules:
  0.0 86.6 jit_solution(7362194022682621384)
XLA Ops:
  0.1 0.8 collective-permute-start.5
  0.9 1.2 %dynamic-slice_bitcast_fusion = (bf16[4,48,352]{2,1,0:T(8,128)(2,1)S(1)}, bf16[4,48,352]{2,1,0:T(8,128)(2,1)S(1)}, bf16[4,48,352]{2,1,0:T(8,128)(2,1)S(1)}, bf16[4,48,352]{2,1,0:T(8,128)(2,1)S(1)}) fusion(bf16[4,1,4,48,352]{4,3,2,1,0:T(8,128)(2,1)} %param.11, s32[]{:T(128)S(6)} %select_n.16, s32[]{:T(128)S(6)} %select_n.14, s32[]{:T(128)S(6)} %select_n.13, ...), kind=kLoop, calls=%fused_computation | loop fusion | bytes 1081360 | tf_op jit(solution)/shard_map/squeeze | solution.py:390
  2.1 4.2 %collective-permute-start = (bf16[4,48,352]{2,1,0:T(8,128)(2,1)S(1)}, bf16[4,48,352]{2,1,0:T(8,128)(2,1)S(1)}, u32[]{:S(2)}, u32[]{:S(2)}) collective-permute-start(bf16[4,48,352]{2,1,0:T(8,128)(2,1)S(1)} %get-tuple-element.72), channel_id=1, source_target_pairs={{28,8},{30,10},{24,12},{26,14},{29,9},{31,11},{25,13},{27,15}} | collective-permute-start | bytes 405512 | tf_op jit(solution)/shard_map/ppermute | solution.py:393
  6.3 2.3 %collective-permute-start.1 = (bf16[4,48,352]{2,1,0:T(8,128)(2,1)S(1)}, bf16[4,48,352]{2,1,0:T(8,128)(2,1)S(1)}, u32[]{:S(2)}, u32[]{:S(2)}) collective-permute-start(bf16[4,48,352]{2,1,0:T(8,128)(2,1)S(1)} %get-tuple-element.74), channel_id=1, source_target_pairs={{30,8},{28,10},{26,12},{24,14},{31,9},{29,11},{27,13},{25,15}} | collective-permute-start | bytes 405512 | tf_op jit(solution)/shard_map/ppermute | solution.py:393
  8.6 1.3 %collective-permute-start.2 = (bf16[4,48,352]{2,1,0:T(8,128)(2,1)S(1)}, bf16[4,48,352]{2,1,0:T(8,128)(2,1)S(1)}, u32[]{:S(2)}, u32[]{:S(2)}) collective-permute-start(bf16[4,48,352]{2,1,0:T(8,128)(2,1)S(1)} %get-tuple-element.71), channel_id=1, source_target_pairs={{26,8},{24,10},{30,12},{28,14},{27,9},{25,11},{31,13},{29,15}} | collective-permute-start | bytes 405512 | tf_op jit(solution)/shard_map/ppermute | solution.py:393
  11.0 1.8 %collective-permute-done.2.refs_3_ = bf16[4,48,352]{2,1,0:T(8,128)(2,1)S(1)} collective-permute-done((bf16[4,48,352]{2,1,0:T(8,128)(2,1)S(1)}, bf16[4,48,352]{2,1,0:T(8,128)(2,1)S(1)}, u32[]{:S(2)}, u32[]{:S(2)}) %collective-permute-start.2) | collective-permute-done | bytes 135200 | tf_op jit(solution)/shard_map/ppermute | solution.py:393
  12.9 0.8 collective-permute-start.6
  13.9 0.7 collective-permute-start.4
  14.7 0.7 collective-permute-start.7
  15.4 0.7 collective-permute-start.8
  16.1 2.1 %collective-permute-start.9 = (bf16[352,704]{1,0:T(8,128)(2,1)S(1)}, bf16[352,704]{1,0:T(8,128)(2,1)S(1)}, u32[]{:S(2)}, u32[]{:S(2)}) collective-permute-start(bf16[352,704]{1,0:T(8,128)(2,1)S(1)} %bitcast.27), channel_id=1, source_target_pairs={{8,9},{9,8},{24,25},{25,24},{10,11},{11,10},{26,27},{27,26},{12,13... | collective-permute-start | bytes 1486856 | tf_op jit(solution)/shard_map/ppermute | solution.py:398
  18.3 3.1 %collective-permute-start.10 = (bf16[704,352]{1,0:T(8,128)(2,1)S(1)}, bf16[704,352]{1,0:T(8,128)(2,1)S(1)}, u32[]{:S(2)}, u32[]{:S(2)}) collective-permute-start(bf16[704,352]{1,0:T(8,128)(2,1)S(1)} %bitcast.15), channel_id=1, source_target_pairs={{8,9},{9,8},{24,25},{25,24},{10,11},{11,10},{26,27},{27,26},{12,13... | collective-permute-start | bytes 1486856 | tf_op jit(solution)/shard_map/ppermute | solution.py:398
  21.5 7.9 %collective-permute-done.9.w_in.in_b = bf16[352,704]{1,0:T(8,128)(2,1)S(1)} collective-permute-done((bf16[352,704]{1,0:T(8,128)(2,1)S(1)}, bf16[352,704]{1,0:T(8,128)(2,1)S(1)}, u32[]{:S(2)}, u32[]{:S(2)}) %collective-permute-start.9) | collective-permute-done | bytes 495648 | tf_op jit(solution)/shard_map/ppermute | solution.py:398
  29.4 5.8 %collective-permute-done.10.out_b = bf16[704,352]{1,0:T(8,128)(2,1)S(1)} collective-permute-done((bf16[704,352]{1,0:T(8,128)(2,1)S(1)}, bf16[704,352]{1,0:T(8,128)(2,1)S(1)}, u32[]{:S(2)}, u32[]{:S(2)}) %collective-permute-start.10) | collective-permute-done | bytes 495648 | tf_op jit(solution)/shard_map/ppermute | solution.py:398
  35.2 0.7 collective-permute-start.11
  38.4 1.3 %collective-permute-start.15 = (bf16[16,48,352]{2,1,0:T(8,128)(2,1)S(1)}, bf16[16,48,352]{2,1,0:T(8,128)(2,1)S(1)}, u32[]{:S(2)}, u32[]{:S(2)}) collective-permute-start(bf16[16,48,352]{2,1,0:T(8,128)(2,1)S(1)} %mlp.1.prev), channel_id=1, source_target_pairs={{16,24},{17,25},{18,26},{19,27},{20,28},{21,29},{22,30},{23,31}} | collective-permute-start | bytes 1622024 | tf_op jit(solution)/shard_map/ppermute | solution.py:420
  39.7 27.2 %collective-permute-done.15.x = bf16[16,48,352]{2,1,0:T(8,128)(2,1)S(1)} collective-permute-done((bf16[16,48,352]{2,1,0:T(8,128)(2,1)S(1)}, bf16[16,48,352]{2,1,0:T(8,128)(2,1)S(1)}, u32[]{:S(2)}, u32[]{:S(2)}) %collective-permute-start.15) | collective-permute-done | bytes 540704 | tf_op jit(solution)/shard_map/ppermute | solution.py:420
  66.8 8.1 %conv_up.1 = (bf16[768,704]{1,0:T(8,128)(2,1)S(1)}, bf16[768,704]{1,0:T(8,128)(2,1)S(1)}, f32[2,1,704]{2,1,0:T(1,128)S(1)}) custom-call(s32[1]{0:T(128)} %bitcast.1.section, bf16[16,48,352]{2,1,0:T(8,128)(2,1)S(1)} %collective-permute-done.15.x, f32[64,384]{1,0:T(8,128)S(1)} %get-tuple-element.38.cpar.refs_7_, bf16[352,704]{1,0:T(8,128)(2,1)S(1)} %bitcast.30, ...), custom_call_target="tpu_custom_call" | custom-call | flops 761266176 | bytes 1647108 | tf_op jit(solution)/shard_map/conv_up/pallas_call | solution.py:334
  75.4 2.4 %collective-permute-start.16 = (bf16[4,48,352]{2,1,0:T(8,128)(2,1)S(1)}, bf16[4,48,352]{2,1,0:T(8,128)(2,1)S(1)}, u32[]{:S(2)}, u32[]{:S(2)}) collective-permute-start(bf16[4,48,352]{2,1,0:T(8,128)(2,1)S(1)} %down_piece.13), channel_id=1, source_target_pairs={{0,4},{2,6},{4,0},{6,2},{1,5},{3,7},{5,1},{7,3},{8,12},{10,14},{12... | collective-permute-start | bytes 405512 | tf_op jit(solution)/shard_map/ppermute | solution.py:539
  78.3 1.1 %collective-permute-start.17 = (bf16[4,48,352]{2,1,0:T(8,128)(2,1)S(1)}, bf16[4,48,352]{2,1,0:T(8,128)(2,1)S(1)}, u32[]{:S(2)}, u32[]{:S(2)}) collective-permute-start(bf16[4,48,352]{2,1,0:T(8,128)(2,1)S(1)} %down_piece.14), channel_id=1, source_target_pairs={{0,6},{2,4},{4,2},{6,0},{1,7},{3,5},{5,3},{7,1},{8,14},{10,12},{12... | collective-permute-start | bytes 405512 | tf_op jit(solution)/shard_map/ppermute | solution.py:539
  80.8 1.2 %collective-permute-done.16.refs_1_ = bf16[4,48,352]{2,1,0:T(8,128)(2,1)S(1)} collective-permute-done((bf16[4,48,352]{2,1,0:T(8,128)(2,1)S(1)}, bf16[4,48,352]{2,1,0:T(8,128)(2,1)S(1)}, u32[]{:S(2)}, u32[]{:S(2)}) %collective-permute-start.16) | collective-permute-done | bytes 135200 | tf_op jit(solution)/shard_map/ppermute | solution.py:539
  82.0 2.3 %collective-permute-done.17.refs_2_ = bf16[4,48,352]{2,1,0:T(8,128)(2,1)S(1)} collective-permute-done((bf16[4,48,352]{2,1,0:T(8,128)(2,1)S(1)}, bf16[4,48,352]{2,1,0:T(8,128)(2,1)S(1)}, u32[]{:S(2)}, u32[]{:S(2)}) %collective-permute-start.17) | collective-permute-done | bytes 135200 | tf_op jit(solution)/shard_map/ppermute | solution.py:539
  84.3 1.2 %collective-permute-done.18.refs_3_ = bf16[4,48,352]{2,1,0:T(8,128)(2,1)S(1)} collective-permute-done((bf16[4,48,352]{2,1,0:T(8,128)(2,1)S(1)}, bf16[4,48,352]{2,1,0:T(8,128)(2,1)S(1)}, u32[]{:S(2)}, u32[]{:S(2)}) %collective-permute-start.18) | collective-permute-done | bytes 135200 | tf_op jit(solution)/shard_map/ppermute | solution.py:539
  85.6 0.8 place.1
  (61 shorter events, 5.9 us)
Async XLA Ops:
  0.0 10.0 %copy-start.2 = (bf16[1,1408]{1,0:T(2,128)(2,1)S(1)}, bf16[1,1408]{1,0:T(2,128)(2,1)}, u32[]{:S(2)}) copy-start(bf16[1,1408]{1,0:T(2,128)(2,1)} %refs_4_.1) | copy-start | bytes 8452
  0.0 10.0 %copy-start.7 = (bf16[1,352]{1,0:T(2,128)(2,1)S(1)}, bf16[1,352]{1,0:T(2,128)(2,1)}, u32[]{:S(2)}) copy-start(bf16[1,352]{1,0:T(2,128)(2,1)} %refs_2_.1) | copy-start | bytes 2116
  0.0 10.0 %copy-start.6 = (bf16[1,352]{1,0:T(2,128)(2,1)S(1)}, bf16[1,352]{1,0:T(2,128)(2,1)}, u32[]{:S(2)}) copy-start(bf16[1,352]{1,0:T(2,128)(2,1)} %refs_1_.1) | copy-start | bytes 2116
  0.0 10.0 %copy-start.5 = (bf16[1,352]{1,0:T(2,128)(2,1)S(1)}, bf16[1,352]{1,0:T(2,128)(2,1)}, u32[]{:S(2)}) copy-start(bf16[1,352]{1,0:T(2,128)(2,1)} %refs_0_.1) | copy-start | bytes 2116
  0.0 10.0 %copy-start.1 = (bf16[1,7,7,352]{3,2,1,0:T(8,128)(2,1)S(1)}, bf16[1,7,7,352]{3,2,1,0:T(8,128)(2,1)}, u32[]{:S(2)}) copy-start(bf16[1,7,7,352]{3,2,1,0:T(8,128)(2,1)} %kernel.1) | copy-start | bytes 103492
  0.1 12.8 %collective-permute-start.5 = (bf16[352,704]{1,0:T(8,128)(2,1)}, bf16[352,704]{1,0:T(8,128)(2,1)S(1)}, u32[]{:S(2)}, u32[]{:S(2)}) collective-permute-start(bf16[352,704]{1,0:T(8,128)(2,1)} %bitcast.25), channel_id=1, source_target_pairs={{0,1},{1,0},{16,17},{17,16},{2,3},{3,2},{18,19},{19,18},{4,5},{5,4... | collective-permute-start | bytes 1486856 | tf_op jit(solution)/shard_map/ppermute | solution.py:398
  2.1 8.9 %collective-permute-start = (bf16[4,48,352]{2,1,0:T(8,128)(2,1)S(1)}, bf16[4,48,352]{2,1,0:T(8,128)(2,1)S(1)}, u32[]{:S(2)}, u32[]{:S(2)}) collective-permute-start(bf16[4,48,352]{2,1,0:T(8,128)(2,1)S(1)} %get-tuple-element.72), channel_id=1, source_target_pairs={{28,8},{30,10},{24,12},{26,14},{29,9},{31,11},{25,13},{27,15}} | collective-permute-start | bytes 405512 | tf_op jit(solution)/shard_map/ppermute | solution.py:393
  6.3 4.7 %collective-permute-start.1 = (bf16[4,48,352]{2,1,0:T(8,128)(2,1)S(1)}, bf16[4,48,352]{2,1,0:T(8,128)(2,1)S(1)}, u32[]{:S(2)}, u32[]{:S(2)}) collective-permute-start(bf16[4,48,352]{2,1,0:T(8,128)(2,1)S(1)} %get-tuple-element.74), channel_id=1, source_target_pairs={{30,8},{28,10},{26,12},{24,14},{31,9},{29,11},{27,13},{25,15}} | collective-permute-start | bytes 405512 | tf_op jit(solution)/shard_map/ppermute | solution.py:393
  8.6 4.3 %collective-permute-start.2 = (bf16[4,48,352]{2,1,0:T(8,128)(2,1)S(1)}, bf16[4,48,352]{2,1,0:T(8,128)(2,1)S(1)}, u32[]{:S(2)}, u32[]{:S(2)}) collective-permute-start(bf16[4,48,352]{2,1,0:T(8,128)(2,1)S(1)} %get-tuple-element.71), channel_id=1, source_target_pairs={{26,8},{24,10},{30,12},{28,14},{27,9},{25,11},{31,13},{29,15}} | collective-permute-start | bytes 405512 | tf_op jit(solution)/shard_map/ppermute | solution.py:393
  10.3 0.7 collective-permute-start.3
  12.9 1.7 %collective-permute-start.6 = (bf16[16,48,352]{2,1,0:T(8,128)(2,1)S(1)}, bf16[16,48,352]{2,1,0:T(8,128)(2,1)S(1)}, u32[]{:S(2)}, u32[]{:S(2)}) collective-permute-start(bf16[16,48,352]{2,1,0:T(8,128)(2,1)S(1)} %get-tuple-element.45), channel_id=1, source_target_pairs={{8,0},{9,1},{10,2},{11,3},{12,4},{13,5},{14,6},{15,7}} | collective-permute-start | bytes 1622024 | tf_op jit(solution)/shard_map/ppermute | solution.py:420
  13.9 0.7 collective-permute-start.4
  14.7 0.7 collective-permute-start.7
  15.4 6.0 %collective-permute-start.8 = (bf16[16,48,352]{2,1,0:T(8,128)(2,1)S(1)}, bf16[16,48,352]{2,1,0:T(8,128)(2,1)S(1)}, u32[]{:S(2)}, u32[]{:S(2)}) collective-permute-start(bf16[16,48,352]{2,1,0:T(8,128)(2,1)S(1)} %down.1.prev.refs_4_), channel_id=1, source_target_pairs={{0,8},{1,9},{2,10},{3,11},{4,12},{5,13},{6,14},{7,15}} | collective-permute-start | bytes 1622024 | tf_op jit(solution)/shard_map/ppermute | solution.py:420
  16.1 13.3 %collective-permute-start.9 = (bf16[352,704]{1,0:T(8,128)(2,1)S(1)}, bf16[352,704]{1,0:T(8,128)(2,1)S(1)}, u32[]{:S(2)}, u32[]{:S(2)}) collective-permute-start(bf16[352,704]{1,0:T(8,128)(2,1)S(1)} %bitcast.27), channel_id=1, source_target_pairs={{8,9},{9,8},{24,25},{25,24},{10,11},{11,10},{26,27},{27,26},{12,13... | collective-permute-start | bytes 1486856 | tf_op jit(solution)/shard_map/ppermute | solution.py:398
  18.3 16.9 %collective-permute-start.10 = (bf16[704,352]{1,0:T(8,128)(2,1)S(1)}, bf16[704,352]{1,0:T(8,128)(2,1)S(1)}, u32[]{:S(2)}, u32[]{:S(2)}) collective-permute-start(bf16[704,352]{1,0:T(8,128)(2,1)S(1)} %bitcast.15), channel_id=1, source_target_pairs={{8,9},{9,8},{24,25},{25,24},{10,11},{11,10},{26,27},{27,26},{12,13... | collective-permute-start | bytes 1486856 | tf_op jit(solution)/shard_map/ppermute | solution.py:398
  35.2 2.8 %collective-permute-start.11 = (bf16[4,48,352]{2,1,0:T(8,128)(2,1)S(1)}, bf16[4,48,352]{2,1,0:T(8,128)(2,1)S(1)}, u32[]{:S(2)}, u32[]{:S(2)}) collective-permute-start(bf16[4,48,352]{2,1,0:T(8,128)(2,1)S(1)} %down_piece.8.refs_0_), channel_id=1, source_target_pairs={{8,16},{9,17},{10,18},{11,19},{12,20},{13,21},{14,22},{15,23}} | collective-permute-start | bytes 405512 | tf_op jit(solution)/shard_map/ppermute | solution.py:420
  35.9 2.1 %collective-permute-start.12 = (bf16[4,48,352]{2,1,0:T(8,128)(2,1)S(1)}, bf16[4,48,352]{2,1,0:T(8,128)(2,1)S(1)}, u32[]{:S(2)}, u32[]{:S(2)}) collective-permute-start(bf16[4,48,352]{2,1,0:T(8,128)(2,1)S(1)} %down_piece.9.refs_1_), channel_id=1, source_target_pairs={{8,16},{9,17},{10,18},{11,19},{12,20},{13,21},{14,22},{15,23}} | collective-permute-start | bytes 405512 | tf_op jit(solution)/shard_map/ppermute | solution.py:420
  36.6 1.5 %collective-permute-start.13 = (bf16[4,48,352]{2,1,0:T(8,128)(2,1)S(1)}, bf16[4,48,352]{2,1,0:T(8,128)(2,1)S(1)}, u32[]{:S(2)}, u32[]{:S(2)}) collective-permute-start(bf16[4,48,352]{2,1,0:T(8,128)(2,1)S(1)} %down_piece.10.refs_2_), channel_id=1, source_target_pairs={{8,16},{9,17},{10,18},{11,19},{12,20},{13,21},{14,22},{15,23}} | collective-permute-start | bytes 405512 | tf_op jit(solution)/shard_map/ppermute | solution.py:420
  37.3 0.8 collective-permute-start.14
  38.4 28.5 %collective-permute-start.15 = (bf16[16,48,352]{2,1,0:T(8,128)(2,1)S(1)}, bf16[16,48,352]{2,1,0:T(8,128)(2,1)S(1)}, u32[]{:S(2)}, u32[]{:S(2)}) collective-permute-start(bf16[16,48,352]{2,1,0:T(8,128)(2,1)S(1)} %mlp.1.prev), channel_id=1, source_target_pairs={{16,24},{17,25},{18,26},{19,27},{20,28},{21,29},{22,30},{23,31}} | collective-permute-start | bytes 1622024 | tf_op jit(solution)/shard_map/ppermute | solution.py:420
  75.4 6.5 %collective-permute-start.16 = (bf16[4,48,352]{2,1,0:T(8,128)(2,1)S(1)}, bf16[4,48,352]{2,1,0:T(8,128)(2,1)S(1)}, u32[]{:S(2)}, u32[]{:S(2)}) collective-permute-start(bf16[4,48,352]{2,1,0:T(8,128)(2,1)S(1)} %down_piece.13), channel_id=1, source_target_pairs={{0,4},{2,6},{4,0},{6,2},{1,5},{3,7},{5,1},{7,3},{8,12},{10,14},{12... | collective-permute-start | bytes 405512 | tf_op jit(solution)/shard_map/ppermute | solution.py:539
  78.3 6.0 %collective-permute-start.17 = (bf16[4,48,352]{2,1,0:T(8,128)(2,1)S(1)}, bf16[4,48,352]{2,1,0:T(8,128)(2,1)S(1)}, u32[]{:S(2)}, u32[]{:S(2)}) collective-permute-start(bf16[4,48,352]{2,1,0:T(8,128)(2,1)S(1)} %down_piece.14), channel_id=1, source_target_pairs={{0,6},{2,4},{4,2},{6,0},{1,7},{3,5},{5,3},{7,1},{8,14},{10,12},{12... | collective-permute-start | bytes 405512 | tf_op jit(solution)/shard_map/ppermute | solution.py:539
  79.9 5.6 %collective-permute-start.18 = (bf16[4,48,352]{2,1,0:T(8,128)(2,1)S(1)}, bf16[4,48,352]{2,1,0:T(8,128)(2,1)S(1)}, u32[]{:S(2)}, u32[]{:S(2)}) collective-permute-start(bf16[4,48,352]{2,1,0:T(8,128)(2,1)S(1)} %down_piece.15), channel_id=1, source_target_pairs={{0,2},{2,0},{4,6},{6,4},{1,3},{3,1},{5,7},{7,5},{8,10},{10,8},{12,... | collective-permute-start | bytes 405512 | tf_op jit(solution)/shard_map/ppermute | solution.py:539
  (5 other events, 32.6 us)

commit v4 on v3

--- a/solution.py
+++ b/solution.py
@@ -482,9 +482,9 @@
     x, flat = conv_pieces(pieces, send(cpar, 0, helper), order, helper)
     flat, other_in = lax.optimization_barrier((flat, other_in))
     flat = send(flat, helper, 0)
+    x, other_out = lax.optimization_barrier((x, other_out))
+    x = send(x, helper, 0)
     act_a, ssq = up_own(flat, 0)
-    x, other_out, act_a = lax.optimization_barrier((x, other_out, act_a))
-    x = send(x, helper, 0)
     act_b, scale = up_other(flat, other_in, ssq, 0)
     result = call(
         first_down_kernel,

time: 87 us -> 89.3 us (1.026)
  local copies, waits for them, and re-layouts: 1.44 us -> 7.76 us
  waiting for transfers between devices: 47.6 us -> 42.7 us
    unnamed x20, local copies, waits for them, and re-layouts: 0.24 us -> 6.57 us
    ppermute x4, waiting for transfers between devices: 13.7 us -> 10.6 us  [other_half(): return lax.ppermute(x, ('section', 'dp'), pairs)]
    ppermute x9, waiting for transfers between devices: 27.2 us -> 24.2 us  [send(): return lax.ppermute(x, 'section', [(start, end)])]
    ppermute x3, waiting for transfers between devices: 1.85 us -> 2.86 us  [image_plan(): piece = lax.ppermute(piece, ('section', 'row'), pairs)]
  transfers between devices with their start and end apart: 19 -> 19, of which waited for: 7 -> 8; matrix products, arithmetic and copies ran while one was open for 1% -> 1% of each run, Pallas kernels for 2% -> 2%
where the time goes in v4:
time: 89.3 us; the launch traced here: 88.7 us
  waiting for transfers between devices  42.7 us (48%)
  starting transfers between devices  26.1 us (29%)
  Pallas kernels  11.5 us (13%)
  local copies, waits for them, and re-layouts  7.76 us (9%)
    ppermute x9, waiting for transfers between devices, send(): return lax.ppermute(x, 'section', [(start, end)])  24.2 us
    pallas_call x26, Pallas kernels, call(): pl.pallas_call(functools.partial(kernel, **static), out_shape=out, in_spe...  11.5 us
    ppermute x4, waiting for transfers between devices, other_half(): return lax.ppermute(x, ('section', 'dp'), pairs)  10.6 us
    ppermute x3, starting transfers between devices, image_plan(): piece = lax.ppermute(piece, ('section', 'row'), pairs)  8.46 us
    ppermute x9, starting transfers between devices, send(): return lax.ppermute(x, 'section', [(start, end)])  6.84 us
    ppermute x4, starting transfers between devices, other_half(): return lax.ppermute(x, ('section', 'dp'), pairs)  6.66 us
    unnamed x20, local copies, waits for them, and re-layouts  6.57 us
    ppermute x3, waiting for transfers between devices, image_plan(): lax.ppermute(piece, 'row', [(p, p ^ order[n]) for p in range(count)])  5.06 us
  transfers between devices with their start and end apart: 19, of which 8 were waited for; matrix products, arithmetic and copies ran while one was open for 1% of the time, Pallas kernels for 2%

profile of v4, /device:TPU:7, one launch (start us, length us, event | category | flops | bytes accessed | tf_op | source)
XLA Modules:
  0.0 88.7 jit_solution(3581090594565373529)
XLA Ops:
  0.7 0.7 collective-permute-start.4
  1.4 0.8 copy-done.1
  7.9 1.2 %dynamic-slice_bitcast_fusion = (bf16[4,48,352]{2,1,0:T(8,128)(2,1)S(1)}, bf16[4,48,352]{2,1,0:T(8,128)(2,1)S(1)}, bf16[4,48,352]{2,1,0:T(8,128)(2,1)S(1)}, bf16[4,48,352]{2,1,0:T(8,128)(2,1)S(1)}) fusion(bf16[4,1,4,48,352]{4,3,2,1,0:T(8,128)(2,1)} %param.11, s32[]{:T(128)S(6)} %select_n.16, s32[]{:T(128)S(6)} %select_n.14, s32[]{:T(128)S(6)} %select_n.13, ...), kind=kLoop, calls=%fused_computation | loop fusion | bytes 1081360 | tf_op jit(solution)/shard_map/squeeze | solution.py:390
  9.1 4.8 %collective-permute-start = (bf16[4,48,352]{2,1,0:T(8,128)(2,1)S(1)}, bf16[4,48,352]{2,1,0:T(8,128)(2,1)S(1)}, u32[]{:S(2)}, u32[]{:S(2)}) collective-permute-start(bf16[4,48,352]{2,1,0:T(8,128)(2,1)S(1)} %get-tuple-element.70), channel_id=1, source_target_pairs={{28,8},{30,10},{24,12},{26,14},{29,9},{31,11},{25,13},{27,15}} | collective-permute-start | bytes 405512 | tf_op jit(solution)/shard_map/ppermute | solution.py:393
  13.9 2.3 %collective-permute-start.1 = (bf16[4,48,352]{2,1,0:T(8,128)(2,1)S(1)}, bf16[4,48,352]{2,1,0:T(8,128)(2,1)S(1)}, u32[]{:S(2)}, u32[]{:S(2)}) collective-permute-start(bf16[4,48,352]{2,1,0:T(8,128)(2,1)S(1)} %get-tuple-element.72), channel_id=1, source_target_pairs={{30,8},{28,10},{26,12},{24,14},{31,9},{29,11},{27,13},{25,15}} | collective-permute-start | bytes 405512 | tf_op jit(solution)/shard_map/ppermute | solution.py:393
  16.2 1.3 %collective-permute-start.2 = (bf16[4,48,352]{2,1,0:T(8,128)(2,1)S(1)}, bf16[4,48,352]{2,1,0:T(8,128)(2,1)S(1)}, u32[]{:S(2)}, u32[]{:S(2)}) collective-permute-start(bf16[4,48,352]{2,1,0:T(8,128)(2,1)S(1)} %get-tuple-element.69), channel_id=1, source_target_pairs={{26,8},{24,10},{30,12},{28,14},{27,9},{25,11},{31,13},{29,15}} | collective-permute-start | bytes 405512 | tf_op jit(solution)/shard_map/ppermute | solution.py:393
  17.6 0.7 collective-permute-done.1.piece.refs_2_
  18.3 2.1 %collective-permute-done.2.refs_3_ = bf16[4,48,352]{2,1,0:T(8,128)(2,1)S(1)} collective-permute-done((bf16[4,48,352]{2,1,0:T(8,128)(2,1)S(1)}, bf16[4,48,352]{2,1,0:T(8,128)(2,1)S(1)}, u32[]{:S(2)}, u32[]{:S(2)}) %collective-permute-start.2) | collective-permute-done | bytes 135200 | tf_op jit(solution)/shard_map/ppermute | solution.py:393
  20.5 0.8 collective-permute-start.7
  21.3 0.7 collective-permute-start.5
  22.1 1.0 %copy-done = bf16[1,704,352]{2,1,0:T(8,128)(2,1)S(1)} copy-done((bf16[1,704,352]{2,1,0:T(8,128)(2,1)S(1)}, bf16[1,704,352]{2,1,0:T(8,128)(2,1)}, u32[]{:S(2)}) %copy-start) | copy-done | bytes 495640
  23.8 2.1 %collective-permute-start.9 = (bf16[352,704]{1,0:T(8,128)(2,1)S(1)}, bf16[352,704]{1,0:T(8,128)(2,1)S(1)}, u32[]{:S(2)}, u32[]{:S(2)}) collective-permute-start(bf16[352,704]{1,0:T(8,128)(2,1)S(1)} %bitcast.27), channel_id=1, source_target_pairs={{8,9},{9,8},{24,25},{25,24},{10,11},{11,10},{26,27},{27,26},{12,13... | collective-permute-start | bytes 1486856 | tf_op jit(solution)/shard_map/ppermute | solution.py:398
  25.9 3.1 %collective-permute-start.10 = (bf16[704,352]{1,0:T(8,128)(2,1)S(1)}, bf16[704,352]{1,0:T(8,128)(2,1)S(1)}, u32[]{:S(2)}, u32[]{:S(2)}) collective-permute-start(bf16[704,352]{1,0:T(8,128)(2,1)S(1)} %bitcast.15), channel_id=1, source_target_pairs={{8,9},{9,8},{24,25},{25,24},{10,11},{11,10},{26,27},{27,26},{12,13... | collective-permute-start | bytes 1486856 | tf_op jit(solution)/shard_map/ppermute | solution.py:398
  29.2 4.8 %collective-permute-done.9.w_in.in_b = bf16[352,704]{1,0:T(8,128)(2,1)S(1)} collective-permute-done((bf16[352,704]{1,0:T(8,128)(2,1)S(1)}, bf16[352,704]{1,0:T(8,128)(2,1)S(1)}, u32[]{:S(2)}, u32[]{:S(2)}) %collective-permute-start.9) | collective-permute-done | bytes 495648 | tf_op jit(solution)/shard_map/ppermute | solution.py:398
  33.9 5.8 %collective-permute-done.10.out_b = bf16[704,352]{1,0:T(8,128)(2,1)S(1)} collective-permute-done((bf16[704,352]{1,0:T(8,128)(2,1)S(1)}, bf16[704,352]{1,0:T(8,128)(2,1)S(1)}, u32[]{:S(2)}, u32[]{:S(2)}) %collective-permute-start.10) | collective-permute-done | bytes 495648 | tf_op jit(solution)/shard_map/ppermute | solution.py:398
  42.9 1.3 %collective-permute-start.15 = (bf16[16,48,352]{2,1,0:T(8,128)(2,1)S(1)}, bf16[16,48,352]{2,1,0:T(8,128)(2,1)S(1)}, u32[]{:S(2)}, u32[]{:S(2)}) collective-permute-start(bf16[16,48,352]{2,1,0:T(8,128)(2,1)S(1)} %mlp.1.prev), channel_id=1, source_target_pairs={{16,24},{17,25},{18,26},{19,27},{20,28},{21,29},{22,30},{23,31}} | collective-permute-start | bytes 1622024 | tf_op jit(solution)/shard_map/ppermute | solution.py:420
  44.2 24.2 %collective-permute-done.15.x = bf16[16,48,352]{2,1,0:T(8,128)(2,1)S(1)} collective-permute-done((bf16[16,48,352]{2,1,0:T(8,128)(2,1)S(1)}, bf16[16,48,352]{2,1,0:T(8,128)(2,1)S(1)}, u32[]{:S(2)}, u32[]{:S(2)}) %collective-permute-start.15) | collective-permute-done | bytes 540704 | tf_op jit(solution)/shard_map/ppermute | solution.py:420
  68.4 8.1 %conv_up.1 = (bf16[768,704]{1,0:T(8,128)(2,1)S(1)}, bf16[768,704]{1,0:T(8,128)(2,1)S(1)}, f32[2,1,704]{2,1,0:T(1,128)S(1)}) custom-call(s32[1]{0:T(128)} %bitcast.1.section, bf16[16,48,352]{2,1,0:T(8,128)(2,1)S(1)} %collective-permute-done.15.x, f32[64,384]{1,0:T(8,128)S(1)} %get-tuple-element.37.cpar.refs_7_, bf16[352,704]{1,0:T(8,128)(2,1)S(1)} %bitcast.30, ...), custom_call_target="tpu_custom_call" | custom-call | flops 761266176 | bytes 1647108 | tf_op jit(solution)/shard_map/conv_up/pallas_call | solution.py:334
  77.0 3.0 %collective-permute-start.16 = (bf16[4,48,352]{2,1,0:T(8,128)(2,1)S(1)}, bf16[4,48,352]{2,1,0:T(8,128)(2,1)S(1)}, u32[]{:S(2)}, u32[]{:S(2)}) collective-permute-start(bf16[4,48,352]{2,1,0:T(8,128)(2,1)S(1)} %down_piece.13), channel_id=1, source_target_pairs={{0,4},{2,6},{4,0},{6,2},{1,5},{3,7},{5,1},{7,3},{8,12},{10,14},{12... | collective-permute-start | bytes 405512 | tf_op jit(solution)/shard_map/ppermute | solution.py:539
  80.5 1.0 %collective-permute-start.17 = (bf16[4,48,352]{2,1,0:T(8,128)(2,1)S(1)}, bf16[4,48,352]{2,1,0:T(8,128)(2,1)S(1)}, u32[]{:S(2)}, u32[]{:S(2)}) collective-permute-start(bf16[4,48,352]{2,1,0:T(8,128)(2,1)S(1)} %down_piece.14), channel_id=1, source_target_pairs={{0,6},{2,4},{4,2},{6,0},{1,7},{3,5},{5,3},{7,1},{8,14},{10,12},{12... | collective-permute-start | bytes 405512 | tf_op jit(solution)/shard_map/ppermute | solution.py:539
  82.6 1.5 %collective-permute-done.16.refs_1_ = bf16[4,48,352]{2,1,0:T(8,128)(2,1)S(1)} collective-permute-done((bf16[4,48,352]{2,1,0:T(8,128)(2,1)S(1)}, bf16[4,48,352]{2,1,0:T(8,128)(2,1)S(1)}, u32[]{:S(2)}, u32[]{:S(2)}) %collective-permute-start.16) | collective-permute-done | bytes 135200 | tf_op jit(solution)/shard_map/ppermute | solution.py:539
  84.1 2.4 %collective-permute-done.17.refs_2_ = bf16[4,48,352]{2,1,0:T(8,128)(2,1)S(1)} collective-permute-done((bf16[4,48,352]{2,1,0:T(8,128)(2,1)S(1)}, bf16[4,48,352]{2,1,0:T(8,128)(2,1)S(1)}, u32[]{:S(2)}, u32[]{:S(2)}) %collective-permute-start.17) | collective-permute-done | bytes 135200 | tf_op jit(solution)/shard_map/ppermute | solution.py:539
  86.5 1.2 %collective-permute-done.18.refs_3_ = bf16[4,48,352]{2,1,0:T(8,128)(2,1)S(1)} collective-permute-done((bf16[4,48,352]{2,1,0:T(8,128)(2,1)S(1)}, bf16[4,48,352]{2,1,0:T(8,128)(2,1)S(1)}, u32[]{:S(2)}, u32[]{:S(2)}) %collective-permute-start.18) | collective-permute-done | bytes 135200 | tf_op jit(solution)/shard_map/ppermute | solution.py:539
  87.7 0.8 place.1
  (61 shorter events, 12.2 us)
Async XLA Ops:
  0.0 20.5 %collective-permute-start.6 = (bf16[352,704]{1,0:T(8,128)(2,1)}, bf16[352,704]{1,0:T(8,128)(2,1)S(1)}, u32[]{:S(2)}, u32[]{:S(2)}) collective-permute-start(bf16[352,704]{1,0:T(8,128)(2,1)} %bitcast.25), channel_id=1, source_target_pairs={{0,1},{1,0},{16,17},{17,16},{2,3},{3,2},{18,19},{19,18},{4,5},{5,4... | collective-permute-start | bytes 1486856 | tf_op jit(solution)/shard_map/ppermute | solution.py:398
  0.7 20.6 %collective-permute-start.4 = (bf16[704,352]{1,0:T(8,128)(2,1)}, bf16[704,352]{1,0:T(8,128)(2,1)S(1)}, u32[]{:S(2)}, u32[]{:S(2)}) collective-permute-start(bf16[704,352]{1,0:T(8,128)(2,1)} %bitcast.13), channel_id=1, source_target_pairs={{0,1},{1,0},{16,17},{17,16},{2,3},{3,2},{18,19},{19,18},{4,5},{5,4... | collective-permute-start | bytes 1486856 | tf_op jit(solution)/shard_map/ppermute | solution.py:398
  1.4 0.8 copy-start.1
  2.2 0.7 copy-start.2
  2.9 0.7 copy-start.3
  7.2 9.0 %collective-permute-start.3 = (f32[64,384]{1,0:T(8,128)S(1)}, f32[64,384]{1,0:T(8,128)S(1)}, u32[]{:S(2)}, u32[]{:S(2)}) collective-permute-start(f32[64,384]{1,0:T(8,128)S(1)} %get-tuple-element.37.cpar.refs_7_), channel_id=1, source_target_pairs={{0,8},{1,9},{2,10},{3,11},{4,12},{5,13},{6,14},{7,15}} | collective-permute-start | bytes 294920 | tf_op jit(solution)/shard_map/ppermute | solution.py:420
  9.1 8.5 %collective-permute-start = (bf16[4,48,352]{2,1,0:T(8,128)(2,1)S(1)}, bf16[4,48,352]{2,1,0:T(8,128)(2,1)S(1)}, u32[]{:S(2)}, u32[]{:S(2)}) collective-permute-start(bf16[4,48,352]{2,1,0:T(8,128)(2,1)S(1)} %get-tuple-element.70), channel_id=1, source_target_pairs={{28,8},{30,10},{24,12},{26,14},{29,9},{31,11},{25,13},{27,15}} | collective-permute-start | bytes 405512 | tf_op jit(solution)/shard_map/ppermute | solution.py:393
  13.9 4.4 %collective-permute-start.1 = (bf16[4,48,352]{2,1,0:T(8,128)(2,1)S(1)}, bf16[4,48,352]{2,1,0:T(8,128)(2,1)S(1)}, u32[]{:S(2)}, u32[]{:S(2)}) collective-permute-start(bf16[4,48,352]{2,1,0:T(8,128)(2,1)S(1)} %get-tuple-element.72), channel_id=1, source_target_pairs={{30,8},{28,10},{26,12},{24,14},{31,9},{29,11},{27,13},{25,15}} | collective-permute-start | bytes 405512 | tf_op jit(solution)/shard_map/ppermute | solution.py:393
  16.2 4.2 %collective-permute-start.2 = (bf16[4,48,352]{2,1,0:T(8,128)(2,1)S(1)}, bf16[4,48,352]{2,1,0:T(8,128)(2,1)S(1)}, u32[]{:S(2)}, u32[]{:S(2)}) collective-permute-start(bf16[4,48,352]{2,1,0:T(8,128)(2,1)S(1)} %get-tuple-element.69), channel_id=1, source_target_pairs={{26,8},{24,10},{30,12},{28,14},{27,9},{25,11},{31,13},{29,15}} | collective-permute-start | bytes 405512 | tf_op jit(solution)/shard_map/ppermute | solution.py:393
  20.5 1.6 %copy-start.9 = (bf16[1,352,704]{2,1,0:T(8,128)(2,1)S(1)}, bf16[1,352,704]{2,1,0:T(8,128)(2,1)}, u32[]{:S(2)}) copy-start(bf16[1,352,704]{2,1,0:T(8,128)(2,1)} %param.16) | copy-start | bytes 1486852
  20.5 1.5 %collective-permute-start.7 = (bf16[16,48,352]{2,1,0:T(8,128)(2,1)S(1)}, bf16[16,48,352]{2,1,0:T(8,128)(2,1)S(1)}, u32[]{:S(2)}, u32[]{:S(2)}) collective-permute-start(bf16[16,48,352]{2,1,0:T(8,128)(2,1)S(1)} %get-tuple-element.45), channel_id=1, source_target_pairs={{8,0},{9,1},{10,2},{11,3},{12,4},{13,5},{14,6},{15,7}} | collective-permute-start | bytes 1622024 | tf_op jit(solution)/shard_map/ppermute | solution.py:420
  21.3 0.8 collective-permute-start.5
  22.1 1.1 %copy-start = (bf16[1,704,352]{2,1,0:T(8,128)(2,1)S(1)}, bf16[1,704,352]{2,1,0:T(8,128)(2,1)}, u32[]{:S(2)}) copy-start(bf16[1,704,352]{2,1,0:T(8,128)(2,1)} %param.20) | copy-start | bytes 1486852
  23.1 6.0 %collective-permute-start.8 = (bf16[16,48,352]{2,1,0:T(8,128)(2,1)S(1)}, bf16[16,48,352]{2,1,0:T(8,128)(2,1)S(1)}, u32[]{:S(2)}, u32[]{:S(2)}) collective-permute-start(bf16[16,48,352]{2,1,0:T(8,128)(2,1)S(1)} %down.1.prev.refs_4_), channel_id=1, source_target_pairs={{0,8},{1,9},{2,10},{3,11},{4,12},{5,13},{6,14},{7,15}} | collective-permute-start | bytes 1622024 | tf_op jit(solution)/shard_map/ppermute | solution.py:420
  23.8 10.1 %collective-permute-start.9 = (bf16[352,704]{1,0:T(8,128)(2,1)S(1)}, bf16[352,704]{1,0:T(8,128)(2,1)S(1)}, u32[]{:S(2)}, u32[]{:S(2)}) collective-permute-start(bf16[352,704]{1,0:T(8,128)(2,1)S(1)} %bitcast.27), channel_id=1, source_target_pairs={{8,9},{9,8},{24,25},{25,24},{10,11},{11,10},{26,27},{27,26},{12,13... | collective-permute-start | bytes 1486856 | tf_op jit(solution)/shard_map/ppermute | solution.py:398
  25.9 13.8 %collective-permute-start.10 = (bf16[704,352]{1,0:T(8,128)(2,1)S(1)}, bf16[704,352]{1,0:T(8,128)(2,1)S(1)}, u32[]{:S(2)}, u32[]{:S(2)}) collective-permute-start(bf16[704,352]{1,0:T(8,128)(2,1)S(1)} %bitcast.15), channel_id=1, source_target_pairs={{8,9},{9,8},{24,25},{25,24},{10,11},{11,10},{26,27},{27,26},{12,13... | collective-permute-start | bytes 1486856 | tf_op jit(solution)/shard_map/ppermute | solution.py:398
  39.7 2.8 %collective-permute-start.11 = (bf16[4,48,352]{2,1,0:T(8,128)(2,1)S(1)}, bf16[4,48,352]{2,1,0:T(8,128)(2,1)S(1)}, u32[]{:S(2)}, u32[]{:S(2)}) collective-permute-start(bf16[4,48,352]{2,1,0:T(8,128)(2,1)S(1)} %down_piece.8.refs_0_), channel_id=1, source_target_pairs={{8,16},{9,17},{10,18},{11,19},{12,20},{13,21},{14,22},{15,23}} | collective-permute-start | bytes 405512 | tf_op jit(solution)/shard_map/ppermute | solution.py:420
  40.4 2.1 %collective-permute-start.12 = (bf16[4,48,352]{2,1,0:T(8,128)(2,1)S(1)}, bf16[4,48,352]{2,1,0:T(8,128)(2,1)S(1)}, u32[]{:S(2)}, u32[]{:S(2)}) collective-permute-start(bf16[4,48,352]{2,1,0:T(8,128)(2,1)S(1)} %down_piece.9.refs_1_), channel_id=1, source_target_pairs={{8,16},{9,17},{10,18},{11,19},{12,20},{13,21},{14,22},{15,23}} | collective-permute-start | bytes 405512 | tf_op jit(solution)/shard_map/ppermute | solution.py:420
  41.1 1.5 %collective-permute-start.13 = (bf16[4,48,352]{2,1,0:T(8,128)(2,1)S(1)}, bf16[4,48,352]{2,1,0:T(8,128)(2,1)S(1)}, u32[]{:S(2)}, u32[]{:S(2)}) collective-permute-start(bf16[4,48,352]{2,1,0:T(8,128)(2,1)S(1)} %down_piece.10.refs_2_), channel_id=1, source_target_pairs={{8,16},{9,17},{10,18},{11,19},{12,20},{13,21},{14,22},{15,23}} | collective-permute-start | bytes 405512 | tf_op jit(solution)/shard_map/ppermute | solution.py:420
  41.9 0.8 collective-permute-start.14
  42.9 25.5 %collective-permute-start.15 = (bf16[16,48,352]{2,1,0:T(8,128)(2,1)S(1)}, bf16[16,48,352]{2,1,0:T(8,128)(2,1)S(1)}, u32[]{:S(2)}, u32[]{:S(2)}) collective-permute-start(bf16[16,48,352]{2,1,0:T(8,128)(2,1)S(1)} %mlp.1.prev), channel_id=1, source_target_pairs={{16,24},{17,25},{18,26},{19,27},{20,28},{21,29},{22,30},{23,31}} | collective-permute-start | bytes 1622024 | tf_op jit(solution)/shard_map/ppermute | solution.py:420
  77.0 7.1 %collective-permute-start.16 = (bf16[4,48,352]{2,1,0:T(8,128)(2,1)S(1)}, bf16[4,48,352]{2,1,0:T(8,128)(2,1)S(1)}, u32[]{:S(2)}, u32[]{:S(2)}) collective-permute-start(bf16[4,48,352]{2,1,0:T(8,128)(2,1)S(1)} %down_piece.13), channel_id=1, source_target_pairs={{0,4},{2,6},{4,0},{6,2},{1,5},{3,7},{5,1},{7,3},{8,12},{10,14},{12... | collective-permute-start | bytes 405512 | tf_op jit(solution)/shard_map/ppermute | solution.py:539
  80.5 6.0 %collective-permute-start.17 = (bf16[4,48,352]{2,1,0:T(8,128)(2,1)S(1)}, bf16[4,48,352]{2,1,0:T(8,128)(2,1)S(1)}, u32[]{:S(2)}, u32[]{:S(2)}) collective-permute-start(bf16[4,48,352]{2,1,0:T(8,128)(2,1)S(1)} %down_piece.14), channel_id=1, source_target_pairs={{0,6},{2,4},{4,2},{6,0},{1,7},{3,5},{5,3},{7,1},{8,14},{10,12},{12... | collective-permute-start | bytes 405512 | tf_op jit(solution)/shard_map/ppermute | solution.py:539
  82.0 5.6 %collective-permute-start.18 = (bf16[4,48,352]{2,1,0:T(8,128)(2,1)S(1)}, bf16[4,48,352]{2,1,0:T(8,128)(2,1)S(1)}, u32[]{:S(2)}, u32[]{:S(2)}) collective-permute-start(bf16[4,48,352]{2,1,0:T(8,128)(2,1)S(1)} %down_piece.15), channel_id=1, source_target_pairs={{0,2},{2,0},{4,6},{6,4},{1,3},{3,1},{5,7},{7,5},{8,10},{10,8},{12,... | collective-permute-start | bytes 405512 | tf_op jit(solution)/shard_map/ppermute | solution.py:539
  (5 other events, 3.4 us)

commit v5 on v4

--- a/solution.py
+++ b/solution.py
@@ -480,10 +480,7 @@
         )
 
     x, flat = conv_pieces(pieces, send(cpar, 0, helper), order, helper)
-    flat, other_in = lax.optimization_barrier((flat, other_in))
-    flat = send(flat, helper, 0)
-    x, other_out = lax.optimization_barrier((x, other_out))
-    x = send(x, helper, 0)
+    flat, x = send(flat, helper, 0), send(x, helper, 0)
     act_a, ssq = up_own(flat, 0)
     act_b, scale = up_other(flat, other_in, ssq, 0)
     result = call(

time: 89.3 us -> 83.5 us (0.935)
  local copies, waits for them, and re-layouts: 7.76 us -> 1.27 us
  waiting for transfers between devices: 42.7 us -> 44.3 us
    unnamed x20, local copies, waits for them, and re-layouts: 6.57 us -> 0.04 us
    ppermute x4, waiting for transfers between devices: 10.6 us -> 13.5 us  [other_half(): return lax.ppermute(x, ('section', 'dp'), pairs)]
    ppermute x3, waiting for transfers between devices: 2.86 us -> 1.85 us  [image_plan(): piece = lax.ppermute(piece, ('section', 'row'), pairs)]
  transfers between devices with their start and end apart: 19 -> 19, of which waited for: 8 -> 7; matrix products, arithmetic and copies ran while one was open for 1% -> 0% of each run, Pallas kernels for 2% -> 2%
where the time goes in v5:
time: 83.5 us; the launch traced here: 83.1 us
  waiting for transfers between devices  44.3 us (53%)
  starting transfers between devices  25.3 us (30%)
  Pallas kernels  11.6 us (14%)
  local copies, waits for them, and re-layouts  1.27 us (2%)
    ppermute x9, waiting for transfers between devices, send(): return lax.ppermute(x, 'section', [(start, end)])  24.3 us
    ppermute x4, waiting for transfers between devices, other_half(): return lax.ppermute(x, ('section', 'dp'), pairs)  13.5 us
    pallas_call x26, Pallas kernels, call(): pl.pallas_call(functools.partial(kernel, **static), out_shape=out, in_spe...  11.6 us
    ppermute x3, starting transfers between devices, image_plan(): piece = lax.ppermute(piece, ('section', 'row'), pairs)  7.8 us
    ppermute x9, starting transfers between devices, send(): return lax.ppermute(x, 'section', [(start, end)])  6.85 us
    ppermute x4, starting transfers between devices, other_half(): return lax.ppermute(x, ('section', 'dp'), pairs)  6.67 us
    ppermute x3, waiting for transfers between devices, image_plan(): lax.ppermute(piece, 'row', [(p, p ^ order[n]) for p in range(count)])  4.65 us
    ppermute x3, starting transfers between devices, image_plan(): lax.ppermute(piece, 'row', [(p, p ^ order[n]) for p in range(count)])  3.94 us
  transfers between devices with their start and end apart: 19, of which 7 were waited for; matrix products, arithmetic and copies ran while one was open for 0% of the time, Pallas kernels for 2%

profile of v5, /device:TPU:7, one launch (start us, length us, event | category | flops | bytes accessed | tf_op | source)
XLA Modules:
  0.0 83.1 jit_solution(13666656137364731026)
XLA Ops:
  0.1 1.2 %dynamic-slice_bitcast_fusion = (bf16[4,48,352]{2,1,0:T(8,128)(2,1)S(1)}, bf16[4,48,352]{2,1,0:T(8,128)(2,1)S(1)}, bf16[4,48,352]{2,1,0:T(8,128)(2,1)S(1)}, bf16[4,48,352]{2,1,0:T(8,128)(2,1)S(1)}) fusion(bf16[4,1,4,48,352]{4,3,2,1,0:T(8,128)(2,1)} %param.11, s32[]{:T(128)S(6)} %select_n.16, s32[]{:T(128)S(6)} %select_n.14, s32[]{:T(128)S(6)} %select_n.13, ...), kind=kLoop, calls=%fused_computation | loop fusion | bytes 1081360 | tf_op jit(solution)/shard_map/squeeze | solution.py:390
  1.3 4.2 %collective-permute-start = (bf16[4,48,352]{2,1,0:T(8,128)(2,1)S(1)}, bf16[4,48,352]{2,1,0:T(8,128)(2,1)S(1)}, u32[]{:S(2)}, u32[]{:S(2)}) collective-permute-start(bf16[4,48,352]{2,1,0:T(8,128)(2,1)S(1)} %get-tuple-element.62), channel_id=1, source_target_pairs={{28,8},{30,10},{24,12},{26,14},{29,9},{31,11},{25,13},{27,15}} | collective-permute-start | bytes 405512 | tf_op jit(solution)/shard_map/ppermute | solution.py:393
  5.5 2.3 %collective-permute-start.1 = (bf16[4,48,352]{2,1,0:T(8,128)(2,1)S(1)}, bf16[4,48,352]{2,1,0:T(8,128)(2,1)S(1)}, u32[]{:S(2)}, u32[]{:S(2)}) collective-permute-start(bf16[4,48,352]{2,1,0:T(8,128)(2,1)S(1)} %get-tuple-element.64), channel_id=1, source_target_pairs={{30,8},{28,10},{26,12},{24,14},{31,9},{29,11},{27,13},{25,15}} | collective-permute-start | bytes 405512 | tf_op jit(solution)/shard_map/ppermute | solution.py:393
  7.8 1.3 %collective-permute-start.2 = (bf16[4,48,352]{2,1,0:T(8,128)(2,1)S(1)}, bf16[4,48,352]{2,1,0:T(8,128)(2,1)S(1)}, u32[]{:S(2)}, u32[]{:S(2)}) collective-permute-start(bf16[4,48,352]{2,1,0:T(8,128)(2,1)S(1)} %get-tuple-element.61), channel_id=1, source_target_pairs={{26,8},{24,10},{30,12},{28,14},{27,9},{25,11},{31,13},{29,15}} | collective-permute-start | bytes 405512 | tf_op jit(solution)/shard_map/ppermute | solution.py:393
  10.2 1.8 %collective-permute-done.2.refs_3_ = bf16[4,48,352]{2,1,0:T(8,128)(2,1)S(1)} collective-permute-done((bf16[4,48,352]{2,1,0:T(8,128)(2,1)S(1)}, bf16[4,48,352]{2,1,0:T(8,128)(2,1)S(1)}, u32[]{:S(2)}, u32[]{:S(2)}) %collective-permute-start.2) | collective-permute-done | bytes 135200 | tf_op jit(solution)/shard_map/ppermute | solution.py:393
  12.1 0.8 collective-permute-start.5
  12.9 0.7 collective-permute-start.4
  13.6 0.7 collective-permute-start.6
  14.3 0.7 collective-permute-start.7
  15.1 0.7 collective-permute-start.8
  15.9 2.1 %collective-permute-start.9 = (bf16[352,704]{1,0:T(8,128)(2,1)S(1)}, bf16[352,704]{1,0:T(8,128)(2,1)S(1)}, u32[]{:S(2)}, u32[]{:S(2)}) collective-permute-start(bf16[352,704]{1,0:T(8,128)(2,1)S(1)} %bitcast.27), channel_id=1, source_target_pairs={{8,9},{9,8},{24,25},{25,24},{10,11},{11,10},{26,27},{27,26},{12,13... | collective-permute-start | bytes 1486856 | tf_op jit(solution)/shard_map/ppermute | solution.py:398
  18.0 3.1 %collective-permute-start.10 = (bf16[704,352]{1,0:T(8,128)(2,1)S(1)}, bf16[704,352]{1,0:T(8,128)(2,1)S(1)}, u32[]{:S(2)}, u32[]{:S(2)}) collective-permute-start(bf16[704,352]{1,0:T(8,128)(2,1)S(1)} %bitcast.15), channel_id=1, source_target_pairs={{8,9},{9,8},{24,25},{25,24},{10,11},{11,10},{26,27},{27,26},{12,13... | collective-permute-start | bytes 1486856 | tf_op jit(solution)/shard_map/ppermute | solution.py:398
  21.2 7.7 %collective-permute-done.9.w_in.in_b = bf16[352,704]{1,0:T(8,128)(2,1)S(1)} collective-permute-done((bf16[352,704]{1,0:T(8,128)(2,1)S(1)}, bf16[352,704]{1,0:T(8,128)(2,1)S(1)}, u32[]{:S(2)}, u32[]{:S(2)}) %collective-permute-start.9) | collective-permute-done | bytes 495648 | tf_op jit(solution)/shard_map/ppermute | solution.py:398
  28.9 5.8 %collective-permute-done.10.out_b = bf16[704,352]{1,0:T(8,128)(2,1)S(1)} collective-permute-done((bf16[704,352]{1,0:T(8,128)(2,1)S(1)}, bf16[704,352]{1,0:T(8,128)(2,1)S(1)}, u32[]{:S(2)}, u32[]{:S(2)}) %collective-permute-start.10) | collective-permute-done | bytes 495648 | tf_op jit(solution)/shard_map/ppermute | solution.py:398
  34.7 0.7 collective-permute-start.11
  37.9 1.3 %collective-permute-start.15 = (bf16[16,48,352]{2,1,0:T(8,128)(2,1)S(1)}, bf16[16,48,352]{2,1,0:T(8,128)(2,1)S(1)}, u32[]{:S(2)}, u32[]{:S(2)}) collective-permute-start(bf16[16,48,352]{2,1,0:T(8,128)(2,1)S(1)} %mlp.1.prev), channel_id=1, source_target_pairs={{16,24},{17,25},{18,26},{19,27},{20,28},{21,29},{22,30},{23,31}} | collective-permute-start | bytes 1622024 | tf_op jit(solution)/shard_map/ppermute | solution.py:420
  39.2 24.3 %collective-permute-done.15.x = bf16[16,48,352]{2,1,0:T(8,128)(2,1)S(1)} collective-permute-done((bf16[16,48,352]{2,1,0:T(8,128)(2,1)S(1)}, bf16[16,48,352]{2,1,0:T(8,128)(2,1)S(1)}, u32[]{:S(2)}, u32[]{:S(2)}) %collective-permute-start.15) | collective-permute-done | bytes 540704 | tf_op jit(solution)/shard_map/ppermute | solution.py:420
  63.4 8.1 %conv_up.1 = (bf16[768,704]{1,0:T(8,128)(2,1)S(1)}, bf16[768,704]{1,0:T(8,128)(2,1)S(1)}, f32[2,1,704]{2,1,0:T(1,128)S(1)}) custom-call(s32[1]{0:T(128)} %bitcast.1.section, bf16[16,48,352]{2,1,0:T(8,128)(2,1)S(1)} %collective-permute-done.15.x, f32[64,384]{1,0:T(8,128)S(1)} %get-tuple-element.33.cpar.refs_7_, bf16[352,704]{1,0:T(8,128)(2,1)S(1)} %bitcast.30, ...), custom_call_target="tpu_custom_call" | custom-call | flops 761266176 | bytes 1647108 | tf_op jit(solution)/shard_map/conv_up/pallas_call | solution.py:334
  72.1 2.0 %collective-permute-start.16 = (bf16[4,48,352]{2,1,0:T(8,128)(2,1)S(1)}, bf16[4,48,352]{2,1,0:T(8,128)(2,1)S(1)}, u32[]{:S(2)}, u32[]{:S(2)}) collective-permute-start(bf16[4,48,352]{2,1,0:T(8,128)(2,1)S(1)} %down_piece.13), channel_id=1, source_target_pairs={{0,4},{2,6},{4,0},{6,2},{1,5},{3,7},{5,1},{7,3},{8,12},{10,14},{12... | collective-permute-start | bytes 405512 | tf_op jit(solution)/shard_map/ppermute | solution.py:536
  74.6 1.6 %collective-permute-start.17 = (bf16[4,48,352]{2,1,0:T(8,128)(2,1)S(1)}, bf16[4,48,352]{2,1,0:T(8,128)(2,1)S(1)}, u32[]{:S(2)}, u32[]{:S(2)}) collective-permute-start(bf16[4,48,352]{2,1,0:T(8,128)(2,1)S(1)} %down_piece.14), channel_id=1, source_target_pairs={{0,6},{2,4},{4,2},{6,0},{1,7},{3,5},{5,3},{7,1},{8,14},{10,12},{12... | collective-permute-start | bytes 405512 | tf_op jit(solution)/shard_map/ppermute | solution.py:536
  77.5 1.1 %collective-permute-done.16.refs_1_ = bf16[4,48,352]{2,1,0:T(8,128)(2,1)S(1)} collective-permute-done((bf16[4,48,352]{2,1,0:T(8,128)(2,1)S(1)}, bf16[4,48,352]{2,1,0:T(8,128)(2,1)S(1)}, u32[]{:S(2)}, u32[]{:S(2)}) %collective-permute-start.16) | collective-permute-done | bytes 135200 | tf_op jit(solution)/shard_map/ppermute | solution.py:536
  78.6 2.1 %collective-permute-done.17.refs_2_ = bf16[4,48,352]{2,1,0:T(8,128)(2,1)S(1)} collective-permute-done((bf16[4,48,352]{2,1,0:T(8,128)(2,1)S(1)}, bf16[4,48,352]{2,1,0:T(8,128)(2,1)S(1)}, u32[]{:S(2)}, u32[]{:S(2)}) %collective-permute-start.17) | collective-permute-done | bytes 135200 | tf_op jit(solution)/shard_map/ppermute | solution.py:536
  80.6 1.5 %collective-permute-done.18.refs_3_ = bf16[4,48,352]{2,1,0:T(8,128)(2,1)S(1)} collective-permute-done((bf16[4,48,352]{2,1,0:T(8,128)(2,1)S(1)}, bf16[4,48,352]{2,1,0:T(8,128)(2,1)S(1)}, u32[]{:S(2)}, u32[]{:S(2)}) %collective-permute-start.18) | collective-permute-done | bytes 135200 | tf_op jit(solution)/shard_map/ppermute | solution.py:536
  82.1 0.8 %place.1 = bf16[1,4,1,4,48,352]{5,4,3,2,1,0:T(8,128)(2,1)} custom-call(s32[1]{0:T(128)} %bitcast.me, bf16[4,48,352]{2,1,0:T(8,128)(2,1)S(1)} %down_piece.12.refs_0_, bf16[4,48,352]{2,1,0:T(8,128)(2,1)S(1)} %collective-permute-done.16.refs_1_, bf16[4,48,352]{2,1,0:T(8,128)(2,1)S(1)} %collective-permute-done.17.refs_2_, ...), custom_call_target="tpu_custom_call" | custom-call | bytes 540676 | tf_op jit(solution)/shard_map/place/pallas_call | solution.py:334
  (61 shorter events, 5.7 us)
Async XLA Ops:
  0.0 9.2 %copy-start.2 = (bf16[1,1408]{1,0:T(2,128)(2,1)S(1)}, bf16[1,1408]{1,0:T(2,128)(2,1)}, u32[]{:S(2)}) copy-start(bf16[1,1408]{1,0:T(2,128)(2,1)} %refs_4_.1) | copy-start | bytes 8452
  0.0 9.2 %copy-start.7 = (bf16[1,352]{1,0:T(2,128)(2,1)S(1)}, bf16[1,352]{1,0:T(2,128)(2,1)}, u32[]{:S(2)}) copy-start(bf16[1,352]{1,0:T(2,128)(2,1)} %refs_2_.1) | copy-start | bytes 2116
  0.0 9.2 %copy-start.6 = (bf16[1,352]{1,0:T(2,128)(2,1)S(1)}, bf16[1,352]{1,0:T(2,128)(2,1)}, u32[]{:S(2)}) copy-start(bf16[1,352]{1,0:T(2,128)(2,1)} %refs_1_.1) | copy-start | bytes 2116
  0.0 9.2 %copy-start.5 = (bf16[1,352]{1,0:T(2,128)(2,1)S(1)}, bf16[1,352]{1,0:T(2,128)(2,1)}, u32[]{:S(2)}) copy-start(bf16[1,352]{1,0:T(2,128)(2,1)} %refs_0_.1) | copy-start | bytes 2116
  0.0 9.2 %copy-start.1 = (bf16[1,7,7,352]{3,2,1,0:T(8,128)(2,1)S(1)}, bf16[1,7,7,352]{3,2,1,0:T(8,128)(2,1)}, u32[]{:S(2)}) copy-start(bf16[1,7,7,352]{3,2,1,0:T(8,128)(2,1)} %kernel.1) | copy-start | bytes 103492
  1.3 8.9 %collective-permute-start = (bf16[4,48,352]{2,1,0:T(8,128)(2,1)S(1)}, bf16[4,48,352]{2,1,0:T(8,128)(2,1)S(1)}, u32[]{:S(2)}, u32[]{:S(2)}) collective-permute-start(bf16[4,48,352]{2,1,0:T(8,128)(2,1)S(1)} %get-tuple-element.62), channel_id=1, source_target_pairs={{28,8},{30,10},{24,12},{26,14},{29,9},{31,11},{25,13},{27,15}} | collective-permute-start | bytes 405512 | tf_op jit(solution)/shard_map/ppermute | solution.py:393
  5.5 4.7 %collective-permute-start.1 = (bf16[4,48,352]{2,1,0:T(8,128)(2,1)S(1)}, bf16[4,48,352]{2,1,0:T(8,128)(2,1)S(1)}, u32[]{:S(2)}, u32[]{:S(2)}) collective-permute-start(bf16[4,48,352]{2,1,0:T(8,128)(2,1)S(1)} %get-tuple-element.64), channel_id=1, source_target_pairs={{30,8},{28,10},{26,12},{24,14},{31,9},{29,11},{27,13},{25,15}} | collective-permute-start | bytes 405512 | tf_op jit(solution)/shard_map/ppermute | solution.py:393
  7.8 4.3 %collective-permute-start.2 = (bf16[4,48,352]{2,1,0:T(8,128)(2,1)S(1)}, bf16[4,48,352]{2,1,0:T(8,128)(2,1)S(1)}, u32[]{:S(2)}, u32[]{:S(2)}) collective-permute-start(bf16[4,48,352]{2,1,0:T(8,128)(2,1)S(1)} %get-tuple-element.61), channel_id=1, source_target_pairs={{26,8},{24,10},{30,12},{28,14},{27,9},{25,11},{31,13},{29,15}} | collective-permute-start | bytes 405512 | tf_op jit(solution)/shard_map/ppermute | solution.py:393
  9.5 0.7 collective-permute-start.3
  12.1 3.0 %collective-permute-start.5 = (bf16[16,48,352]{2,1,0:T(8,128)(2,1)S(1)}, bf16[16,48,352]{2,1,0:T(8,128)(2,1)S(1)}, u32[]{:S(2)}, u32[]{:S(2)}) collective-permute-start(bf16[16,48,352]{2,1,0:T(8,128)(2,1)S(1)} %get-tuple-element.39), channel_id=1, source_target_pairs={{8,0},{9,1},{10,2},{11,3},{12,4},{13,5},{14,6},{15,7}} | collective-permute-start | bytes 1622024 | tf_op jit(solution)/shard_map/ppermute | solution.py:420
  12.9 2.2 %collective-permute-start.4 = (bf16[16,48,352]{2,1,0:T(8,128)(2,1)S(1)}, bf16[16,48,352]{2,1,0:T(8,128)(2,1)S(1)}, u32[]{:S(2)}, u32[]{:S(2)}) collective-permute-start(bf16[16,48,352]{2,1,0:T(8,128)(2,1)S(1)} %get-tuple-element.38), channel_id=1, source_target_pairs={{8,0},{9,1},{10,2},{11,3},{12,4},{13,5},{14,6},{15,7}} | collective-permute-start | bytes 1622024 | tf_op jit(solution)/shard_map/ppermute | solution.py:420
  13.6 1.4 %collective-permute-start.6 = (bf16[352,704]{1,0:T(8,128)(2,1)S(1)}, bf16[352,704]{1,0:T(8,128)(2,1)S(1)}, u32[]{:S(2)}, u32[]{:S(2)}) collective-permute-start(bf16[352,704]{1,0:T(8,128)(2,1)S(1)} %bitcast.25), channel_id=1, source_target_pairs={{0,1},{1,0},{16,17},{17,16},{2,3},{3,2},{18,19},{19,18},{4,5},{5,4... | collective-permute-start | bytes 1486856 | tf_op jit(solution)/shard_map/ppermute | solution.py:398
  14.3 0.8 collective-permute-start.7
  15.1 6.0 %collective-permute-start.8 = (bf16[16,48,352]{2,1,0:T(8,128)(2,1)S(1)}, bf16[16,48,352]{2,1,0:T(8,128)(2,1)S(1)}, u32[]{:S(2)}, u32[]{:S(2)}) collective-permute-start(bf16[16,48,352]{2,1,0:T(8,128)(2,1)S(1)} %down.1.prev.refs_4_), channel_id=1, source_target_pairs={{0,8},{1,9},{2,10},{3,11},{4,12},{5,13},{6,14},{7,15}} | collective-permute-start | bytes 1622024 | tf_op jit(solution)/shard_map/ppermute | solution.py:420
  15.9 13.0 %collective-permute-start.9 = (bf16[352,704]{1,0:T(8,128)(2,1)S(1)}, bf16[352,704]{1,0:T(8,128)(2,1)S(1)}, u32[]{:S(2)}, u32[]{:S(2)}) collective-permute-start(bf16[352,704]{1,0:T(8,128)(2,1)S(1)} %bitcast.27), channel_id=1, source_target_pairs={{8,9},{9,8},{24,25},{25,24},{10,11},{11,10},{26,27},{27,26},{12,13... | collective-permute-start | bytes 1486856 | tf_op jit(solution)/shard_map/ppermute | solution.py:398
  18.0 16.7 %collective-permute-start.10 = (bf16[704,352]{1,0:T(8,128)(2,1)S(1)}, bf16[704,352]{1,0:T(8,128)(2,1)S(1)}, u32[]{:S(2)}, u32[]{:S(2)}) collective-permute-start(bf16[704,352]{1,0:T(8,128)(2,1)S(1)} %bitcast.15), channel_id=1, source_target_pairs={{8,9},{9,8},{24,25},{25,24},{10,11},{11,10},{26,27},{27,26},{12,13... | collective-permute-start | bytes 1486856 | tf_op jit(solution)/shard_map/ppermute | solution.py:398
  34.7 2.8 %collective-permute-start.11 = (bf16[4,48,352]{2,1,0:T(8,128)(2,1)S(1)}, bf16[4,48,352]{2,1,0:T(8,128)(2,1)S(1)}, u32[]{:S(2)}, u32[]{:S(2)}) collective-permute-start(bf16[4,48,352]{2,1,0:T(8,128)(2,1)S(1)} %down_piece.8.refs_0_), channel_id=1, source_target_pairs={{8,16},{9,17},{10,18},{11,19},{12,20},{13,21},{14,22},{15,23}} | collective-permute-start | bytes 405512 | tf_op jit(solution)/shard_map/ppermute | solution.py:420
  35.4 2.1 %collective-permute-start.12 = (bf16[4,48,352]{2,1,0:T(8,128)(2,1)S(1)}, bf16[4,48,352]{2,1,0:T(8,128)(2,1)S(1)}, u32[]{:S(2)}, u32[]{:S(2)}) collective-permute-start(bf16[4,48,352]{2,1,0:T(8,128)(2,1)S(1)} %down_piece.9.refs_1_), channel_id=1, source_target_pairs={{8,16},{9,17},{10,18},{11,19},{12,20},{13,21},{14,22},{15,23}} | collective-permute-start | bytes 405512 | tf_op jit(solution)/shard_map/ppermute | solution.py:420
  36.1 1.5 %collective-permute-start.13 = (bf16[4,48,352]{2,1,0:T(8,128)(2,1)S(1)}, bf16[4,48,352]{2,1,0:T(8,128)(2,1)S(1)}, u32[]{:S(2)}, u32[]{:S(2)}) collective-permute-start(bf16[4,48,352]{2,1,0:T(8,128)(2,1)S(1)} %down_piece.10.refs_2_), channel_id=1, source_target_pairs={{8,16},{9,17},{10,18},{11,19},{12,20},{13,21},{14,22},{15,23}} | collective-permute-start | bytes 405512 | tf_op jit(solution)/shard_map/ppermute | solution.py:420
  36.8 0.8 collective-permute-start.14
  37.9 25.6 %collective-permute-start.15 = (bf16[16,48,352]{2,1,0:T(8,128)(2,1)S(1)}, bf16[16,48,352]{2,1,0:T(8,128)(2,1)S(1)}, u32[]{:S(2)}, u32[]{:S(2)}) collective-permute-start(bf16[16,48,352]{2,1,0:T(8,128)(2,1)S(1)} %mlp.1.prev), channel_id=1, source_target_pairs={{16,24},{17,25},{18,26},{19,27},{20,28},{21,29},{22,30},{23,31}} | collective-permute-start | bytes 1622024 | tf_op jit(solution)/shard_map/ppermute | solution.py:420
  72.1 6.5 %collective-permute-start.16 = (bf16[4,48,352]{2,1,0:T(8,128)(2,1)S(1)}, bf16[4,48,352]{2,1,0:T(8,128)(2,1)S(1)}, u32[]{:S(2)}, u32[]{:S(2)}) collective-permute-start(bf16[4,48,352]{2,1,0:T(8,128)(2,1)S(1)} %down_piece.13), channel_id=1, source_target_pairs={{0,4},{2,6},{4,0},{6,2},{1,5},{3,7},{5,1},{7,3},{8,12},{10,14},{12... | collective-permute-start | bytes 405512 | tf_op jit(solution)/shard_map/ppermute | solution.py:536
  74.6 6.1 %collective-permute-start.17 = (bf16[4,48,352]{2,1,0:T(8,128)(2,1)S(1)}, bf16[4,48,352]{2,1,0:T(8,128)(2,1)S(1)}, u32[]{:S(2)}, u32[]{:S(2)}) collective-permute-start(bf16[4,48,352]{2,1,0:T(8,128)(2,1)S(1)} %down_piece.14), channel_id=1, source_target_pairs={{0,6},{2,4},{4,2},{6,0},{1,7},{3,5},{5,3},{7,1},{8,14},{10,12},{12... | collective-permute-start | bytes 405512 | tf_op jit(solution)/shard_map/ppermute | solution.py:536
  76.6 5.5 %collective-permute-start.18 = (bf16[4,48,352]{2,1,0:T(8,128)(2,1)S(1)}, bf16[4,48,352]{2,1,0:T(8,128)(2,1)S(1)}, u32[]{:S(2)}, u32[]{:S(2)}) collective-permute-start(bf16[4,48,352]{2,1,0:T(8,128)(2,1)S(1)} %down_piece.15), channel_id=1, source_target_pairs={{0,2},{2,0},{4,6},{6,4},{1,3},{3,1},{5,7},{7,5},{8,10},{10,8},{12,... | collective-permute-start | bytes 405512 | tf_op jit(solution)/shard_map/ppermute | solution.py:536
  (5 other events, 31.2 us)

commit v6 on v4

--- a/solution.py
+++ b/solution.py
@@ -11,6 +11,7 @@
 EPS_GRN = 1e-06
 LANES = 128
 VMEM_BYTES = 20 * 1024 * 1024
+PREPARE_VMEM_BYTES = 60 * 1024 * 1024
 REACH = 3
 CHUNK = 4
 NORM_ROWS = 4
@@ -325,7 +326,9 @@
 HBM = pl.BlockSpec(memory_space=pltpu.HBM)
 
 
-def call(kernel, name, args, out, specs=None, out_specs=None, scratch=(), flops=0, **static):
+def call(
+    kernel, name, args, out, specs=None, out_specs=None, scratch=(), flops=0, vmem=VMEM_BYTES, **static
+):
     if specs is None:
         specs = [SMEM if a.dtype == jnp.int32 else VMEM for a in args]
     if out_specs is None:
@@ -337,7 +340,7 @@
         in_specs=specs,
         out_specs=out_specs,
         scratch_shapes=list(scratch),
-        compiler_params=pltpu.CompilerParams(vmem_limit_bytes=VMEM_BYTES),
+        compiler_params=pltpu.CompilerParams(vmem_limit_bytes=vmem),
         cost_estimate=pl.CostEstimate(flops=flops, bytes_accessed=moved, transcendentals=0),
         name=name,
     )(*args)
@@ -400,8 +403,6 @@
     w_in, w_out = proj_in[0], proj_out[0]
     even = range(0, sections, 2)
     odd = range(1, sections, 2)
-    other_in = other_half(w_in, even)
-    other_out = other_half(w_out, even)
 
     held = (
         depth_kernel, depth_bias, norm_gain, norm_bias, bias_out, bias_in, grn_gamma, grn_beta
@@ -414,10 +415,16 @@
         specs=[SMEM] + [HBM] * len(held),
         scratch=[pltpu.VMEM(v.shape, v.dtype) for v in held]
         + [pltpu.SemaphoreType.DMA((len(held),))],
+        vmem=PREPARE_VMEM_BYTES,
     )
 
     def send(x, start, end):
         return lax.ppermute(x, "section", [(start, end)])
+
+    lent_cpar = send(cpar, 0, helper)
+    early_in, early_out, lent_cpar = lax.optimization_barrier((w_in, w_out, lent_cpar))
+    other_in = other_half(early_in, even)
+    other_out = other_half(early_out, even)
 
     def conv_pieces(pieces, cpar, order, on):
         out_rows = rows + 2 * REACH
@@ -479,10 +486,9 @@
             n=n,
         )
 
-    x, flat = conv_pieces(pieces, send(cpar, 0, helper), order, helper)
-    flat, other_in = lax.optimization_barrier((flat, other_in))
+    x, flat = conv_pieces(pieces, lent_cpar, order, helper)
     flat = send(flat, helper, 0)
-    x, other_out = lax.optimization_barrier((x, other_out))
+    x, other_in, other_out = lax.optimization_barrier((x, other_in, other_out))
     x = send(x, helper, 0)
     act_a, ssq = up_own(flat, 0)
     act_b, scale = up_other(flat, other_in, ssq, 0)

time: 89.3 us -> 86.7 us (0.971)
  local copies, waits for them, and re-layouts: 7.76 us -> 2.2 us
  starting transfers between devices: 26.1 us -> 28.4 us
  Pallas kernels: 11.5 us -> 12.9 us
    unnamed x20 -> x8, local copies, waits for them, and re-layouts: 6.57 us -> 1 us
    ppermute x3, starting transfers between devices: 8.46 us -> 10.5 us  [image_plan(): piece = lax.ppermute(piece, ('section', 'row'), pairs)]
    pallas_call x26, Pallas kernels: 11.5 us -> 12.9 us  [call(): pl.pallas_call(functools.partial(kernel, **static), out_shape=out, in_spe...]
  transfers between devices with their start and end apart: 19 -> 19, of which waited for: 8 -> 7; matrix products, arithmetic and copies ran while one was open for 1% -> 1% of each run, Pallas kernels for 2% -> 2%
where the time goes in v6:
time: 86.7 us; the launch traced here: 86.3 us
  waiting for transfers between devices  42.2 us (49%)
  starting transfers between devices  28.4 us (33%)
  Pallas kernels  12.9 us (15%)
  local copies, waits for them, and re-layouts  2.2 us (3%)
    ppermute x9, waiting for transfers between devices, send(): return lax.ppermute(x, 'section', [(start, end)])  23.9 us
    pallas_call x26, Pallas kernels, call(): pl.pallas_call(functools.partial(kernel, **static), out_shape=out, in_spe...  12.9 us
    ppermute x4, waiting for transfers between devices, other_half(): return lax.ppermute(x, ('section', 'dp'), pairs)  10.6 us
    ppermute x3, starting transfers between devices, image_plan(): piece = lax.ppermute(piece, ('section', 'row'), pairs)  10.5 us
    ppermute x9, starting transfers between devices, send(): return lax.ppermute(x, 'section', [(start, end)])  6.84 us
    ppermute x4, starting transfers between devices, other_half(): return lax.ppermute(x, ('section', 'dp'), pairs)  6.67 us
    ppermute x3, waiting for transfers between devices, image_plan(): lax.ppermute(piece, 'row', [(p, p ^ order[n]) for p in range(count)])  4.83 us
    ppermute x3, starting transfers between devices, image_plan(): lax.ppermute(piece, 'row', [(p, p ^ order[n]) for p in range(count)])  4.41 us
  transfers between devices with their start and end apart: 19, of which 7 were waited for; matrix products, arithmetic and copies ran while one was open for 1% of the time, Pallas kernels for 2%

profile of v6, /device:TPU:7, one launch (start us, length us, event | category | flops | bytes accessed | tf_op | source)
XLA Modules:
  0.0 86.3 jit_solution(13513016120349100270)
XLA Ops:
  0.0 1.6 %prepare.1 = (f32[64,384]{1,0:T(8,128)}, f32[2,3,704]{2,1,0:T(4,128)}) custom-call(s32[1]{0:T(128)} %bitcast.8.part, bf16[1,7,7,352]{3,2,1,0:T(8,128)(2,1)} %kernel.1, bf16[1,352]{1,0:T(2,128)(2,1)} %refs_0_.1, bf16[1,352]{1,0:T(2,128)(2,1)} %refs_1_.1, bf16[1,352]{1,0:T(2,128)(2,1)} %refs_2_.1, bf16[1,352]{1,0:T(2,128)(2,1)} %refs_3_.1, ...), custom_call_target="tpu_custom_call" | custom-call | bytes 45764 | tf_op jit(solution)/shard_map/prepare/pallas_call | solution.py:337
  2.2 0.7 collective-permute-start.4
  3.0 0.7 collective-permute-start.5
  3.7 1.2 %dynamic-slice_bitcast_fusion = (bf16[4,48,352]{2,1,0:T(8,128)(2,1)S(1)}, bf16[4,48,352]{2,1,0:T(8,128)(2,1)S(1)}, bf16[4,48,352]{2,1,0:T(8,128)(2,1)S(1)}, bf16[4,48,352]{2,1,0:T(8,128)(2,1)S(1)}) fusion(bf16[4,1,4,48,352]{4,3,2,1,0:T(8,128)(2,1)} %param.11, s32[]{:T(128)S(6)} %select_n.16, s32[]{:T(128)S(6)} %select_n.14, s32[]{:T(128)S(6)} %select_n.13, ...), kind=kLoop, calls=%fused_computation | loop fusion | bytes 1081360 | tf_op jit(solution)/shard_map/squeeze | solution.py:393
  4.9 6.9 %collective-permute-start = (bf16[4,48,352]{2,1,0:T(8,128)(2,1)S(1)}, bf16[4,48,352]{2,1,0:T(8,128)(2,1)S(1)}, u32[]{:S(2)}, u32[]{:S(2)}) collective-permute-start(bf16[4,48,352]{2,1,0:T(8,128)(2,1)S(1)} %get-tuple-element.74), channel_id=1, source_target_pairs={{28,8},{30,10},{24,12},{26,14},{29,9},{31,11},{25,13},{27,15}} | collective-permute-start | bytes 405512 | tf_op jit(solution)/shard_map/ppermute | solution.py:396
  11.8 2.3 %collective-permute-start.1 = (bf16[4,48,352]{2,1,0:T(8,128)(2,1)S(1)}, bf16[4,48,352]{2,1,0:T(8,128)(2,1)S(1)}, u32[]{:S(2)}, u32[]{:S(2)}) collective-permute-start(bf16[4,48,352]{2,1,0:T(8,128)(2,1)S(1)} %get-tuple-element.76), channel_id=1, source_target_pairs={{30,8},{28,10},{26,12},{24,14},{31,9},{29,11},{27,13},{25,15}} | collective-permute-start | bytes 405512 | tf_op jit(solution)/shard_map/ppermute | solution.py:396
  14.1 1.3 %collective-permute-start.2 = (bf16[4,48,352]{2,1,0:T(8,128)(2,1)S(1)}, bf16[4,48,352]{2,1,0:T(8,128)(2,1)S(1)}, u32[]{:S(2)}, u32[]{:S(2)}) collective-permute-start(bf16[4,48,352]{2,1,0:T(8,128)(2,1)S(1)} %get-tuple-element.73), channel_id=1, source_target_pairs={{26,8},{24,10},{30,12},{28,14},{27,9},{25,11},{31,13},{29,15}} | collective-permute-start | bytes 405512 | tf_op jit(solution)/shard_map/ppermute | solution.py:396
  15.4 0.8 collective-permute-done.1.piece.refs_2_
  16.2 2.1 %collective-permute-done.2.refs_3_ = bf16[4,48,352]{2,1,0:T(8,128)(2,1)S(1)} collective-permute-done((bf16[4,48,352]{2,1,0:T(8,128)(2,1)S(1)}, bf16[4,48,352]{2,1,0:T(8,128)(2,1)S(1)}, u32[]{:S(2)}, u32[]{:S(2)}) %collective-permute-start.2) | collective-permute-done | bytes 135200 | tf_op jit(solution)/shard_map/ppermute | solution.py:396
  18.4 0.8 collective-permute-start.7
  19.2 0.7 collective-permute-start.6
  20.0 1.0 %copy-done = bf16[1,704,352]{2,1,0:T(8,128)(2,1)S(1)} copy-done((bf16[1,704,352]{2,1,0:T(8,128)(2,1)S(1)}, bf16[1,704,352]{2,1,0:T(8,128)(2,1)}, u32[]{:S(2)}) %copy-start) | copy-done | bytes 495640
  21.7 2.1 %collective-permute-start.9 = (bf16[352,704]{1,0:T(8,128)(2,1)S(1)}, bf16[352,704]{1,0:T(8,128)(2,1)S(1)}, u32[]{:S(2)}, u32[]{:S(2)}) collective-permute-start(bf16[352,704]{1,0:T(8,128)(2,1)S(1)} %bitcast.27), channel_id=1, source_target_pairs={{8,9},{9,8},{24,25},{25,24},{10,11},{11,10},{26,27},{27,26},{12,13... | collective-permute-start | bytes 1486856 | tf_op jit(solution)/shard_map/ppermute | solution.py:401
  23.8 3.1 %collective-permute-start.10 = (bf16[704,352]{1,0:T(8,128)(2,1)S(1)}, bf16[704,352]{1,0:T(8,128)(2,1)S(1)}, u32[]{:S(2)}, u32[]{:S(2)}) collective-permute-start(bf16[704,352]{1,0:T(8,128)(2,1)S(1)} %bitcast.15), channel_id=1, source_target_pairs={{8,9},{9,8},{24,25},{25,24},{10,11},{11,10},{26,27},{27,26},{12,13... | collective-permute-start | bytes 1486856 | tf_op jit(solution)/shard_map/ppermute | solution.py:401
  27.0 4.8 %collective-permute-done.9.w_in.in_b = bf16[352,704]{1,0:T(8,128)(2,1)S(1)} collective-permute-done((bf16[352,704]{1,0:T(8,128)(2,1)S(1)}, bf16[352,704]{1,0:T(8,128)(2,1)S(1)}, u32[]{:S(2)}, u32[]{:S(2)}) %collective-permute-start.9) | collective-permute-done | bytes 495648 | tf_op jit(solution)/shard_map/ppermute | solution.py:401
  31.8 5.8 %collective-permute-done.10.out_b = bf16[704,352]{1,0:T(8,128)(2,1)S(1)} collective-permute-done((bf16[704,352]{1,0:T(8,128)(2,1)S(1)}, bf16[704,352]{1,0:T(8,128)(2,1)S(1)}, u32[]{:S(2)}, u32[]{:S(2)}) %collective-permute-start.10) | collective-permute-done | bytes 495648 | tf_op jit(solution)/shard_map/ppermute | solution.py:401
  40.8 1.3 %collective-permute-start.15 = (bf16[16,48,352]{2,1,0:T(8,128)(2,1)S(1)}, bf16[16,48,352]{2,1,0:T(8,128)(2,1)S(1)}, u32[]{:S(2)}, u32[]{:S(2)}) collective-permute-start(bf16[16,48,352]{2,1,0:T(8,128)(2,1)S(1)} %mlp.1.prev), channel_id=1, source_target_pairs={{16,24},{17,25},{18,26},{19,27},{20,28},{21,29},{22,30},{23,31}} | collective-permute-start | bytes 1622024 | tf_op jit(solution)/shard_map/ppermute | solution.py:422
  42.1 23.9 %collective-permute-done.15.x = bf16[16,48,352]{2,1,0:T(8,128)(2,1)S(1)} collective-permute-done((bf16[16,48,352]{2,1,0:T(8,128)(2,1)S(1)}, bf16[16,48,352]{2,1,0:T(8,128)(2,1)S(1)}, u32[]{:S(2)}, u32[]{:S(2)}) %collective-permute-start.15) | collective-permute-done | bytes 540704 | tf_op jit(solution)/shard_map/ppermute | solution.py:422
  66.0 8.1 %conv_up.1 = (bf16[768,704]{1,0:T(8,128)(2,1)S(1)}, bf16[768,704]{1,0:T(8,128)(2,1)S(1)}, f32[2,1,704]{2,1,0:T(1,128)S(1)}) custom-call(s32[1]{0:T(128)} %bitcast.1.section, bf16[16,48,352]{2,1,0:T(8,128)(2,1)S(1)} %collective-permute-done.15.x, f32[64,384]{1,0:T(8,128)S(1)} %copy-done.1, bf16[352,704]{1,0:T(8,128)(2,1)S(1)} %bitcast.30, ...), custom_call_target="tpu_custom_call" | custom-call | flops 761266176 | bytes 1647108 | tf_op jit(solution)/shard_map/conv_up/pallas_call | solution.py:337
  74.6 2.7 %collective-permute-start.16 = (bf16[4,48,352]{2,1,0:T(8,128)(2,1)S(1)}, bf16[4,48,352]{2,1,0:T(8,128)(2,1)S(1)}, u32[]{:S(2)}, u32[]{:S(2)}) collective-permute-start(bf16[4,48,352]{2,1,0:T(8,128)(2,1)S(1)} %down_piece.13), channel_id=1, source_target_pairs={{0,4},{2,6},{4,0},{6,2},{1,5},{3,7},{5,1},{7,3},{8,12},{10,14},{12... | collective-permute-start | bytes 405512 | tf_op jit(solution)/shard_map/ppermute | solution.py:545
  77.8 1.6 %collective-permute-start.17 = (bf16[4,48,352]{2,1,0:T(8,128)(2,1)S(1)}, bf16[4,48,352]{2,1,0:T(8,128)(2,1)S(1)}, u32[]{:S(2)}, u32[]{:S(2)}) collective-permute-start(bf16[4,48,352]{2,1,0:T(8,128)(2,1)S(1)} %down_piece.14), channel_id=1, source_target_pairs={{0,6},{2,4},{4,2},{6,0},{1,7},{3,5},{5,3},{7,1},{8,14},{10,12},{12... | collective-permute-start | bytes 405512 | tf_op jit(solution)/shard_map/ppermute | solution.py:545
  80.5 3.4 %collective-permute-done.17.refs_2_ = bf16[4,48,352]{2,1,0:T(8,128)(2,1)S(1)} collective-permute-done((bf16[4,48,352]{2,1,0:T(8,128)(2,1)S(1)}, bf16[4,48,352]{2,1,0:T(8,128)(2,1)S(1)}, u32[]{:S(2)}, u32[]{:S(2)}) %collective-permute-start.17) | collective-permute-done | bytes 135200 | tf_op jit(solution)/shard_map/ppermute | solution.py:545
  83.8 1.5 %collective-permute-done.18.refs_3_ = bf16[4,48,352]{2,1,0:T(8,128)(2,1)S(1)} collective-permute-done((bf16[4,48,352]{2,1,0:T(8,128)(2,1)S(1)}, bf16[4,48,352]{2,1,0:T(8,128)(2,1)S(1)}, u32[]{:S(2)}, u32[]{:S(2)}) %collective-permute-start.18) | collective-permute-done | bytes 135200 | tf_op jit(solution)/shard_map/ppermute | solution.py:545
  85.3 0.8 place.1
  (49 shorter events, 6.5 us)
Async XLA Ops:
  1.6 0.7 collective-permute-start.3
  2.2 16.9 %collective-permute-start.4 = (bf16[352,704]{1,0:T(8,128)(2,1)}, bf16[352,704]{1,0:T(8,128)(2,1)S(1)}, u32[]{:S(2)}, u32[]{:S(2)}) collective-permute-start(bf16[352,704]{1,0:T(8,128)(2,1)} %bitcast.25), channel_id=1, source_target_pairs={{0,1},{1,0},{16,17},{17,16},{2,3},{3,2},{18,19},{19,18},{4,5},{5,4... | collective-permute-start | bytes 1486856 | tf_op jit(solution)/shard_map/ppermute | solution.py:401
  3.0 16.2 %collective-permute-start.5 = (bf16[704,352]{1,0:T(8,128)(2,1)}, bf16[704,352]{1,0:T(8,128)(2,1)S(1)}, u32[]{:S(2)}, u32[]{:S(2)}) collective-permute-start(bf16[704,352]{1,0:T(8,128)(2,1)} %bitcast.13), channel_id=1, source_target_pairs={{0,1},{1,0},{16,17},{17,16},{2,3},{3,2},{18,19},{19,18},{4,5},{5,4... | collective-permute-start | bytes 1486856 | tf_op jit(solution)/shard_map/ppermute | solution.py:401
  4.9 10.6 %collective-permute-start = (bf16[4,48,352]{2,1,0:T(8,128)(2,1)S(1)}, bf16[4,48,352]{2,1,0:T(8,128)(2,1)S(1)}, u32[]{:S(2)}, u32[]{:S(2)}) collective-permute-start(bf16[4,48,352]{2,1,0:T(8,128)(2,1)S(1)} %get-tuple-element.74), channel_id=1, source_target_pairs={{28,8},{30,10},{24,12},{26,14},{29,9},{31,11},{25,13},{27,15}} | collective-permute-start | bytes 405512 | tf_op jit(solution)/shard_map/ppermute | solution.py:396
  11.8 4.4 %collective-permute-start.1 = (bf16[4,48,352]{2,1,0:T(8,128)(2,1)S(1)}, bf16[4,48,352]{2,1,0:T(8,128)(2,1)S(1)}, u32[]{:S(2)}, u32[]{:S(2)}) collective-permute-start(bf16[4,48,352]{2,1,0:T(8,128)(2,1)S(1)} %get-tuple-element.76), channel_id=1, source_target_pairs={{30,8},{28,10},{26,12},{24,14},{31,9},{29,11},{27,13},{25,15}} | collective-permute-start | bytes 405512 | tf_op jit(solution)/shard_map/ppermute | solution.py:396
  14.1 4.3 %collective-permute-start.2 = (bf16[4,48,352]{2,1,0:T(8,128)(2,1)S(1)}, bf16[4,48,352]{2,1,0:T(8,128)(2,1)S(1)}, u32[]{:S(2)}, u32[]{:S(2)}) collective-permute-start(bf16[4,48,352]{2,1,0:T(8,128)(2,1)S(1)} %get-tuple-element.73), channel_id=1, source_target_pairs={{26,8},{24,10},{30,12},{28,14},{27,9},{25,11},{31,13},{29,15}} | collective-permute-start | bytes 405512 | tf_op jit(solution)/shard_map/ppermute | solution.py:396
  18.3 1.6 %copy-start.2 = (f32[2,3,704]{2,1,0:T(4,128)S(1)}, f32[2,3,704]{2,1,0:T(4,128)}, u32[]{:S(2)}) copy-start(f32[2,3,704]{2,1,0:T(4,128)} %get-tuple-element.50.fvec) | copy-start | bytes 50692
  18.4 1.6 %copy-start.3 = (bf16[1,352,704]{2,1,0:T(8,128)(2,1)S(1)}, bf16[1,352,704]{2,1,0:T(8,128)(2,1)}, u32[]{:S(2)}) copy-start(bf16[1,352,704]{2,1,0:T(8,128)(2,1)} %param.16) | copy-start | bytes 1486852
  18.4 1.6 %collective-permute-start.7 = (bf16[16,48,352]{2,1,0:T(8,128)(2,1)S(1)}, bf16[16,48,352]{2,1,0:T(8,128)(2,1)S(1)}, u32[]{:S(2)}, u32[]{:S(2)}) collective-permute-start(bf16[16,48,352]{2,1,0:T(8,128)(2,1)S(1)} %get-tuple-element.49), channel_id=1, source_target_pairs={{8,0},{9,1},{10,2},{11,3},{12,4},{13,5},{14,6},{15,7}} | collective-permute-start | bytes 1622024 | tf_op jit(solution)/shard_map/ppermute | solution.py:422
  19.2 0.8 collective-permute-start.6
  19.9 1.1 %copy-start = (bf16[1,704,352]{2,1,0:T(8,128)(2,1)S(1)}, bf16[1,704,352]{2,1,0:T(8,128)(2,1)}, u32[]{:S(2)}) copy-start(bf16[1,704,352]{2,1,0:T(8,128)(2,1)} %param.20) | copy-start | bytes 1486852
  19.9 1.0 %copy-start.1 = (f32[64,384]{1,0:T(8,128)S(1)}, f32[64,384]{1,0:T(8,128)}, u32[]{:S(2)}) copy-start(f32[64,384]{1,0:T(8,128)} %get-tuple-element.39.cpar.refs_7_) | copy-start | bytes 294916
  21.0 6.0 %collective-permute-start.8 = (bf16[16,48,352]{2,1,0:T(8,128)(2,1)S(1)}, bf16[16,48,352]{2,1,0:T(8,128)(2,1)S(1)}, u32[]{:S(2)}, u32[]{:S(2)}) collective-permute-start(bf16[16,48,352]{2,1,0:T(8,128)(2,1)S(1)} %down.1.prev.refs_4_), channel_id=1, source_target_pairs={{0,8},{1,9},{2,10},{3,11},{4,12},{5,13},{6,14},{7,15}} | collective-permute-start | bytes 1622024 | tf_op jit(solution)/shard_map/ppermute | solution.py:422
  21.7 10.1 %collective-permute-start.9 = (bf16[352,704]{1,0:T(8,128)(2,1)S(1)}, bf16[352,704]{1,0:T(8,128)(2,1)S(1)}, u32[]{:S(2)}, u32[]{:S(2)}) collective-permute-start(bf16[352,704]{1,0:T(8,128)(2,1)S(1)} %bitcast.27), channel_id=1, source_target_pairs={{8,9},{9,8},{24,25},{25,24},{10,11},{11,10},{26,27},{27,26},{12,13... | collective-permute-start | bytes 1486856 | tf_op jit(solution)/shard_map/ppermute | solution.py:401
  23.8 13.8 %collective-permute-start.10 = (bf16[704,352]{1,0:T(8,128)(2,1)S(1)}, bf16[704,352]{1,0:T(8,128)(2,1)S(1)}, u32[]{:S(2)}, u32[]{:S(2)}) collective-permute-start(bf16[704,352]{1,0:T(8,128)(2,1)S(1)} %bitcast.15), channel_id=1, source_target_pairs={{8,9},{9,8},{24,25},{25,24},{10,11},{11,10},{26,27},{27,26},{12,13... | collective-permute-start | bytes 1486856 | tf_op jit(solution)/shard_map/ppermute | solution.py:401
  37.6 2.8 %collective-permute-start.11 = (bf16[4,48,352]{2,1,0:T(8,128)(2,1)S(1)}, bf16[4,48,352]{2,1,0:T(8,128)(2,1)S(1)}, u32[]{:S(2)}, u32[]{:S(2)}) collective-permute-start(bf16[4,48,352]{2,1,0:T(8,128)(2,1)S(1)} %down_piece.8.refs_0_), channel_id=1, source_target_pairs={{8,16},{9,17},{10,18},{11,19},{12,20},{13,21},{14,22},{15,23}} | collective-permute-start | bytes 405512 | tf_op jit(solution)/shard_map/ppermute | solution.py:422
  38.3 2.1 %collective-permute-start.12 = (bf16[4,48,352]{2,1,0:T(8,128)(2,1)S(1)}, bf16[4,48,352]{2,1,0:T(8,128)(2,1)S(1)}, u32[]{:S(2)}, u32[]{:S(2)}) collective-permute-start(bf16[4,48,352]{2,1,0:T(8,128)(2,1)S(1)} %down_piece.9.refs_1_), channel_id=1, source_target_pairs={{8,16},{9,17},{10,18},{11,19},{12,20},{13,21},{14,22},{15,23}} | collective-permute-start | bytes 405512 | tf_op jit(solution)/shard_map/ppermute | solution.py:422
  39.0 1.5 %collective-permute-start.13 = (bf16[4,48,352]{2,1,0:T(8,128)(2,1)S(1)}, bf16[4,48,352]{2,1,0:T(8,128)(2,1)S(1)}, u32[]{:S(2)}, u32[]{:S(2)}) collective-permute-start(bf16[4,48,352]{2,1,0:T(8,128)(2,1)S(1)} %down_piece.10.refs_2_), channel_id=1, source_target_pairs={{8,16},{9,17},{10,18},{11,19},{12,20},{13,21},{14,22},{15,23}} | collective-permute-start | bytes 405512 | tf_op jit(solution)/shard_map/ppermute | solution.py:422
  39.7 0.8 collective-permute-start.14
  40.8 25.2 %collective-permute-start.15 = (bf16[16,48,352]{2,1,0:T(8,128)(2,1)S(1)}, bf16[16,48,352]{2,1,0:T(8,128)(2,1)S(1)}, u32[]{:S(2)}, u32[]{:S(2)}) collective-permute-start(bf16[16,48,352]{2,1,0:T(8,128)(2,1)S(1)} %mlp.1.prev), channel_id=1, source_target_pairs={{16,24},{17,25},{18,26},{19,27},{20,28},{21,29},{22,30},{23,31}} | collective-permute-start | bytes 1622024 | tf_op jit(solution)/shard_map/ppermute | solution.py:422
  74.6 5.9 %collective-permute-start.16 = (bf16[4,48,352]{2,1,0:T(8,128)(2,1)S(1)}, bf16[4,48,352]{2,1,0:T(8,128)(2,1)S(1)}, u32[]{:S(2)}, u32[]{:S(2)}) collective-permute-start(bf16[4,48,352]{2,1,0:T(8,128)(2,1)S(1)} %down_piece.13), channel_id=1, source_target_pairs={{0,4},{2,6},{4,0},{6,2},{1,5},{3,7},{5,1},{7,3},{8,12},{10,14},{12... | collective-permute-start | bytes 405512 | tf_op jit(solution)/shard_map/ppermute | solution.py:545
  77.8 6.1 %collective-permute-start.17 = (bf16[4,48,352]{2,1,0:T(8,128)(2,1)S(1)}, bf16[4,48,352]{2,1,0:T(8,128)(2,1)S(1)}, u32[]{:S(2)}, u32[]{:S(2)}) collective-permute-start(bf16[4,48,352]{2,1,0:T(8,128)(2,1)S(1)} %down_piece.14), channel_id=1, source_target_pairs={{0,6},{2,4},{4,2},{6,0},{1,7},{3,5},{5,3},{7,1},{8,14},{10,12},{12... | collective-permute-start | bytes 405512 | tf_op jit(solution)/shard_map/ppermute | solution.py:545
  79.9 5.4 %collective-permute-start.18 = (bf16[4,48,352]{2,1,0:T(8,128)(2,1)S(1)}, bf16[4,48,352]{2,1,0:T(8,128)(2,1)S(1)}, u32[]{:S(2)}, u32[]{:S(2)}) collective-permute-start(bf16[4,48,352]{2,1,0:T(8,128)(2,1)S(1)} %down_piece.15), channel_id=1, source_target_pairs={{0,2},{2,0},{4,6},{6,4},{1,3},{3,1},{5,7},{7,5},{8,10},{10,8},{12,... | collective-permute-start | bytes 405512 | tf_op jit(solution)/shard_map/ppermute | solution.py:545

commit v7 on v5

--- a/solution.py
+++ b/solution.py
@@ -480,6 +480,7 @@
         )
 
     x, flat = conv_pieces(pieces, send(cpar, 0, helper), order, helper)
+    flat, other_in = lax.optimization_barrier((flat, other_in))
     flat, x = send(flat, helper, 0), send(x, helper, 0)
     act_a, ssq = up_own(flat, 0)
     act_b, scale = up_other(flat, other_in, ssq, 0)

time: 83.5 us -> 81.5 us (0.976)
  waiting for transfers between devices: 44.3 us -> 41.9 us
    ppermute x9, waiting for transfers between devices: 24.3 us -> 20.4 us  [send(): return lax.ppermute(x, 'section', [(start, end)])]
    ppermute x4, waiting for transfers between devices: 13.5 us -> 14.6 us  [other_half(): return lax.ppermute(x, ('section', 'dp'), pairs)]
  transfers between devices with their start and end apart: 19 -> 19, of which waited for: 7 -> 7; matrix products, arithmetic and copies ran while one was open for 0% -> 1% of each run, Pallas kernels for 2% -> 2%
where the time goes in v7:
time: 81.5 us; the launch traced here: 81 us
  waiting for transfers between devices  41.9 us (51%)
  starting transfers between devices  25.6 us (31%)
  Pallas kernels  11.6 us (14%)
  local copies, waits for them, and re-layouts  1.23 us (2%)
    ppermute x9, waiting for transfers between devices, send(): return lax.ppermute(x, 'section', [(start, end)])  20.4 us
    ppermute x4, waiting for transfers between devices, other_half(): return lax.ppermute(x, ('section', 'dp'), pairs)  14.6 us
    pallas_call x26, Pallas kernels, call(): pl.pallas_call(functools.partial(kernel, **static), out_shape=out, in_spe...  11.6 us
    ppermute x3, starting transfers between devices, image_plan(): piece = lax.ppermute(piece, ('section', 'row'), pairs)  7.8 us
    ppermute x9, starting transfers between devices, send(): return lax.ppermute(x, 'section', [(start, end)])  6.86 us
    ppermute x4, starting transfers between devices, other_half(): return lax.ppermute(x, ('section', 'dp'), pairs)  6.8 us
    ppermute x3, waiting for transfers between devices, image_plan(): lax.ppermute(piece, 'row', [(p, p ^ order[n]) for p in range(count)])  5.05 us
    ppermute x3, starting transfers between devices, image_plan(): lax.ppermute(piece, 'row', [(p, p ^ order[n]) for p in range(count)])  4.12 us
  transfers between devices with their start and end apart: 19, of which 7 were waited for; matrix products, arithmetic and copies ran while one was open for 1% of the time, Pallas kernels for 2%

profile of v7, /device:TPU:7, one launch (start us, length us, event | category | flops | bytes accessed | tf_op | source)
XLA Modules:
  0.0 81.0 jit_solution(7159076136507214165)
XLA Ops:
  0.1 0.8 %collective-permute-start.5 = (bf16[352,704]{1,0:T(8,128)(2,1)}, bf16[352,704]{1,0:T(8,128)(2,1)S(1)}, u32[]{:S(2)}, u32[]{:S(2)}) collective-permute-start(bf16[352,704]{1,0:T(8,128)(2,1)} %bitcast.25), channel_id=1, source_target_pairs={{0,1},{1,0},{16,17},{17,16},{2,3},{3,2},{18,19},{19,18},{4,5},{5,4... | collective-permute-start | bytes 1486856 | tf_op jit(solution)/shard_map/ppermute | solution.py:398
  0.9 1.2 %dynamic-slice_bitcast_fusion = (bf16[4,48,352]{2,1,0:T(8,128)(2,1)S(1)}, bf16[4,48,352]{2,1,0:T(8,128)(2,1)S(1)}, bf16[4,48,352]{2,1,0:T(8,128)(2,1)S(1)}, bf16[4,48,352]{2,1,0:T(8,128)(2,1)S(1)}) fusion(bf16[4,1,4,48,352]{4,3,2,1,0:T(8,128)(2,1)} %param.11, s32[]{:T(128)S(6)} %select_n.16, s32[]{:T(128)S(6)} %select_n.14, s32[]{:T(128)S(6)} %select_n.13, ...), kind=kLoop, calls=%fused_computation | loop fusion | bytes 1081360 | tf_op jit(solution)/shard_map/squeeze | solution.py:390
  2.1 4.2 %collective-permute-start = (bf16[4,48,352]{2,1,0:T(8,128)(2,1)S(1)}, bf16[4,48,352]{2,1,0:T(8,128)(2,1)S(1)}, u32[]{:S(2)}, u32[]{:S(2)}) collective-permute-start(bf16[4,48,352]{2,1,0:T(8,128)(2,1)S(1)} %get-tuple-element.66), channel_id=1, source_target_pairs={{28,8},{30,10},{24,12},{26,14},{29,9},{31,11},{25,13},{27,15}} | collective-permute-start | bytes 405512 | tf_op jit(solution)/shard_map/ppermute | solution.py:393
  6.3 2.3 %collective-permute-start.1 = (bf16[4,48,352]{2,1,0:T(8,128)(2,1)S(1)}, bf16[4,48,352]{2,1,0:T(8,128)(2,1)S(1)}, u32[]{:S(2)}, u32[]{:S(2)}) collective-permute-start(bf16[4,48,352]{2,1,0:T(8,128)(2,1)S(1)} %get-tuple-element.68), channel_id=1, source_target_pairs={{30,8},{28,10},{26,12},{24,14},{31,9},{29,11},{27,13},{25,15}} | collective-permute-start | bytes 405512 | tf_op jit(solution)/shard_map/ppermute | solution.py:393
  8.6 1.3 %collective-permute-start.2 = (bf16[4,48,352]{2,1,0:T(8,128)(2,1)S(1)}, bf16[4,48,352]{2,1,0:T(8,128)(2,1)S(1)}, u32[]{:S(2)}, u32[]{:S(2)}) collective-permute-start(bf16[4,48,352]{2,1,0:T(8,128)(2,1)S(1)} %get-tuple-element.65), channel_id=1, source_target_pairs={{26,8},{24,10},{30,12},{28,14},{27,9},{25,11},{31,13},{29,15}} | collective-permute-start | bytes 405512 | tf_op jit(solution)/shard_map/ppermute | solution.py:393
  11.0 1.8 %collective-permute-done.2.refs_3_ = bf16[4,48,352]{2,1,0:T(8,128)(2,1)S(1)} collective-permute-done((bf16[4,48,352]{2,1,0:T(8,128)(2,1)S(1)}, bf16[4,48,352]{2,1,0:T(8,128)(2,1)S(1)}, u32[]{:S(2)}, u32[]{:S(2)}) %collective-permute-start.2) | collective-permute-done | bytes 135200 | tf_op jit(solution)/shard_map/ppermute | solution.py:393
  12.9 0.8 %collective-permute-start.6 = (bf16[16,48,352]{2,1,0:T(8,128)(2,1)S(1)}, bf16[16,48,352]{2,1,0:T(8,128)(2,1)S(1)}, u32[]{:S(2)}, u32[]{:S(2)}) collective-permute-start(bf16[16,48,352]{2,1,0:T(8,128)(2,1)S(1)} %get-tuple-element.42), channel_id=1, source_target_pairs={{8,0},{9,1},{10,2},{11,3},{12,4},{13,5},{14,6},{15,7}} | collective-permute-start | bytes 1622024 | tf_op jit(solution)/shard_map/ppermute | solution.py:420
  13.7 0.7 collective-permute-start.4
  14.4 0.7 collective-permute-start.7
  15.2 0.7 collective-permute-start.8
  15.9 2.1 %collective-permute-start.9 = (bf16[352,704]{1,0:T(8,128)(2,1)S(1)}, bf16[352,704]{1,0:T(8,128)(2,1)S(1)}, u32[]{:S(2)}, u32[]{:S(2)}) collective-permute-start(bf16[352,704]{1,0:T(8,128)(2,1)S(1)} %bitcast.27), channel_id=1, source_target_pairs={{8,9},{9,8},{24,25},{25,24},{10,11},{11,10},{26,27},{27,26},{12,13... | collective-permute-start | bytes 1486856 | tf_op jit(solution)/shard_map/ppermute | solution.py:398
  18.1 3.1 %collective-permute-start.10 = (bf16[704,352]{1,0:T(8,128)(2,1)S(1)}, bf16[704,352]{1,0:T(8,128)(2,1)S(1)}, u32[]{:S(2)}, u32[]{:S(2)}) collective-permute-start(bf16[704,352]{1,0:T(8,128)(2,1)S(1)} %bitcast.15), channel_id=1, source_target_pairs={{8,9},{9,8},{24,25},{25,24},{10,11},{11,10},{26,27},{27,26},{12,13... | collective-permute-start | bytes 1486856 | tf_op jit(solution)/shard_map/ppermute | solution.py:398
  21.3 8.8 %collective-permute-done.9.w_in.in_b = bf16[352,704]{1,0:T(8,128)(2,1)S(1)} collective-permute-done((bf16[352,704]{1,0:T(8,128)(2,1)S(1)}, bf16[352,704]{1,0:T(8,128)(2,1)S(1)}, u32[]{:S(2)}, u32[]{:S(2)}) %collective-permute-start.9) | collective-permute-done | bytes 495648 | tf_op jit(solution)/shard_map/ppermute | solution.py:398
  30.1 5.8 %collective-permute-done.10.out_b = bf16[704,352]{1,0:T(8,128)(2,1)S(1)} collective-permute-done((bf16[704,352]{1,0:T(8,128)(2,1)S(1)}, bf16[704,352]{1,0:T(8,128)(2,1)S(1)}, u32[]{:S(2)}, u32[]{:S(2)}) %collective-permute-start.10) | collective-permute-done | bytes 495648 | tf_op jit(solution)/shard_map/ppermute | solution.py:398
  35.9 0.7 collective-permute-start.11
  39.1 1.3 %collective-permute-start.15 = (bf16[16,48,352]{2,1,0:T(8,128)(2,1)S(1)}, bf16[16,48,352]{2,1,0:T(8,128)(2,1)S(1)}, u32[]{:S(2)}, u32[]{:S(2)}) collective-permute-start(bf16[16,48,352]{2,1,0:T(8,128)(2,1)S(1)} %mlp.1.prev), channel_id=1, source_target_pairs={{16,24},{17,25},{18,26},{19,27},{20,28},{21,29},{22,30},{23,31}} | collective-permute-start | bytes 1622024 | tf_op jit(solution)/shard_map/ppermute | solution.py:420
  40.4 20.4 %collective-permute-done.15.x = bf16[16,48,352]{2,1,0:T(8,128)(2,1)S(1)} collective-permute-done((bf16[16,48,352]{2,1,0:T(8,128)(2,1)S(1)}, bf16[16,48,352]{2,1,0:T(8,128)(2,1)S(1)}, u32[]{:S(2)}, u32[]{:S(2)}) %collective-permute-start.15) | collective-permute-done | bytes 540704 | tf_op jit(solution)/shard_map/ppermute | solution.py:420
  60.8 8.1 %conv_up.1 = (bf16[768,704]{1,0:T(8,128)(2,1)S(1)}, bf16[768,704]{1,0:T(8,128)(2,1)S(1)}, f32[2,1,704]{2,1,0:T(1,128)S(1)}) custom-call(s32[1]{0:T(128)} %bitcast.1.section, bf16[16,48,352]{2,1,0:T(8,128)(2,1)S(1)} %collective-permute-done.15.x, f32[64,384]{1,0:T(8,128)S(1)} %get-tuple-element.35.cpar.refs_7_, bf16[352,704]{1,0:T(8,128)(2,1)S(1)} %bitcast.30, ...), custom_call_target="tpu_custom_call" | custom-call | flops 761266176 | bytes 1647108 | tf_op jit(solution)/shard_map/conv_up/pallas_call | solution.py:334
  69.4 2.7 %collective-permute-start.16 = (bf16[4,48,352]{2,1,0:T(8,128)(2,1)S(1)}, bf16[4,48,352]{2,1,0:T(8,128)(2,1)S(1)}, u32[]{:S(2)}, u32[]{:S(2)}) collective-permute-start(bf16[4,48,352]{2,1,0:T(8,128)(2,1)S(1)} %down_piece.13), channel_id=1, source_target_pairs={{0,4},{2,6},{4,0},{6,2},{1,5},{3,7},{5,1},{7,3},{8,12},{10,14},{12... | collective-permute-start | bytes 405512 | tf_op jit(solution)/shard_map/ppermute | solution.py:537
  72.6 1.3 %collective-permute-start.17 = (bf16[4,48,352]{2,1,0:T(8,128)(2,1)S(1)}, bf16[4,48,352]{2,1,0:T(8,128)(2,1)S(1)}, u32[]{:S(2)}, u32[]{:S(2)}) collective-permute-start(bf16[4,48,352]{2,1,0:T(8,128)(2,1)S(1)} %down_piece.14), channel_id=1, source_target_pairs={{0,6},{2,4},{4,2},{6,0},{1,7},{3,5},{5,3},{7,1},{8,14},{10,12},{12... | collective-permute-start | bytes 405512 | tf_op jit(solution)/shard_map/ppermute | solution.py:537
  75.0 1.2 %collective-permute-done.16.refs_1_ = bf16[4,48,352]{2,1,0:T(8,128)(2,1)S(1)} collective-permute-done((bf16[4,48,352]{2,1,0:T(8,128)(2,1)S(1)}, bf16[4,48,352]{2,1,0:T(8,128)(2,1)S(1)}, u32[]{:S(2)}, u32[]{:S(2)}) %collective-permute-start.16) | collective-permute-done | bytes 135200 | tf_op jit(solution)/shard_map/ppermute | solution.py:537
  76.2 2.4 %collective-permute-done.17.refs_2_ = bf16[4,48,352]{2,1,0:T(8,128)(2,1)S(1)} collective-permute-done((bf16[4,48,352]{2,1,0:T(8,128)(2,1)S(1)}, bf16[4,48,352]{2,1,0:T(8,128)(2,1)S(1)}, u32[]{:S(2)}, u32[]{:S(2)}) %collective-permute-start.17) | collective-permute-done | bytes 135200 | tf_op jit(solution)/shard_map/ppermute | solution.py:537
  78.7 1.4 %collective-permute-done.18.refs_3_ = bf16[4,48,352]{2,1,0:T(8,128)(2,1)S(1)} collective-permute-done((bf16[4,48,352]{2,1,0:T(8,128)(2,1)S(1)}, bf16[4,48,352]{2,1,0:T(8,128)(2,1)S(1)}, u32[]{:S(2)}, u32[]{:S(2)}) %collective-permute-start.18) | collective-permute-done | bytes 135200 | tf_op jit(solution)/shard_map/ppermute | solution.py:537
  80.0 0.8 %place.1 = bf16[1,4,1,4,48,352]{5,4,3,2,1,0:T(8,128)(2,1)} custom-call(s32[1]{0:T(128)} %bitcast.me, bf16[4,48,352]{2,1,0:T(8,128)(2,1)S(1)} %down_piece.12.refs_0_, bf16[4,48,352]{2,1,0:T(8,128)(2,1)S(1)} %collective-permute-done.16.refs_1_, bf16[4,48,352]{2,1,0:T(8,128)(2,1)S(1)} %collective-permute-done.17.refs_2_, ...), custom_call_target="tpu_custom_call" | custom-call | bytes 540676 | tf_op jit(solution)/shard_map/place/pallas_call | solution.py:334
  (61 shorter events, 5.5 us)
Async XLA Ops:
  0.0 10.0 %copy-start.2 = (bf16[1,1408]{1,0:T(2,128)(2,1)S(1)}, bf16[1,1408]{1,0:T(2,128)(2,1)}, u32[]{:S(2)}) copy-start(bf16[1,1408]{1,0:T(2,128)(2,1)} %refs_4_.1) | copy-start | bytes 8452
  0.0 10.0 %copy-start.7 = (bf16[1,352]{1,0:T(2,128)(2,1)S(1)}, bf16[1,352]{1,0:T(2,128)(2,1)}, u32[]{:S(2)}) copy-start(bf16[1,352]{1,0:T(2,128)(2,1)} %refs_2_.1) | copy-start | bytes 2116
  0.0 10.0 %copy-start.6 = (bf16[1,352]{1,0:T(2,128)(2,1)S(1)}, bf16[1,352]{1,0:T(2,128)(2,1)}, u32[]{:S(2)}) copy-start(bf16[1,352]{1,0:T(2,128)(2,1)} %refs_1_.1) | copy-start | bytes 2116
  0.0 10.0 %copy-start.5 = (bf16[1,352]{1,0:T(2,128)(2,1)S(1)}, bf16[1,352]{1,0:T(2,128)(2,1)}, u32[]{:S(2)}) copy-start(bf16[1,352]{1,0:T(2,128)(2,1)} %refs_0_.1) | copy-start | bytes 2116
  0.0 10.0 %copy-start.1 = (bf16[1,7,7,352]{3,2,1,0:T(8,128)(2,1)S(1)}, bf16[1,7,7,352]{3,2,1,0:T(8,128)(2,1)}, u32[]{:S(2)}) copy-start(bf16[1,7,7,352]{3,2,1,0:T(8,128)(2,1)} %kernel.1) | copy-start | bytes 103492
  0.1 12.8 %collective-permute-start.5 = (bf16[352,704]{1,0:T(8,128)(2,1)}, bf16[352,704]{1,0:T(8,128)(2,1)S(1)}, u32[]{:S(2)}, u32[]{:S(2)}) collective-permute-start(bf16[352,704]{1,0:T(8,128)(2,1)} %bitcast.25), channel_id=1, source_target_pairs={{0,1},{1,0},{16,17},{17,16},{2,3},{3,2},{18,19},{19,18},{4,5},{5,4... | collective-permute-start | bytes 1486856 | tf_op jit(solution)/shard_map/ppermute | solution.py:398
  2.1 8.9 %collective-permute-start = (bf16[4,48,352]{2,1,0:T(8,128)(2,1)S(1)}, bf16[4,48,352]{2,1,0:T(8,128)(2,1)S(1)}, u32[]{:S(2)}, u32[]{:S(2)}) collective-permute-start(bf16[4,48,352]{2,1,0:T(8,128)(2,1)S(1)} %get-tuple-element.66), channel_id=1, source_target_pairs={{28,8},{30,10},{24,12},{26,14},{29,9},{31,11},{25,13},{27,15}} | collective-permute-start | bytes 405512 | tf_op jit(solution)/shard_map/ppermute | solution.py:393
  6.3 4.7 %collective-permute-start.1 = (bf16[4,48,352]{2,1,0:T(8,128)(2,1)S(1)}, bf16[4,48,352]{2,1,0:T(8,128)(2,1)S(1)}, u32[]{:S(2)}, u32[]{:S(2)}) collective-permute-start(bf16[4,48,352]{2,1,0:T(8,128)(2,1)S(1)} %get-tuple-element.68), channel_id=1, source_target_pairs={{30,8},{28,10},{26,12},{24,14},{31,9},{29,11},{27,13},{25,15}} | collective-permute-start | bytes 405512 | tf_op jit(solution)/shard_map/ppermute | solution.py:393
  8.6 4.3 %collective-permute-start.2 = (bf16[4,48,352]{2,1,0:T(8,128)(2,1)S(1)}, bf16[4,48,352]{2,1,0:T(8,128)(2,1)S(1)}, u32[]{:S(2)}, u32[]{:S(2)}) collective-permute-start(bf16[4,48,352]{2,1,0:T(8,128)(2,1)S(1)} %get-tuple-element.65), channel_id=1, source_target_pairs={{26,8},{24,10},{30,12},{28,14},{27,9},{25,11},{31,13},{29,15}} | collective-permute-start | bytes 405512 | tf_op jit(solution)/shard_map/ppermute | solution.py:393
  10.3 0.7 collective-permute-start.3
  12.9 2.3 %collective-permute-start.6 = (bf16[16,48,352]{2,1,0:T(8,128)(2,1)S(1)}, bf16[16,48,352]{2,1,0:T(8,128)(2,1)S(1)}, u32[]{:S(2)}, u32[]{:S(2)}) collective-permute-start(bf16[16,48,352]{2,1,0:T(8,128)(2,1)S(1)} %get-tuple-element.42), channel_id=1, source_target_pairs={{8,0},{9,1},{10,2},{11,3},{12,4},{13,5},{14,6},{15,7}} | collective-permute-start | bytes 1622024 | tf_op jit(solution)/shard_map/ppermute | solution.py:420
  13.7 1.5 %collective-permute-start.4 = (bf16[16,48,352]{2,1,0:T(8,128)(2,1)S(1)}, bf16[16,48,352]{2,1,0:T(8,128)(2,1)S(1)}, u32[]{:S(2)}, u32[]{:S(2)}) collective-permute-start(bf16[16,48,352]{2,1,0:T(8,128)(2,1)S(1)} %get-tuple-element.40), channel_id=1, source_target_pairs={{8,0},{9,1},{10,2},{11,3},{12,4},{13,5},{14,6},{15,7}} | collective-permute-start | bytes 1622024 | tf_op jit(solution)/shard_map/ppermute | solution.py:420
  14.4 0.8 collective-permute-start.7
  15.2 6.0 %collective-permute-start.8 = (bf16[16,48,352]{2,1,0:T(8,128)(2,1)S(1)}, bf16[16,48,352]{2,1,0:T(8,128)(2,1)S(1)}, u32[]{:S(2)}, u32[]{:S(2)}) collective-permute-start(bf16[16,48,352]{2,1,0:T(8,128)(2,1)S(1)} %down.1.prev.refs_4_), channel_id=1, source_target_pairs={{0,8},{1,9},{2,10},{3,11},{4,12},{5,13},{6,14},{7,15}} | collective-permute-start | bytes 1622024 | tf_op jit(solution)/shard_map/ppermute | solution.py:420
  15.9 14.2 %collective-permute-start.9 = (bf16[352,704]{1,0:T(8,128)(2,1)S(1)}, bf16[352,704]{1,0:T(8,128)(2,1)S(1)}, u32[]{:S(2)}, u32[]{:S(2)}) collective-permute-start(bf16[352,704]{1,0:T(8,128)(2,1)S(1)} %bitcast.27), channel_id=1, source_target_pairs={{8,9},{9,8},{24,25},{25,24},{10,11},{11,10},{26,27},{27,26},{12,13... | collective-permute-start | bytes 1486856 | tf_op jit(solution)/shard_map/ppermute | solution.py:398
  18.1 17.8 %collective-permute-start.10 = (bf16[704,352]{1,0:T(8,128)(2,1)S(1)}, bf16[704,352]{1,0:T(8,128)(2,1)S(1)}, u32[]{:S(2)}, u32[]{:S(2)}) collective-permute-start(bf16[704,352]{1,0:T(8,128)(2,1)S(1)} %bitcast.15), channel_id=1, source_target_pairs={{8,9},{9,8},{24,25},{25,24},{10,11},{11,10},{26,27},{27,26},{12,13... | collective-permute-start | bytes 1486856 | tf_op jit(solution)/shard_map/ppermute | solution.py:398
  35.9 2.8 %collective-permute-start.11 = (bf16[4,48,352]{2,1,0:T(8,128)(2,1)S(1)}, bf16[4,48,352]{2,1,0:T(8,128)(2,1)S(1)}, u32[]{:S(2)}, u32[]{:S(2)}) collective-permute-start(bf16[4,48,352]{2,1,0:T(8,128)(2,1)S(1)} %down_piece.8.refs_0_), channel_id=1, source_target_pairs={{8,16},{9,17},{10,18},{11,19},{12,20},{13,21},{14,22},{15,23}} | collective-permute-start | bytes 405512 | tf_op jit(solution)/shard_map/ppermute | solution.py:420
  36.6 2.1 %collective-permute-start.12 = (bf16[4,48,352]{2,1,0:T(8,128)(2,1)S(1)}, bf16[4,48,352]{2,1,0:T(8,128)(2,1)S(1)}, u32[]{:S(2)}, u32[]{:S(2)}) collective-permute-start(bf16[4,48,352]{2,1,0:T(8,128)(2,1)S(1)} %down_piece.9.refs_1_), channel_id=1, source_target_pairs={{8,16},{9,17},{10,18},{11,19},{12,20},{13,21},{14,22},{15,23}} | collective-permute-start | bytes 405512 | tf_op jit(solution)/shard_map/ppermute | solution.py:420
  37.3 1.5 %collective-permute-start.13 = (bf16[4,48,352]{2,1,0:T(8,128)(2,1)S(1)}, bf16[4,48,352]{2,1,0:T(8,128)(2,1)S(1)}, u32[]{:S(2)}, u32[]{:S(2)}) collective-permute-start(bf16[4,48,352]{2,1,0:T(8,128)(2,1)S(1)} %down_piece.10.refs_2_), channel_id=1, source_target_pairs={{8,16},{9,17},{10,18},{11,19},{12,20},{13,21},{14,22},{15,23}} | collective-permute-start | bytes 405512 | tf_op jit(solution)/shard_map/ppermute | solution.py:420
  38.0 0.8 collective-permute-start.14
  39.1 21.7 %collective-permute-start.15 = (bf16[16,48,352]{2,1,0:T(8,128)(2,1)S(1)}, bf16[16,48,352]{2,1,0:T(8,128)(2,1)S(1)}, u32[]{:S(2)}, u32[]{:S(2)}) collective-permute-start(bf16[16,48,352]{2,1,0:T(8,128)(2,1)S(1)} %mlp.1.prev), channel_id=1, source_target_pairs={{16,24},{17,25},{18,26},{19,27},{20,28},{21,29},{22,30},{23,31}} | collective-permute-start | bytes 1622024 | tf_op jit(solution)/shard_map/ppermute | solution.py:420
  69.4 6.8 %collective-permute-start.16 = (bf16[4,48,352]{2,1,0:T(8,128)(2,1)S(1)}, bf16[4,48,352]{2,1,0:T(8,128)(2,1)S(1)}, u32[]{:S(2)}, u32[]{:S(2)}) collective-permute-start(bf16[4,48,352]{2,1,0:T(8,128)(2,1)S(1)} %down_piece.13), channel_id=1, source_target_pairs={{0,4},{2,6},{4,0},{6,2},{1,5},{3,7},{5,1},{7,3},{8,12},{10,14},{12... | collective-permute-start | bytes 405512 | tf_op jit(solution)/shard_map/ppermute | solution.py:537
  72.6 6.1 %collective-permute-start.17 = (bf16[4,48,352]{2,1,0:T(8,128)(2,1)S(1)}, bf16[4,48,352]{2,1,0:T(8,128)(2,1)S(1)}, u32[]{:S(2)}, u32[]{:S(2)}) collective-permute-start(bf16[4,48,352]{2,1,0:T(8,128)(2,1)S(1)} %down_piece.14), channel_id=1, source_target_pairs={{0,6},{2,4},{4,2},{6,0},{1,7},{3,5},{5,3},{7,1},{8,14},{10,12},{12... | collective-permute-start | bytes 405512 | tf_op jit(solution)/shard_map/ppermute | solution.py:537
  74.4 5.6 %collective-permute-start.18 = (bf16[4,48,352]{2,1,0:T(8,128)(2,1)S(1)}, bf16[4,48,352]{2,1,0:T(8,128)(2,1)S(1)}, u32[]{:S(2)}, u32[]{:S(2)}) collective-permute-start(bf16[4,48,352]{2,1,0:T(8,128)(2,1)S(1)} %down_piece.15), channel_id=1, source_target_pairs={{0,2},{2,0},{4,6},{6,4},{1,3},{3,1},{5,7},{7,5},{8,10},{10,8},{12,... | collective-permute-start | bytes 405512 | tf_op jit(solution)/shard_map/ppermute | solution.py:537
  (5 other events, 33.7 us)

commit v8 on v4

--- a/solution.py
+++ b/solution.py
@@ -164,7 +164,7 @@
     _, width, channels = x_rows.shape
     cells = CHUNK * width
     at = pl.ds(pl.multiple_of(first_row * width, cells), cells)
-    update = cpar[VECTORS + 3 : VECTORS + 4, 0:channels]
+    update = cpar[VECTORS + 3 : VECTORS + 4, :].astype(jnp.float32)
     for which in range(2):
         a = acts[which][at, :].astype(jnp.float32)
         hidden = (a * scale[which] + fvec[which, 2:3, :]).astype(jnp.bfloat16)
@@ -183,37 +183,29 @@
     lax.fori_loop(0, x.shape[0] // CHUNK, rows, 0)
 
 
-def prepare_kernel(part, kernel, *refs):
-    vectors, (cpar, fvec), (held, *staged), sems = refs[:7], refs[7:9], refs[9:-1], refs[-1]
-    moves = [(kernel, held), *zip(vectors, staged)]
-    copies = [pltpu.make_async_copy(a, b, sems.at[n]) for n, (a, b) in enumerate(moves)]
-    for copy in copies:
-        copy.start()
-    cpar[...] = jnp.zeros(cpar.shape, jnp.float32)
-    for copy in copies:
-        copy.wait()
-    channels = kernel.shape[3]
-    span = kernel.shape[1]
+def prepare_kernel(part, bias_in, gamma, beta, fvec):
     half = fvec.shape[2]
-    for i in range(span):
-        cpar[i * span : (i + 1) * span, 0:channels] = held[0, i].astype(jnp.float32)
-    for n in range(4):
-        cpar[VECTORS + n : VECTORS + n + 1, 0:channels] = staged[n][...].astype(jnp.float32)
     first = part[0] == 0
-    for n in range(3):
-        v = staged[4 + n][...].astype(jnp.float32)
+    for n, ref in enumerate((bias_in, gamma, beta)):
+        v = ref[...].astype(jnp.float32)
         low, high = v[:, 0:half], v[:, half:]
         fvec[0, n : n + 1, :] = jnp.where(first, low, high)
         fvec[1, n : n + 1, :] = jnp.where(first, high, low)
 
 
+def widen(raw, cpar):
+    cpar[...] = jnp.zeros(cpar.shape, jnp.float32)
+    cpar[:, 0 : raw.shape[1]] = raw[...].astype(jnp.float32)
+
+
 def block_of(me, order, n):
     return n if order is None else me[0] ^ order[n]
 
 
-def piece_kernel(section, piece, cpar, part, xp, xs, *, on):
+def piece_kernel(section, piece, raw, part, xp, xs, cpar, *, on):
     @pl.when(section[0] == on)
     def _():
+        widen(raw, cpar)
         fill_columns(xp, xs, piece, piece.shape[2])
         conv(xs, cpar, part)
 
@@ -221,11 +213,12 @@
 def last_piece_kernel(section, me, *refs, order, on):
     count = len(order or IN_ORDER)
     pieces, parts = refs[:count], refs[count : 2 * count - 1]
-    cpar, x, flat, xp, xs, own, cq = refs[2 * count - 1 :]
+    raw, x, flat, xp, xs, own, cq, cpar = refs[2 * count - 1 :]
     rows = pieces[0].shape[0]
 
     @pl.when(section[0] == on)
     def _():
+        widen(raw, cpar)
         bias = cpar[VECTORS : VECTORS + 1, :].reshape(1, 1, 1, cq.shape[3])
         cq[...] = jnp.broadcast_to(bias, cq.shape)
         fill_columns(xp, xs, pieces[-1], x.shape[2])
@@ -237,9 +230,10 @@
         norm(cq, cpar, xp, flat, REACH)
 
 
-def conv_kernel(section, x, cpar, flat, xp, xs, cq, *, tick):
+def conv_kernel(section, x, raw, flat, xp, xs, cq, cpar, *, tick):
     @pl.when(section[0] == tick)
     def _():
+        widen(raw, cpar)
         conv_norm(x, cpar, flat, xp, xs, cq)
 
 
@@ -297,11 +291,12 @@
         out[...] = prev[...]
 
 
-def conv_up_kernel(section, x, cpar, in_a, in_b, fvec, *refs, tick):
-    act_a, act_b, scale, xp, xs, cq, flat, ssq_a, ssq_b = refs
+def conv_up_kernel(section, x, raw, in_a, in_b, fvec, *refs, tick):
+    act_a, act_b, scale, xp, xs, cq, cpar, flat, ssq_a, ssq_b = refs
 
     @pl.when(section[0] == tick)
     def _():
+        widen(raw, cpar)
         conv_norm(x, cpar, flat, xp, xs, cq)
         up(flat, in_a, fvec.at[0], act_a, ssq_a)
         up(flat, in_b, fvec.at[1], act_b, ssq_b)
@@ -403,18 +398,15 @@
     other_in = other_half(w_in, even)
     other_out = other_half(w_out, even)
 
-    held = (
-        depth_kernel, depth_bias, norm_gain, norm_bias, bias_out, bias_in, grn_gamma, grn_beta
-    )
-    cpar, fvec = call(
-        prepare_kernel,
-        "prepare",
-        (part, *held),
-        (shape(VECTORS + 8, lanes), shape(2, 3, half)),
-        specs=[SMEM] + [HBM] * len(held),
-        scratch=[pltpu.VMEM(v.shape, v.dtype) for v in held]
-        + [pltpu.SemaphoreType.DMA((len(held),))],
-    )
+    fvec = call(
+        prepare_kernel, "prepare", (part, bias_in, grn_gamma, grn_beta), shape(2, 3, half)
+    )
+    taps = depth_kernel.reshape(span * span, channels)
+    gap = jnp.zeros((VECTORS - span * span, channels), bf16)
+    cpar = jnp.concatenate(
+        [taps, gap, depth_bias, norm_gain, norm_bias, bias_out, jnp.zeros((4, channels), bf16)]
+    )
+    wide_cpar = pltpu.VMEM((VECTORS + 8, lanes), jnp.float32)
 
     def send(x, start, end):
         return lax.ppermute(x, "section", [(start, end)])
@@ -431,7 +423,7 @@
                 "conv_piece",
                 (section, piece, cpar),
                 shape(out_rows, width // 8, 8, lanes),
-                scratch=scratch[:2],
+                scratch=scratch[:2] + [wide_cpar],
                 on=on,
             )
             parts.append(part)
@@ -440,7 +432,7 @@
             "last_piece",
             (section, me_ref, *pieces, *parts, cpar),
             (whole, whole),
-            scratch=scratch + [conv_scratch(1, height + 2 * REACH, width, lanes)[2]],
+            scratch=scratch + [conv_scratch(1, height + 2 * REACH, width, lanes)[2], wide_cpar],
             order=order,
             on=on,
         )
@@ -502,7 +494,7 @@
         "conv",
         (section, x, cpar),
         whole,
-        scratch=conv_scratch(height, height, width, lanes),
+        scratch=conv_scratch(height, height, width, lanes) + [wide_cpar],
         tick=1,
     )
     act_a, ssq = up_own(flat, 1)
@@ -527,6 +519,7 @@
         (section, x, cpar, w_in, odd_in, fvec),
         (act_shape, act_shape, scale_shape),
         scratch=conv_scratch(height, height, width, lanes)
+        + [wide_cpar]
         + [pltpu.VMEM((height, width, channels), bf16)]
         + [ssq_scratch(half)] * 2,
         flops=2 * matmul,

time: 89.3 us -> 86.7 us (0.971)
  local copies, waits for them, and re-layouts: 7.76 us -> 5.77 us
    unnamed x20 -> x14, local copies, waits for them, and re-layouts: 6.57 us -> 2.95 us
  transfers between devices with their start and end apart: 19 -> 19, of which waited for: 8 -> 8; matrix products, arithmetic and copies ran while one was open for 1% -> 3% of each run, Pallas kernels for 2% -> 2%
where the time goes in v8:
time: 86.7 us; the launch traced here: 86.2 us
  waiting for transfers between devices  42.5 us (49%)
  starting transfers between devices  25.9 us (30%)
  Pallas kernels  11.4 us (13%)
  local copies, waits for them, and re-layouts  5.77 us (7%)
    ppermute x9, waiting for transfers between devices, send(): return lax.ppermute(x, 'section', [(start, end)])  24 us
    pallas_call x26, Pallas kernels, call(): pl.pallas_call(functools.partial(kernel, **static), out_shape=out, in_spe...  11.4 us
    ppermute x4, waiting for transfers between devices, other_half(): return lax.ppermute(x, ('section', 'dp'), pairs)  10.6 us
    ppermute x3, starting transfers between devices, image_plan(): piece = lax.ppermute(piece, ('section', 'row'), pairs)  8.42 us
    ppermute x9, starting transfers between devices, send(): return lax.ppermute(x, 'section', [(start, end)])  6.71 us
    ppermute x4, starting transfers between devices, other_half(): return lax.ppermute(x, ('section', 'dp'), pairs)  6.66 us
    ppermute x3, waiting for transfers between devices, image_plan(): lax.ppermute(piece, 'row', [(p, p ^ order[n]) for p in range(count)])  5.05 us
    ppermute x3, starting transfers between devices, image_plan(): lax.ppermute(piece, 'row', [(p, p ^ order[n]) for p in range(count)])  4.11 us
  transfers between devices with their start and end apart: 19, of which 8 were waited for; matrix products, arithmetic and copies ran while one was open for 3% of the time, Pallas kernels for 2%

profile of v8, /device:TPU:7, one launch (start us, length us, event | category | flops | bytes accessed | tf_op | source)
XLA Modules:
  0.0 86.2 jit_solution(4709311206121524536)
XLA Ops:
  1.4 0.8 reshape.18
  2.2 0.8 concatenate.3.cpar.raw.refs_7_
  3.7 1.2 %dynamic-slice_bitcast_fusion = (bf16[4,48,352]{2,1,0:T(8,128)(2,1)S(1)}, bf16[4,48,352]{2,1,0:T(8,128)(2,1)S(1)}, bf16[4,48,352]{2,1,0:T(8,128)(2,1)S(1)}, bf16[4,48,352]{2,1,0:T(8,128)(2,1)S(1)}) fusion(bf16[4,1,4,48,352]{4,3,2,1,0:T(8,128)(2,1)} %param.11, s32[]{:T(128)S(6)} %select_n.16, s32[]{:T(128)S(6)} %select_n.14, s32[]{:T(128)S(6)} %select_n.13, ...), kind=kLoop, calls=%fused_computation | loop fusion | bytes 1081360 | tf_op jit(solution)/shard_map/squeeze | solution.py:385
  4.9 4.8 %collective-permute-start = (bf16[4,48,352]{2,1,0:T(8,128)(2,1)S(1)}, bf16[4,48,352]{2,1,0:T(8,128)(2,1)S(1)}, u32[]{:S(2)}, u32[]{:S(2)}) collective-permute-start(bf16[4,48,352]{2,1,0:T(8,128)(2,1)S(1)} %get-tuple-element.66), channel_id=1, source_target_pairs={{28,8},{30,10},{24,12},{26,14},{29,9},{31,11},{25,13},{27,15}} | collective-permute-start | bytes 405512 | tf_op jit(solution)/shard_map/ppermute | solution.py:388
  9.7 2.3 %collective-permute-start.1 = (bf16[4,48,352]{2,1,0:T(8,128)(2,1)S(1)}, bf16[4,48,352]{2,1,0:T(8,128)(2,1)S(1)}, u32[]{:S(2)}, u32[]{:S(2)}) collective-permute-start(bf16[4,48,352]{2,1,0:T(8,128)(2,1)S(1)} %get-tuple-element.68), channel_id=1, source_target_pairs={{30,8},{28,10},{26,12},{24,14},{31,9},{29,11},{27,13},{25,15}} | collective-permute-start | bytes 405512 | tf_op jit(solution)/shard_map/ppermute | solution.py:388
  12.1 1.3 %collective-permute-start.2 = (bf16[4,48,352]{2,1,0:T(8,128)(2,1)S(1)}, bf16[4,48,352]{2,1,0:T(8,128)(2,1)S(1)}, u32[]{:S(2)}, u32[]{:S(2)}) collective-permute-start(bf16[4,48,352]{2,1,0:T(8,128)(2,1)S(1)} %get-tuple-element.65), channel_id=1, source_target_pairs={{26,8},{24,10},{30,12},{28,14},{27,9},{25,11},{31,13},{29,15}} | collective-permute-start | bytes 405512 | tf_op jit(solution)/shard_map/ppermute | solution.py:388
  13.4 0.7 collective-permute-done.1.piece.refs_2_
  14.2 2.1 %collective-permute-done.2.refs_3_ = bf16[4,48,352]{2,1,0:T(8,128)(2,1)S(1)} collective-permute-done((bf16[4,48,352]{2,1,0:T(8,128)(2,1)S(1)}, bf16[4,48,352]{2,1,0:T(8,128)(2,1)S(1)}, u32[]{:S(2)}, u32[]{:S(2)}) %collective-permute-start.2) | collective-permute-done | bytes 135200 | tf_op jit(solution)/shard_map/ppermute | solution.py:388
  16.3 0.8 copy-done.5
  18.7 1.1 %copy-done.4 = bf16[1,352,704]{2,1,0:T(8,128)(2,1)S(1)} copy-done((bf16[1,352,704]{2,1,0:T(8,128)(2,1)S(1)}, bf16[1,352,704]{2,1,0:T(8,128)(2,1)}, u32[]{:S(2)}) %copy-start.4) | copy-done | bytes 495640
  19.8 1.0 %copy-done.6 = bf16[352,704]{1,0:T(8,128)(2,1)S(1)} copy-done((bf16[352,704]{1,0:T(8,128)(2,1)S(1)}, bf16[352,704]{1,0:T(8,128)(2,1)}, u32[]{:S(2)}) %copy-start.6) | copy-done | bytes 495640
  21.5 2.1 %collective-permute-start.9 = (bf16[352,704]{1,0:T(8,128)(2,1)S(1)}, bf16[352,704]{1,0:T(8,128)(2,1)S(1)}, u32[]{:S(2)}, u32[]{:S(2)}) collective-permute-start(bf16[352,704]{1,0:T(8,128)(2,1)S(1)} %bitcast.27), channel_id=1, source_target_pairs={{8,9},{9,8},{24,25},{25,24},{10,11},{11,10},{26,27},{27,26},{12,13... | collective-permute-start | bytes 1486856 | tf_op jit(solution)/shard_map/ppermute | solution.py:393
  23.7 3.1 %collective-permute-start.10 = (bf16[704,352]{1,0:T(8,128)(2,1)S(1)}, bf16[704,352]{1,0:T(8,128)(2,1)S(1)}, u32[]{:S(2)}, u32[]{:S(2)}) collective-permute-start(bf16[704,352]{1,0:T(8,128)(2,1)S(1)} %bitcast.15), channel_id=1, source_target_pairs={{8,9},{9,8},{24,25},{25,24},{10,11},{11,10},{26,27},{27,26},{12,13... | collective-permute-start | bytes 1486856 | tf_op jit(solution)/shard_map/ppermute | solution.py:393
  26.9 4.8 %collective-permute-done.9.w_in.in_b = bf16[352,704]{1,0:T(8,128)(2,1)S(1)} collective-permute-done((bf16[352,704]{1,0:T(8,128)(2,1)S(1)}, bf16[352,704]{1,0:T(8,128)(2,1)S(1)}, u32[]{:S(2)}, u32[]{:S(2)}) %collective-permute-start.9) | collective-permute-done | bytes 495648 | tf_op jit(solution)/shard_map/ppermute | solution.py:393
  31.7 5.8 %collective-permute-done.10.out_b = bf16[704,352]{1,0:T(8,128)(2,1)S(1)} collective-permute-done((bf16[704,352]{1,0:T(8,128)(2,1)S(1)}, bf16[704,352]{1,0:T(8,128)(2,1)S(1)}, u32[]{:S(2)}, u32[]{:S(2)}) %collective-permute-start.10) | collective-permute-done | bytes 495648 | tf_op jit(solution)/shard_map/ppermute | solution.py:393
  40.6 1.3 %collective-permute-start.15 = (bf16[16,48,352]{2,1,0:T(8,128)(2,1)S(1)}, bf16[16,48,352]{2,1,0:T(8,128)(2,1)S(1)}, u32[]{:S(2)}, u32[]{:S(2)}) collective-permute-start(bf16[16,48,352]{2,1,0:T(8,128)(2,1)S(1)} %mlp.1.prev), channel_id=1, source_target_pairs={{16,24},{17,25},{18,26},{19,27},{20,28},{21,29},{22,30},{23,31}} | collective-permute-start | bytes 1622024 | tf_op jit(solution)/shard_map/ppermute | solution.py:412
  41.9 24.0 %collective-permute-done.15.x = bf16[16,48,352]{2,1,0:T(8,128)(2,1)S(1)} collective-permute-done((bf16[16,48,352]{2,1,0:T(8,128)(2,1)S(1)}, bf16[16,48,352]{2,1,0:T(8,128)(2,1)S(1)}, u32[]{:S(2)}, u32[]{:S(2)}) %collective-permute-start.15) | collective-permute-done | bytes 540704 | tf_op jit(solution)/shard_map/ppermute | solution.py:412
  65.9 8.1 %conv_up.1 = (bf16[768,704]{1,0:T(8,128)(2,1)S(1)}, bf16[768,704]{1,0:T(8,128)(2,1)S(1)}, f32[2,1,704]{2,1,0:T(1,128)S(1)}) custom-call(s32[1]{0:T(128)} %bitcast.1.section, bf16[16,48,352]{2,1,0:T(8,128)(2,1)S(1)} %collective-permute-done.15.x, bf16[64,352]{1,0:T(8,128)(2,1)S(1)} %concatenate.3.cpar.raw.refs_7_, bf16[352,704]{1,0:T(8,128)(2,1)S(1)} %bitcast.30, ...), custom_call_target="tpu_custom_call" | custom-call | flops 761266176 | bytes 1593860 | tf_op jit(solution)/shard_map/conv_up/pallas_call | solution.py:329
  74.5 2.9 %collective-permute-start.16 = (bf16[4,48,352]{2,1,0:T(8,128)(2,1)S(1)}, bf16[4,48,352]{2,1,0:T(8,128)(2,1)S(1)}, u32[]{:S(2)}, u32[]{:S(2)}) collective-permute-start(bf16[4,48,352]{2,1,0:T(8,128)(2,1)S(1)} %down_piece.13), channel_id=1, source_target_pairs={{0,4},{2,6},{4,0},{6,2},{1,5},{3,7},{5,1},{7,3},{8,12},{10,14},{12... | collective-permute-start | bytes 405512 | tf_op jit(solution)/shard_map/ppermute | solution.py:532
  77.9 1.1 %collective-permute-start.17 = (bf16[4,48,352]{2,1,0:T(8,128)(2,1)S(1)}, bf16[4,48,352]{2,1,0:T(8,128)(2,1)S(1)}, u32[]{:S(2)}, u32[]{:S(2)}) collective-permute-start(bf16[4,48,352]{2,1,0:T(8,128)(2,1)S(1)} %down_piece.14), channel_id=1, source_target_pairs={{0,6},{2,4},{4,2},{6,0},{1,7},{3,5},{5,3},{7,1},{8,14},{10,12},{12... | collective-permute-start | bytes 405512 | tf_op jit(solution)/shard_map/ppermute | solution.py:532
  80.1 1.4 %collective-permute-done.16.refs_1_ = bf16[4,48,352]{2,1,0:T(8,128)(2,1)S(1)} collective-permute-done((bf16[4,48,352]{2,1,0:T(8,128)(2,1)S(1)}, bf16[4,48,352]{2,1,0:T(8,128)(2,1)S(1)}, u32[]{:S(2)}, u32[]{:S(2)}) %collective-permute-start.16) | collective-permute-done | bytes 135200 | tf_op jit(solution)/shard_map/ppermute | solution.py:532
  81.5 2.4 %collective-permute-done.17.refs_2_ = bf16[4,48,352]{2,1,0:T(8,128)(2,1)S(1)} collective-permute-done((bf16[4,48,352]{2,1,0:T(8,128)(2,1)S(1)}, bf16[4,48,352]{2,1,0:T(8,128)(2,1)S(1)}, u32[]{:S(2)}, u32[]{:S(2)}) %collective-permute-start.17) | collective-permute-done | bytes 135200 | tf_op jit(solution)/shard_map/ppermute | solution.py:532
  83.9 1.2 %collective-permute-done.18.refs_3_ = bf16[4,48,352]{2,1,0:T(8,128)(2,1)S(1)} collective-permute-done((bf16[4,48,352]{2,1,0:T(8,128)(2,1)S(1)}, bf16[4,48,352]{2,1,0:T(8,128)(2,1)S(1)}, u32[]{:S(2)}, u32[]{:S(2)}) %collective-permute-start.18) | collective-permute-done | bytes 135200 | tf_op jit(solution)/shard_map/ppermute | solution.py:532
  85.2 0.8 place.1
  (59 shorter events, 9.4 us)
Async XLA Ops:
  0.0 16.3 %collective-permute-start.6 = (bf16[352,704]{1,0:T(8,128)(2,1)}, bf16[352,704]{1,0:T(8,128)(2,1)S(1)}, u32[]{:S(2)}, u32[]{:S(2)}) collective-permute-start(bf16[352,704]{1,0:T(8,128)(2,1)} %bitcast.25), channel_id=1, source_target_pairs={{0,1},{1,0},{16,17},{17,16},{2,3},{3,2},{18,19},{19,18},{4,5},{5,4... | collective-permute-start | bytes 1486856 | tf_op jit(solution)/shard_map/ppermute | solution.py:393
  0.7 17.1 %collective-permute-start.4 = (bf16[704,352]{1,0:T(8,128)(2,1)}, bf16[704,352]{1,0:T(8,128)(2,1)S(1)}, u32[]{:S(2)}, u32[]{:S(2)}) collective-permute-start(bf16[704,352]{1,0:T(8,128)(2,1)} %bitcast.13), channel_id=1, source_target_pairs={{0,1},{1,0},{16,17},{17,16},{2,3},{3,2},{18,19},{19,18},{4,5},{5,4... | collective-permute-start | bytes 1486856 | tf_op jit(solution)/shard_map/ppermute | solution.py:393
  3.0 9.0 %collective-permute-start.3 = (bf16[64,352]{1,0:T(8,128)(2,1)S(1)}, bf16[64,352]{1,0:T(8,128)(2,1)S(1)}, u32[]{:S(2)}, u32[]{:S(2)}) collective-permute-start(bf16[64,352]{1,0:T(8,128)(2,1)S(1)} %concatenate.3.cpar.raw.refs_7_), channel_id=1, source_target_pairs={{0,8},{1,9},{2,10},{3,11},{4,12},{5,13},{6,14},{7,15}} | collective-permute-start | bytes 135176 | tf_op jit(solution)/shard_map/ppermute | solution.py:412
  4.9 8.5 %collective-permute-start = (bf16[4,48,352]{2,1,0:T(8,128)(2,1)S(1)}, bf16[4,48,352]{2,1,0:T(8,128)(2,1)S(1)}, u32[]{:S(2)}, u32[]{:S(2)}) collective-permute-start(bf16[4,48,352]{2,1,0:T(8,128)(2,1)S(1)} %get-tuple-element.66), channel_id=1, source_target_pairs={{28,8},{30,10},{24,12},{26,14},{29,9},{31,11},{25,13},{27,15}} | collective-permute-start | bytes 405512 | tf_op jit(solution)/shard_map/ppermute | solution.py:388
  9.7 4.4 %collective-permute-start.1 = (bf16[4,48,352]{2,1,0:T(8,128)(2,1)S(1)}, bf16[4,48,352]{2,1,0:T(8,128)(2,1)S(1)}, u32[]{:S(2)}, u32[]{:S(2)}) collective-permute-start(bf16[4,48,352]{2,1,0:T(8,128)(2,1)S(1)} %get-tuple-element.68), channel_id=1, source_target_pairs={{30,8},{28,10},{26,12},{24,14},{31,9},{29,11},{27,13},{25,15}} | collective-permute-start | bytes 405512 | tf_op jit(solution)/shard_map/ppermute | solution.py:388
  12.1 4.2 %collective-permute-start.2 = (bf16[4,48,352]{2,1,0:T(8,128)(2,1)S(1)}, bf16[4,48,352]{2,1,0:T(8,128)(2,1)S(1)}, u32[]{:S(2)}, u32[]{:S(2)}) collective-permute-start(bf16[4,48,352]{2,1,0:T(8,128)(2,1)S(1)} %get-tuple-element.65), channel_id=1, source_target_pairs={{26,8},{24,10},{30,12},{28,14},{27,9},{25,11},{31,13},{29,15}} | collective-permute-start | bytes 405512 | tf_op jit(solution)/shard_map/ppermute | solution.py:388
  16.3 2.2 %copy-start.1 = (bf16[1,1408]{1,0:T(2,128)(2,1)S(1)}, bf16[1,1408]{1,0:T(2,128)(2,1)}, u32[]{:S(2)}) copy-start(bf16[1,1408]{1,0:T(2,128)(2,1)} %bias_in.1) | copy-start | bytes 8452
  16.3 2.2 %copy-start.2 = (bf16[1,1408]{1,0:T(2,128)(2,1)S(1)}, bf16[1,1408]{1,0:T(2,128)(2,1)}, u32[]{:S(2)}) copy-start(bf16[1,1408]{1,0:T(2,128)(2,1)} %gamma.1) | copy-start | bytes 8452
  16.3 2.2 %copy-start.3 = (bf16[1,1408]{1,0:T(2,128)(2,1)S(1)}, bf16[1,1408]{1,0:T(2,128)(2,1)}, u32[]{:S(2)}) copy-start(bf16[1,1408]{1,0:T(2,128)(2,1)} %beta.1) | copy-start | bytes 8452
  17.1 1.5 %collective-permute-start.7 = (bf16[16,48,352]{2,1,0:T(8,128)(2,1)S(1)}, bf16[16,48,352]{2,1,0:T(8,128)(2,1)S(1)}, u32[]{:S(2)}, u32[]{:S(2)}) collective-permute-start(bf16[16,48,352]{2,1,0:T(8,128)(2,1)S(1)} %get-tuple-element.42), channel_id=1, source_target_pairs={{8,0},{9,1},{10,2},{11,3},{12,4},{13,5},{14,6},{15,7}} | collective-permute-start | bytes 1622024 | tf_op jit(solution)/shard_map/ppermute | solution.py:412
  17.8 3.0 %collective-permute-start.5 = (bf16[16,48,352]{2,1,0:T(8,128)(2,1)S(1)}, bf16[16,48,352]{2,1,0:T(8,128)(2,1)S(1)}, u32[]{:S(2)}, u32[]{:S(2)}) collective-permute-start(bf16[16,48,352]{2,1,0:T(8,128)(2,1)S(1)} %get-tuple-element.40), channel_id=1, source_target_pairs={{8,0},{9,1},{10,2},{11,3},{12,4},{13,5},{14,6},{15,7}} | collective-permute-start | bytes 1622024 | tf_op jit(solution)/shard_map/ppermute | solution.py:412
  18.7 2.2 %copy-start = (bf16[1,704,352]{2,1,0:T(8,128)(2,1)S(1)}, bf16[1,704,352]{2,1,0:T(8,128)(2,1)}, u32[]{:S(2)}) copy-start(bf16[1,704,352]{2,1,0:T(8,128)(2,1)} %param.20) | copy-start | bytes 1486852
  18.7 1.1 %copy-start.4 = (bf16[1,352,704]{2,1,0:T(8,128)(2,1)S(1)}, bf16[1,352,704]{2,1,0:T(8,128)(2,1)}, u32[]{:S(2)}) copy-start(bf16[1,352,704]{2,1,0:T(8,128)(2,1)} %param.16) | copy-start | bytes 1486852
  20.8 6.0 %collective-permute-start.8 = (bf16[16,48,352]{2,1,0:T(8,128)(2,1)S(1)}, bf16[16,48,352]{2,1,0:T(8,128)(2,1)S(1)}, u32[]{:S(2)}, u32[]{:S(2)}) collective-permute-start(bf16[16,48,352]{2,1,0:T(8,128)(2,1)S(1)} %down.1.prev.refs_4_), channel_id=1, source_target_pairs={{0,8},{1,9},{2,10},{3,11},{4,12},{5,13},{6,14},{7,15}} | collective-permute-start | bytes 1622024 | tf_op jit(solution)/shard_map/ppermute | solution.py:412
  21.5 10.1 %collective-permute-start.9 = (bf16[352,704]{1,0:T(8,128)(2,1)S(1)}, bf16[352,704]{1,0:T(8,128)(2,1)S(1)}, u32[]{:S(2)}, u32[]{:S(2)}) collective-permute-start(bf16[352,704]{1,0:T(8,128)(2,1)S(1)} %bitcast.27), channel_id=1, source_target_pairs={{8,9},{9,8},{24,25},{25,24},{10,11},{11,10},{26,27},{27,26},{12,13... | collective-permute-start | bytes 1486856 | tf_op jit(solution)/shard_map/ppermute | solution.py:393
  23.7 13.8 %collective-permute-start.10 = (bf16[704,352]{1,0:T(8,128)(2,1)S(1)}, bf16[704,352]{1,0:T(8,128)(2,1)S(1)}, u32[]{:S(2)}, u32[]{:S(2)}) collective-permute-start(bf16[704,352]{1,0:T(8,128)(2,1)S(1)} %bitcast.15), channel_id=1, source_target_pairs={{8,9},{9,8},{24,25},{25,24},{10,11},{11,10},{26,27},{27,26},{12,13... | collective-permute-start | bytes 1486856 | tf_op jit(solution)/shard_map/ppermute | solution.py:393
  37.5 2.8 %collective-permute-start.11 = (bf16[4,48,352]{2,1,0:T(8,128)(2,1)S(1)}, bf16[4,48,352]{2,1,0:T(8,128)(2,1)S(1)}, u32[]{:S(2)}, u32[]{:S(2)}) collective-permute-start(bf16[4,48,352]{2,1,0:T(8,128)(2,1)S(1)} %down_piece.8.refs_0_), channel_id=1, source_target_pairs={{8,16},{9,17},{10,18},{11,19},{12,20},{13,21},{14,22},{15,23}} | collective-permute-start | bytes 405512 | tf_op jit(solution)/shard_map/ppermute | solution.py:412
  38.2 2.1 %collective-permute-start.12 = (bf16[4,48,352]{2,1,0:T(8,128)(2,1)S(1)}, bf16[4,48,352]{2,1,0:T(8,128)(2,1)S(1)}, u32[]{:S(2)}, u32[]{:S(2)}) collective-permute-start(bf16[4,48,352]{2,1,0:T(8,128)(2,1)S(1)} %down_piece.9.refs_1_), channel_id=1, source_target_pairs={{8,16},{9,17},{10,18},{11,19},{12,20},{13,21},{14,22},{15,23}} | collective-permute-start | bytes 405512 | tf_op jit(solution)/shard_map/ppermute | solution.py:412
  38.9 1.5 %collective-permute-start.13 = (bf16[4,48,352]{2,1,0:T(8,128)(2,1)S(1)}, bf16[4,48,352]{2,1,0:T(8,128)(2,1)S(1)}, u32[]{:S(2)}, u32[]{:S(2)}) collective-permute-start(bf16[4,48,352]{2,1,0:T(8,128)(2,1)S(1)} %down_piece.10.refs_2_), channel_id=1, source_target_pairs={{8,16},{9,17},{10,18},{11,19},{12,20},{13,21},{14,22},{15,23}} | collective-permute-start | bytes 405512 | tf_op jit(solution)/shard_map/ppermute | solution.py:412
  39.6 0.8 collective-permute-start.14
  40.6 25.3 %collective-permute-start.15 = (bf16[16,48,352]{2,1,0:T(8,128)(2,1)S(1)}, bf16[16,48,352]{2,1,0:T(8,128)(2,1)S(1)}, u32[]{:S(2)}, u32[]{:S(2)}) collective-permute-start(bf16[16,48,352]{2,1,0:T(8,128)(2,1)S(1)} %mlp.1.prev), channel_id=1, source_target_pairs={{16,24},{17,25},{18,26},{19,27},{20,28},{21,29},{22,30},{23,31}} | collective-permute-start | bytes 1622024 | tf_op jit(solution)/shard_map/ppermute | solution.py:412
  74.5 7.0 %collective-permute-start.16 = (bf16[4,48,352]{2,1,0:T(8,128)(2,1)S(1)}, bf16[4,48,352]{2,1,0:T(8,128)(2,1)S(1)}, u32[]{:S(2)}, u32[]{:S(2)}) collective-permute-start(bf16[4,48,352]{2,1,0:T(8,128)(2,1)S(1)} %down_piece.13), channel_id=1, source_target_pairs={{0,4},{2,6},{4,0},{6,2},{1,5},{3,7},{5,1},{7,3},{8,12},{10,14},{12... | collective-permute-start | bytes 405512 | tf_op jit(solution)/shard_map/ppermute | solution.py:532
  77.9 6.0 %collective-permute-start.17 = (bf16[4,48,352]{2,1,0:T(8,128)(2,1)S(1)}, bf16[4,48,352]{2,1,0:T(8,128)(2,1)S(1)}, u32[]{:S(2)}, u32[]{:S(2)}) collective-permute-start(bf16[4,48,352]{2,1,0:T(8,128)(2,1)S(1)} %down_piece.14), channel_id=1, source_target_pairs={{0,6},{2,4},{4,2},{6,0},{1,7},{3,5},{5,3},{7,1},{8,14},{10,12},{12... | collective-permute-start | bytes 405512 | tf_op jit(solution)/shard_map/ppermute | solution.py:532
  79.5 5.6 %collective-permute-start.18 = (bf16[4,48,352]{2,1,0:T(8,128)(2,1)S(1)}, bf16[4,48,352]{2,1,0:T(8,128)(2,1)S(1)}, u32[]{:S(2)}, u32[]{:S(2)}) collective-permute-start(bf16[4,48,352]{2,1,0:T(8,128)(2,1)S(1)} %down_piece.15), channel_id=1, source_target_pairs={{0,2},{2,0},{4,6},{6,4},{1,3},{3,1},{5,7},{7,5},{8,10},{10,8},{12,... | collective-permute-start | bytes 405512 | tf_op jit(solution)/shard_map/ppermute | solution.py:532
  (2 other events, 1.8 us)

commit v9 on v7

--- a/solution.py
+++ b/solution.py
@@ -18,7 +18,7 @@
 VECTORS = 56
 
 
-def fill_columns(xp, xs, x, channels):
+def fill_columns(xp, xs, x, channels, first=0):
     height, reach_cols, blocks, lanes = xs.shape
     stride = reach_cols - 2 * REACH
     width = stride * blocks
@@ -28,7 +28,7 @@
     def rows(n, carry):
         for k in range(2):
             r = 2 * n + k
-            row = x[r].astype(jnp.float32)
+            row = x[first + r].astype(jnp.float32)
             for g in range(groups):
                 at = slice(g * LANES, (g + 1) * LANES)
                 own = row[:, g * LANES : min((g + 1) * LANES, channels)]
@@ -41,30 +41,31 @@
     lax.fori_loop(0, height // 2, rows, 0)
 
 
-def conv(xs, cpar, cq):
+def conv(xs, cpar, cq, above=0):
     rows = xs.shape[0]
     height, stride, blocks, lanes = cq.shape
     span = 2 * REACH + 1
-    above = (height - rows) // 2
 
     def group(g, carry):
         at = pl.ds(pl.multiple_of(g * LANES, LANES), LANES)
 
         def column(q, carry):
             bias = jnp.broadcast_to(cpar[VECTORS : VECTORS + 1, at], (blocks, LANES))
-            acc = [None if above else bias] * height
+            acc = [None if above > 0 else bias] * height
             for j in range(span):
                 kern = [
                     jnp.broadcast_to(cpar[i * span + j : i * span + j + 1, at], (blocks, LANES))
                     for i in range(span)
                 ]
                 for r in range(rows):
+                    taken = [i for i in range(span) if 0 <= r + above + REACH - i < height]
+                    if not taken:
+                        continue
                     x_row = xs[r, q + j, :, at]
-                    for i in range(span):
+                    for i in taken:
                         h = r + above + REACH - i
-                        if 0 <= h < height:
-                            term = kern[i] * x_row
-                            acc[h] = term if acc[h] is None else acc[h] + term
+                        term = kern[i] * x_row
+                        acc[h] = term if acc[h] is None else acc[h] + term
             for h in range(height):
                 cq[h, q, :, at] = acc[h]
             return carry
@@ -112,6 +113,14 @@
     norm(cq, cpar, xp, flat)
 
 
+def conv_norm_half(x, cpar, flat, xp, xs, cq, lower):
+    height = x.shape[0]
+    first = height - xs.shape[0] if lower else 0
+    fill_columns(xp, xs, x, x.shape[2], first)
+    conv(xs, cpar, cq, first - height // 2 if lower else 0)
+    norm(cq, cpar, xp, flat)
+
+
 def conv_scratch(rows, out_rows, width, lanes):
     return [
         pltpu.VMEM((NORM_ROWS * lanes // LANES, width + 16, LANES), jnp.float32),
@@ -163,7 +172,7 @@
 def down(x_rows, first_row, acts, outs, scale, fvec, cpar):
     _, width, channels = x_rows.shape
     cells = CHUNK * width
-    at = pl.ds(pl.multiple_of(first_row * width, cells), cells)
+    at = pl.ds(pl.multiple_of(first_row * width, 16), cells)
     update = cpar[VECTORS + 3 : VECTORS + 4, 0:channels]
     for which in range(2):
         a = acts[which][at, :].astype(jnp.float32)
@@ -215,7 +224,7 @@
     @pl.when(section[0] == on)
     def _():
         fill_columns(xp, xs, piece, piece.shape[2])
-        conv(xs, cpar, part)
+        conv(xs, cpar, part, REACH)
 
 
 def last_piece_kernel(section, me, *refs, order, on):
@@ -229,7 +238,7 @@
         bias = cpar[VECTORS : VECTORS + 1, :].reshape(1, 1, 1, cq.shape[3])
         cq[...] = jnp.broadcast_to(bias, cq.shape)
         fill_columns(xp, xs, pieces[-1], x.shape[2])
-        conv(xs, cpar, own)
+        conv(xs, cpar, own, REACH)
         for n, (piece, part) in enumerate(zip(pieces, (*parts, own))):
             at = block_of(me, order, n) * rows
             x[pl.ds(at, rows)] = piece[...]
@@ -263,14 +272,21 @@
 
 
 def down_piece_kernel(
-    section, me, x, act_a, act_b, out_a, out_b, scale, fvec, cpar, prev, out, *, order, tick, n
+    section, me, x, out_a, out_b, scale, fvec, cpar, prev, *refs, order, tick, n
 ):
-    first_row = block_of(me, order, n) * CHUNK
-    at = pl.ds(first_row, CHUNK)
-
-    @pl.when(section[0] == tick)
-    def _():
-        out[...] = down(x[at], first_row, (act_a, act_b), (out_a, out_b), scale, fvec, cpar)
+    *acts, out = refs
+    block = block_of(me, order, n)
+    at = pl.ds(block * CHUNK, CHUNK)
+    parts = len(acts) // 2
+    blocks = prev.shape[0] // CHUNK // parts
+
+    for part in range(parts):
+
+        @pl.when(jnp.logical_and(section[0] == tick, block // blocks == part))
+        def _():
+            first_row = (block - part * blocks) * CHUNK
+            pair = acts[2 * part : 2 * part + 2]
+            out[...] = down(x[at], first_row, pair, (out_a, out_b), scale, fvec, cpar)
 
     @pl.when(section[0] != tick)
     def _():
@@ -297,14 +313,31 @@
         out[...] = prev[...]
 
 
-def conv_up_kernel(section, x, cpar, in_a, in_b, fvec, *refs, tick):
-    act_a, act_b, scale, xp, xs, cq, flat, ssq_a, ssq_b = refs
+def conv_lower_kernel(section, x, cpar, flat, xp, xs, cq, *, on):
+    @pl.when(section[0] == on)
+    def _():
+        conv_norm_half(x, cpar, flat, xp, xs, cq, True)
+
+
+def conv_up_upper_kernel(section, x, cpar, in_a, in_b, fvec, *refs, tick):
+    act_a, act_b, ssq_a, ssq_b, xp, xs, cq, flat = refs
 
     @pl.when(section[0] == tick)
     def _():
-        conv_norm(x, cpar, flat, xp, xs, cq)
+        conv_norm_half(x, cpar, flat, xp, xs, cq, False)
         up(flat, in_a, fvec.at[0], act_a, ssq_a)
         up(flat, in_b, fvec.at[1], act_b, ssq_b)
+
+
+def up_lower_kernel(section, flat, in_a, in_b, fvec, upper_a, upper_b, *refs, tick):
+    act_a, act_b, scale, ssq_a, ssq_b = refs
+
+    @pl.when(section[0] == tick)
+    def _():
+        up(flat, in_a, fvec.at[0], act_a, ssq_a)
+        up(flat, in_b, fvec.at[1], act_b, ssq_b)
+        ssq_a[...] += upper_a[...]
+        ssq_b[...] += upper_b[...]
         norm_scale((ssq_a, ssq_b), fvec, scale)
 
 
@@ -384,12 +417,13 @@
     scale_shape = shape(2, 1, half)
     matmul = 2 * cells * channels * half
 
-    helper, source = 1, sections - 1
+    helper = 1
+    sources = {1: sections - 1, 2: sections - 1, 3: helper}
     pieces = []
     for by in order:
         piece = lax.dynamic_index_in_dim(inputs, me ^ by, 0, keepdims=False)[0]
         if by:
-            pairs = [(source * count + (p ^ by), helper * count + p) for p in range(count)]
+            pairs = [(sources[by] * count + (p ^ by), helper * count + p) for p in range(count)]
             piece = lax.ppermute(piece, ("section", "row"), pairs)
         pieces.append(piece)
 
@@ -466,12 +500,11 @@
             tick=tick,
         )
 
-    def down_piece(x, acts, other_out, prev, order, tick, n):
-        act_a, act_b, scale = acts
+    def down_piece(x, acts, scale, other_out, prev, order, tick, n):
         return call(
             down_piece_kernel,
             "down_piece",
-            (section, me_ref, x, act_a, act_b, w_out, other_out, scale, fvec, cpar, prev),
+            (section, me_ref, x, w_out, other_out, scale, fvec, cpar, prev, *acts),
             piece_shape,
             flops=2 * matmul // count,
             order=order,
@@ -479,7 +512,8 @@
             n=n,
         )
 
-    x, flat = conv_pieces(pieces, send(cpar, 0, helper), order, helper)
+    lent_cpar = lax.ppermute(cpar, "section", [(0, helper), (3, 2)])
+    x, flat = conv_pieces(pieces, lent_cpar, order, helper)
     flat, other_in = lax.optimization_barrier((flat, other_in))
     flat, x = send(flat, helper, 0), send(x, helper, 0)
     act_a, ssq = up_own(flat, 0)
@@ -504,8 +538,8 @@
         tick=1,
     )
     act_a, ssq = up_own(flat, 1)
-    acts = (act_a, *up_other(flat, odd_in, ssq, 1))
-    kept = [down_piece(x, acts, odd_out, result, None, 1, n) for n in range(count)]
+    act_b, scale = up_other(flat, odd_in, ssq, 1)
+    kept = [down_piece(x, (act_a, act_b), scale, odd_out, result, None, 1, n) for n in range(count)]
     x, flat = conv_pieces([send(piece, 1, 2) for piece in kept], cpar, None, 2)
     result = call(
         mlp_kernel,
@@ -519,20 +553,40 @@
         tick=2,
     )
     x = send(result, 2, 3)
-    acts = call(
-        conv_up_kernel,
-        "conv_up",
+    half_map = shape(height // 2, width, channels, dtype=bf16)
+    half_act = shape(cells // 2, half, dtype=bf16)
+    half_scratch = conv_scratch(height // 2 + 4, height // 2, width, lanes)
+    lower = call(
+        conv_lower_kernel,
+        "conv_lower",
+        (section, result, lent_cpar),
+        half_map,
+        scratch=half_scratch,
+        on=2,
+    )
+    lower = send(lower, 2, 3)
+    upper_a, upper_b, ssq_a, ssq_b = call(
+        conv_up_upper_kernel,
+        "conv_up_upper",
         (section, x, cpar, w_in, odd_in, fvec),
-        (act_shape, act_shape, scale_shape),
-        scratch=conv_scratch(height, height, width, lanes)
-        + [pltpu.VMEM((height, width, channels), bf16)]
-        + [ssq_scratch(half)] * 2,
-        flops=2 * matmul,
+        (half_act, half_act, shape(8, half), shape(8, half)),
+        scratch=half_scratch + [pltpu.VMEM((height // 2, width, channels), bf16)],
+        flops=matmul,
         tick=3,
     )
+    lower_a, lower_b, scale = call(
+        up_lower_kernel,
+        "up_lower",
+        (section, lower, w_in, odd_in, fvec, ssq_a, ssq_b),
+        (half_act, half_act, scale_shape),
+        scratch=[ssq_scratch(half)] * 2,
+        flops=matmul,
+        tick=3,
+    )
+    acts = (upper_a, upper_b, lower_a, lower_b)
     done = []
     for n in (1, 2, 3, 0):
-        piece = down_piece(x, acts, odd_out, result, order, 3, n)
+        piece = down_piece(x, acts, scale, odd_out, result, order, 3, n)
         if n:
             piece = lax.ppermute(piece, "row", [(p, p ^ order[n]) for p in range(count)])
         done.append(piece)

time: 81.5 us -> 82.1 us (level)
  Pallas kernels: 11.6 us -> 10.1 us
  waiting for transfers between devices: 41.9 us -> 42.9 us
    ppermute x3, waiting for transfers between devices: 1.85 us -> 0.01 us  [image_plan(): piece = lax.ppermute(piece, ('section', 'row'), pairs)]
    pallas_call x26 -> x28, Pallas kernels: 11.6 us -> 10.1 us  [call(): pl.pallas_call(functools.partial(kernel, **static), out_shape=out, in_spe...]
    ppermute x3, waiting for transfers between devices: 5.05 us -> 6.49 us  [image_plan(): lax.ppermute(piece, 'row', [(p, p ^ order[n]) for p in range(count)])]
    ppermute x0 -> x1, starting transfers between devices: none -> 1.3 us  [image_plan(): lent_cpar = lax.ppermute(cpar, 'section', [(0, helper), (3, 2)])]
    ppermute x3, starting transfers between devices: 4.12 us -> 2.85 us  [image_plan(): lax.ppermute(piece, 'row', [(p, p ^ order[n]) for p in range(count)])]
    ppermute x4, waiting for transfers between devices: 14.6 us -> 15.7 us  [other_half(): return lax.ppermute(x, ('section', 'dp'), pairs)]
    ppermute x0 -> x1, waiting for transfers between devices: none -> 0.92 us  [image_plan(): lent_cpar = lax.ppermute(cpar, 'section', [(0, helper), (3, 2)])]
  transfers between devices with their start and end apart: 19 -> 20, of which waited for: 7 -> 6; matrix products, arithmetic and copies ran while one was open for 1% -> 1% of each run, Pallas kernels for 2% -> 8%
where the time goes in v9:
time: 82.1 us; the launch traced here: 81 us
  waiting for transfers between devices  42.9 us (52%)
  starting transfers between devices  26.1 us (32%)
  Pallas kernels  10.1 us (12%)
  local copies, waits for them, and re-layouts  1.24 us (2%)
    ppermute x9, waiting for transfers between devices, send(): return lax.ppermute(x, 'section', [(start, end)])  19.8 us
    ppermute x4, waiting for transfers between devices, other_half(): return lax.ppermute(x, ('section', 'dp'), pairs)  15.7 us
    pallas_call x28, Pallas kernels, call(): pl.pallas_call(functools.partial(kernel, **static), out_shape=out, in_spe...  10.1 us
    ppermute x3, starting transfers between devices, image_plan(): piece = lax.ppermute(piece, ('section', 'row'), pairs)  7.68 us
    ppermute x9, starting transfers between devices, send(): return lax.ppermute(x, 'section', [(start, end)])  7.49 us
    ppermute x4, starting transfers between devices, other_half(): return lax.ppermute(x, ('section', 'dp'), pairs)  6.8 us
    ppermute x3, waiting for transfers between devices, image_plan(): lax.ppermute(piece, 'row', [(p, p ^ order[n]) for p in range(count)])  6.49 us
    ppermute x3, starting transfers between devices, image_plan(): lax.ppermute(piece, 'row', [(p, p ^ order[n]) for p in range(count)])  2.85 us
  transfers between devices with their start and end apart: 20, of which 6 were waited for; matrix products, arithmetic and copies ran while one was open for 1% of the time, Pallas kernels for 8%

profile of v9, /device:TPU:7, one launch (start us, length us, event | category | flops | bytes accessed | tf_op | source)
XLA Modules:
  0.0 81.0 jit_solution(6886048992136637167)
XLA Ops:
  0.1 0.8 %collective-permute-start.5 = (bf16[352,704]{1,0:T(8,128)(2,1)}, bf16[352,704]{1,0:T(8,128)(2,1)S(1)}, u32[]{:S(2)}, u32[]{:S(2)}) collective-permute-start(bf16[352,704]{1,0:T(8,128)(2,1)} %bitcast.25), channel_id=1, source_target_pairs={{0,1},{1,0},{16,17},{17,16},{2,3},{3,2},{18,19},{19,18},{4,5},{5,4... | collective-permute-start | bytes 1486856 | tf_op jit(solution)/shard_map/ppermute | solution.py:432
  0.9 1.2 %dynamic-slice_bitcast_fusion = (bf16[4,48,352]{2,1,0:T(8,128)(2,1)S(1)}, bf16[4,48,352]{2,1,0:T(8,128)(2,1)S(1)}, bf16[4,48,352]{2,1,0:T(8,128)(2,1)S(1)}, bf16[4,48,352]{2,1,0:T(8,128)(2,1)S(1)}) fusion(bf16[4,1,4,48,352]{4,3,2,1,0:T(8,128)(2,1)} %param.11, s32[]{:T(128)S(6)} %select_n.16, s32[]{:T(128)S(6)} %select_n.14, s32[]{:T(128)S(6)} %select_n.13, ...), kind=kLoop, calls=%fused_computation | loop fusion | bytes 1081360 | tf_op jit(solution)/shard_map/squeeze | solution.py:424
  2.1 4.2 %collective-permute-start = (bf16[4,48,352]{2,1,0:T(8,128)(2,1)S(1)}, bf16[4,48,352]{2,1,0:T(8,128)(2,1)S(1)}, u32[]{:S(2)}, u32[]{:S(2)}) collective-permute-start(bf16[4,48,352]{2,1,0:T(8,128)(2,1)S(1)} %get-tuple-element.74), channel_id=1, source_target_pairs={{28,8},{30,10},{24,12},{26,14},{29,9},{31,11},{25,13},{27,15}} | collective-permute-start | bytes 405512 | tf_op jit(solution)/shard_map/ppermute | solution.py:427
  6.3 0.7 collective-permute-start.1
  7.0 2.8 %collective-permute-start.2 = (bf16[4,48,352]{2,1,0:T(8,128)(2,1)S(1)}, bf16[4,48,352]{2,1,0:T(8,128)(2,1)S(1)}, u32[]{:S(2)}, u32[]{:S(2)}) collective-permute-start(bf16[4,48,352]{2,1,0:T(8,128)(2,1)S(1)} %get-tuple-element.73), channel_id=1, source_target_pairs={{26,8},{24,10},{30,12},{28,14},{27,9},{25,11},{31,13},{29,15}} | collective-permute-start | bytes 405512 | tf_op jit(solution)/shard_map/ppermute | solution.py:427
  10.2 1.3 %collective-permute-start.3 = (f32[64,384]{1,0:T(8,128)S(1)}, f32[64,384]{1,0:T(8,128)S(1)}, u32[]{:S(2)}, u32[]{:S(2)}) collective-permute-start(f32[64,384]{1,0:T(8,128)S(1)} %get-tuple-element.39.cpar.refs_7_), channel_id=1, source_target_pairs={{0,8},{24,16},{1,9},{25,17},{2,10},{26,18},{3,11},{27,19},{4,12},{... | collective-permute-start | bytes 294920 | tf_op jit(solution)/shard_map/ppermute | solution.py:515
  11.5 0.9 %collective-permute-done.3.cpar.refs_7_ = f32[64,384]{1,0:T(8,128)S(1)} collective-permute-done((f32[64,384]{1,0:T(8,128)S(1)}, f32[64,384]{1,0:T(8,128)S(1)}, u32[]{:S(2)}, u32[]{:S(2)}) %collective-permute-start.3) | collective-permute-done | bytes 98336 | tf_op jit(solution)/shard_map/ppermute | solution.py:515
  12.5 0.8 %collective-permute-start.6 = (bf16[16,48,352]{2,1,0:T(8,128)(2,1)S(1)}, bf16[16,48,352]{2,1,0:T(8,128)(2,1)S(1)}, u32[]{:S(2)}, u32[]{:S(2)}) collective-permute-start(bf16[16,48,352]{2,1,0:T(8,128)(2,1)S(1)} %get-tuple-element.46), channel_id=1, source_target_pairs={{8,0},{9,1},{10,2},{11,3},{12,4},{13,5},{14,6},{15,7}} | collective-permute-start | bytes 1622024 | tf_op jit(solution)/shard_map/ppermute | solution.py:454
  13.3 0.7 collective-permute-start.4
  14.0 0.7 collective-permute-start.7
  14.8 0.7 collective-permute-start.8
  15.5 2.1 %collective-permute-start.10 = (bf16[352,704]{1,0:T(8,128)(2,1)S(1)}, bf16[352,704]{1,0:T(8,128)(2,1)S(1)}, u32[]{:S(2)}, u32[]{:S(2)}) collective-permute-start(bf16[352,704]{1,0:T(8,128)(2,1)S(1)} %bitcast.27), channel_id=1, source_target_pairs={{8,9},{9,8},{24,25},{25,24},{10,11},{11,10},{26,27},{27,26},{12,13... | collective-permute-start | bytes 1486856 | tf_op jit(solution)/shard_map/ppermute | solution.py:432
  17.7 3.1 %collective-permute-start.9 = (bf16[704,352]{1,0:T(8,128)(2,1)S(1)}, bf16[704,352]{1,0:T(8,128)(2,1)S(1)}, u32[]{:S(2)}, u32[]{:S(2)}) collective-permute-start(bf16[704,352]{1,0:T(8,128)(2,1)S(1)} %bitcast.15), channel_id=1, source_target_pairs={{8,9},{9,8},{24,25},{25,24},{10,11},{11,10},{26,27},{27,26},{12,13... | collective-permute-start | bytes 1486856 | tf_op jit(solution)/shard_map/ppermute | solution.py:432
  20.9 9.9 %collective-permute-done.10.w_in.in_b = bf16[352,704]{1,0:T(8,128)(2,1)S(1)} collective-permute-done((bf16[352,704]{1,0:T(8,128)(2,1)S(1)}, bf16[352,704]{1,0:T(8,128)(2,1)S(1)}, u32[]{:S(2)}, u32[]{:S(2)}) %collective-permute-start.10) | collective-permute-done | bytes 495648 | tf_op jit(solution)/shard_map/ppermute | solution.py:432
  30.7 5.8 %collective-permute-done.9.out_b = bf16[704,352]{1,0:T(8,128)(2,1)S(1)} collective-permute-done((bf16[704,352]{1,0:T(8,128)(2,1)S(1)}, bf16[704,352]{1,0:T(8,128)(2,1)S(1)}, u32[]{:S(2)}, u32[]{:S(2)}) %collective-permute-start.9) | collective-permute-done | bytes 495648 | tf_op jit(solution)/shard_map/ppermute | solution.py:432
  39.7 1.3 %collective-permute-start.15 = (bf16[16,48,352]{2,1,0:T(8,128)(2,1)S(1)}, bf16[16,48,352]{2,1,0:T(8,128)(2,1)S(1)}, u32[]{:S(2)}, u32[]{:S(2)}) collective-permute-start(bf16[16,48,352]{2,1,0:T(8,128)(2,1)S(1)} %mlp.1.x.prev), channel_id=1, source_target_pairs={{16,24},{17,25},{18,26},{19,27},{20,28},{21,29},{22,30},{23,31}} | collective-permute-start | bytes 1622024 | tf_op jit(solution)/shard_map/ppermute | solution.py:454
  41.0 1.3 %collective-permute-start.16 = (bf16[8,48,352]{2,1,0:T(8,128)(2,1)S(1)}, bf16[8,48,352]{2,1,0:T(8,128)(2,1)S(1)}, u32[]{:S(2)}, u32[]{:S(2)}) collective-permute-start(bf16[8,48,352]{2,1,0:T(8,128)(2,1)S(1)} %conv_lower.1), channel_id=1, source_target_pairs={{16,24},{17,25},{18,26},{19,27},{20,28},{21,29},{22,30},{23,31}} | collective-permute-start | bytes 811016 | tf_op jit(solution)/shard_map/ppermute | solution.py:454
  42.3 19.8 %collective-permute-done.15.x = bf16[16,48,352]{2,1,0:T(8,128)(2,1)S(1)} collective-permute-done((bf16[16,48,352]{2,1,0:T(8,128)(2,1)S(1)}, bf16[16,48,352]{2,1,0:T(8,128)(2,1)S(1)}, u32[]{:S(2)}, u32[]{:S(2)}) %collective-permute-start.15) | collective-permute-done | bytes 540704 | tf_op jit(solution)/shard_map/ppermute | solution.py:454
  62.1 4.6 %conv_up_upper.1 = (bf16[384,704]{1,0:T(8,128)(2,1)S(1)}, bf16[384,704]{1,0:T(8,128)(2,1)S(1)}, f32[8,704]{1,0:T(8,128)S(1)}, f32[8,704]{1,0:T(8,128)S(1)}) custom-call(s32[1]{0:T(128)} %bitcast.1.section, bf16[16,48,352]{2,1,0:T(8,128)(2,1)S(1)} %collective-permute-done.15.x, f32[64,384]{1,0:T(8,128)S(1)} %get-tuple-element.39.cpar.refs_7_, ...), custom_call_target="tpu_custom_call" | custom-call | flops 380633088 | bytes 1647108 | tf_op jit(solution)/shard_map/conv_up_upper/pallas_call | solution.py:367
  66.7 1.9 %up_lower.1 = (bf16[384,704]{1,0:T(8,128)(2,1)S(1)}, bf16[384,704]{1,0:T(8,128)(2,1)S(1)}, f32[2,1,704]{2,1,0:T(1,128)S(1)}) custom-call(s32[1]{0:T(128)} %bitcast.1.section, bf16[8,48,352]{2,1,0:T(8,128)(2,1)S(1)} %collective-permute-done.16.flat, bf16[352,704]{1,0:T(8,128)(2,1)S(1)} %bitcast.31, bf16[352,704]{1,0:T(8,128)(2,1)S(1)} %collective-permute-done.10.w_in.in_b, ...), custom_call_target="tpu_custom_call" | custom-call | flops 380633088 | bytes 1323524 | tf_op jit(solution)/shard_map/up_lower/pallas_call | solution.py:367
  69.9 1.3 %collective-permute-start.18 = (bf16[4,48,352]{2,1,0:T(8,128)(2,1)S(1)}, bf16[4,48,352]{2,1,0:T(8,128)(2,1)S(1)}, u32[]{:S(2)}, u32[]{:S(2)}) collective-permute-start(bf16[4,48,352]{2,1,0:T(8,128)(2,1)S(1)} %down_piece.14), channel_id=1, source_target_pairs={{0,6},{2,4},{4,2},{6,0},{1,7},{3,5},{5,3},{7,1},{8,14},{10,12},{12... | collective-permute-start | bytes 405512 | tf_op jit(solution)/shard_map/ppermute | solution.py:591
  71.7 1.4 %collective-permute-start.19 = (bf16[4,48,352]{2,1,0:T(8,128)(2,1)S(1)}, bf16[4,48,352]{2,1,0:T(8,128)(2,1)S(1)}, u32[]{:S(2)}, u32[]{:S(2)}) collective-permute-start(bf16[4,48,352]{2,1,0:T(8,128)(2,1)S(1)} %down_piece.15), channel_id=1, source_target_pairs={{0,2},{2,0},{4,6},{6,4},{1,3},{3,1},{5,7},{7,5},{8,10},{10,8},{12,... | collective-permute-start | bytes 405512 | tf_op jit(solution)/shard_map/ppermute | solution.py:591
  73.6 5.9 %collective-permute-done.17.refs_1_ = bf16[4,48,352]{2,1,0:T(8,128)(2,1)S(1)} collective-permute-done((bf16[4,48,352]{2,1,0:T(8,128)(2,1)S(1)}, bf16[4,48,352]{2,1,0:T(8,128)(2,1)S(1)}, u32[]{:S(2)}, u32[]{:S(2)}) %collective-permute-start.17) | collective-permute-done | bytes 135200 | tf_op jit(solution)/shard_map/ppermute | solution.py:591
  80.0 0.8 %place.1 = bf16[1,4,1,4,48,352]{5,4,3,2,1,0:T(8,128)(2,1)} custom-call(s32[1]{0:T(128)} %bitcast.me, bf16[4,48,352]{2,1,0:T(8,128)(2,1)S(1)} %down_piece.12.refs_0_, bf16[4,48,352]{2,1,0:T(8,128)(2,1)S(1)} %collective-permute-done.17.refs_1_, bf16[4,48,352]{2,1,0:T(8,128)(2,1)S(1)} %collective-permute-done.18.refs_2_, ...), custom_call_target="tpu_custom_call" | custom-call | bytes 540676 | tf_op jit(solution)/shard_map/place/pallas_call | solution.py:367
  (65 shorter events, 6.2 us)
Async XLA Ops:
  0.0 9.8 %copy-start.3 = (bf16[1,1408]{1,0:T(2,128)(2,1)S(1)}, bf16[1,1408]{1,0:T(2,128)(2,1)}, u32[]{:S(2)}) copy-start(bf16[1,1408]{1,0:T(2,128)(2,1)} %refs_4_.1) | copy-start | bytes 8452
  0.0 9.8 %copy-start.8 = (bf16[1,352]{1,0:T(2,128)(2,1)S(1)}, bf16[1,352]{1,0:T(2,128)(2,1)}, u32[]{:S(2)}) copy-start(bf16[1,352]{1,0:T(2,128)(2,1)} %refs_2_.1) | copy-start | bytes 2116
  0.0 9.8 %copy-start.7 = (bf16[1,352]{1,0:T(2,128)(2,1)S(1)}, bf16[1,352]{1,0:T(2,128)(2,1)}, u32[]{:S(2)}) copy-start(bf16[1,352]{1,0:T(2,128)(2,1)} %refs_1_.1) | copy-start | bytes 2116
  0.0 9.8 %copy-start.6 = (bf16[1,352]{1,0:T(2,128)(2,1)S(1)}, bf16[1,352]{1,0:T(2,128)(2,1)}, u32[]{:S(2)}) copy-start(bf16[1,352]{1,0:T(2,128)(2,1)} %refs_0_.1) | copy-start | bytes 2116
  0.1 12.4 %collective-permute-start.5 = (bf16[352,704]{1,0:T(8,128)(2,1)}, bf16[352,704]{1,0:T(8,128)(2,1)S(1)}, u32[]{:S(2)}, u32[]{:S(2)}) collective-permute-start(bf16[352,704]{1,0:T(8,128)(2,1)} %bitcast.25), channel_id=1, source_target_pairs={{0,1},{1,0},{16,17},{17,16},{2,3},{3,2},{18,19},{19,18},{4,5},{5,4... | collective-permute-start | bytes 1486856 | tf_op jit(solution)/shard_map/ppermute | solution.py:432
  2.1 10.3 %collective-permute-start = (bf16[4,48,352]{2,1,0:T(8,128)(2,1)S(1)}, bf16[4,48,352]{2,1,0:T(8,128)(2,1)S(1)}, u32[]{:S(2)}, u32[]{:S(2)}) collective-permute-start(bf16[4,48,352]{2,1,0:T(8,128)(2,1)S(1)} %get-tuple-element.74), channel_id=1, source_target_pairs={{28,8},{30,10},{24,12},{26,14},{29,9},{31,11},{25,13},{27,15}} | collective-permute-start | bytes 405512 | tf_op jit(solution)/shard_map/ppermute | solution.py:427
  6.3 6.1 %collective-permute-start.1 = (bf16[4,48,352]{2,1,0:T(8,128)(2,1)S(1)}, bf16[4,48,352]{2,1,0:T(8,128)(2,1)S(1)}, u32[]{:S(2)}, u32[]{:S(2)}) collective-permute-start(bf16[4,48,352]{2,1,0:T(8,128)(2,1)S(1)} %get-tuple-element.76), channel_id=1, source_target_pairs={{14,8},{12,10},{10,12},{8,14},{15,9},{13,11},{11,13},{9,15}} | collective-permute-start | bytes 405512 | tf_op jit(solution)/shard_map/ppermute | solution.py:427
  7.0 5.4 %collective-permute-start.2 = (bf16[4,48,352]{2,1,0:T(8,128)(2,1)S(1)}, bf16[4,48,352]{2,1,0:T(8,128)(2,1)S(1)}, u32[]{:S(2)}, u32[]{:S(2)}) collective-permute-start(bf16[4,48,352]{2,1,0:T(8,128)(2,1)S(1)} %get-tuple-element.73), channel_id=1, source_target_pairs={{26,8},{24,10},{30,12},{28,14},{27,9},{25,11},{31,13},{29,15}} | collective-permute-start | bytes 405512 | tf_op jit(solution)/shard_map/ppermute | solution.py:427
  10.2 2.2 %collective-permute-start.3 = (f32[64,384]{1,0:T(8,128)S(1)}, f32[64,384]{1,0:T(8,128)S(1)}, u32[]{:S(2)}, u32[]{:S(2)}) collective-permute-start(f32[64,384]{1,0:T(8,128)S(1)} %get-tuple-element.39.cpar.refs_7_), channel_id=1, source_target_pairs={{0,8},{24,16},{1,9},{25,17},{2,10},{26,18},{3,11},{27,19},{4,12},{... | collective-permute-start | bytes 294920 | tf_op jit(solution)/shard_map/ppermute | solution.py:515
  12.5 2.3 %collective-permute-start.6 = (bf16[16,48,352]{2,1,0:T(8,128)(2,1)S(1)}, bf16[16,48,352]{2,1,0:T(8,128)(2,1)S(1)}, u32[]{:S(2)}, u32[]{:S(2)}) collective-permute-start(bf16[16,48,352]{2,1,0:T(8,128)(2,1)S(1)} %get-tuple-element.46), channel_id=1, source_target_pairs={{8,0},{9,1},{10,2},{11,3},{12,4},{13,5},{14,6},{15,7}} | collective-permute-start | bytes 1622024 | tf_op jit(solution)/shard_map/ppermute | solution.py:454
  13.3 1.5 %collective-permute-start.4 = (bf16[16,48,352]{2,1,0:T(8,128)(2,1)S(1)}, bf16[16,48,352]{2,1,0:T(8,128)(2,1)S(1)}, u32[]{:S(2)}, u32[]{:S(2)}) collective-permute-start(bf16[16,48,352]{2,1,0:T(8,128)(2,1)S(1)} %get-tuple-element.44), channel_id=1, source_target_pairs={{8,0},{9,1},{10,2},{11,3},{12,4},{13,5},{14,6},{15,7}} | collective-permute-start | bytes 1622024 | tf_op jit(solution)/shard_map/ppermute | solution.py:454
  14.0 0.8 collective-permute-start.7
  14.8 6.0 %collective-permute-start.8 = (bf16[16,48,352]{2,1,0:T(8,128)(2,1)S(1)}, bf16[16,48,352]{2,1,0:T(8,128)(2,1)S(1)}, u32[]{:S(2)}, u32[]{:S(2)}) collective-permute-start(bf16[16,48,352]{2,1,0:T(8,128)(2,1)S(1)} %down.1.prev.refs_4_), channel_id=1, source_target_pairs={{0,8},{1,9},{2,10},{3,11},{4,12},{5,13},{6,14},{7,15}} | collective-permute-start | bytes 1622024 | tf_op jit(solution)/shard_map/ppermute | solution.py:454
  15.5 15.2 %collective-permute-start.10 = (bf16[352,704]{1,0:T(8,128)(2,1)S(1)}, bf16[352,704]{1,0:T(8,128)(2,1)S(1)}, u32[]{:S(2)}, u32[]{:S(2)}) collective-permute-start(bf16[352,704]{1,0:T(8,128)(2,1)S(1)} %bitcast.27), channel_id=1, source_target_pairs={{8,9},{9,8},{24,25},{25,24},{10,11},{11,10},{26,27},{27,26},{12,13... | collective-permute-start | bytes 1486856 | tf_op jit(solution)/shard_map/ppermute | solution.py:432
  17.7 18.9 %collective-permute-start.9 = (bf16[704,352]{1,0:T(8,128)(2,1)S(1)}, bf16[704,352]{1,0:T(8,128)(2,1)S(1)}, u32[]{:S(2)}, u32[]{:S(2)}) collective-permute-start(bf16[704,352]{1,0:T(8,128)(2,1)S(1)} %bitcast.15), channel_id=1, source_target_pairs={{8,9},{9,8},{24,25},{25,24},{10,11},{11,10},{26,27},{27,26},{12,13... | collective-permute-start | bytes 1486856 | tf_op jit(solution)/shard_map/ppermute | solution.py:432
  36.6 2.8 %collective-permute-start.11 = (bf16[4,48,352]{2,1,0:T(8,128)(2,1)S(1)}, bf16[4,48,352]{2,1,0:T(8,128)(2,1)S(1)}, u32[]{:S(2)}, u32[]{:S(2)}) collective-permute-start(bf16[4,48,352]{2,1,0:T(8,128)(2,1)S(1)} %down_piece.8.refs_0_), channel_id=1, source_target_pairs={{8,16},{9,17},{10,18},{11,19},{12,20},{13,21},{14,22},{15,23}} | collective-permute-start | bytes 405512 | tf_op jit(solution)/shard_map/ppermute | solution.py:454
  37.3 2.1 %collective-permute-start.12 = (bf16[4,48,352]{2,1,0:T(8,128)(2,1)S(1)}, bf16[4,48,352]{2,1,0:T(8,128)(2,1)S(1)}, u32[]{:S(2)}, u32[]{:S(2)}) collective-permute-start(bf16[4,48,352]{2,1,0:T(8,128)(2,1)S(1)} %down_piece.9.refs_1_), channel_id=1, source_target_pairs={{8,16},{9,17},{10,18},{11,19},{12,20},{13,21},{14,22},{15,23}} | collective-permute-start | bytes 405512 | tf_op jit(solution)/shard_map/ppermute | solution.py:454
  38.0 1.5 %collective-permute-start.13 = (bf16[4,48,352]{2,1,0:T(8,128)(2,1)S(1)}, bf16[4,48,352]{2,1,0:T(8,128)(2,1)S(1)}, u32[]{:S(2)}, u32[]{:S(2)}) collective-permute-start(bf16[4,48,352]{2,1,0:T(8,128)(2,1)S(1)} %down_piece.10.refs_2_), channel_id=1, source_target_pairs={{8,16},{9,17},{10,18},{11,19},{12,20},{13,21},{14,22},{15,23}} | collective-permute-start | bytes 405512 | tf_op jit(solution)/shard_map/ppermute | solution.py:454
  38.7 0.8 collective-permute-start.14
  39.7 22.4 %collective-permute-start.15 = (bf16[16,48,352]{2,1,0:T(8,128)(2,1)S(1)}, bf16[16,48,352]{2,1,0:T(8,128)(2,1)S(1)}, u32[]{:S(2)}, u32[]{:S(2)}) collective-permute-start(bf16[16,48,352]{2,1,0:T(8,128)(2,1)S(1)} %mlp.1.x.prev), channel_id=1, source_target_pairs={{16,24},{17,25},{18,26},{19,27},{20,28},{21,29},{22,30},{23,31}} | collective-permute-start | bytes 1622024 | tf_op jit(solution)/shard_map/ppermute | solution.py:454
  41.0 25.7 %collective-permute-start.16 = (bf16[8,48,352]{2,1,0:T(8,128)(2,1)S(1)}, bf16[8,48,352]{2,1,0:T(8,128)(2,1)S(1)}, u32[]{:S(2)}, u32[]{:S(2)}) collective-permute-start(bf16[8,48,352]{2,1,0:T(8,128)(2,1)S(1)} %conv_lower.1), channel_id=1, source_target_pairs={{16,24},{17,25},{18,26},{19,27},{20,28},{21,29},{22,30},{23,31}} | collective-permute-start | bytes 811016 | tf_op jit(solution)/shard_map/ppermute | solution.py:454
  69.2 10.3 %collective-permute-start.17 = (bf16[4,48,352]{2,1,0:T(8,128)(2,1)S(1)}, bf16[4,48,352]{2,1,0:T(8,128)(2,1)S(1)}, u32[]{:S(2)}, u32[]{:S(2)}) collective-permute-start(bf16[4,48,352]{2,1,0:T(8,128)(2,1)S(1)} %down_piece.13), channel_id=1, source_target_pairs={{0,4},{2,6},{4,0},{6,2},{1,5},{3,7},{5,1},{7,3},{8,12},{10,14},{12... | collective-permute-start | bytes 405512 | tf_op jit(solution)/shard_map/ppermute | solution.py:591
  69.9 9.5 %collective-permute-start.18 = (bf16[4,48,352]{2,1,0:T(8,128)(2,1)S(1)}, bf16[4,48,352]{2,1,0:T(8,128)(2,1)S(1)}, u32[]{:S(2)}, u32[]{:S(2)}) collective-permute-start(bf16[4,48,352]{2,1,0:T(8,128)(2,1)S(1)} %down_piece.14), channel_id=1, source_target_pairs={{0,6},{2,4},{4,2},{6,0},{1,7},{3,5},{5,3},{7,1},{8,14},{10,12},{12... | collective-permute-start | bytes 405512 | tf_op jit(solution)/shard_map/ppermute | solution.py:591
  71.7 8.3 %collective-permute-start.19 = (bf16[4,48,352]{2,1,0:T(8,128)(2,1)S(1)}, bf16[4,48,352]{2,1,0:T(8,128)(2,1)S(1)}, u32[]{:S(2)}, u32[]{:S(2)}) collective-permute-start(bf16[4,48,352]{2,1,0:T(8,128)(2,1)S(1)} %down_piece.15), channel_id=1, source_target_pairs={{0,2},{2,0},{4,6},{6,4},{1,3},{3,1},{5,7},{7,5},{8,10},{10,8},{12,... | collective-permute-start | bytes 405512 | tf_op jit(solution)/shard_map/ppermute | solution.py:591
  (6 other events, 43.2 us)

commit v10 on v5

--- a/solution.py
+++ b/solution.py
@@ -221,7 +221,8 @@
 def last_piece_kernel(section, me, *refs, order, on):
     count = len(order or IN_ORDER)
     pieces, parts = refs[:count], refs[count : 2 * count - 1]
-    cpar, x, flat, xp, xs, own, cq = refs[2 * count - 1 :]
+    cpar, both, xp, xs, own, cq = refs[2 * count - 1 :]
+    x, flat = both.at[0], both.at[1]
     rows = pieces[0].shape[0]
 
     @pl.when(section[0] == on)
@@ -243,23 +244,27 @@
         conv_norm(x, cpar, flat, xp, xs, cq)
 
 
+def normed_part(ref):
+    return ref if len(ref.shape) == 3 else ref.at[1]
+
+
 def up_first_kernel(section, flat, w_in, fvec, act, ssq, *, tick):
     @pl.when(section[0] == tick)
     def _():
-        up(flat, w_in, fvec.at[0], act, ssq)
+        up(normed_part(flat), w_in, fvec.at[0], act, ssq)
 
 
 def up_second_kernel(section, flat, w_in, fvec, other, act, scale, ssq, *, tick):
     @pl.when(section[0] == tick)
     def _():
-        up(flat, w_in, fvec.at[1], act, ssq)
+        up(normed_part(flat), w_in, fvec.at[1], act, ssq)
         norm_scale((other, ssq), fvec, scale)
 
 
-def first_down_kernel(section, x, act_a, act_b, out_a, out_b, scale, fvec, cpar, out):
+def first_down_kernel(section, both, act_a, act_b, out_a, out_b, scale, fvec, cpar, out):
     @pl.when(section[0] == 0)
     def _():
-        down_all(x, (act_a, act_b), (out_a, out_b), scale, fvec, cpar, out)
+        down_all(both.at[0], (act_a, act_b), (out_a, out_b), scale, fvec, cpar, out)
 
 
 def down_piece_kernel(
@@ -277,8 +282,9 @@
         out[...] = prev[at]
 
 
-def mlp_kernel(section, x, flat, in_a, in_b, out_a, out_b, fvec, cpar, *refs, tick):
+def mlp_kernel(section, both, in_a, in_b, out_a, out_b, fvec, cpar, *refs, tick):
     *pieces, prev, out, act_a, act_b, ssq_a, ssq_b, scale = refs
+    x, flat = both.at[0], both.at[1]
 
     @pl.when(section[0] == tick)
     def _():
@@ -439,7 +445,7 @@
             last_piece_kernel,
             "last_piece",
             (section, me_ref, *pieces, *parts, cpar),
-            (whole, whole),
+            shape(2, height, width, channels, dtype=bf16),
             scratch=scratch + [conv_scratch(1, height + 2 * REACH, width, lanes)[2]],
             order=order,
             on=on,
@@ -479,14 +485,15 @@
             n=n,
         )
 
-    x, flat = conv_pieces(pieces, send(cpar, 0, helper), order, helper)
-    flat, x = send(flat, helper, 0), send(x, helper, 0)
-    act_a, ssq = up_own(flat, 0)
-    act_b, scale = up_other(flat, other_in, ssq, 0)
+    both = conv_pieces(pieces, send(cpar, 0, helper), order, helper)
+    both, other_in = lax.optimization_barrier((both, other_in))
+    both = send(both, helper, 0)
+    act_a, ssq = up_own(both, 0)
+    act_b, scale = up_other(both, other_in, ssq, 0)
     result = call(
         first_down_kernel,
         "down",
-        (section, x, act_a, act_b, w_out, other_out, scale, fvec, cpar),
+        (section, both, act_a, act_b, w_out, other_out, scale, fvec, cpar),
         whole,
         flops=2 * matmul,
     )
@@ -505,11 +512,11 @@
     act_a, ssq = up_own(flat, 1)
     acts = (act_a, *up_other(flat, odd_in, ssq, 1))
     kept = [down_piece(x, acts, odd_out, result, None, 1, n) for n in range(count)]
-    x, flat = conv_pieces([send(piece, 1, 2) for piece in kept], cpar, None, 2)
+    both = conv_pieces([send(piece, 1, 2) for piece in kept], cpar, None, 2)
     result = call(
         mlp_kernel,
         "mlp",
-        (section, x, flat, w_in, other_in, w_out, other_out, fvec, cpar, *kept, result),
+        (section, both, w_in, other_in, w_out, other_out, fvec, cpar, *kept, result),
         whole,
         scratch=[pltpu.VMEM((cells, half), bf16)] * 2
         + [ssq_scratch(half)] * 2

time: 83.5 us -> 81 us (0.970)
  waiting for transfers between devices: 44.3 us -> 42 us
    ppermute x9 -> x8, waiting for transfers between devices: 24.3 us -> 20.6 us  [send(): return lax.ppermute(x, 'section', [(start, end)])]
    ppermute x4, waiting for transfers between devices: 13.5 us -> 14.5 us  [other_half(): return lax.ppermute(x, ('section', 'dp'), pairs)]
    ppermute x9 -> x8, starting transfers between devices: 6.85 us -> 6.2 us  [send(): return lax.ppermute(x, 'section', [(start, end)])]
  transfers between devices with their start and end apart: 19 -> 18, of which waited for: 7 -> 7; matrix products, arithmetic and copies ran while one was open for 0% -> 1% of each run, Pallas kernels for 2% -> 2%
where the time goes in v10:
time: 81 us; the launch traced here: 80.6 us
  waiting for transfers between devices  42 us (52%)
  starting transfers between devices  24.9 us (31%)
  Pallas kernels  11.6 us (14%)
  local copies, waits for them, and re-layouts  1.4 us (2%)
    ppermute x8, waiting for transfers between devices, send(): return lax.ppermute(x, 'section', [(start, end)])  20.6 us
    ppermute x4, waiting for transfers between devices, other_half(): return lax.ppermute(x, ('section', 'dp'), pairs)  14.5 us
    pallas_call x26, Pallas kernels, call(): pl.pallas_call(functools.partial(kernel, **static), out_shape=out, in_spe...  11.6 us
    ppermute x3, starting transfers between devices, image_plan(): piece = lax.ppermute(piece, ('section', 'row'), pairs)  7.8 us
    ppermute x4, starting transfers between devices, other_half(): return lax.ppermute(x, ('section', 'dp'), pairs)  6.79 us
    ppermute x8, starting transfers between devices, send(): return lax.ppermute(x, 'section', [(start, end)])  6.2 us
    ppermute x3, waiting for transfers between devices, image_plan(): lax.ppermute(piece, 'row', [(p, p ^ order[n]) for p in range(count)])  5.05 us
    ppermute x3, starting transfers between devices, image_plan(): lax.ppermute(piece, 'row', [(p, p ^ order[n]) for p in range(count)])  4.12 us
  transfers between devices with their start and end apart: 18, of which 7 were waited for; matrix products, arithmetic and copies ran while one was open for 1% of the time, Pallas kernels for 2%

profile of v10, /device:TPU:7, one launch (start us, length us, event | category | flops | bytes accessed | tf_op | source)
XLA Modules:
  0.0 80.6 jit_solution(11297757431434965203)
XLA Ops:
  0.1 0.8 %collective-permute-start.4 = (bf16[352,704]{1,0:T(8,128)(2,1)}, bf16[352,704]{1,0:T(8,128)(2,1)S(1)}, u32[]{:S(2)}, u32[]{:S(2)}) collective-permute-start(bf16[352,704]{1,0:T(8,128)(2,1)} %bitcast.25), channel_id=1, source_target_pairs={{0,1},{1,0},{16,17},{17,16},{2,3},{3,2},{18,19},{19,18},{4,5},{5,4... | collective-permute-start | bytes 1486856 | tf_op jit(solution)/shard_map/ppermute | solution.py:404
  0.9 1.2 %dynamic-slice_bitcast_fusion = (bf16[4,48,352]{2,1,0:T(8,128)(2,1)S(1)}, bf16[4,48,352]{2,1,0:T(8,128)(2,1)S(1)}, bf16[4,48,352]{2,1,0:T(8,128)(2,1)S(1)}, bf16[4,48,352]{2,1,0:T(8,128)(2,1)S(1)}) fusion(bf16[4,1,4,48,352]{4,3,2,1,0:T(8,128)(2,1)} %param.11, s32[]{:T(128)S(6)} %select_n.16, s32[]{:T(128)S(6)} %select_n.14, s32[]{:T(128)S(6)} %select_n.13, ...), kind=kLoop, calls=%fused_computation | loop fusion | bytes 1081360 | tf_op jit(solution)/shard_map/squeeze | solution.py:396
  2.1 4.2 %collective-permute-start = (bf16[4,48,352]{2,1,0:T(8,128)(2,1)S(1)}, bf16[4,48,352]{2,1,0:T(8,128)(2,1)S(1)}, u32[]{:S(2)}, u32[]{:S(2)}) collective-permute-start(bf16[4,48,352]{2,1,0:T(8,128)(2,1)S(1)} %get-tuple-element.58), channel_id=1, source_target_pairs={{28,8},{30,10},{24,12},{26,14},{29,9},{31,11},{25,13},{27,15}} | collective-permute-start | bytes 405512 | tf_op jit(solution)/shard_map/ppermute | solution.py:399
  6.3 2.3 %collective-permute-start.1 = (bf16[4,48,352]{2,1,0:T(8,128)(2,1)S(1)}, bf16[4,48,352]{2,1,0:T(8,128)(2,1)S(1)}, u32[]{:S(2)}, u32[]{:S(2)}) collective-permute-start(bf16[4,48,352]{2,1,0:T(8,128)(2,1)S(1)} %get-tuple-element.60), channel_id=1, source_target_pairs={{30,8},{28,10},{26,12},{24,14},{31,9},{29,11},{27,13},{25,15}} | collective-permute-start | bytes 405512 | tf_op jit(solution)/shard_map/ppermute | solution.py:399
  8.6 1.3 %collective-permute-start.2 = (bf16[4,48,352]{2,1,0:T(8,128)(2,1)S(1)}, bf16[4,48,352]{2,1,0:T(8,128)(2,1)S(1)}, u32[]{:S(2)}, u32[]{:S(2)}) collective-permute-start(bf16[4,48,352]{2,1,0:T(8,128)(2,1)S(1)} %get-tuple-element.57), channel_id=1, source_target_pairs={{26,8},{24,10},{30,12},{28,14},{27,9},{25,11},{31,13},{29,15}} | collective-permute-start | bytes 405512 | tf_op jit(solution)/shard_map/ppermute | solution.py:399
  11.0 1.8 %collective-permute-done.2.refs_3_ = bf16[4,48,352]{2,1,0:T(8,128)(2,1)S(1)} collective-permute-done((bf16[4,48,352]{2,1,0:T(8,128)(2,1)S(1)}, bf16[4,48,352]{2,1,0:T(8,128)(2,1)S(1)}, u32[]{:S(2)}, u32[]{:S(2)}) %collective-permute-start.2) | collective-permute-done | bytes 135200 | tf_op jit(solution)/shard_map/ppermute | solution.py:399
  12.9 0.9 %collective-permute-start.5 = (bf16[2,16,48,352]{3,2,1,0:T(8,128)(2,1)S(1)}, bf16[2,16,48,352]{3,2,1,0:T(8,128)(2,1)S(1)}, u32[]{:S(2)}, u32[]{:S(2)}) collective-permute-start(bf16[2,16,48,352]{3,2,1,0:T(8,128)(2,1)S(1)} %last_piece.2), channel_id=1, source_target_pairs={{8,0},{9,1},{10,2},{11,3},{12,4},{13,5},{14,6},{15,7}} | collective-permute-start | bytes 3244040 | tf_op jit(solution)/shard_map/ppermute | solution.py:426
  13.9 0.7 collective-permute-start.6
  14.7 0.7 collective-permute-start.7
  15.4 2.1 %collective-permute-start.8 = (bf16[352,704]{1,0:T(8,128)(2,1)S(1)}, bf16[352,704]{1,0:T(8,128)(2,1)S(1)}, u32[]{:S(2)}, u32[]{:S(2)}) collective-permute-start(bf16[352,704]{1,0:T(8,128)(2,1)S(1)} %bitcast.27), channel_id=1, source_target_pairs={{8,9},{9,8},{24,25},{25,24},{10,11},{11,10},{26,27},{27,26},{12,13... | collective-permute-start | bytes 1486856 | tf_op jit(solution)/shard_map/ppermute | solution.py:404
  17.6 3.1 %collective-permute-start.9 = (bf16[704,352]{1,0:T(8,128)(2,1)S(1)}, bf16[704,352]{1,0:T(8,128)(2,1)S(1)}, u32[]{:S(2)}, u32[]{:S(2)}) collective-permute-start(bf16[704,352]{1,0:T(8,128)(2,1)S(1)} %bitcast.15), channel_id=1, source_target_pairs={{8,9},{9,8},{24,25},{25,24},{10,11},{11,10},{26,27},{27,26},{12,13... | collective-permute-start | bytes 1486856 | tf_op jit(solution)/shard_map/ppermute | solution.py:404
  20.8 8.7 %collective-permute-done.8.w_in.in_b = bf16[352,704]{1,0:T(8,128)(2,1)S(1)} collective-permute-done((bf16[352,704]{1,0:T(8,128)(2,1)S(1)}, bf16[352,704]{1,0:T(8,128)(2,1)S(1)}, u32[]{:S(2)}, u32[]{:S(2)}) %collective-permute-start.8) | collective-permute-done | bytes 495648 | tf_op jit(solution)/shard_map/ppermute | solution.py:404
  29.4 5.8 %collective-permute-done.9.out_b = bf16[704,352]{1,0:T(8,128)(2,1)S(1)} collective-permute-done((bf16[704,352]{1,0:T(8,128)(2,1)S(1)}, bf16[704,352]{1,0:T(8,128)(2,1)S(1)}, u32[]{:S(2)}, u32[]{:S(2)}) %collective-permute-start.9) | collective-permute-done | bytes 495648 | tf_op jit(solution)/shard_map/ppermute | solution.py:404
  35.2 0.7 collective-permute-start.10
  36.0 0.7 collective-permute-start.11
  38.4 1.3 %collective-permute-start.14 = (bf16[16,48,352]{2,1,0:T(8,128)(2,1)S(1)}, bf16[16,48,352]{2,1,0:T(8,128)(2,1)S(1)}, u32[]{:S(2)}, u32[]{:S(2)}) collective-permute-start(bf16[16,48,352]{2,1,0:T(8,128)(2,1)S(1)} %mlp.1.prev), channel_id=1, source_target_pairs={{16,24},{17,25},{18,26},{19,27},{20,28},{21,29},{22,30},{23,31}} | collective-permute-start | bytes 1622024 | tf_op jit(solution)/shard_map/ppermute | solution.py:426
  39.7 20.6 %collective-permute-done.14.x = bf16[16,48,352]{2,1,0:T(8,128)(2,1)S(1)} collective-permute-done((bf16[16,48,352]{2,1,0:T(8,128)(2,1)S(1)}, bf16[16,48,352]{2,1,0:T(8,128)(2,1)S(1)}, u32[]{:S(2)}, u32[]{:S(2)}) %collective-permute-start.14) | collective-permute-done | bytes 540704 | tf_op jit(solution)/shard_map/ppermute | solution.py:426
  60.3 8.1 %conv_up.1 = (bf16[768,704]{1,0:T(8,128)(2,1)S(1)}, bf16[768,704]{1,0:T(8,128)(2,1)S(1)}, f32[2,1,704]{2,1,0:T(1,128)S(1)}) custom-call(s32[1]{0:T(128)} %bitcast.1.section, bf16[16,48,352]{2,1,0:T(8,128)(2,1)S(1)} %collective-permute-done.14.x, f32[64,384]{1,0:T(8,128)S(1)} %get-tuple-element.31.cpar.refs_7_, bf16[352,704]{1,0:T(8,128)(2,1)S(1)} %bitcast.30, ...), custom_call_target="tpu_custom_call" | custom-call | flops 761266176 | bytes 1647108 | tf_op jit(solution)/shard_map/conv_up/pallas_call | solution.py:340
  68.9 2.7 %collective-permute-start.15 = (bf16[4,48,352]{2,1,0:T(8,128)(2,1)S(1)}, bf16[4,48,352]{2,1,0:T(8,128)(2,1)S(1)}, u32[]{:S(2)}, u32[]{:S(2)}) collective-permute-start(bf16[4,48,352]{2,1,0:T(8,128)(2,1)S(1)} %down_piece.13), channel_id=1, source_target_pairs={{0,4},{2,6},{4,0},{6,2},{1,5},{3,7},{5,1},{7,3},{8,12},{10,14},{12... | collective-permute-start | bytes 405512 | tf_op jit(solution)/shard_map/ppermute | solution.py:543
  72.1 1.3 %collective-permute-start.16 = (bf16[4,48,352]{2,1,0:T(8,128)(2,1)S(1)}, bf16[4,48,352]{2,1,0:T(8,128)(2,1)S(1)}, u32[]{:S(2)}, u32[]{:S(2)}) collective-permute-start(bf16[4,48,352]{2,1,0:T(8,128)(2,1)S(1)} %down_piece.14), channel_id=1, source_target_pairs={{0,6},{2,4},{4,2},{6,0},{1,7},{3,5},{5,3},{7,1},{8,14},{10,12},{12... | collective-permute-start | bytes 405512 | tf_op jit(solution)/shard_map/ppermute | solution.py:543
  74.5 1.2 %collective-permute-done.15.refs_1_ = bf16[4,48,352]{2,1,0:T(8,128)(2,1)S(1)} collective-permute-done((bf16[4,48,352]{2,1,0:T(8,128)(2,1)S(1)}, bf16[4,48,352]{2,1,0:T(8,128)(2,1)S(1)}, u32[]{:S(2)}, u32[]{:S(2)}) %collective-permute-start.15) | collective-permute-done | bytes 135200 | tf_op jit(solution)/shard_map/ppermute | solution.py:543
  75.7 2.4 %collective-permute-done.16.refs_2_ = bf16[4,48,352]{2,1,0:T(8,128)(2,1)S(1)} collective-permute-done((bf16[4,48,352]{2,1,0:T(8,128)(2,1)S(1)}, bf16[4,48,352]{2,1,0:T(8,128)(2,1)S(1)}, u32[]{:S(2)}, u32[]{:S(2)}) %collective-permute-start.16) | collective-permute-done | bytes 135200 | tf_op jit(solution)/shard_map/ppermute | solution.py:543
  78.2 1.4 %collective-permute-done.17.refs_3_ = bf16[4,48,352]{2,1,0:T(8,128)(2,1)S(1)} collective-permute-done((bf16[4,48,352]{2,1,0:T(8,128)(2,1)S(1)}, bf16[4,48,352]{2,1,0:T(8,128)(2,1)S(1)}, u32[]{:S(2)}, u32[]{:S(2)}) %collective-permute-start.17) | collective-permute-done | bytes 135200 | tf_op jit(solution)/shard_map/ppermute | solution.py:543
  79.6 0.8 %place.1 = bf16[1,4,1,4,48,352]{5,4,3,2,1,0:T(8,128)(2,1)} custom-call(s32[1]{0:T(128)} %bitcast.me, bf16[4,48,352]{2,1,0:T(8,128)(2,1)S(1)} %down_piece.12.refs_0_, bf16[4,48,352]{2,1,0:T(8,128)(2,1)S(1)} %collective-permute-done.15.refs_1_, bf16[4,48,352]{2,1,0:T(8,128)(2,1)S(1)} %collective-permute-done.16.refs_2_, ...), custom_call_target="tpu_custom_call" | custom-call | bytes 540676 | tf_op jit(solution)/shard_map/place/pallas_call | solution.py:340
  (59 shorter events, 5.0 us)
Async XLA Ops:
  0.0 10.0 %copy-start.4 = (bf16[1,1408]{1,0:T(2,128)(2,1)S(1)}, bf16[1,1408]{1,0:T(2,128)(2,1)}, u32[]{:S(2)}) copy-start(bf16[1,1408]{1,0:T(2,128)(2,1)} %refs_5_.1) | copy-start | bytes 8452
  0.0 10.0 %copy-start.3 = (bf16[1,1408]{1,0:T(2,128)(2,1)S(1)}, bf16[1,1408]{1,0:T(2,128)(2,1)}, u32[]{:S(2)}) copy-start(bf16[1,1408]{1,0:T(2,128)(2,1)} %refs_4_.1) | copy-start | bytes 8452
  0.0 10.0 %copy-start.8 = (bf16[1,352]{1,0:T(2,128)(2,1)S(1)}, bf16[1,352]{1,0:T(2,128)(2,1)}, u32[]{:S(2)}) copy-start(bf16[1,352]{1,0:T(2,128)(2,1)} %refs_2_.1) | copy-start | bytes 2116
  0.0 10.0 %copy-start.7 = (bf16[1,352]{1,0:T(2,128)(2,1)S(1)}, bf16[1,352]{1,0:T(2,128)(2,1)}, u32[]{:S(2)}) copy-start(bf16[1,352]{1,0:T(2,128)(2,1)} %refs_1_.1) | copy-start | bytes 2116
  0.0 10.0 %copy-start.6 = (bf16[1,352]{1,0:T(2,128)(2,1)S(1)}, bf16[1,352]{1,0:T(2,128)(2,1)}, u32[]{:S(2)}) copy-start(bf16[1,352]{1,0:T(2,128)(2,1)} %refs_0_.1) | copy-start | bytes 2116
  0.0 10.0 %copy-start.2 = (bf16[1,7,7,352]{3,2,1,0:T(8,128)(2,1)S(1)}, bf16[1,7,7,352]{3,2,1,0:T(8,128)(2,1)}, u32[]{:S(2)}) copy-start(bf16[1,7,7,352]{3,2,1,0:T(8,128)(2,1)} %kernel.1) | copy-start | bytes 103492
  0.1 12.8 %collective-permute-start.4 = (bf16[352,704]{1,0:T(8,128)(2,1)}, bf16[352,704]{1,0:T(8,128)(2,1)S(1)}, u32[]{:S(2)}, u32[]{:S(2)}) collective-permute-start(bf16[352,704]{1,0:T(8,128)(2,1)} %bitcast.25), channel_id=1, source_target_pairs={{0,1},{1,0},{16,17},{17,16},{2,3},{3,2},{18,19},{19,18},{4,5},{5,4... | collective-permute-start | bytes 1486856 | tf_op jit(solution)/shard_map/ppermute | solution.py:404
  2.1 8.9 %collective-permute-start = (bf16[4,48,352]{2,1,0:T(8,128)(2,1)S(1)}, bf16[4,48,352]{2,1,0:T(8,128)(2,1)S(1)}, u32[]{:S(2)}, u32[]{:S(2)}) collective-permute-start(bf16[4,48,352]{2,1,0:T(8,128)(2,1)S(1)} %get-tuple-element.58), channel_id=1, source_target_pairs={{28,8},{30,10},{24,12},{26,14},{29,9},{31,11},{25,13},{27,15}} | collective-permute-start | bytes 405512 | tf_op jit(solution)/shard_map/ppermute | solution.py:399
  6.3 4.7 %collective-permute-start.1 = (bf16[4,48,352]{2,1,0:T(8,128)(2,1)S(1)}, bf16[4,48,352]{2,1,0:T(8,128)(2,1)S(1)}, u32[]{:S(2)}, u32[]{:S(2)}) collective-permute-start(bf16[4,48,352]{2,1,0:T(8,128)(2,1)S(1)} %get-tuple-element.60), channel_id=1, source_target_pairs={{30,8},{28,10},{26,12},{24,14},{31,9},{29,11},{27,13},{25,15}} | collective-permute-start | bytes 405512 | tf_op jit(solution)/shard_map/ppermute | solution.py:399
  8.6 4.3 %collective-permute-start.2 = (bf16[4,48,352]{2,1,0:T(8,128)(2,1)S(1)}, bf16[4,48,352]{2,1,0:T(8,128)(2,1)S(1)}, u32[]{:S(2)}, u32[]{:S(2)}) collective-permute-start(bf16[4,48,352]{2,1,0:T(8,128)(2,1)S(1)} %get-tuple-element.57), channel_id=1, source_target_pairs={{26,8},{24,10},{30,12},{28,14},{27,9},{25,11},{31,13},{29,15}} | collective-permute-start | bytes 405512 | tf_op jit(solution)/shard_map/ppermute | solution.py:399
  10.3 0.7 collective-permute-start.3
  12.9 1.7 %collective-permute-start.5 = (bf16[2,16,48,352]{3,2,1,0:T(8,128)(2,1)S(1)}, bf16[2,16,48,352]{3,2,1,0:T(8,128)(2,1)S(1)}, u32[]{:S(2)}, u32[]{:S(2)}) collective-permute-start(bf16[2,16,48,352]{3,2,1,0:T(8,128)(2,1)S(1)} %last_piece.2), channel_id=1, source_target_pairs={{8,0},{9,1},{10,2},{11,3},{12,4},{13,5},{14,6},{15,7}} | collective-permute-start | bytes 3244040 | tf_op jit(solution)/shard_map/ppermute | solution.py:426
  13.9 0.8 collective-permute-start.6
  14.7 6.0 %collective-permute-start.7 = (bf16[16,48,352]{2,1,0:T(8,128)(2,1)S(1)}, bf16[16,48,352]{2,1,0:T(8,128)(2,1)S(1)}, u32[]{:S(2)}, u32[]{:S(2)}) collective-permute-start(bf16[16,48,352]{2,1,0:T(8,128)(2,1)S(1)} %down.1.prev.refs_4_), channel_id=1, source_target_pairs={{0,8},{1,9},{2,10},{3,11},{4,12},{5,13},{6,14},{7,15}} | collective-permute-start | bytes 1622024 | tf_op jit(solution)/shard_map/ppermute | solution.py:426
  15.4 14.0 %collective-permute-start.8 = (bf16[352,704]{1,0:T(8,128)(2,1)S(1)}, bf16[352,704]{1,0:T(8,128)(2,1)S(1)}, u32[]{:S(2)}, u32[]{:S(2)}) collective-permute-start(bf16[352,704]{1,0:T(8,128)(2,1)S(1)} %bitcast.27), channel_id=1, source_target_pairs={{8,9},{9,8},{24,25},{25,24},{10,11},{11,10},{26,27},{27,26},{12,13... | collective-permute-start | bytes 1486856 | tf_op jit(solution)/shard_map/ppermute | solution.py:404
  17.6 17.7 %collective-permute-start.9 = (bf16[704,352]{1,0:T(8,128)(2,1)S(1)}, bf16[704,352]{1,0:T(8,128)(2,1)S(1)}, u32[]{:S(2)}, u32[]{:S(2)}) collective-permute-start(bf16[704,352]{1,0:T(8,128)(2,1)S(1)} %bitcast.15), channel_id=1, source_target_pairs={{8,9},{9,8},{24,25},{25,24},{10,11},{11,10},{26,27},{27,26},{12,13... | collective-permute-start | bytes 1486856 | tf_op jit(solution)/shard_map/ppermute | solution.py:404
  35.2 2.8 %collective-permute-start.10 = (bf16[4,48,352]{2,1,0:T(8,128)(2,1)S(1)}, bf16[4,48,352]{2,1,0:T(8,128)(2,1)S(1)}, u32[]{:S(2)}, u32[]{:S(2)}) collective-permute-start(bf16[4,48,352]{2,1,0:T(8,128)(2,1)S(1)} %down_piece.8.refs_0_), channel_id=1, source_target_pairs={{8,16},{9,17},{10,18},{11,19},{12,20},{13,21},{14,22},{15,23}} | collective-permute-start | bytes 405512 | tf_op jit(solution)/shard_map/ppermute | solution.py:426
  36.0 2.1 %collective-permute-start.11 = (bf16[4,48,352]{2,1,0:T(8,128)(2,1)S(1)}, bf16[4,48,352]{2,1,0:T(8,128)(2,1)S(1)}, u32[]{:S(2)}, u32[]{:S(2)}) collective-permute-start(bf16[4,48,352]{2,1,0:T(8,128)(2,1)S(1)} %down_piece.9.refs_1_), channel_id=1, source_target_pairs={{8,16},{9,17},{10,18},{11,19},{12,20},{13,21},{14,22},{15,23}} | collective-permute-start | bytes 405512 | tf_op jit(solution)/shard_map/ppermute | solution.py:426
  36.7 1.5 %collective-permute-start.12 = (bf16[4,48,352]{2,1,0:T(8,128)(2,1)S(1)}, bf16[4,48,352]{2,1,0:T(8,128)(2,1)S(1)}, u32[]{:S(2)}, u32[]{:S(2)}) collective-permute-start(bf16[4,48,352]{2,1,0:T(8,128)(2,1)S(1)} %down_piece.10.refs_2_), channel_id=1, source_target_pairs={{8,16},{9,17},{10,18},{11,19},{12,20},{13,21},{14,22},{15,23}} | collective-permute-start | bytes 405512 | tf_op jit(solution)/shard_map/ppermute | solution.py:426
  37.4 0.8 collective-permute-start.13
  38.4 21.9 %collective-permute-start.14 = (bf16[16,48,352]{2,1,0:T(8,128)(2,1)S(1)}, bf16[16,48,352]{2,1,0:T(8,128)(2,1)S(1)}, u32[]{:S(2)}, u32[]{:S(2)}) collective-permute-start(bf16[16,48,352]{2,1,0:T(8,128)(2,1)S(1)} %mlp.1.prev), channel_id=1, source_target_pairs={{16,24},{17,25},{18,26},{19,27},{20,28},{21,29},{22,30},{23,31}} | collective-permute-start | bytes 1622024 | tf_op jit(solution)/shard_map/ppermute | solution.py:426
  68.9 6.8 %collective-permute-start.15 = (bf16[4,48,352]{2,1,0:T(8,128)(2,1)S(1)}, bf16[4,48,352]{2,1,0:T(8,128)(2,1)S(1)}, u32[]{:S(2)}, u32[]{:S(2)}) collective-permute-start(bf16[4,48,352]{2,1,0:T(8,128)(2,1)S(1)} %down_piece.13), channel_id=1, source_target_pairs={{0,4},{2,6},{4,0},{6,2},{1,5},{3,7},{5,1},{7,3},{8,12},{10,14},{12... | collective-permute-start | bytes 405512 | tf_op jit(solution)/shard_map/ppermute | solution.py:543
  72.1 6.1 %collective-permute-start.16 = (bf16[4,48,352]{2,1,0:T(8,128)(2,1)S(1)}, bf16[4,48,352]{2,1,0:T(8,128)(2,1)S(1)}, u32[]{:S(2)}, u32[]{:S(2)}) collective-permute-start(bf16[4,48,352]{2,1,0:T(8,128)(2,1)S(1)} %down_piece.14), channel_id=1, source_target_pairs={{0,6},{2,4},{4,2},{6,0},{1,7},{3,5},{5,3},{7,1},{8,14},{10,12},{12... | collective-permute-start | bytes 405512 | tf_op jit(solution)/shard_map/ppermute | solution.py:543
  74.0 5.6 %collective-permute-start.17 = (bf16[4,48,352]{2,1,0:T(8,128)(2,1)S(1)}, bf16[4,48,352]{2,1,0:T(8,128)(2,1)S(1)}, u32[]{:S(2)}, u32[]{:S(2)}) collective-permute-start(bf16[4,48,352]{2,1,0:T(8,128)(2,1)S(1)} %down_piece.15), channel_id=1, source_target_pairs={{0,2},{2,0},{4,6},{6,4},{1,3},{3,1},{5,7},{7,5},{8,10},{10,8},{12,... | collective-permute-start | bytes 405512 | tf_op jit(solution)/shard_map/ppermute | solution.py:543
  (4 other events, 22.7 us)

commit v11 on v10

--- a/solution.py
+++ b/solution.py
@@ -13,6 +13,8 @@
 VMEM_BYTES = 20 * 1024 * 1024
 REACH = 3
 CHUNK = 4
+SUBLANES = 16
+CONV_ROWS = 10
 NORM_ROWS = 4
 IN_ORDER = (0, 1, 2, 3)
 VECTORS = 56
@@ -35,38 +37,48 @@
                 xp[k * groups + g, 8 : 8 + width, 0 : own.shape[1]] = own
                 for q in range(reach_cols):
                     near = pl.ds(8 - REACH + q, blocks, stride=stride)
-                    xs[r, q, :, at] = xp[k * groups + g, near, :]
+                    xs[r, q, :, at] = xp[k * groups + g, near, :].astype(jnp.bfloat16)
         return carry
 
     lax.fori_loop(0, height // 2, rows, 0)
 
 
-def conv(xs, cpar, cq):
+def conv(xs, cpar, kernels, cq):
     rows = xs.shape[0]
     height, stride, blocks, lanes = cq.shape
     span = 2 * REACH + 1
     above = (height - rows) // 2
+    for tap in range(span * span):
+        kernels[tap] = jnp.broadcast_to(cpar[tap : tap + 1, :], (blocks, lanes)).astype(jnp.bfloat16)
+    parts = -(-height // CONV_ROWS)
+    size = height // parts
 
     def group(g, carry):
         at = pl.ds(pl.multiple_of(g * LANES, LANES), LANES)
 
         def column(q, carry):
-            bias = jnp.broadcast_to(cpar[VECTORS : VECTORS + 1, at], (blocks, LANES))
-            acc = [None if above else bias] * height
-            for j in range(span):
-                kern = [
-                    jnp.broadcast_to(cpar[i * span + j : i * span + j + 1, at], (blocks, LANES))
-                    for i in range(span)
-                ]
-                for r in range(rows):
-                    x_row = xs[r, q + j, :, at]
-                    for i in range(span):
-                        h = r + above + REACH - i
-                        if 0 <= h < height:
+            for first in range(0, height, size):
+                if above:
+                    acc = [jnp.zeros((blocks, LANES), jnp.float32)] * size
+                else:
+                    bias = cpar[VECTORS : VECTORS + 1, at]
+                    acc = [jnp.broadcast_to(bias, (blocks, LANES))] * size
+                for j in range(span):
+                    kern = [kernels[i * span + j, :, at] for i in range(span)]
+                    part = [None] * size
+                    for r in range(rows):
+                        low = r + above + REACH - first
+                        taken = [i for i in range(span) if 0 <= low - i < size]
+                        if not taken:
+                            continue
+                        x_row = xs[r, q + j, :, at]
+                        for i in taken:
+                            h = low - i
                             term = kern[i] * x_row
-                            acc[h] = term if acc[h] is None else acc[h] + term
-            for h in range(height):
-                cq[h, q, :, at] = acc[h]
+                            part[h] = term if part[h] is None else part[h] + term
+                    acc = [a + p.astype(jnp.float32) for a, p in zip(acc, part)]
+                for h in range(size):
+                    cq[first + h, q, :, at] = acc[h]
             return carry
 
         return lax.fori_loop(0, stride, column, carry)
@@ -106,17 +118,18 @@
     lax.fori_loop(0, height // NORM_ROWS, rows, 0)
 
 
-def conv_norm(x, cpar, flat, xp, xs, cq):
+def conv_norm(x, cpar, flat, xp, xs, kernels, cq):
     fill_columns(xp, xs, x, x.shape[2])
-    conv(xs, cpar, cq)
+    conv(xs, cpar, kernels, cq)
     norm(cq, cpar, xp, flat)
 
 
 def conv_scratch(rows, out_rows, width, lanes):
     return [
         pltpu.VMEM((NORM_ROWS * lanes // LANES, width + 16, LANES), jnp.float32),
-        pltpu.VMEM((rows, width // 8 + 2 * REACH, 8, lanes), jnp.float32),
-        pltpu.VMEM((out_rows, width // 8, 8, lanes), jnp.float32),
+        pltpu.VMEM((rows, width // SUBLANES + 2 * REACH, SUBLANES, lanes), jnp.bfloat16),
+        pltpu.VMEM(((2 * REACH + 1) ** 2, SUBLANES, lanes), jnp.bfloat16),
+        pltpu.VMEM((out_rows, width // SUBLANES, SUBLANES, lanes), jnp.float32),
     ]
 
 
@@ -211,17 +224,17 @@
     return n if order is None else me[0] ^ order[n]
 
 
-def piece_kernel(section, piece, cpar, part, xp, xs, *, on):
+def piece_kernel(section, piece, cpar, part, xp, xs, kernels, *, on):
     @pl.when(section[0] == on)
     def _():
         fill_columns(xp, xs, piece, piece.shape[2])
-        conv(xs, cpar, part)
+        conv(xs, cpar, kernels, part)
 
 
 def last_piece_kernel(section, me, *refs, order, on):
     count = len(order or IN_ORDER)
     pieces, parts = refs[:count], refs[count : 2 * count - 1]
-    cpar, both, xp, xs, own, cq = refs[2 * count - 1 :]
+    cpar, both, xp, xs, kernels, own, cq = refs[2 * count - 1 :]
     x, flat = both.at[0], both.at[1]
     rows = pieces[0].shape[0]
 
@@ -230,7 +243,7 @@
         bias = cpar[VECTORS : VECTORS + 1, :].reshape(1, 1, 1, cq.shape[3])
         cq[...] = jnp.broadcast_to(bias, cq.shape)
         fill_columns(xp, xs, pieces[-1], x.shape[2])
-        conv(xs, cpar, own)
+        conv(xs, cpar, kernels, own)
         for n, (piece, part) in enumerate(zip(pieces, (*parts, own))):
             at = block_of(me, order, n) * rows
             x[pl.ds(at, rows)] = piece[...]
@@ -238,10 +251,10 @@
         norm(cq, cpar, xp, flat, REACH)
 
 
-def conv_kernel(section, x, cpar, flat, xp, xs, cq, *, tick):
+def conv_kernel(section, x, cpar, flat, xp, xs, kernels, cq, *, tick):
     @pl.when(section[0] == tick)
     def _():
-        conv_norm(x, cpar, flat, xp, xs, cq)
+        conv_norm(x, cpar, flat, xp, xs, kernels, cq)
 
 
 def normed_part(ref):
@@ -304,11 +317,11 @@
 
 
 def conv_up_kernel(section, x, cpar, in_a, in_b, fvec, *refs, tick):
-    act_a, act_b, scale, xp, xs, cq, flat, ssq_a, ssq_b = refs
+    act_a, act_b, scale, xp, xs, kernels, cq, flat, ssq_a, ssq_b = refs
 
     @pl.when(section[0] == tick)
     def _():
-        conv_norm(x, cpar, flat, xp, xs, cq)
+        conv_norm(x, cpar, flat, xp, xs, kernels, cq)
         up(flat, in_a, fvec.at[0], act_a, ssq_a)
         up(flat, in_b, fvec.at[1], act_b, ssq_b)
         norm_scale((ssq_a, ssq_b), fvec, scale)
@@ -436,8 +449,8 @@
                 piece_kernel,
                 "conv_piece",
                 (section, piece, cpar),
-                shape(out_rows, width // 8, 8, lanes),
-                scratch=scratch[:2],
+                shape(out_rows, width // SUBLANES, SUBLANES, lanes),
+                scratch=scratch[:3],
                 on=on,
             )
             parts.append(part)
@@ -446,7 +459,7 @@
             "last_piece",
             (section, me_ref, *pieces, *parts, cpar),
             shape(2, height, width, channels, dtype=bf16),
-            scratch=scratch + [conv_scratch(1, height + 2 * REACH, width, lanes)[2]],
+            scratch=scratch + [conv_scratch(1, height + 2 * REACH, width, lanes)[3]],
             order=order,
             on=on,
         )

time: 81 us -> 83.3 us (1.028)
  Pallas kernels: 11.6 us -> 13 us
  waiting for transfers between devices: 42 us -> 43.2 us
    pallas_call x26, Pallas kernels: 11.6 us -> 13 us  [call(): pl.pallas_call(functools.partial(kernel, **static), out_shape=out, in_spe...]
    ppermute x8, waiting for transfers between devices: 20.6 us -> 21.8 us  [send(): return lax.ppermute(x, 'section', [(start, end)])]
where the time goes in v11:
time: 83.3 us; the launch traced here: 82.9 us
  waiting for transfers between devices  43.2 us (52%)
  starting transfers between devices  24.6 us (30%)
  Pallas kernels  13 us (16%)
  local copies, waits for them, and re-layouts  1.4 us (2%)
    ppermute x8, waiting for transfers between devices, send(): return lax.ppermute(x, 'section', [(start, end)])  21.8 us
    ppermute x4, waiting for transfers between devices, other_half(): return lax.ppermute(x, ('section', 'dp'), pairs)  14.5 us
    pallas_call x26, Pallas kernels, call(): pl.pallas_call(functools.partial(kernel, **static), out_shape=out, in_spe...  13 us
    ppermute x3, starting transfers between devices, image_plan(): piece = lax.ppermute(piece, ('section', 'row'), pairs)  7.8 us
    ppermute x4, starting transfers between devices, other_half(): return lax.ppermute(x, ('section', 'dp'), pairs)  6.79 us
    ppermute x8, starting transfers between devices, send(): return lax.ppermute(x, 'section', [(start, end)])  6.2 us
    ppermute x3, waiting for transfers between devices, image_plan(): lax.ppermute(piece, 'row', [(p, p ^ order[n]) for p in range(count)])  5.05 us
    ppermute x3, starting transfers between devices, image_plan(): lax.ppermute(piece, 'row', [(p, p ^ order[n]) for p in range(count)])  3.83 us
  transfers between devices with their start and end apart: 18, of which 7 were waited for; matrix products, arithmetic and copies ran while one was open for 1% of the time, Pallas kernels for 2%

profile of v11, /device:TPU:7, one launch (start us, length us, event | category | flops | bytes accessed | tf_op | source)
XLA Modules:
  0.0 82.9 jit_solution(16151933838964675433)
XLA Ops:
  0.1 0.8 collective-permute-start.4
  0.9 1.2 %dynamic-slice_bitcast_fusion = (bf16[4,48,352]{2,1,0:T(8,128)(2,1)S(1)}, bf16[4,48,352]{2,1,0:T(8,128)(2,1)S(1)}, bf16[4,48,352]{2,1,0:T(8,128)(2,1)S(1)}, bf16[4,48,352]{2,1,0:T(8,128)(2,1)S(1)}) fusion(bf16[4,1,4,48,352]{4,3,2,1,0:T(8,128)(2,1)} %param.11, s32[]{:T(128)S(6)} %select_n.16, s32[]{:T(128)S(6)} %select_n.14, s32[]{:T(128)S(6)} %select_n.13, ...), kind=kLoop, calls=%fused_computation | loop fusion | bytes 1081360 | tf_op jit(solution)/shard_map/squeeze | solution.py:409
  2.1 4.2 %collective-permute-start = (bf16[4,48,352]{2,1,0:T(8,128)(2,1)S(1)}, bf16[4,48,352]{2,1,0:T(8,128)(2,1)S(1)}, u32[]{:S(2)}, u32[]{:S(2)}) collective-permute-start(bf16[4,48,352]{2,1,0:T(8,128)(2,1)S(1)} %get-tuple-element.58), channel_id=1, source_target_pairs={{28,8},{30,10},{24,12},{26,14},{29,9},{31,11},{25,13},{27,15}} | collective-permute-start | bytes 405512 | tf_op jit(solution)/shard_map/ppermute | solution.py:412
  6.3 2.3 %collective-permute-start.1 = (bf16[4,48,352]{2,1,0:T(8,128)(2,1)S(1)}, bf16[4,48,352]{2,1,0:T(8,128)(2,1)S(1)}, u32[]{:S(2)}, u32[]{:S(2)}) collective-permute-start(bf16[4,48,352]{2,1,0:T(8,128)(2,1)S(1)} %get-tuple-element.60), channel_id=1, source_target_pairs={{30,8},{28,10},{26,12},{24,14},{31,9},{29,11},{27,13},{25,15}} | collective-permute-start | bytes 405512 | tf_op jit(solution)/shard_map/ppermute | solution.py:412
  8.6 1.3 %collective-permute-start.2 = (bf16[4,48,352]{2,1,0:T(8,128)(2,1)S(1)}, bf16[4,48,352]{2,1,0:T(8,128)(2,1)S(1)}, u32[]{:S(2)}, u32[]{:S(2)}) collective-permute-start(bf16[4,48,352]{2,1,0:T(8,128)(2,1)S(1)} %get-tuple-element.57), channel_id=1, source_target_pairs={{26,8},{24,10},{30,12},{28,14},{27,9},{25,11},{31,13},{29,15}} | collective-permute-start | bytes 405512 | tf_op jit(solution)/shard_map/ppermute | solution.py:412
  11.0 1.8 %collective-permute-done.2.refs_3_ = bf16[4,48,352]{2,1,0:T(8,128)(2,1)S(1)} collective-permute-done((bf16[4,48,352]{2,1,0:T(8,128)(2,1)S(1)}, bf16[4,48,352]{2,1,0:T(8,128)(2,1)S(1)}, u32[]{:S(2)}, u32[]{:S(2)}) %collective-permute-start.2) | collective-permute-done | bytes 135200 | tf_op jit(solution)/shard_map/ppermute | solution.py:412
  12.9 0.9 %collective-permute-start.5 = (bf16[2,16,48,352]{3,2,1,0:T(8,128)(2,1)S(1)}, bf16[2,16,48,352]{3,2,1,0:T(8,128)(2,1)S(1)}, u32[]{:S(2)}, u32[]{:S(2)}) collective-permute-start(bf16[2,16,48,352]{3,2,1,0:T(8,128)(2,1)S(1)} %last_piece.2), channel_id=1, source_target_pairs={{8,0},{9,1},{10,2},{11,3},{12,4},{13,5},{14,6},{15,7}} | collective-permute-start | bytes 3244040 | tf_op jit(solution)/shard_map/ppermute | solution.py:439
  13.9 0.7 collective-permute-start.6
  14.7 0.7 collective-permute-start.7
  15.4 2.1 %collective-permute-start.8 = (bf16[352,704]{1,0:T(8,128)(2,1)S(1)}, bf16[352,704]{1,0:T(8,128)(2,1)S(1)}, u32[]{:S(2)}, u32[]{:S(2)}) collective-permute-start(bf16[352,704]{1,0:T(8,128)(2,1)S(1)} %bitcast.27), channel_id=1, source_target_pairs={{8,9},{9,8},{24,25},{25,24},{10,11},{11,10},{26,27},{27,26},{12,13... | collective-permute-start | bytes 1486856 | tf_op jit(solution)/shard_map/ppermute | solution.py:417
  17.6 3.1 %collective-permute-start.9 = (bf16[704,352]{1,0:T(8,128)(2,1)S(1)}, bf16[704,352]{1,0:T(8,128)(2,1)S(1)}, u32[]{:S(2)}, u32[]{:S(2)}) collective-permute-start(bf16[704,352]{1,0:T(8,128)(2,1)S(1)} %bitcast.15), channel_id=1, source_target_pairs={{8,9},{9,8},{24,25},{25,24},{10,11},{11,10},{26,27},{27,26},{12,13... | collective-permute-start | bytes 1486856 | tf_op jit(solution)/shard_map/ppermute | solution.py:417
  20.8 8.7 %collective-permute-done.8.w_in.in_b = bf16[352,704]{1,0:T(8,128)(2,1)S(1)} collective-permute-done((bf16[352,704]{1,0:T(8,128)(2,1)S(1)}, bf16[352,704]{1,0:T(8,128)(2,1)S(1)}, u32[]{:S(2)}, u32[]{:S(2)}) %collective-permute-start.8) | collective-permute-done | bytes 495648 | tf_op jit(solution)/shard_map/ppermute | solution.py:417
  29.4 5.8 %collective-permute-done.9.out_b = bf16[704,352]{1,0:T(8,128)(2,1)S(1)} collective-permute-done((bf16[704,352]{1,0:T(8,128)(2,1)S(1)}, bf16[704,352]{1,0:T(8,128)(2,1)S(1)}, u32[]{:S(2)}, u32[]{:S(2)}) %collective-permute-start.9) | collective-permute-done | bytes 495648 | tf_op jit(solution)/shard_map/ppermute | solution.py:417
  35.2 0.7 collective-permute-start.10
  36.0 0.7 collective-permute-start.11
  38.4 1.3 %collective-permute-start.14 = (bf16[16,48,352]{2,1,0:T(8,128)(2,1)S(1)}, bf16[16,48,352]{2,1,0:T(8,128)(2,1)S(1)}, u32[]{:S(2)}, u32[]{:S(2)}) collective-permute-start(bf16[16,48,352]{2,1,0:T(8,128)(2,1)S(1)} %mlp.1.prev), channel_id=1, source_target_pairs={{16,24},{17,25},{18,26},{19,27},{20,28},{21,29},{22,30},{23,31}} | collective-permute-start | bytes 1622024 | tf_op jit(solution)/shard_map/ppermute | solution.py:439
  39.7 21.8 %collective-permute-done.14.x = bf16[16,48,352]{2,1,0:T(8,128)(2,1)S(1)} collective-permute-done((bf16[16,48,352]{2,1,0:T(8,128)(2,1)S(1)}, bf16[16,48,352]{2,1,0:T(8,128)(2,1)S(1)}, u32[]{:S(2)}, u32[]{:S(2)}) %collective-permute-start.14) | collective-permute-done | bytes 540704 | tf_op jit(solution)/shard_map/ppermute | solution.py:439
  61.5 9.5 %conv_up.1 = (bf16[768,704]{1,0:T(8,128)(2,1)S(1)}, bf16[768,704]{1,0:T(8,128)(2,1)S(1)}, f32[2,1,704]{2,1,0:T(1,128)S(1)}) custom-call(s32[1]{0:T(128)} %bitcast.1.section, bf16[16,48,352]{2,1,0:T(8,128)(2,1)S(1)} %collective-permute-done.14.x, f32[64,384]{1,0:T(8,128)S(1)} %get-tuple-element.31.cpar.refs_7_, bf16[352,704]{1,0:T(8,128)(2,1)S(1)} %bitcast.30, ...), custom_call_target="tpu_custom_call" | custom-call | flops 761266176 | bytes 1647108 | tf_op jit(solution)/shard_map/conv_up/pallas_call | solution.py:353
  71.5 2.4 %collective-permute-start.15 = (bf16[4,48,352]{2,1,0:T(8,128)(2,1)S(1)}, bf16[4,48,352]{2,1,0:T(8,128)(2,1)S(1)}, u32[]{:S(2)}, u32[]{:S(2)}) collective-permute-start(bf16[4,48,352]{2,1,0:T(8,128)(2,1)S(1)} %down_piece.13), channel_id=1, source_target_pairs={{0,4},{2,6},{4,0},{6,2},{1,5},{3,7},{5,1},{7,3},{8,12},{10,14},{12... | collective-permute-start | bytes 405512 | tf_op jit(solution)/shard_map/ppermute | solution.py:556
  74.4 1.3 %collective-permute-start.16 = (bf16[4,48,352]{2,1,0:T(8,128)(2,1)S(1)}, bf16[4,48,352]{2,1,0:T(8,128)(2,1)S(1)}, u32[]{:S(2)}, u32[]{:S(2)}) collective-permute-start(bf16[4,48,352]{2,1,0:T(8,128)(2,1)S(1)} %down_piece.14), channel_id=1, source_target_pairs={{0,6},{2,4},{4,2},{6,0},{1,7},{3,5},{5,3},{7,1},{8,14},{10,12},{12... | collective-permute-start | bytes 405512 | tf_op jit(solution)/shard_map/ppermute | solution.py:556
  76.8 1.2 %collective-permute-done.15.refs_1_ = bf16[4,48,352]{2,1,0:T(8,128)(2,1)S(1)} collective-permute-done((bf16[4,48,352]{2,1,0:T(8,128)(2,1)S(1)}, bf16[4,48,352]{2,1,0:T(8,128)(2,1)S(1)}, u32[]{:S(2)}, u32[]{:S(2)}) %collective-permute-start.15) | collective-permute-done | bytes 135200 | tf_op jit(solution)/shard_map/ppermute | solution.py:556
  78.1 2.4 %collective-permute-done.16.refs_2_ = bf16[4,48,352]{2,1,0:T(8,128)(2,1)S(1)} collective-permute-done((bf16[4,48,352]{2,1,0:T(8,128)(2,1)S(1)}, bf16[4,48,352]{2,1,0:T(8,128)(2,1)S(1)}, u32[]{:S(2)}, u32[]{:S(2)}) %collective-permute-start.16) | collective-permute-done | bytes 135200 | tf_op jit(solution)/shard_map/ppermute | solution.py:556
  80.5 1.4 %collective-permute-done.17.refs_3_ = bf16[4,48,352]{2,1,0:T(8,128)(2,1)S(1)} collective-permute-done((bf16[4,48,352]{2,1,0:T(8,128)(2,1)S(1)}, bf16[4,48,352]{2,1,0:T(8,128)(2,1)S(1)}, u32[]{:S(2)}, u32[]{:S(2)}) %collective-permute-start.17) | collective-permute-done | bytes 135200 | tf_op jit(solution)/shard_map/ppermute | solution.py:556
  81.9 0.8 %place.1 = bf16[1,4,1,4,48,352]{5,4,3,2,1,0:T(8,128)(2,1)} custom-call(s32[1]{0:T(128)} %bitcast.me, bf16[4,48,352]{2,1,0:T(8,128)(2,1)S(1)} %down_piece.12.refs_0_, bf16[4,48,352]{2,1,0:T(8,128)(2,1)S(1)} %collective-permute-done.15.refs_1_, bf16[4,48,352]{2,1,0:T(8,128)(2,1)S(1)} %collective-permute-done.16.refs_2_, ...), custom_call_target="tpu_custom_call" | custom-call | bytes 540676 | tf_op jit(solution)/shard_map/place/pallas_call | solution.py:353
  (59 shorter events, 5.0 us)
Async XLA Ops:
  0.0 10.0 %copy-start.4 = (bf16[1,1408]{1,0:T(2,128)(2,1)S(1)}, bf16[1,1408]{1,0:T(2,128)(2,1)}, u32[]{:S(2)}) copy-start(bf16[1,1408]{1,0:T(2,128)(2,1)} %refs_5_.1) | copy-start | bytes 8452
  0.0 10.0 %copy-start.3 = (bf16[1,1408]{1,0:T(2,128)(2,1)S(1)}, bf16[1,1408]{1,0:T(2,128)(2,1)}, u32[]{:S(2)}) copy-start(bf16[1,1408]{1,0:T(2,128)(2,1)} %refs_4_.1) | copy-start | bytes 8452
  0.0 10.0 %copy-start.8 = (bf16[1,352]{1,0:T(2,128)(2,1)S(1)}, bf16[1,352]{1,0:T(2,128)(2,1)}, u32[]{:S(2)}) copy-start(bf16[1,352]{1,0:T(2,128)(2,1)} %refs_2_.1) | copy-start | bytes 2116
  0.0 10.0 %copy-start.7 = (bf16[1,352]{1,0:T(2,128)(2,1)S(1)}, bf16[1,352]{1,0:T(2,128)(2,1)}, u32[]{:S(2)}) copy-start(bf16[1,352]{1,0:T(2,128)(2,1)} %refs_1_.1) | copy-start | bytes 2116
  0.0 10.0 %copy-start.6 = (bf16[1,352]{1,0:T(2,128)(2,1)S(1)}, bf16[1,352]{1,0:T(2,128)(2,1)}, u32[]{:S(2)}) copy-start(bf16[1,352]{1,0:T(2,128)(2,1)} %refs_0_.1) | copy-start | bytes 2116
  0.0 10.0 %copy-start.2 = (bf16[1,7,7,352]{3,2,1,0:T(8,128)(2,1)S(1)}, bf16[1,7,7,352]{3,2,1,0:T(8,128)(2,1)}, u32[]{:S(2)}) copy-start(bf16[1,7,7,352]{3,2,1,0:T(8,128)(2,1)} %kernel.1) | copy-start | bytes 103492
  0.1 12.8 %collective-permute-start.4 = (bf16[352,704]{1,0:T(8,128)(2,1)}, bf16[352,704]{1,0:T(8,128)(2,1)S(1)}, u32[]{:S(2)}, u32[]{:S(2)}) collective-permute-start(bf16[352,704]{1,0:T(8,128)(2,1)} %bitcast.25), channel_id=1, source_target_pairs={{0,1},{1,0},{16,17},{17,16},{2,3},{3,2},{18,19},{19,18},{4,5},{5,4... | collective-permute-start | bytes 1486856 | tf_op jit(solution)/shard_map/ppermute | solution.py:417
  2.1 8.9 %collective-permute-start = (bf16[4,48,352]{2,1,0:T(8,128)(2,1)S(1)}, bf16[4,48,352]{2,1,0:T(8,128)(2,1)S(1)}, u32[]{:S(2)}, u32[]{:S(2)}) collective-permute-start(bf16[4,48,352]{2,1,0:T(8,128)(2,1)S(1)} %get-tuple-element.58), channel_id=1, source_target_pairs={{28,8},{30,10},{24,12},{26,14},{29,9},{31,11},{25,13},{27,15}} | collective-permute-start | bytes 405512 | tf_op jit(solution)/shard_map/ppermute | solution.py:412
  6.3 4.7 %collective-permute-start.1 = (bf16[4,48,352]{2,1,0:T(8,128)(2,1)S(1)}, bf16[4,48,352]{2,1,0:T(8,128)(2,1)S(1)}, u32[]{:S(2)}, u32[]{:S(2)}) collective-permute-start(bf16[4,48,352]{2,1,0:T(8,128)(2,1)S(1)} %get-tuple-element.60), channel_id=1, source_target_pairs={{30,8},{28,10},{26,12},{24,14},{31,9},{29,11},{27,13},{25,15}} | collective-permute-start | bytes 405512 | tf_op jit(solution)/shard_map/ppermute | solution.py:412
  8.6 4.3 %collective-permute-start.2 = (bf16[4,48,352]{2,1,0:T(8,128)(2,1)S(1)}, bf16[4,48,352]{2,1,0:T(8,128)(2,1)S(1)}, u32[]{:S(2)}, u32[]{:S(2)}) collective-permute-start(bf16[4,48,352]{2,1,0:T(8,128)(2,1)S(1)} %get-tuple-element.57), channel_id=1, source_target_pairs={{26,8},{24,10},{30,12},{28,14},{27,9},{25,11},{31,13},{29,15}} | collective-permute-start | bytes 405512 | tf_op jit(solution)/shard_map/ppermute | solution.py:412
  10.3 0.7 collective-permute-start.3
  12.9 1.7 %collective-permute-start.5 = (bf16[2,16,48,352]{3,2,1,0:T(8,128)(2,1)S(1)}, bf16[2,16,48,352]{3,2,1,0:T(8,128)(2,1)S(1)}, u32[]{:S(2)}, u32[]{:S(2)}) collective-permute-start(bf16[2,16,48,352]{3,2,1,0:T(8,128)(2,1)S(1)} %last_piece.2), channel_id=1, source_target_pairs={{8,0},{9,1},{10,2},{11,3},{12,4},{13,5},{14,6},{15,7}} | collective-permute-start | bytes 3244040 | tf_op jit(solution)/shard_map/ppermute | solution.py:439
  13.9 0.8 collective-permute-start.6
  14.7 6.0 %collective-permute-start.7 = (bf16[16,48,352]{2,1,0:T(8,128)(2,1)S(1)}, bf16[16,48,352]{2,1,0:T(8,128)(2,1)S(1)}, u32[]{:S(2)}, u32[]{:S(2)}) collective-permute-start(bf16[16,48,352]{2,1,0:T(8,128)(2,1)S(1)} %down.1.prev.refs_4_), channel_id=1, source_target_pairs={{0,8},{1,9},{2,10},{3,11},{4,12},{5,13},{6,14},{7,15}} | collective-permute-start | bytes 1622024 | tf_op jit(solution)/shard_map/ppermute | solution.py:439
  15.4 14.0 %collective-permute-start.8 = (bf16[352,704]{1,0:T(8,128)(2,1)S(1)}, bf16[352,704]{1,0:T(8,128)(2,1)S(1)}, u32[]{:S(2)}, u32[]{:S(2)}) collective-permute-start(bf16[352,704]{1,0:T(8,128)(2,1)S(1)} %bitcast.27), channel_id=1, source_target_pairs={{8,9},{9,8},{24,25},{25,24},{10,11},{11,10},{26,27},{27,26},{12,13... | collective-permute-start | bytes 1486856 | tf_op jit(solution)/shard_map/ppermute | solution.py:417
  17.6 17.7 %collective-permute-start.9 = (bf16[704,352]{1,0:T(8,128)(2,1)S(1)}, bf16[704,352]{1,0:T(8,128)(2,1)S(1)}, u32[]{:S(2)}, u32[]{:S(2)}) collective-permute-start(bf16[704,352]{1,0:T(8,128)(2,1)S(1)} %bitcast.15), channel_id=1, source_target_pairs={{8,9},{9,8},{24,25},{25,24},{10,11},{11,10},{26,27},{27,26},{12,13... | collective-permute-start | bytes 1486856 | tf_op jit(solution)/shard_map/ppermute | solution.py:417
  35.2 2.8 %collective-permute-start.10 = (bf16[4,48,352]{2,1,0:T(8,128)(2,1)S(1)}, bf16[4,48,352]{2,1,0:T(8,128)(2,1)S(1)}, u32[]{:S(2)}, u32[]{:S(2)}) collective-permute-start(bf16[4,48,352]{2,1,0:T(8,128)(2,1)S(1)} %down_piece.8.refs_0_), channel_id=1, source_target_pairs={{8,16},{9,17},{10,18},{11,19},{12,20},{13,21},{14,22},{15,23}} | collective-permute-start | bytes 405512 | tf_op jit(solution)/shard_map/ppermute | solution.py:439
  36.0 2.1 %collective-permute-start.11 = (bf16[4,48,352]{2,1,0:T(8,128)(2,1)S(1)}, bf16[4,48,352]{2,1,0:T(8,128)(2,1)S(1)}, u32[]{:S(2)}, u32[]{:S(2)}) collective-permute-start(bf16[4,48,352]{2,1,0:T(8,128)(2,1)S(1)} %down_piece.9.refs_1_), channel_id=1, source_target_pairs={{8,16},{9,17},{10,18},{11,19},{12,20},{13,21},{14,22},{15,23}} | collective-permute-start | bytes 405512 | tf_op jit(solution)/shard_map/ppermute | solution.py:439
  36.7 1.5 %collective-permute-start.12 = (bf16[4,48,352]{2,1,0:T(8,128)(2,1)S(1)}, bf16[4,48,352]{2,1,0:T(8,128)(2,1)S(1)}, u32[]{:S(2)}, u32[]{:S(2)}) collective-permute-start(bf16[4,48,352]{2,1,0:T(8,128)(2,1)S(1)} %down_piece.10.refs_2_), channel_id=1, source_target_pairs={{8,16},{9,17},{10,18},{11,19},{12,20},{13,21},{14,22},{15,23}} | collective-permute-start | bytes 405512 | tf_op jit(solution)/shard_map/ppermute | solution.py:439
  37.4 0.8 collective-permute-start.13
  38.4 23.1 %collective-permute-start.14 = (bf16[16,48,352]{2,1,0:T(8,128)(2,1)S(1)}, bf16[16,48,352]{2,1,0:T(8,128)(2,1)S(1)}, u32[]{:S(2)}, u32[]{:S(2)}) collective-permute-start(bf16[16,48,352]{2,1,0:T(8,128)(2,1)S(1)} %mlp.1.prev), channel_id=1, source_target_pairs={{16,24},{17,25},{18,26},{19,27},{20,28},{21,29},{22,30},{23,31}} | collective-permute-start | bytes 1622024 | tf_op jit(solution)/shard_map/ppermute | solution.py:439
  71.5 6.5 %collective-permute-start.15 = (bf16[4,48,352]{2,1,0:T(8,128)(2,1)S(1)}, bf16[4,48,352]{2,1,0:T(8,128)(2,1)S(1)}, u32[]{:S(2)}, u32[]{:S(2)}) collective-permute-start(bf16[4,48,352]{2,1,0:T(8,128)(2,1)S(1)} %down_piece.13), channel_id=1, source_target_pairs={{0,4},{2,6},{4,0},{6,2},{1,5},{3,7},{5,1},{7,3},{8,12},{10,14},{12... | collective-permute-start | bytes 405512 | tf_op jit(solution)/shard_map/ppermute | solution.py:556
  74.4 6.1 %collective-permute-start.16 = (bf16[4,48,352]{2,1,0:T(8,128)(2,1)S(1)}, bf16[4,48,352]{2,1,0:T(8,128)(2,1)S(1)}, u32[]{:S(2)}, u32[]{:S(2)}) collective-permute-start(bf16[4,48,352]{2,1,0:T(8,128)(2,1)S(1)} %down_piece.14), channel_id=1, source_target_pairs={{0,6},{2,4},{4,2},{6,0},{1,7},{3,5},{5,3},{7,1},{8,14},{10,12},{12... | collective-permute-start | bytes 405512 | tf_op jit(solution)/shard_map/ppermute | solution.py:556
  76.3 5.6 %collective-permute-start.17 = (bf16[4,48,352]{2,1,0:T(8,128)(2,1)S(1)}, bf16[4,48,352]{2,1,0:T(8,128)(2,1)S(1)}, u32[]{:S(2)}, u32[]{:S(2)}) collective-permute-start(bf16[4,48,352]{2,1,0:T(8,128)(2,1)S(1)} %down_piece.15), channel_id=1, source_target_pairs={{0,2},{2,0},{4,6},{6,4},{1,3},{3,1},{5,7},{7,5},{8,10},{10,8},{12,... | collective-permute-start | bytes 405512 | tf_op jit(solution)/shard_map/ppermute | solution.py:556
  (4 other events, 22.7 us)

commit v12 on v10

--- a/solution.py
+++ b/solution.py
@@ -13,7 +13,7 @@
 VMEM_BYTES = 20 * 1024 * 1024
 REACH = 3
 CHUNK = 4
-NORM_ROWS = 4
+NORM_ROWS = 8
 IN_ORDER = (0, 1, 2, 3)
 VECTORS = 56
 
@@ -136,10 +136,10 @@
             w_in[:, pl.ds(start, count)],
             preferred_element_type=jnp.float32,
         )
-        active = gelu(raised + bias[0:1, pl.ds(start, count)]).astype(jnp.bfloat16)
-        act[:, pl.ds(start, count)] = active
-        wide = active.astype(jnp.float32)
-        ssq[:, pl.ds(start, count)] = jnp.sum((wide * wide).reshape(cells // 8, 8, count), axis=0)
+        active = gelu(raised + bias[0:1, pl.ds(start, count)])
+        act[:, pl.ds(start, count)] = active.astype(jnp.bfloat16)
+        squares = (active * active).reshape(cells // 8, 8, count)
+        ssq[:, pl.ds(start, count)] = jnp.sum(squares, axis=0)
 
     def full(n, carry):
         units(pl.multiple_of(n * step, step), step)

time: 81 us -> 79.4 us (0.980)
  waiting for transfers between devices: 42 us -> 41.1 us
    ppermute x8, waiting for transfers between devices: 20.6 us -> 19.7 us  [send(): return lax.ppermute(x, 'section', [(start, end)])]
  transfers between devices with their start and end apart: 18 -> 18, of which waited for: 7 -> 7; matrix products, arithmetic and copies ran while one was open for 1% -> 2% of each run, Pallas kernels for 2% -> 2%
where the time goes in v12:
time: 79.4 us; the launch traced here: 79 us
  waiting for transfers between devices  41.1 us (52%)
  starting transfers between devices  24.9 us (31%)
  Pallas kernels  11 us (14%)
  local copies, waits for them, and re-layouts  1.4 us (2%)
    ppermute x8, waiting for transfers between devices, send(): return lax.ppermute(x, 'section', [(start, end)])  19.7 us
    ppermute x4, waiting for transfers between devices, other_half(): return lax.ppermute(x, ('section', 'dp'), pairs)  14.5 us
    pallas_call x26, Pallas kernels, call(): pl.pallas_call(functools.partial(kernel, **static), out_shape=out, in_spe...  11 us
    ppermute x3, starting transfers between devices, image_plan(): piece = lax.ppermute(piece, ('section', 'row'), pairs)  7.8 us
    ppermute x4, starting transfers between devices, other_half(): return lax.ppermute(x, ('section', 'dp'), pairs)  6.79 us
    ppermute x8, starting transfers between devices, send(): return lax.ppermute(x, 'section', [(start, end)])  6.2 us
    ppermute x3, waiting for transfers between devices, image_plan(): lax.ppermute(piece, 'row', [(p, p ^ order[n]) for p in range(count)])  5.04 us
    ppermute x3, starting transfers between devices, image_plan(): lax.ppermute(piece, 'row', [(p, p ^ order[n]) for p in range(count)])  4.12 us
  transfers between devices with their start and end apart: 18, of which 7 were waited for; matrix products, arithmetic and copies ran while one was open for 2% of the time, Pallas kernels for 2%

profile of v12, /device:TPU:7, one launch (start us, length us, event | category | flops | bytes accessed | tf_op | source)
XLA Modules:
  0.0 79.0 jit_solution(9151743151651019379)
XLA Ops:
  0.1 0.8 %collective-permute-start.4 = (bf16[352,704]{1,0:T(8,128)(2,1)}, bf16[352,704]{1,0:T(8,128)(2,1)S(1)}, u32[]{:S(2)}, u32[]{:S(2)}) collective-permute-start(bf16[352,704]{1,0:T(8,128)(2,1)} %bitcast.25), channel_id=1, source_target_pairs={{0,1},{1,0},{16,17},{17,16},{2,3},{3,2},{18,19},{19,18},{4,5},{5,4... | collective-permute-start | bytes 1486856 | tf_op jit(solution)/shard_map/ppermute | solution.py:404
  0.9 1.2 %dynamic-slice_bitcast_fusion = (bf16[4,48,352]{2,1,0:T(8,128)(2,1)S(1)}, bf16[4,48,352]{2,1,0:T(8,128)(2,1)S(1)}, bf16[4,48,352]{2,1,0:T(8,128)(2,1)S(1)}, bf16[4,48,352]{2,1,0:T(8,128)(2,1)S(1)}) fusion(bf16[4,1,4,48,352]{4,3,2,1,0:T(8,128)(2,1)} %param.11, s32[]{:T(128)S(6)} %select_n.16, s32[]{:T(128)S(6)} %select_n.14, s32[]{:T(128)S(6)} %select_n.13, ...), kind=kLoop, calls=%fused_computation | loop fusion | bytes 1081360 | tf_op jit(solution)/shard_map/squeeze | solution.py:396
  2.1 4.2 %collective-permute-start = (bf16[4,48,352]{2,1,0:T(8,128)(2,1)S(1)}, bf16[4,48,352]{2,1,0:T(8,128)(2,1)S(1)}, u32[]{:S(2)}, u32[]{:S(2)}) collective-permute-start(bf16[4,48,352]{2,1,0:T(8,128)(2,1)S(1)} %get-tuple-element.58), channel_id=1, source_target_pairs={{28,8},{30,10},{24,12},{26,14},{29,9},{31,11},{25,13},{27,15}} | collective-permute-start | bytes 405512 | tf_op jit(solution)/shard_map/ppermute | solution.py:399
  6.3 2.3 %collective-permute-start.1 = (bf16[4,48,352]{2,1,0:T(8,128)(2,1)S(1)}, bf16[4,48,352]{2,1,0:T(8,128)(2,1)S(1)}, u32[]{:S(2)}, u32[]{:S(2)}) collective-permute-start(bf16[4,48,352]{2,1,0:T(8,128)(2,1)S(1)} %get-tuple-element.60), channel_id=1, source_target_pairs={{30,8},{28,10},{26,12},{24,14},{31,9},{29,11},{27,13},{25,15}} | collective-permute-start | bytes 405512 | tf_op jit(solution)/shard_map/ppermute | solution.py:399
  8.6 1.3 %collective-permute-start.2 = (bf16[4,48,352]{2,1,0:T(8,128)(2,1)S(1)}, bf16[4,48,352]{2,1,0:T(8,128)(2,1)S(1)}, u32[]{:S(2)}, u32[]{:S(2)}) collective-permute-start(bf16[4,48,352]{2,1,0:T(8,128)(2,1)S(1)} %get-tuple-element.57), channel_id=1, source_target_pairs={{26,8},{24,10},{30,12},{28,14},{27,9},{25,11},{31,13},{29,15}} | collective-permute-start | bytes 405512 | tf_op jit(solution)/shard_map/ppermute | solution.py:399
  11.0 1.8 %collective-permute-done.2.refs_3_ = bf16[4,48,352]{2,1,0:T(8,128)(2,1)S(1)} collective-permute-done((bf16[4,48,352]{2,1,0:T(8,128)(2,1)S(1)}, bf16[4,48,352]{2,1,0:T(8,128)(2,1)S(1)}, u32[]{:S(2)}, u32[]{:S(2)}) %collective-permute-start.2) | collective-permute-done | bytes 135200 | tf_op jit(solution)/shard_map/ppermute | solution.py:399
  12.9 0.9 %collective-permute-start.5 = (bf16[2,16,48,352]{3,2,1,0:T(8,128)(2,1)S(1)}, bf16[2,16,48,352]{3,2,1,0:T(8,128)(2,1)S(1)}, u32[]{:S(2)}, u32[]{:S(2)}) collective-permute-start(bf16[2,16,48,352]{3,2,1,0:T(8,128)(2,1)S(1)} %last_piece.2), channel_id=1, source_target_pairs={{8,0},{9,1},{10,2},{11,3},{12,4},{13,5},{14,6},{15,7}} | collective-permute-start | bytes 3244040 | tf_op jit(solution)/shard_map/ppermute | solution.py:426
  13.9 0.7 collective-permute-start.6
  14.7 0.7 collective-permute-start.7
  15.4 2.1 %collective-permute-start.8 = (bf16[352,704]{1,0:T(8,128)(2,1)S(1)}, bf16[352,704]{1,0:T(8,128)(2,1)S(1)}, u32[]{:S(2)}, u32[]{:S(2)}) collective-permute-start(bf16[352,704]{1,0:T(8,128)(2,1)S(1)} %bitcast.27), channel_id=1, source_target_pairs={{8,9},{9,8},{24,25},{25,24},{10,11},{11,10},{26,27},{27,26},{12,13... | collective-permute-start | bytes 1486856 | tf_op jit(solution)/shard_map/ppermute | solution.py:404
  17.6 3.1 %collective-permute-start.9 = (bf16[704,352]{1,0:T(8,128)(2,1)S(1)}, bf16[704,352]{1,0:T(8,128)(2,1)S(1)}, u32[]{:S(2)}, u32[]{:S(2)}) collective-permute-start(bf16[704,352]{1,0:T(8,128)(2,1)S(1)} %bitcast.15), channel_id=1, source_target_pairs={{8,9},{9,8},{24,25},{25,24},{10,11},{11,10},{26,27},{27,26},{12,13... | collective-permute-start | bytes 1486856 | tf_op jit(solution)/shard_map/ppermute | solution.py:404
  20.8 8.7 %collective-permute-done.8.w_in.in_b = bf16[352,704]{1,0:T(8,128)(2,1)S(1)} collective-permute-done((bf16[352,704]{1,0:T(8,128)(2,1)S(1)}, bf16[352,704]{1,0:T(8,128)(2,1)S(1)}, u32[]{:S(2)}, u32[]{:S(2)}) %collective-permute-start.8) | collective-permute-done | bytes 495648 | tf_op jit(solution)/shard_map/ppermute | solution.py:404
  29.4 5.8 %collective-permute-done.9.out_b = bf16[704,352]{1,0:T(8,128)(2,1)S(1)} collective-permute-done((bf16[704,352]{1,0:T(8,128)(2,1)S(1)}, bf16[704,352]{1,0:T(8,128)(2,1)S(1)}, u32[]{:S(2)}, u32[]{:S(2)}) %collective-permute-start.9) | collective-permute-done | bytes 495648 | tf_op jit(solution)/shard_map/ppermute | solution.py:404
  35.2 0.7 collective-permute-start.10
  36.0 0.7 collective-permute-start.11
  38.4 1.3 %collective-permute-start.14 = (bf16[16,48,352]{2,1,0:T(8,128)(2,1)S(1)}, bf16[16,48,352]{2,1,0:T(8,128)(2,1)S(1)}, u32[]{:S(2)}, u32[]{:S(2)}) collective-permute-start(bf16[16,48,352]{2,1,0:T(8,128)(2,1)S(1)} %mlp.1.prev), channel_id=1, source_target_pairs={{16,24},{17,25},{18,26},{19,27},{20,28},{21,29},{22,30},{23,31}} | collective-permute-start | bytes 1622024 | tf_op jit(solution)/shard_map/ppermute | solution.py:426
  39.7 19.7 %collective-permute-done.14.x = bf16[16,48,352]{2,1,0:T(8,128)(2,1)S(1)} collective-permute-done((bf16[16,48,352]{2,1,0:T(8,128)(2,1)S(1)}, bf16[16,48,352]{2,1,0:T(8,128)(2,1)S(1)}, u32[]{:S(2)}, u32[]{:S(2)}) %collective-permute-start.14) | collective-permute-done | bytes 540704 | tf_op jit(solution)/shard_map/ppermute | solution.py:426
  59.4 7.5 %conv_up.1 = (bf16[768,704]{1,0:T(8,128)(2,1)S(1)}, bf16[768,704]{1,0:T(8,128)(2,1)S(1)}, f32[2,1,704]{2,1,0:T(1,128)S(1)}) custom-call(s32[1]{0:T(128)} %bitcast.1.section, bf16[16,48,352]{2,1,0:T(8,128)(2,1)S(1)} %collective-permute-done.14.x, f32[64,384]{1,0:T(8,128)S(1)} %get-tuple-element.31.cpar.refs_7_, bf16[352,704]{1,0:T(8,128)(2,1)S(1)} %bitcast.30, ...), custom_call_target="tpu_custom_call" | custom-call | flops 761266176 | bytes 1647108 | tf_op jit(solution)/shard_map/conv_up/pallas_call | solution.py:340
  67.4 2.7 %collective-permute-start.15 = (bf16[4,48,352]{2,1,0:T(8,128)(2,1)S(1)}, bf16[4,48,352]{2,1,0:T(8,128)(2,1)S(1)}, u32[]{:S(2)}, u32[]{:S(2)}) collective-permute-start(bf16[4,48,352]{2,1,0:T(8,128)(2,1)S(1)} %down_piece.13), channel_id=1, source_target_pairs={{0,4},{2,6},{4,0},{6,2},{1,5},{3,7},{5,1},{7,3},{8,12},{10,14},{12... | collective-permute-start | bytes 405512 | tf_op jit(solution)/shard_map/ppermute | solution.py:543
  70.6 1.3 %collective-permute-start.16 = (bf16[4,48,352]{2,1,0:T(8,128)(2,1)S(1)}, bf16[4,48,352]{2,1,0:T(8,128)(2,1)S(1)}, u32[]{:S(2)}, u32[]{:S(2)}) collective-permute-start(bf16[4,48,352]{2,1,0:T(8,128)(2,1)S(1)} %down_piece.14), channel_id=1, source_target_pairs={{0,6},{2,4},{4,2},{6,0},{1,7},{3,5},{5,3},{7,1},{8,14},{10,12},{12... | collective-permute-start | bytes 405512 | tf_op jit(solution)/shard_map/ppermute | solution.py:543
  73.0 1.2 %collective-permute-done.15.refs_1_ = bf16[4,48,352]{2,1,0:T(8,128)(2,1)S(1)} collective-permute-done((bf16[4,48,352]{2,1,0:T(8,128)(2,1)S(1)}, bf16[4,48,352]{2,1,0:T(8,128)(2,1)S(1)}, u32[]{:S(2)}, u32[]{:S(2)}) %collective-permute-start.15) | collective-permute-done | bytes 135200 | tf_op jit(solution)/shard_map/ppermute | solution.py:543
  74.2 2.4 %collective-permute-done.16.refs_2_ = bf16[4,48,352]{2,1,0:T(8,128)(2,1)S(1)} collective-permute-done((bf16[4,48,352]{2,1,0:T(8,128)(2,1)S(1)}, bf16[4,48,352]{2,1,0:T(8,128)(2,1)S(1)}, u32[]{:S(2)}, u32[]{:S(2)}) %collective-permute-start.16) | collective-permute-done | bytes 135200 | tf_op jit(solution)/shard_map/ppermute | solution.py:543
  76.7 1.4 %collective-permute-done.17.refs_3_ = bf16[4,48,352]{2,1,0:T(8,128)(2,1)S(1)} collective-permute-done((bf16[4,48,352]{2,1,0:T(8,128)(2,1)S(1)}, bf16[4,48,352]{2,1,0:T(8,128)(2,1)S(1)}, u32[]{:S(2)}, u32[]{:S(2)}) %collective-permute-start.17) | collective-permute-done | bytes 135200 | tf_op jit(solution)/shard_map/ppermute | solution.py:543
  78.0 0.8 %place.1 = bf16[1,4,1,4,48,352]{5,4,3,2,1,0:T(8,128)(2,1)} custom-call(s32[1]{0:T(128)} %bitcast.me, bf16[4,48,352]{2,1,0:T(8,128)(2,1)S(1)} %down_piece.12.refs_0_, bf16[4,48,352]{2,1,0:T(8,128)(2,1)S(1)} %collective-permute-done.15.refs_1_, bf16[4,48,352]{2,1,0:T(8,128)(2,1)S(1)} %collective-permute-done.16.refs_2_, ...), custom_call_target="tpu_custom_call" | custom-call | bytes 540676 | tf_op jit(solution)/shard_map/place/pallas_call | solution.py:340
  (59 shorter events, 5.0 us)
Async XLA Ops:
  0.0 10.0 %copy-start.4 = (bf16[1,1408]{1,0:T(2,128)(2,1)S(1)}, bf16[1,1408]{1,0:T(2,128)(2,1)}, u32[]{:S(2)}) copy-start(bf16[1,1408]{1,0:T(2,128)(2,1)} %refs_5_.1) | copy-start | bytes 8452
  0.0 10.0 %copy-start.3 = (bf16[1,1408]{1,0:T(2,128)(2,1)S(1)}, bf16[1,1408]{1,0:T(2,128)(2,1)}, u32[]{:S(2)}) copy-start(bf16[1,1408]{1,0:T(2,128)(2,1)} %refs_4_.1) | copy-start | bytes 8452
  0.0 10.0 %copy-start.8 = (bf16[1,352]{1,0:T(2,128)(2,1)S(1)}, bf16[1,352]{1,0:T(2,128)(2,1)}, u32[]{:S(2)}) copy-start(bf16[1,352]{1,0:T(2,128)(2,1)} %refs_2_.1) | copy-start | bytes 2116
  0.0 10.0 %copy-start.7 = (bf16[1,352]{1,0:T(2,128)(2,1)S(1)}, bf16[1,352]{1,0:T(2,128)(2,1)}, u32[]{:S(2)}) copy-start(bf16[1,352]{1,0:T(2,128)(2,1)} %refs_1_.1) | copy-start | bytes 2116
  0.0 10.0 %copy-start.6 = (bf16[1,352]{1,0:T(2,128)(2,1)S(1)}, bf16[1,352]{1,0:T(2,128)(2,1)}, u32[]{:S(2)}) copy-start(bf16[1,352]{1,0:T(2,128)(2,1)} %refs_0_.1) | copy-start | bytes 2116
  0.0 10.0 %copy-start.2 = (bf16[1,7,7,352]{3,2,1,0:T(8,128)(2,1)S(1)}, bf16[1,7,7,352]{3,2,1,0:T(8,128)(2,1)}, u32[]{:S(2)}) copy-start(bf16[1,7,7,352]{3,2,1,0:T(8,128)(2,1)} %kernel.1) | copy-start | bytes 103492
  0.1 12.8 %collective-permute-start.4 = (bf16[352,704]{1,0:T(8,128)(2,1)}, bf16[352,704]{1,0:T(8,128)(2,1)S(1)}, u32[]{:S(2)}, u32[]{:S(2)}) collective-permute-start(bf16[352,704]{1,0:T(8,128)(2,1)} %bitcast.25), channel_id=1, source_target_pairs={{0,1},{1,0},{16,17},{17,16},{2,3},{3,2},{18,19},{19,18},{4,5},{5,4... | collective-permute-start | bytes 1486856 | tf_op jit(solution)/shard_map/ppermute | solution.py:404
  2.1 8.9 %collective-permute-start = (bf16[4,48,352]{2,1,0:T(8,128)(2,1)S(1)}, bf16[4,48,352]{2,1,0:T(8,128)(2,1)S(1)}, u32[]{:S(2)}, u32[]{:S(2)}) collective-permute-start(bf16[4,48,352]{2,1,0:T(8,128)(2,1)S(1)} %get-tuple-element.58), channel_id=1, source_target_pairs={{28,8},{30,10},{24,12},{26,14},{29,9},{31,11},{25,13},{27,15}} | collective-permute-start | bytes 405512 | tf_op jit(solution)/shard_map/ppermute | solution.py:399
  6.3 4.7 %collective-permute-start.1 = (bf16[4,48,352]{2,1,0:T(8,128)(2,1)S(1)}, bf16[4,48,352]{2,1,0:T(8,128)(2,1)S(1)}, u32[]{:S(2)}, u32[]{:S(2)}) collective-permute-start(bf16[4,48,352]{2,1,0:T(8,128)(2,1)S(1)} %get-tuple-element.60), channel_id=1, source_target_pairs={{30,8},{28,10},{26,12},{24,14},{31,9},{29,11},{27,13},{25,15}} | collective-permute-start | bytes 405512 | tf_op jit(solution)/shard_map/ppermute | solution.py:399
  8.6 4.3 %collective-permute-start.2 = (bf16[4,48,352]{2,1,0:T(8,128)(2,1)S(1)}, bf16[4,48,352]{2,1,0:T(8,128)(2,1)S(1)}, u32[]{:S(2)}, u32[]{:S(2)}) collective-permute-start(bf16[4,48,352]{2,1,0:T(8,128)(2,1)S(1)} %get-tuple-element.57), channel_id=1, source_target_pairs={{26,8},{24,10},{30,12},{28,14},{27,9},{25,11},{31,13},{29,15}} | collective-permute-start | bytes 405512 | tf_op jit(solution)/shard_map/ppermute | solution.py:399
  10.3 0.7 collective-permute-start.3
  12.9 1.7 %collective-permute-start.5 = (bf16[2,16,48,352]{3,2,1,0:T(8,128)(2,1)S(1)}, bf16[2,16,48,352]{3,2,1,0:T(8,128)(2,1)S(1)}, u32[]{:S(2)}, u32[]{:S(2)}) collective-permute-start(bf16[2,16,48,352]{3,2,1,0:T(8,128)(2,1)S(1)} %last_piece.2), channel_id=1, source_target_pairs={{8,0},{9,1},{10,2},{11,3},{12,4},{13,5},{14,6},{15,7}} | collective-permute-start | bytes 3244040 | tf_op jit(solution)/shard_map/ppermute | solution.py:426
  13.9 0.8 collective-permute-start.6
  14.7 6.0 %collective-permute-start.7 = (bf16[16,48,352]{2,1,0:T(8,128)(2,1)S(1)}, bf16[16,48,352]{2,1,0:T(8,128)(2,1)S(1)}, u32[]{:S(2)}, u32[]{:S(2)}) collective-permute-start(bf16[16,48,352]{2,1,0:T(8,128)(2,1)S(1)} %down.1.prev.refs_4_), channel_id=1, source_target_pairs={{0,8},{1,9},{2,10},{3,11},{4,12},{5,13},{6,14},{7,15}} | collective-permute-start | bytes 1622024 | tf_op jit(solution)/shard_map/ppermute | solution.py:426
  15.4 14.0 %collective-permute-start.8 = (bf16[352,704]{1,0:T(8,128)(2,1)S(1)}, bf16[352,704]{1,0:T(8,128)(2,1)S(1)}, u32[]{:S(2)}, u32[]{:S(2)}) collective-permute-start(bf16[352,704]{1,0:T(8,128)(2,1)S(1)} %bitcast.27), channel_id=1, source_target_pairs={{8,9},{9,8},{24,25},{25,24},{10,11},{11,10},{26,27},{27,26},{12,13... | collective-permute-start | bytes 1486856 | tf_op jit(solution)/shard_map/ppermute | solution.py:404
  17.6 17.7 %collective-permute-start.9 = (bf16[704,352]{1,0:T(8,128)(2,1)S(1)}, bf16[704,352]{1,0:T(8,128)(2,1)S(1)}, u32[]{:S(2)}, u32[]{:S(2)}) collective-permute-start(bf16[704,352]{1,0:T(8,128)(2,1)S(1)} %bitcast.15), channel_id=1, source_target_pairs={{8,9},{9,8},{24,25},{25,24},{10,11},{11,10},{26,27},{27,26},{12,13... | collective-permute-start | bytes 1486856 | tf_op jit(solution)/shard_map/ppermute | solution.py:404
  35.2 2.8 %collective-permute-start.10 = (bf16[4,48,352]{2,1,0:T(8,128)(2,1)S(1)}, bf16[4,48,352]{2,1,0:T(8,128)(2,1)S(1)}, u32[]{:S(2)}, u32[]{:S(2)}) collective-permute-start(bf16[4,48,352]{2,1,0:T(8,128)(2,1)S(1)} %down_piece.8.refs_0_), channel_id=1, source_target_pairs={{8,16},{9,17},{10,18},{11,19},{12,20},{13,21},{14,22},{15,23}} | collective-permute-start | bytes 405512 | tf_op jit(solution)/shard_map/ppermute | solution.py:426
  36.0 2.1 %collective-permute-start.11 = (bf16[4,48,352]{2,1,0:T(8,128)(2,1)S(1)}, bf16[4,48,352]{2,1,0:T(8,128)(2,1)S(1)}, u32[]{:S(2)}, u32[]{:S(2)}) collective-permute-start(bf16[4,48,352]{2,1,0:T(8,128)(2,1)S(1)} %down_piece.9.refs_1_), channel_id=1, source_target_pairs={{8,16},{9,17},{10,18},{11,19},{12,20},{13,21},{14,22},{15,23}} | collective-permute-start | bytes 405512 | tf_op jit(solution)/shard_map/ppermute | solution.py:426
  36.7 1.5 %collective-permute-start.12 = (bf16[4,48,352]{2,1,0:T(8,128)(2,1)S(1)}, bf16[4,48,352]{2,1,0:T(8,128)(2,1)S(1)}, u32[]{:S(2)}, u32[]{:S(2)}) collective-permute-start(bf16[4,48,352]{2,1,0:T(8,128)(2,1)S(1)} %down_piece.10.refs_2_), channel_id=1, source_target_pairs={{8,16},{9,17},{10,18},{11,19},{12,20},{13,21},{14,22},{15,23}} | collective-permute-start | bytes 405512 | tf_op jit(solution)/shard_map/ppermute | solution.py:426
  37.4 0.8 collective-permute-start.13
  38.4 21.0 %collective-permute-start.14 = (bf16[16,48,352]{2,1,0:T(8,128)(2,1)S(1)}, bf16[16,48,352]{2,1,0:T(8,128)(2,1)S(1)}, u32[]{:S(2)}, u32[]{:S(2)}) collective-permute-start(bf16[16,48,352]{2,1,0:T(8,128)(2,1)S(1)} %mlp.1.prev), channel_id=1, source_target_pairs={{16,24},{17,25},{18,26},{19,27},{20,28},{21,29},{22,30},{23,31}} | collective-permute-start | bytes 1622024 | tf_op jit(solution)/shard_map/ppermute | solution.py:426
  67.4 6.8 %collective-permute-start.15 = (bf16[4,48,352]{2,1,0:T(8,128)(2,1)S(1)}, bf16[4,48,352]{2,1,0:T(8,128)(2,1)S(1)}, u32[]{:S(2)}, u32[]{:S(2)}) collective-permute-start(bf16[4,48,352]{2,1,0:T(8,128)(2,1)S(1)} %down_piece.13), channel_id=1, source_target_pairs={{0,4},{2,6},{4,0},{6,2},{1,5},{3,7},{5,1},{7,3},{8,12},{10,14},{12... | collective-permute-start | bytes 405512 | tf_op jit(solution)/shard_map/ppermute | solution.py:543
  70.6 6.1 %collective-permute-start.16 = (bf16[4,48,352]{2,1,0:T(8,128)(2,1)S(1)}, bf16[4,48,352]{2,1,0:T(8,128)(2,1)S(1)}, u32[]{:S(2)}, u32[]{:S(2)}) collective-permute-start(bf16[4,48,352]{2,1,0:T(8,128)(2,1)S(1)} %down_piece.14), channel_id=1, source_target_pairs={{0,6},{2,4},{4,2},{6,0},{1,7},{3,5},{5,3},{7,1},{8,14},{10,12},{12... | collective-permute-start | bytes 405512 | tf_op jit(solution)/shard_map/ppermute | solution.py:543
  72.4 5.6 %collective-permute-start.17 = (bf16[4,48,352]{2,1,0:T(8,128)(2,1)S(1)}, bf16[4,48,352]{2,1,0:T(8,128)(2,1)S(1)}, u32[]{:S(2)}, u32[]{:S(2)}) collective-permute-start(bf16[4,48,352]{2,1,0:T(8,128)(2,1)S(1)} %down_piece.15), channel_id=1, source_target_pairs={{0,2},{2,0},{4,6},{6,4},{1,3},{3,1},{5,7},{7,5},{8,10},{10,8},{12,... | collective-permute-start | bytes 405512 | tf_op jit(solution)/shard_map/ppermute | solution.py:543
  (4 other events, 22.7 us)

commit v13 on v12

--- a/solution.py
+++ b/solution.py
@@ -25,9 +25,11 @@
     groups = lanes // LANES
     xp[...] = jnp.zeros(xp.shape, jnp.float32)
 
+    unroll = min(height, NORM_ROWS)
+
     def rows(n, carry):
-        for k in range(2):
-            r = 2 * n + k
+        for k in range(unroll):
+            r = unroll * n + k
             row = x[r].astype(jnp.float32)
             for g in range(groups):
                 at = slice(g * LANES, (g + 1) * LANES)
@@ -38,7 +40,7 @@
                     xs[r, q, :, at] = xp[k * groups + g, near, :]
         return carry
 
-    lax.fori_loop(0, height // 2, rows, 0)
+    lax.fori_loop(0, height // unroll, rows, 0)
 
 
 def conv(xs, cpar, cq):
@@ -141,14 +143,8 @@
         squares = (active * active).reshape(cells // 8, 8, count)
         ssq[:, pl.ds(start, count)] = jnp.sum(squares, axis=0)
 
-    def full(n, carry):
-        units(pl.multiple_of(n * step, step), step)
-        return carry
-
-    whole = half // step
-    lax.fori_loop(0, whole, full, 0)
-    if half % step:
-        units(whole * step, half % step)
+    for start in range(0, half, step):
+        units(start, min(step, half - start))
 
 
 def norm_scale(ssqs, fvec, scale):

time: 79.4 us -> 78.6 us (0.990)
  no operation moved by 1% of the time
where the time goes in v13:
time: 78.6 us; the launch traced here: 78.2 us
  waiting for transfers between devices  40.7 us (52%)
  starting transfers between devices  24.9 us (32%)
  Pallas kernels  10.5 us (13%)
  local copies, waits for them, and re-layouts  1.4 us (2%)
    ppermute x8, waiting for transfers between devices, send(): return lax.ppermute(x, 'section', [(start, end)])  19.3 us
    ppermute x4, waiting for transfers between devices, other_half(): return lax.ppermute(x, ('section', 'dp'), pairs)  14.5 us
    pallas_call x26, Pallas kernels, call(): pl.pallas_call(functools.partial(kernel, **static), out_shape=out, in_spe...  10.5 us
    ppermute x3, starting transfers between devices, image_plan(): piece = lax.ppermute(piece, ('section', 'row'), pairs)  7.8 us
    ppermute x4, starting transfers between devices, other_half(): return lax.ppermute(x, ('section', 'dp'), pairs)  6.79 us
    ppermute x8, starting transfers between devices, send(): return lax.ppermute(x, 'section', [(start, end)])  6.2 us
    ppermute x3, waiting for transfers between devices, image_plan(): lax.ppermute(piece, 'row', [(p, p ^ order[n]) for p in range(count)])  5.06 us
    ppermute x3, starting transfers between devices, image_plan(): lax.ppermute(piece, 'row', [(p, p ^ order[n]) for p in range(count)])  4.1 us
  transfers between devices with their start and end apart: 18, of which 7 were waited for; matrix products, arithmetic and copies ran while one was open for 2% of the time, Pallas kernels for 2%

profile of v13, /device:TPU:7, one launch (start us, length us, event | category | flops | bytes accessed | tf_op | source)
XLA Modules:
  0.0 78.2 jit_solution(9926175114463538899)
XLA Ops:
  0.1 0.8 %collective-permute-start.4 = (bf16[352,704]{1,0:T(8,128)(2,1)}, bf16[352,704]{1,0:T(8,128)(2,1)S(1)}, u32[]{:S(2)}, u32[]{:S(2)}) collective-permute-start(bf16[352,704]{1,0:T(8,128)(2,1)} %bitcast.25), channel_id=1, source_target_pairs={{0,1},{1,0},{16,17},{17,16},{2,3},{3,2},{18,19},{19,18},{4,5},{5,4... | collective-permute-start | bytes 1486856 | tf_op jit(solution)/shard_map/ppermute | solution.py:400
  0.9 1.2 %dynamic-slice_bitcast_fusion = (bf16[4,48,352]{2,1,0:T(8,128)(2,1)S(1)}, bf16[4,48,352]{2,1,0:T(8,128)(2,1)S(1)}, bf16[4,48,352]{2,1,0:T(8,128)(2,1)S(1)}, bf16[4,48,352]{2,1,0:T(8,128)(2,1)S(1)}) fusion(bf16[4,1,4,48,352]{4,3,2,1,0:T(8,128)(2,1)} %param.11, s32[]{:T(128)S(6)} %select_n.16, s32[]{:T(128)S(6)} %select_n.14, s32[]{:T(128)S(6)} %select_n.13, ...), kind=kLoop, calls=%fused_computation | loop fusion | bytes 1081360 | tf_op jit(solution)/shard_map/squeeze | solution.py:392
  2.1 4.2 %collective-permute-start = (bf16[4,48,352]{2,1,0:T(8,128)(2,1)S(1)}, bf16[4,48,352]{2,1,0:T(8,128)(2,1)S(1)}, u32[]{:S(2)}, u32[]{:S(2)}) collective-permute-start(bf16[4,48,352]{2,1,0:T(8,128)(2,1)S(1)} %get-tuple-element.58), channel_id=1, source_target_pairs={{28,8},{30,10},{24,12},{26,14},{29,9},{31,11},{25,13},{27,15}} | collective-permute-start | bytes 405512 | tf_op jit(solution)/shard_map/ppermute | solution.py:395
  6.3 2.3 %collective-permute-start.1 = (bf16[4,48,352]{2,1,0:T(8,128)(2,1)S(1)}, bf16[4,48,352]{2,1,0:T(8,128)(2,1)S(1)}, u32[]{:S(2)}, u32[]{:S(2)}) collective-permute-start(bf16[4,48,352]{2,1,0:T(8,128)(2,1)S(1)} %get-tuple-element.60), channel_id=1, source_target_pairs={{30,8},{28,10},{26,12},{24,14},{31,9},{29,11},{27,13},{25,15}} | collective-permute-start | bytes 405512 | tf_op jit(solution)/shard_map/ppermute | solution.py:395
  8.6 1.3 %collective-permute-start.2 = (bf16[4,48,352]{2,1,0:T(8,128)(2,1)S(1)}, bf16[4,48,352]{2,1,0:T(8,128)(2,1)S(1)}, u32[]{:S(2)}, u32[]{:S(2)}) collective-permute-start(bf16[4,48,352]{2,1,0:T(8,128)(2,1)S(1)} %get-tuple-element.57), channel_id=1, source_target_pairs={{26,8},{24,10},{30,12},{28,14},{27,9},{25,11},{31,13},{29,15}} | collective-permute-start | bytes 405512 | tf_op jit(solution)/shard_map/ppermute | solution.py:395
  11.0 1.8 %collective-permute-done.2.refs_3_ = bf16[4,48,352]{2,1,0:T(8,128)(2,1)S(1)} collective-permute-done((bf16[4,48,352]{2,1,0:T(8,128)(2,1)S(1)}, bf16[4,48,352]{2,1,0:T(8,128)(2,1)S(1)}, u32[]{:S(2)}, u32[]{:S(2)}) %collective-permute-start.2) | collective-permute-done | bytes 135200 | tf_op jit(solution)/shard_map/ppermute | solution.py:395
  12.9 0.9 %collective-permute-start.5 = (bf16[2,16,48,352]{3,2,1,0:T(8,128)(2,1)S(1)}, bf16[2,16,48,352]{3,2,1,0:T(8,128)(2,1)S(1)}, u32[]{:S(2)}, u32[]{:S(2)}) collective-permute-start(bf16[2,16,48,352]{3,2,1,0:T(8,128)(2,1)S(1)} %last_piece.2), channel_id=1, source_target_pairs={{8,0},{9,1},{10,2},{11,3},{12,4},{13,5},{14,6},{15,7}} | collective-permute-start | bytes 3244040 | tf_op jit(solution)/shard_map/ppermute | solution.py:422
  13.9 0.7 collective-permute-start.6
  14.7 0.7 collective-permute-start.7
  15.4 2.1 %collective-permute-start.8 = (bf16[352,704]{1,0:T(8,128)(2,1)S(1)}, bf16[352,704]{1,0:T(8,128)(2,1)S(1)}, u32[]{:S(2)}, u32[]{:S(2)}) collective-permute-start(bf16[352,704]{1,0:T(8,128)(2,1)S(1)} %bitcast.27), channel_id=1, source_target_pairs={{8,9},{9,8},{24,25},{25,24},{10,11},{11,10},{26,27},{27,26},{12,13... | collective-permute-start | bytes 1486856 | tf_op jit(solution)/shard_map/ppermute | solution.py:400
  17.6 3.1 %collective-permute-start.9 = (bf16[704,352]{1,0:T(8,128)(2,1)S(1)}, bf16[704,352]{1,0:T(8,128)(2,1)S(1)}, u32[]{:S(2)}, u32[]{:S(2)}) collective-permute-start(bf16[704,352]{1,0:T(8,128)(2,1)S(1)} %bitcast.15), channel_id=1, source_target_pairs={{8,9},{9,8},{24,25},{25,24},{10,11},{11,10},{26,27},{27,26},{12,13... | collective-permute-start | bytes 1486856 | tf_op jit(solution)/shard_map/ppermute | solution.py:400
  20.8 8.7 %collective-permute-done.8.w_in.in_b = bf16[352,704]{1,0:T(8,128)(2,1)S(1)} collective-permute-done((bf16[352,704]{1,0:T(8,128)(2,1)S(1)}, bf16[352,704]{1,0:T(8,128)(2,1)S(1)}, u32[]{:S(2)}, u32[]{:S(2)}) %collective-permute-start.8) | collective-permute-done | bytes 495648 | tf_op jit(solution)/shard_map/ppermute | solution.py:400
  29.4 5.8 %collective-permute-done.9.out_b = bf16[704,352]{1,0:T(8,128)(2,1)S(1)} collective-permute-done((bf16[704,352]{1,0:T(8,128)(2,1)S(1)}, bf16[704,352]{1,0:T(8,128)(2,1)S(1)}, u32[]{:S(2)}, u32[]{:S(2)}) %collective-permute-start.9) | collective-permute-done | bytes 495648 | tf_op jit(solution)/shard_map/ppermute | solution.py:400
  35.2 0.7 collective-permute-start.10
  36.0 0.7 collective-permute-start.11
  38.4 1.3 %collective-permute-start.14 = (bf16[16,48,352]{2,1,0:T(8,128)(2,1)S(1)}, bf16[16,48,352]{2,1,0:T(8,128)(2,1)S(1)}, u32[]{:S(2)}, u32[]{:S(2)}) collective-permute-start(bf16[16,48,352]{2,1,0:T(8,128)(2,1)S(1)} %mlp.1.prev), channel_id=1, source_target_pairs={{16,24},{17,25},{18,26},{19,27},{20,28},{21,29},{22,30},{23,31}} | collective-permute-start | bytes 1622024 | tf_op jit(solution)/shard_map/ppermute | solution.py:422
  39.7 19.3 %collective-permute-done.14.x = bf16[16,48,352]{2,1,0:T(8,128)(2,1)S(1)} collective-permute-done((bf16[16,48,352]{2,1,0:T(8,128)(2,1)S(1)}, bf16[16,48,352]{2,1,0:T(8,128)(2,1)S(1)}, u32[]{:S(2)}, u32[]{:S(2)}) %collective-permute-start.14) | collective-permute-done | bytes 540704 | tf_op jit(solution)/shard_map/ppermute | solution.py:422
  59.0 7.0 %conv_up.1 = (bf16[768,704]{1,0:T(8,128)(2,1)S(1)}, bf16[768,704]{1,0:T(8,128)(2,1)S(1)}, f32[2,1,704]{2,1,0:T(1,128)S(1)}) custom-call(s32[1]{0:T(128)} %bitcast.1.section, bf16[16,48,352]{2,1,0:T(8,128)(2,1)S(1)} %collective-permute-done.14.x, f32[64,384]{1,0:T(8,128)S(1)} %get-tuple-element.31.cpar.refs_7_, bf16[352,704]{1,0:T(8,128)(2,1)S(1)} %bitcast.30, ...), custom_call_target="tpu_custom_call" | custom-call | flops 761266176 | bytes 1647108 | tf_op jit(solution)/shard_map/conv_up/pallas_call | solution.py:336
  66.5 2.7 %collective-permute-start.15 = (bf16[4,48,352]{2,1,0:T(8,128)(2,1)S(1)}, bf16[4,48,352]{2,1,0:T(8,128)(2,1)S(1)}, u32[]{:S(2)}, u32[]{:S(2)}) collective-permute-start(bf16[4,48,352]{2,1,0:T(8,128)(2,1)S(1)} %down_piece.13), channel_id=1, source_target_pairs={{0,4},{2,6},{4,0},{6,2},{1,5},{3,7},{5,1},{7,3},{8,12},{10,14},{12... | collective-permute-start | bytes 405512 | tf_op jit(solution)/shard_map/ppermute | solution.py:539
  69.7 1.3 %collective-permute-start.16 = (bf16[4,48,352]{2,1,0:T(8,128)(2,1)S(1)}, bf16[4,48,352]{2,1,0:T(8,128)(2,1)S(1)}, u32[]{:S(2)}, u32[]{:S(2)}) collective-permute-start(bf16[4,48,352]{2,1,0:T(8,128)(2,1)S(1)} %down_piece.14), channel_id=1, source_target_pairs={{0,6},{2,4},{4,2},{6,0},{1,7},{3,5},{5,3},{7,1},{8,14},{10,12},{12... | collective-permute-start | bytes 405512 | tf_op jit(solution)/shard_map/ppermute | solution.py:539
  72.1 1.2 %collective-permute-done.15.refs_1_ = bf16[4,48,352]{2,1,0:T(8,128)(2,1)S(1)} collective-permute-done((bf16[4,48,352]{2,1,0:T(8,128)(2,1)S(1)}, bf16[4,48,352]{2,1,0:T(8,128)(2,1)S(1)}, u32[]{:S(2)}, u32[]{:S(2)}) %collective-permute-start.15) | collective-permute-done | bytes 135200 | tf_op jit(solution)/shard_map/ppermute | solution.py:539
  73.4 2.4 %collective-permute-done.16.refs_2_ = bf16[4,48,352]{2,1,0:T(8,128)(2,1)S(1)} collective-permute-done((bf16[4,48,352]{2,1,0:T(8,128)(2,1)S(1)}, bf16[4,48,352]{2,1,0:T(8,128)(2,1)S(1)}, u32[]{:S(2)}, u32[]{:S(2)}) %collective-permute-start.16) | collective-permute-done | bytes 135200 | tf_op jit(solution)/shard_map/ppermute | solution.py:539
  75.8 1.4 %collective-permute-done.17.refs_3_ = bf16[4,48,352]{2,1,0:T(8,128)(2,1)S(1)} collective-permute-done((bf16[4,48,352]{2,1,0:T(8,128)(2,1)S(1)}, bf16[4,48,352]{2,1,0:T(8,128)(2,1)S(1)}, u32[]{:S(2)}, u32[]{:S(2)}) %collective-permute-start.17) | collective-permute-done | bytes 135200 | tf_op jit(solution)/shard_map/ppermute | solution.py:539
  77.2 0.8 %place.1 = bf16[1,4,1,4,48,352]{5,4,3,2,1,0:T(8,128)(2,1)} custom-call(s32[1]{0:T(128)} %bitcast.me, bf16[4,48,352]{2,1,0:T(8,128)(2,1)S(1)} %down_piece.12.refs_0_, bf16[4,48,352]{2,1,0:T(8,128)(2,1)S(1)} %collective-permute-done.15.refs_1_, bf16[4,48,352]{2,1,0:T(8,128)(2,1)S(1)} %collective-permute-done.16.refs_2_, ...), custom_call_target="tpu_custom_call" | custom-call | bytes 540676 | tf_op jit(solution)/shard_map/place/pallas_call | solution.py:336
  (59 shorter events, 5.0 us)
Async XLA Ops:
  0.0 10.0 %copy-start.4 = (bf16[1,1408]{1,0:T(2,128)(2,1)S(1)}, bf16[1,1408]{1,0:T(2,128)(2,1)}, u32[]{:S(2)}) copy-start(bf16[1,1408]{1,0:T(2,128)(2,1)} %refs_5_.1) | copy-start | bytes 8452
  0.0 10.0 %copy-start.3 = (bf16[1,1408]{1,0:T(2,128)(2,1)S(1)}, bf16[1,1408]{1,0:T(2,128)(2,1)}, u32[]{:S(2)}) copy-start(bf16[1,1408]{1,0:T(2,128)(2,1)} %refs_4_.1) | copy-start | bytes 8452
  0.0 10.0 %copy-start.8 = (bf16[1,352]{1,0:T(2,128)(2,1)S(1)}, bf16[1,352]{1,0:T(2,128)(2,1)}, u32[]{:S(2)}) copy-start(bf16[1,352]{1,0:T(2,128)(2,1)} %refs_2_.1) | copy-start | bytes 2116
  0.0 10.0 %copy-start.7 = (bf16[1,352]{1,0:T(2,128)(2,1)S(1)}, bf16[1,352]{1,0:T(2,128)(2,1)}, u32[]{:S(2)}) copy-start(bf16[1,352]{1,0:T(2,128)(2,1)} %refs_1_.1) | copy-start | bytes 2116
  0.0 10.0 %copy-start.6 = (bf16[1,352]{1,0:T(2,128)(2,1)S(1)}, bf16[1,352]{1,0:T(2,128)(2,1)}, u32[]{:S(2)}) copy-start(bf16[1,352]{1,0:T(2,128)(2,1)} %refs_0_.1) | copy-start | bytes 2116
  0.0 10.0 %copy-start.2 = (bf16[1,7,7,352]{3,2,1,0:T(8,128)(2,1)S(1)}, bf16[1,7,7,352]{3,2,1,0:T(8,128)(2,1)}, u32[]{:S(2)}) copy-start(bf16[1,7,7,352]{3,2,1,0:T(8,128)(2,1)} %kernel.1) | copy-start | bytes 103492
  0.1 12.8 %collective-permute-start.4 = (bf16[352,704]{1,0:T(8,128)(2,1)}, bf16[352,704]{1,0:T(8,128)(2,1)S(1)}, u32[]{:S(2)}, u32[]{:S(2)}) collective-permute-start(bf16[352,704]{1,0:T(8,128)(2,1)} %bitcast.25), channel_id=1, source_target_pairs={{0,1},{1,0},{16,17},{17,16},{2,3},{3,2},{18,19},{19,18},{4,5},{5,4... | collective-permute-start | bytes 1486856 | tf_op jit(solution)/shard_map/ppermute | solution.py:400
  2.1 8.9 %collective-permute-start = (bf16[4,48,352]{2,1,0:T(8,128)(2,1)S(1)}, bf16[4,48,352]{2,1,0:T(8,128)(2,1)S(1)}, u32[]{:S(2)}, u32[]{:S(2)}) collective-permute-start(bf16[4,48,352]{2,1,0:T(8,128)(2,1)S(1)} %get-tuple-element.58), channel_id=1, source_target_pairs={{28,8},{30,10},{24,12},{26,14},{29,9},{31,11},{25,13},{27,15}} | collective-permute-start | bytes 405512 | tf_op jit(solution)/shard_map/ppermute | solution.py:395
  6.3 4.7 %collective-permute-start.1 = (bf16[4,48,352]{2,1,0:T(8,128)(2,1)S(1)}, bf16[4,48,352]{2,1,0:T(8,128)(2,1)S(1)}, u32[]{:S(2)}, u32[]{:S(2)}) collective-permute-start(bf16[4,48,352]{2,1,0:T(8,128)(2,1)S(1)} %get-tuple-element.60), channel_id=1, source_target_pairs={{30,8},{28,10},{26,12},{24,14},{31,9},{29,11},{27,13},{25,15}} | collective-permute-start | bytes 405512 | tf_op jit(solution)/shard_map/ppermute | solution.py:395
  8.6 4.3 %collective-permute-start.2 = (bf16[4,48,352]{2,1,0:T(8,128)(2,1)S(1)}, bf16[4,48,352]{2,1,0:T(8,128)(2,1)S(1)}, u32[]{:S(2)}, u32[]{:S(2)}) collective-permute-start(bf16[4,48,352]{2,1,0:T(8,128)(2,1)S(1)} %get-tuple-element.57), channel_id=1, source_target_pairs={{26,8},{24,10},{30,12},{28,14},{27,9},{25,11},{31,13},{29,15}} | collective-permute-start | bytes 405512 | tf_op jit(solution)/shard_map/ppermute | solution.py:395
  10.3 0.7 collective-permute-start.3
  12.9 1.7 %collective-permute-start.5 = (bf16[2,16,48,352]{3,2,1,0:T(8,128)(2,1)S(1)}, bf16[2,16,48,352]{3,2,1,0:T(8,128)(2,1)S(1)}, u32[]{:S(2)}, u32[]{:S(2)}) collective-permute-start(bf16[2,16,48,352]{3,2,1,0:T(8,128)(2,1)S(1)} %last_piece.2), channel_id=1, source_target_pairs={{8,0},{9,1},{10,2},{11,3},{12,4},{13,5},{14,6},{15,7}} | collective-permute-start | bytes 3244040 | tf_op jit(solution)/shard_map/ppermute | solution.py:422
  13.9 0.8 collective-permute-start.6
  14.7 6.0 %collective-permute-start.7 = (bf16[16,48,352]{2,1,0:T(8,128)(2,1)S(1)}, bf16[16,48,352]{2,1,0:T(8,128)(2,1)S(1)}, u32[]{:S(2)}, u32[]{:S(2)}) collective-permute-start(bf16[16,48,352]{2,1,0:T(8,128)(2,1)S(1)} %down.1.prev.refs_4_), channel_id=1, source_target_pairs={{0,8},{1,9},{2,10},{3,11},{4,12},{5,13},{6,14},{7,15}} | collective-permute-start | bytes 1622024 | tf_op jit(solution)/shard_map/ppermute | solution.py:422
  15.4 14.0 %collective-permute-start.8 = (bf16[352,704]{1,0:T(8,128)(2,1)S(1)}, bf16[352,704]{1,0:T(8,128)(2,1)S(1)}, u32[]{:S(2)}, u32[]{:S(2)}) collective-permute-start(bf16[352,704]{1,0:T(8,128)(2,1)S(1)} %bitcast.27), channel_id=1, source_target_pairs={{8,9},{9,8},{24,25},{25,24},{10,11},{11,10},{26,27},{27,26},{12,13... | collective-permute-start | bytes 1486856 | tf_op jit(solution)/shard_map/ppermute | solution.py:400
  17.6 17.7 %collective-permute-start.9 = (bf16[704,352]{1,0:T(8,128)(2,1)S(1)}, bf16[704,352]{1,0:T(8,128)(2,1)S(1)}, u32[]{:S(2)}, u32[]{:S(2)}) collective-permute-start(bf16[704,352]{1,0:T(8,128)(2,1)S(1)} %bitcast.15), channel_id=1, source_target_pairs={{8,9},{9,8},{24,25},{25,24},{10,11},{11,10},{26,27},{27,26},{12,13... | collective-permute-start | bytes 1486856 | tf_op jit(solution)/shard_map/ppermute | solution.py:400
  35.2 2.8 %collective-permute-start.10 = (bf16[4,48,352]{2,1,0:T(8,128)(2,1)S(1)}, bf16[4,48,352]{2,1,0:T(8,128)(2,1)S(1)}, u32[]{:S(2)}, u32[]{:S(2)}) collective-permute-start(bf16[4,48,352]{2,1,0:T(8,128)(2,1)S(1)} %down_piece.8.refs_0_), channel_id=1, source_target_pairs={{8,16},{9,17},{10,18},{11,19},{12,20},{13,21},{14,22},{15,23}} | collective-permute-start | bytes 405512 | tf_op jit(solution)/shard_map/ppermute | solution.py:422
  36.0 2.1 %collective-permute-start.11 = (bf16[4,48,352]{2,1,0:T(8,128)(2,1)S(1)}, bf16[4,48,352]{2,1,0:T(8,128)(2,1)S(1)}, u32[]{:S(2)}, u32[]{:S(2)}) collective-permute-start(bf16[4,48,352]{2,1,0:T(8,128)(2,1)S(1)} %down_piece.9.refs_1_), channel_id=1, source_target_pairs={{8,16},{9,17},{10,18},{11,19},{12,20},{13,21},{14,22},{15,23}} | collective-permute-start | bytes 405512 | tf_op jit(solution)/shard_map/ppermute | solution.py:422
  36.7 1.5 %collective-permute-start.12 = (bf16[4,48,352]{2,1,0:T(8,128)(2,1)S(1)}, bf16[4,48,352]{2,1,0:T(8,128)(2,1)S(1)}, u32[]{:S(2)}, u32[]{:S(2)}) collective-permute-start(bf16[4,48,352]{2,1,0:T(8,128)(2,1)S(1)} %down_piece.10.refs_2_), channel_id=1, source_target_pairs={{8,16},{9,17},{10,18},{11,19},{12,20},{13,21},{14,22},{15,23}} | collective-permute-start | bytes 405512 | tf_op jit(solution)/shard_map/ppermute | solution.py:422
  37.4 0.8 collective-permute-start.13
  38.4 20.6 %collective-permute-start.14 = (bf16[16,48,352]{2,1,0:T(8,128)(2,1)S(1)}, bf16[16,48,352]{2,1,0:T(8,128)(2,1)S(1)}, u32[]{:S(2)}, u32[]{:S(2)}) collective-permute-start(bf16[16,48,352]{2,1,0:T(8,128)(2,1)S(1)} %mlp.1.prev), channel_id=1, source_target_pairs={{16,24},{17,25},{18,26},{19,27},{20,28},{21,29},{22,30},{23,31}} | collective-permute-start | bytes 1622024 | tf_op jit(solution)/shard_map/ppermute | solution.py:422
  66.5 6.8 %collective-permute-start.15 = (bf16[4,48,352]{2,1,0:T(8,128)(2,1)S(1)}, bf16[4,48,352]{2,1,0:T(8,128)(2,1)S(1)}, u32[]{:S(2)}, u32[]{:S(2)}) collective-permute-start(bf16[4,48,352]{2,1,0:T(8,128)(2,1)S(1)} %down_piece.13), channel_id=1, source_target_pairs={{0,4},{2,6},{4,0},{6,2},{1,5},{3,7},{5,1},{7,3},{8,12},{10,14},{12... | collective-permute-start | bytes 405512 | tf_op jit(solution)/shard_map/ppermute | solution.py:539
  69.7 6.1 %collective-permute-start.16 = (bf16[4,48,352]{2,1,0:T(8,128)(2,1)S(1)}, bf16[4,48,352]{2,1,0:T(8,128)(2,1)S(1)}, u32[]{:S(2)}, u32[]{:S(2)}) collective-permute-start(bf16[4,48,352]{2,1,0:T(8,128)(2,1)S(1)} %down_piece.14), channel_id=1, source_target_pairs={{0,6},{2,4},{4,2},{6,0},{1,7},{3,5},{5,3},{7,1},{8,14},{10,12},{12... | collective-permute-start | bytes 405512 | tf_op jit(solution)/shard_map/ppermute | solution.py:539
  71.5 5.6 %collective-permute-start.17 = (bf16[4,48,352]{2,1,0:T(8,128)(2,1)S(1)}, bf16[4,48,352]{2,1,0:T(8,128)(2,1)S(1)}, u32[]{:S(2)}, u32[]{:S(2)}) collective-permute-start(bf16[4,48,352]{2,1,0:T(8,128)(2,1)S(1)} %down_piece.15), channel_id=1, source_target_pairs={{0,2},{2,0},{4,6},{6,4},{1,3},{3,1},{5,7},{7,5},{8,10},{10,8},{12,... | collective-permute-start | bytes 405512 | tf_op jit(solution)/shard_map/ppermute | solution.py:539
  (4 other events, 22.7 us)

commit v14 on v13

--- a/solution.py
+++ b/solution.py
@@ -135,7 +135,7 @@
     def units(start, count):
         raised = jnp.dot(
             flat[...].reshape(cells, channels),
-            w_in[:, pl.ds(start, count)],
+            w_in[0:channels, pl.ds(start, count)],
             preferred_element_type=jnp.float32,
         )
         active = gelu(raised + bias[0:1, pl.ds(start, count)])
@@ -242,6 +242,13 @@
 
 def normed_part(ref):
     return ref if len(ref.shape) == 3 else ref.at[1]
+
+
+def unpack_kernel(packed, w_out):
+    cut, channels = w_out.shape[0] // 2, w_out.shape[1]
+    first = packed.shape[0] - cut
+    w_out[0:cut] = packed[first:, 0:channels]
+    w_out[cut:] = packed[first:, channels : 2 * channels]
 
 
 def up_first_kernel(section, flat, w_in, fvec, act, ssq, *, tick):
@@ -400,10 +407,13 @@
         return lax.ppermute(x, ("section", "dp"), pairs)
 
     w_in, w_out = proj_in[0], proj_out[0]
+    cut = half // 2
+    packed = jnp.concatenate(
+        [w_in, jnp.concatenate([w_out[:cut], w_out[cut:]], axis=1)], axis=0
+    )
     even = range(0, sections, 2)
     odd = range(1, sections, 2)
-    other_in = other_half(w_in, even)
-    other_out = other_half(w_out, even)
+    other = other_half(packed, even)
 
     held = (
         depth_kernel, depth_bias, norm_gain, norm_bias, bias_out, bias_in, grn_gamma, grn_beta
@@ -468,6 +478,9 @@
             tick=tick,
         )
 
+    def unpack(packed):
+        return call(unpack_kernel, "unpack", (packed,), shape(half, channels, dtype=bf16))
+
     def down_piece(x, acts, other_out, prev, order, tick, n):
         act_a, act_b, scale = acts
         return call(
@@ -482,10 +495,12 @@
         )
 
     both = conv_pieces(pieces, send(cpar, 0, helper), order, helper)
-    both, other_in = lax.optimization_barrier((both, other_in))
+    both, other, late = lax.optimization_barrier((both, other, packed))
+    odd_other = other_half(late, odd)
     both = send(both, helper, 0)
+    other_out = unpack(other)
     act_a, ssq = up_own(both, 0)
-    act_b, scale = up_other(both, other_in, ssq, 0)
+    act_b, scale = up_other(both, other, ssq, 0)
     result = call(
         first_down_kernel,
         "down",
@@ -494,9 +509,6 @@
         flops=2 * matmul,
     )
     x = send(result, 0, 1)
-    late_in, late_out, result = lax.optimization_barrier((w_in, w_out, result))
-    odd_in = other_half(late_in, odd)
-    odd_out = other_half(late_out, odd)
     flat = call(
         conv_kernel,
         "conv",
@@ -506,13 +518,15 @@
         tick=1,
     )
     act_a, ssq = up_own(flat, 1)
-    acts = (act_a, *up_other(flat, odd_in, ssq, 1))
+    odd_other, act_a = lax.optimization_barrier((odd_other, act_a))
+    odd_out = unpack(odd_other)
+    acts = (act_a, *up_other(flat, odd_other, ssq, 1))
     kept = [down_piece(x, acts, odd_out, result, None, 1, n) for n in range(count)]
     both = conv_pieces([send(piece, 1, 2) for piece in kept], cpar, None, 2)
     result = call(
         mlp_kernel,
         "mlp",
-        (section, both, w_in, other_in, w_out, other_out, fvec, cpar, *kept, result),
+        (section, both, w_in, other, w_out, other_out, fvec, cpar, *kept, result),
         whole,
         scratch=[pltpu.VMEM((cells, half), bf16)] * 2
         + [ssq_scratch(half)] * 2
@@ -524,7 +538,7 @@
     acts = call(
         conv_up_kernel,
         "conv_up",
-        (section, x, cpar, w_in, odd_in, fvec),
+        (section, x, cpar, w_in, odd_other, fvec),
         (act_shape, act_shape, scale_shape),
         scratch=conv_scratch(height, height, width, lanes)
         + [pltpu.VMEM((height, width, channels), bf16)]
@@ -683,7 +697,7 @@
 
 
 def on_device(inputs, *weights):
-    num_micro, images, local_rows, width, _ = inputs.shape
+    num_micro, images, local_rows, width, channels = inputs.shape
     one_image_each = (
         images == 1
         and lax.axis_size("row") == num_micro == 4
@@ -691,6 +705,7 @@
         and lax.axis_size("section") == 4
         and local_rows % 4 == 0
         and width % 16 == 0
+        and weights[4].shape[2] == 2 * channels
     )
     plan = image_plan if one_image_each else rows_plan
     return plan(inputs, *weights)

time: 78.6 us -> 78.1 us (level)
  starting transfers between devices: 24.9 us -> 20.8 us
  local copies, waits for them, and re-layouts: 1.4 us -> 4.16 us
    ppermute x4 -> x2, starting transfers between devices: 6.79 us -> 2.86 us  [other_half(): return lax.ppermute(x, ('section', 'dp'), pairs)]
    ppermute x8, waiting for transfers between devices: 19.3 us -> 22 us  [send(): return lax.ppermute(x, 'section', [(start, end)])]
    ppermute x4 -> x2, waiting for transfers between devices: 14.5 us -> 11.8 us  [other_half(): return lax.ppermute(x, ('section', 'dp'), pairs)]
    slice x0 -> x1, local copies, waits for them, and re-layouts: none -> 1.15 us  [image_plan(): w_out[:cut]]
    unnamed x20, local copies, waits for them, and re-layouts: 0.21 us -> 1.12 us
    pallas_call x26 -> x28, Pallas kernels: 10.5 us -> 10.8 us  [call(): pl.pallas_call(functools.partial(kernel, **static), out_shape=out, in_spe...]
  transfers between devices with their start and end apart: 18 -> 16, of which waited for: 7 -> 6; matrix products, arithmetic and copies ran while one was open for 2% -> 2% of each run, Pallas kernels for 2% -> 3%
where the time goes in v14:
time: 78.1 us; the launch traced here: 77.7 us
  waiting for transfers between devices  41 us (52%)
  starting transfers between devices  20.8 us (27%)
  Pallas kernels  10.8 us (14%)
  local copies, waits for them, and re-layouts  4.16 us (5%)
    ppermute x8, waiting for transfers between devices, send(): return lax.ppermute(x, 'section', [(start, end)])  22 us
    ppermute x2, waiting for transfers between devices, other_half(): return lax.ppermute(x, ('section', 'dp'), pairs)  11.8 us
    pallas_call x28, Pallas kernels, call(): pl.pallas_call(functools.partial(kernel, **static), out_shape=out, in_spe...  10.8 us
    ppermute x3, starting transfers between devices, image_plan(): piece = lax.ppermute(piece, ('section', 'row'), pairs)  7.78 us
    ppermute x8, starting transfers between devices, send(): return lax.ppermute(x, 'section', [(start, end)])  6.05 us
    ppermute x3, waiting for transfers between devices, image_plan(): lax.ppermute(piece, 'row', [(p, p ^ order[n]) for p in range(count)])  5.05 us
    ppermute x3, starting transfers between devices, image_plan(): lax.ppermute(piece, 'row', [(p, p ^ order[n]) for p in range(count)])  4.13 us
    ppermute x2, starting transfers between devices, other_half(): return lax.ppermute(x, ('section', 'dp'), pairs)  2.86 us
  transfers between devices with their start and end apart: 16, of which 6 were waited for; matrix products, arithmetic and copies ran while one was open for 2% of the time, Pallas kernels for 3%

profile of v14, /device:TPU:7, one launch (start us, length us, event | category | flops | bytes accessed | tf_op | source)
XLA Modules:
  0.0 77.7 jit_solution(2939070406941102181)
XLA Ops:
  0.0 1.1 %slice_bitcast_fusion.1 = (bf16[352,352]{1,0:T(8,128)(2,1)S(1)}, bf16[352,352]{1,0:T(8,128)(2,1)S(1)}) fusion(bf16[1,704,352]{2,1,0:T(8,128)(2,1)} %param.20), kind=kLoop, calls=%fused_computation.2 | loop fusion | bytes 991232 | tf_op jit(solution)/shard_map/slice | solution.py:412
  1.5 0.7 collective-permute-start.4
  2.2 1.9 %dynamic-slice_bitcast_fusion = (bf16[4,48,352]{2,1,0:T(8,128)(2,1)}, bf16[4,48,352]{2,1,0:T(8,128)(2,1)}, bf16[4,48,352]{2,1,0:T(8,128)(2,1)S(1)}, bf16[4,48,352]{2,1,0:T(8,128)(2,1)}) fusion(bf16[4,1,4,48,352]{4,3,2,1,0:T(8,128)(2,1)} %param.11, s32[]{:T(128)S(6)} %select_n.16, s32[]{:T(128)S(6)} %select_n.14, s32[]{:T(128)S(6)} %select_n.13, s32[]{:T(128)S(6)} %select_n.15), kind=kLoop, calls=%fused_computation.3 | loop fusion | bytes 1081360 | tf_op jit(solution)/shard_map/squeeze | solution.py:399
  4.1 4.2 %collective-permute-start = (bf16[4,48,352]{2,1,0:T(8,128)(2,1)}, bf16[4,48,352]{2,1,0:T(8,128)(2,1)S(1)}, u32[]{:S(2)}, u32[]{:S(2)}) collective-permute-start(bf16[4,48,352]{2,1,0:T(8,128)(2,1)} %get-tuple-element.58), channel_id=1, source_target_pairs={{28,8},{30,10},{24,12},{26,14},{29,9},{31,11},{25,13},{27,15}} | collective-permute-start | bytes 405512 | tf_op jit(solution)/shard_map/ppermute | solution.py:402
  8.3 2.3 %collective-permute-start.1 = (bf16[4,48,352]{2,1,0:T(8,128)(2,1)}, bf16[4,48,352]{2,1,0:T(8,128)(2,1)S(1)}, u32[]{:S(2)}, u32[]{:S(2)}) collective-permute-start(bf16[4,48,352]{2,1,0:T(8,128)(2,1)} %get-tuple-element.60), channel_id=1, source_target_pairs={{30,8},{28,10},{26,12},{24,14},{31,9},{29,11},{27,13},{25,15}} | collective-permute-start | bytes 405512 | tf_op jit(solution)/shard_map/ppermute | solution.py:402
  10.6 1.3 %collective-permute-start.2 = (bf16[4,48,352]{2,1,0:T(8,128)(2,1)}, bf16[4,48,352]{2,1,0:T(8,128)(2,1)S(1)}, u32[]{:S(2)}, u32[]{:S(2)}) collective-permute-start(bf16[4,48,352]{2,1,0:T(8,128)(2,1)} %get-tuple-element.57), channel_id=1, source_target_pairs={{26,8},{24,10},{30,12},{28,14},{27,9},{25,11},{31,13},{29,15}} | collective-permute-start | bytes 405512 | tf_op jit(solution)/shard_map/ppermute | solution.py:402
  13.1 2.1 %collective-permute-done.2.refs_3_ = bf16[4,48,352]{2,1,0:T(8,128)(2,1)S(1)} collective-permute-done((bf16[4,48,352]{2,1,0:T(8,128)(2,1)}, bf16[4,48,352]{2,1,0:T(8,128)(2,1)S(1)}, u32[]{:S(2)}, u32[]{:S(2)}) %collective-permute-start.2) | collective-permute-done | bytes 135200 | tf_op jit(solution)/shard_map/ppermute | solution.py:402
  15.2 0.7 collective-permute-start.5
  15.9 2.1 %collective-permute-start.7 = (bf16[704,704]{1,0:T(8,128)(2,1)S(1)}, bf16[704,704]{1,0:T(8,128)(2,1)S(1)}, u32[]{:S(2)}, u32[]{:S(2)}) collective-permute-start(bf16[704,704]{1,0:T(8,128)(2,1)S(1)} %maximum_maximum_fusion), channel_id=1, source_target_pairs={{8,9},{9,8},{24,25},{25,24},{10,11},{11,10},{26,27},{27,26},{12,13... | collective-permute-start | bytes 2973704 | tf_op jit(solution)/shard_map/ppermute | solution.py:407
  18.3 1.0 %copy-done = bf16[1,704,352]{2,1,0:T(8,128)(2,1)S(1)} copy-done((bf16[1,704,352]{2,1,0:T(8,128)(2,1)S(1)}, bf16[1,704,352]{2,1,0:T(8,128)(2,1)}, u32[]{:S(2)}) %copy-start) | copy-done | bytes 495640
  19.3 0.7 collective-permute-start.6
  20.1 11.8 %collective-permute-done.7.w_in.packed.in_b = bf16[704,704]{1,0:T(8,128)(2,1)S(1)} collective-permute-done((bf16[704,704]{1,0:T(8,128)(2,1)S(1)}, bf16[704,704]{1,0:T(8,128)(2,1)S(1)}, u32[]{:S(2)}, u32[]{:S(2)}) %collective-permute-start.7) | collective-permute-done | bytes 991264 | tf_op jit(solution)/shard_map/ppermute | solution.py:407
  32.0 0.7 collective-permute-start.8
  32.8 0.7 collective-permute-start.9
  33.5 0.7 collective-permute-start.10
  35.2 1.3 %collective-permute-start.12 = (bf16[16,48,352]{2,1,0:T(8,128)(2,1)S(1)}, bf16[16,48,352]{2,1,0:T(8,128)(2,1)S(1)}, u32[]{:S(2)}, u32[]{:S(2)}) collective-permute-start(bf16[16,48,352]{2,1,0:T(8,128)(2,1)S(1)} %mlp.1.prev), channel_id=1, source_target_pairs={{16,24},{17,25},{18,26},{19,27},{20,28},{21,29},{22,30},{23,31}} | collective-permute-start | bytes 1622024 | tf_op jit(solution)/shard_map/ppermute | solution.py:432
  36.5 22.0 %collective-permute-done.12.x = bf16[16,48,352]{2,1,0:T(8,128)(2,1)S(1)} collective-permute-done((bf16[16,48,352]{2,1,0:T(8,128)(2,1)S(1)}, bf16[16,48,352]{2,1,0:T(8,128)(2,1)S(1)}, u32[]{:S(2)}, u32[]{:S(2)}) %collective-permute-start.12) | collective-permute-done | bytes 540704 | tf_op jit(solution)/shard_map/ppermute | solution.py:432
  58.5 7.0 %conv_up.1 = (bf16[768,704]{1,0:T(8,128)(2,1)S(1)}, bf16[768,704]{1,0:T(8,128)(2,1)S(1)}, f32[2,1,704]{2,1,0:T(1,128)S(1)}) custom-call(s32[1]{0:T(128)} %bitcast.1.section, bf16[16,48,352]{2,1,0:T(8,128)(2,1)S(1)} %collective-permute-done.12.x, f32[64,384]{1,0:T(8,128)S(1)} %get-tuple-element.31.cpar.refs_7_, bf16[352,704]{1,0:T(8,128)(2,1)S(1)} %bitcast.31, ...), custom_call_target="tpu_custom_call" | custom-call | flops 761266176 | bytes 2142724 | tf_op jit(solution)/shard_map/conv_up/pallas_call | solution.py:343
  66.0 2.7 %collective-permute-start.13 = (bf16[4,48,352]{2,1,0:T(8,128)(2,1)S(1)}, bf16[4,48,352]{2,1,0:T(8,128)(2,1)S(1)}, u32[]{:S(2)}, u32[]{:S(2)}) collective-permute-start(bf16[4,48,352]{2,1,0:T(8,128)(2,1)S(1)} %down_piece.13), channel_id=1, source_target_pairs={{0,4},{2,6},{4,0},{6,2},{1,5},{3,7},{5,1},{7,3},{8,12},{10,14},{12... | collective-permute-start | bytes 405512 | tf_op jit(solution)/shard_map/ppermute | solution.py:553
  69.2 1.3 %collective-permute-start.14 = (bf16[4,48,352]{2,1,0:T(8,128)(2,1)S(1)}, bf16[4,48,352]{2,1,0:T(8,128)(2,1)S(1)}, u32[]{:S(2)}, u32[]{:S(2)}) collective-permute-start(bf16[4,48,352]{2,1,0:T(8,128)(2,1)S(1)} %down_piece.14), channel_id=1, source_target_pairs={{0,6},{2,4},{4,2},{6,0},{1,7},{3,5},{5,3},{7,1},{8,14},{10,12},{12... | collective-permute-start | bytes 405512 | tf_op jit(solution)/shard_map/ppermute | solution.py:553
  71.6 1.2 %collective-permute-done.13.refs_1_ = bf16[4,48,352]{2,1,0:T(8,128)(2,1)S(1)} collective-permute-done((bf16[4,48,352]{2,1,0:T(8,128)(2,1)S(1)}, bf16[4,48,352]{2,1,0:T(8,128)(2,1)S(1)}, u32[]{:S(2)}, u32[]{:S(2)}) %collective-permute-start.13) | collective-permute-done | bytes 135200 | tf_op jit(solution)/shard_map/ppermute | solution.py:553
  72.9 2.4 %collective-permute-done.14.refs_2_ = bf16[4,48,352]{2,1,0:T(8,128)(2,1)S(1)} collective-permute-done((bf16[4,48,352]{2,1,0:T(8,128)(2,1)S(1)}, bf16[4,48,352]{2,1,0:T(8,128)(2,1)S(1)}, u32[]{:S(2)}, u32[]{:S(2)}) %collective-permute-start.14) | collective-permute-done | bytes 135200 | tf_op jit(solution)/shard_map/ppermute | solution.py:553
  75.3 1.4 %collective-permute-done.15.refs_3_ = bf16[4,48,352]{2,1,0:T(8,128)(2,1)S(1)} collective-permute-done((bf16[4,48,352]{2,1,0:T(8,128)(2,1)S(1)}, bf16[4,48,352]{2,1,0:T(8,128)(2,1)S(1)}, u32[]{:S(2)}, u32[]{:S(2)}) %collective-permute-start.15) | collective-permute-done | bytes 135200 | tf_op jit(solution)/shard_map/ppermute | solution.py:553
  76.7 0.8 %place.1 = bf16[1,4,1,4,48,352]{5,4,3,2,1,0:T(8,128)(2,1)} custom-call(s32[1]{0:T(128)} %bitcast.me, bf16[4,48,352]{2,1,0:T(8,128)(2,1)S(1)} %down_piece.12.refs_0_, bf16[4,48,352]{2,1,0:T(8,128)(2,1)S(1)} %collective-permute-done.13.refs_1_, bf16[4,48,352]{2,1,0:T(8,128)(2,1)S(1)} %collective-permute-done.14.refs_2_, ...), custom_call_target="tpu_custom_call" | custom-call | bytes 540676 | tf_op jit(solution)/shard_map/place/pallas_call | solution.py:343
  (59 shorter events, 4.7 us)
Async XLA Ops:
  1.2 10.7 %copy-start.2 = (bf16[1,7,7,352]{3,2,1,0:T(8,128)(2,1)S(1)}, bf16[1,7,7,352]{3,2,1,0:T(8,128)(2,1)}, u32[]{:S(2)}) copy-start(bf16[1,7,7,352]{3,2,1,0:T(8,128)(2,1)} %kernel.1) | copy-start | bytes 103492
  1.2 10.7 %copy-start.3 = (bf16[1,1408]{1,0:T(2,128)(2,1)S(1)}, bf16[1,1408]{1,0:T(2,128)(2,1)}, u32[]{:S(2)}) copy-start(bf16[1,1408]{1,0:T(2,128)(2,1)} %refs_4_.1) | copy-start | bytes 8452
  1.2 10.7 %copy-start.4 = (bf16[1,1408]{1,0:T(2,128)(2,1)S(1)}, bf16[1,1408]{1,0:T(2,128)(2,1)}, u32[]{:S(2)}) copy-start(bf16[1,1408]{1,0:T(2,128)(2,1)} %refs_5_.1) | copy-start | bytes 8452
  1.2 10.8 %copy-start.5 = (bf16[1,1408]{1,0:T(2,128)(2,1)S(1)}, bf16[1,1408]{1,0:T(2,128)(2,1)}, u32[]{:S(2)}) copy-start(bf16[1,1408]{1,0:T(2,128)(2,1)} %refs_6_.1) | copy-start | bytes 8452
  1.2 10.8 %copy-start.6 = (bf16[1,352]{1,0:T(2,128)(2,1)S(1)}, bf16[1,352]{1,0:T(2,128)(2,1)}, u32[]{:S(2)}) copy-start(bf16[1,352]{1,0:T(2,128)(2,1)} %refs_0_.1) | copy-start | bytes 2116
  1.2 10.8 %copy-start.7 = (bf16[1,352]{1,0:T(2,128)(2,1)S(1)}, bf16[1,352]{1,0:T(2,128)(2,1)}, u32[]{:S(2)}) copy-start(bf16[1,352]{1,0:T(2,128)(2,1)} %refs_1_.1) | copy-start | bytes 2116
  1.2 10.8 %copy-start.8 = (bf16[1,352]{1,0:T(2,128)(2,1)S(1)}, bf16[1,352]{1,0:T(2,128)(2,1)}, u32[]{:S(2)}) copy-start(bf16[1,352]{1,0:T(2,128)(2,1)} %refs_2_.1) | copy-start | bytes 2116
  1.3 10.7 %copy-start.9 = (bf16[1,352]{1,0:T(2,128)(2,1)S(1)}, bf16[1,352]{1,0:T(2,128)(2,1)}, u32[]{:S(2)}) copy-start(bf16[1,352]{1,0:T(2,128)(2,1)} %refs_3_.1) | copy-start | bytes 2116
  1.5 13.7 %collective-permute-start.4 = (bf16[704,704]{1,0:T(8,128)(2,1)S(1)}, bf16[704,704]{1,0:T(8,128)(2,1)S(1)}, u32[]{:S(2)}, u32[]{:S(2)}) collective-permute-start(bf16[704,704]{1,0:T(8,128)(2,1)S(1)} %maximum_maximum_fusion), channel_id=1, source_target_pairs={{0,1},{1,0},{16,17},{17,16},{2,3},{3,2},{18,19},{19,18},{4,5},{5,4... | collective-permute-start | bytes 2973704 | tf_op jit(solution)/shard_map/ppermute | solution.py:407
  4.1 8.9 %collective-permute-start = (bf16[4,48,352]{2,1,0:T(8,128)(2,1)}, bf16[4,48,352]{2,1,0:T(8,128)(2,1)S(1)}, u32[]{:S(2)}, u32[]{:S(2)}) collective-permute-start(bf16[4,48,352]{2,1,0:T(8,128)(2,1)} %get-tuple-element.58), channel_id=1, source_target_pairs={{28,8},{30,10},{24,12},{26,14},{29,9},{31,11},{25,13},{27,15}} | collective-permute-start | bytes 405512 | tf_op jit(solution)/shard_map/ppermute | solution.py:402
  8.3 4.7 %collective-permute-start.1 = (bf16[4,48,352]{2,1,0:T(8,128)(2,1)}, bf16[4,48,352]{2,1,0:T(8,128)(2,1)S(1)}, u32[]{:S(2)}, u32[]{:S(2)}) collective-permute-start(bf16[4,48,352]{2,1,0:T(8,128)(2,1)} %get-tuple-element.60), channel_id=1, source_target_pairs={{30,8},{28,10},{26,12},{24,14},{31,9},{29,11},{27,13},{25,15}} | collective-permute-start | bytes 405512 | tf_op jit(solution)/shard_map/ppermute | solution.py:402
  10.6 4.6 %collective-permute-start.2 = (bf16[4,48,352]{2,1,0:T(8,128)(2,1)}, bf16[4,48,352]{2,1,0:T(8,128)(2,1)S(1)}, u32[]{:S(2)}, u32[]{:S(2)}) collective-permute-start(bf16[4,48,352]{2,1,0:T(8,128)(2,1)} %get-tuple-element.57), channel_id=1, source_target_pairs={{26,8},{24,10},{30,12},{28,14},{27,9},{25,11},{31,13},{29,15}} | collective-permute-start | bytes 405512 | tf_op jit(solution)/shard_map/ppermute | solution.py:402
  12.3 0.7 collective-permute-start.3
  15.2 3.0 %collective-permute-start.5 = (bf16[2,16,48,352]{3,2,1,0:T(8,128)(2,1)S(1)}, bf16[2,16,48,352]{3,2,1,0:T(8,128)(2,1)S(1)}, u32[]{:S(2)}, u32[]{:S(2)}) collective-permute-start(bf16[2,16,48,352]{3,2,1,0:T(8,128)(2,1)S(1)} %last_piece.2), channel_id=1, source_target_pairs={{8,0},{9,1},{10,2},{11,3},{12,4},{13,5},{14,6},{15,7}} | collective-permute-start | bytes 3244040 | tf_op jit(solution)/shard_map/ppermute | solution.py:432
  15.9 15.9 %collective-permute-start.7 = (bf16[704,704]{1,0:T(8,128)(2,1)S(1)}, bf16[704,704]{1,0:T(8,128)(2,1)S(1)}, u32[]{:S(2)}, u32[]{:S(2)}) collective-permute-start(bf16[704,704]{1,0:T(8,128)(2,1)S(1)} %maximum_maximum_fusion), channel_id=1, source_target_pairs={{8,9},{9,8},{24,25},{25,24},{10,11},{11,10},{26,27},{27,26},{12,13... | collective-permute-start | bytes 2973704 | tf_op jit(solution)/shard_map/ppermute | solution.py:407
  19.3 0.7 collective-permute-start.6
  32.0 2.8 %collective-permute-start.8 = (bf16[4,48,352]{2,1,0:T(8,128)(2,1)S(1)}, bf16[4,48,352]{2,1,0:T(8,128)(2,1)S(1)}, u32[]{:S(2)}, u32[]{:S(2)}) collective-permute-start(bf16[4,48,352]{2,1,0:T(8,128)(2,1)S(1)} %down_piece.8.refs_0_), channel_id=1, source_target_pairs={{8,16},{9,17},{10,18},{11,19},{12,20},{13,21},{14,22},{15,23}} | collective-permute-start | bytes 405512 | tf_op jit(solution)/shard_map/ppermute | solution.py:432
  32.8 2.1 %collective-permute-start.9 = (bf16[4,48,352]{2,1,0:T(8,128)(2,1)S(1)}, bf16[4,48,352]{2,1,0:T(8,128)(2,1)S(1)}, u32[]{:S(2)}, u32[]{:S(2)}) collective-permute-start(bf16[4,48,352]{2,1,0:T(8,128)(2,1)S(1)} %down_piece.9.refs_1_), channel_id=1, source_target_pairs={{8,16},{9,17},{10,18},{11,19},{12,20},{13,21},{14,22},{15,23}} | collective-permute-start | bytes 405512 | tf_op jit(solution)/shard_map/ppermute | solution.py:432
  33.5 1.5 %collective-permute-start.10 = (bf16[4,48,352]{2,1,0:T(8,128)(2,1)S(1)}, bf16[4,48,352]{2,1,0:T(8,128)(2,1)S(1)}, u32[]{:S(2)}, u32[]{:S(2)}) collective-permute-start(bf16[4,48,352]{2,1,0:T(8,128)(2,1)S(1)} %down_piece.10.refs_2_), channel_id=1, source_target_pairs={{8,16},{9,17},{10,18},{11,19},{12,20},{13,21},{14,22},{15,23}} | collective-permute-start | bytes 405512 | tf_op jit(solution)/shard_map/ppermute | solution.py:432
  34.2 0.8 collective-permute-start.11
  35.2 23.3 %collective-permute-start.12 = (bf16[16,48,352]{2,1,0:T(8,128)(2,1)S(1)}, bf16[16,48,352]{2,1,0:T(8,128)(2,1)S(1)}, u32[]{:S(2)}, u32[]{:S(2)}) collective-permute-start(bf16[16,48,352]{2,1,0:T(8,128)(2,1)S(1)} %mlp.1.prev), channel_id=1, source_target_pairs={{16,24},{17,25},{18,26},{19,27},{20,28},{21,29},{22,30},{23,31}} | collective-permute-start | bytes 1622024 | tf_op jit(solution)/shard_map/ppermute | solution.py:432
  66.0 6.8 %collective-permute-start.13 = (bf16[4,48,352]{2,1,0:T(8,128)(2,1)S(1)}, bf16[4,48,352]{2,1,0:T(8,128)(2,1)S(1)}, u32[]{:S(2)}, u32[]{:S(2)}) collective-permute-start(bf16[4,48,352]{2,1,0:T(8,128)(2,1)S(1)} %down_piece.13), channel_id=1, source_target_pairs={{0,4},{2,6},{4,0},{6,2},{1,5},{3,7},{5,1},{7,3},{8,12},{10,14},{12... | collective-permute-start | bytes 405512 | tf_op jit(solution)/shard_map/ppermute | solution.py:553
  69.2 6.1 %collective-permute-start.14 = (bf16[4,48,352]{2,1,0:T(8,128)(2,1)S(1)}, bf16[4,48,352]{2,1,0:T(8,128)(2,1)S(1)}, u32[]{:S(2)}, u32[]{:S(2)}) collective-permute-start(bf16[4,48,352]{2,1,0:T(8,128)(2,1)S(1)} %down_piece.14), channel_id=1, source_target_pairs={{0,6},{2,4},{4,2},{6,0},{1,7},{3,5},{5,3},{7,1},{8,14},{10,12},{12... | collective-permute-start | bytes 405512 | tf_op jit(solution)/shard_map/ppermute | solution.py:553
  71.1 5.6 %collective-permute-start.15 = (bf16[4,48,352]{2,1,0:T(8,128)(2,1)S(1)}, bf16[4,48,352]{2,1,0:T(8,128)(2,1)S(1)}, u32[]{:S(2)}, u32[]{:S(2)}) collective-permute-start(bf16[4,48,352]{2,1,0:T(8,128)(2,1)S(1)} %down_piece.15), channel_id=1, source_target_pairs={{0,2},{2,0},{4,6},{6,4},{1,3},{3,1},{5,7},{7,5},{8,10},{10,8},{12,... | collective-permute-start | bytes 405512 | tf_op jit(solution)/shard_map/ppermute | solution.py:553
  (2 other events, 2.3 us)

commit v15 on v14

--- a/solution.py
+++ b/solution.py
@@ -408,12 +408,10 @@
 
     w_in, w_out = proj_in[0], proj_out[0]
     cut = half // 2
-    packed = jnp.concatenate(
-        [w_in, jnp.concatenate([w_out[:cut], w_out[cut:]], axis=1)], axis=0
-    )
     even = range(0, sections, 2)
     odd = range(1, sections, 2)
-    other = other_half(packed, even)
+    other_in = other_half(w_in, even)
+    other_out = other_half(w_out, even)
 
     held = (
         depth_kernel, depth_bias, norm_gain, norm_bias, bias_out, bias_in, grn_gamma, grn_beta
@@ -495,12 +493,14 @@
         )
 
     both = conv_pieces(pieces, send(cpar, 0, helper), order, helper)
-    both, other, late = lax.optimization_barrier((both, other, packed))
+    both, other_in, late_in, late_out = lax.optimization_barrier((both, other_in, w_in, w_out))
+    late = jnp.concatenate(
+        [late_in, jnp.concatenate([late_out[:cut], late_out[cut:]], axis=1)], axis=0
+    )
     odd_other = other_half(late, odd)
     both = send(both, helper, 0)
-    other_out = unpack(other)
     act_a, ssq = up_own(both, 0)
-    act_b, scale = up_other(both, other, ssq, 0)
+    act_b, scale = up_other(both, other_in, ssq, 0)
     result = call(
         first_down_kernel,
         "down",
@@ -526,7 +526,7 @@
     result = call(
         mlp_kernel,
         "mlp",
-        (section, both, w_in, other, w_out, other_out, fvec, cpar, *kept, result),
+        (section, both, w_in, other_in, w_out, other_out, fvec, cpar, *kept, result),
         whole,
         scratch=[pltpu.VMEM((cells, half), bf16)] * 2
         + [ssq_scratch(half)] * 2

time: 78.1 us -> 77 us (0.986)
  local copies, waits for them, and re-layouts: 4.16 us -> 1.45 us
  starting transfers between devices: 20.8 us -> 21.8 us
  waiting for transfers between devices: 41 us -> 41.8 us
    ppermute x2 -> x3, waiting for transfers between devices: 11.8 us -> 17.4 us  [other_half(): return lax.ppermute(x, ('section', 'dp'), pairs)]
    ppermute x8, waiting for transfers between devices: 22 us -> 17.5 us  [send(): return lax.ppermute(x, 'section', [(start, end)])]
    slice x1, local copies, waits for them, and re-layouts: 1.15 us -> 0.06 us  [image_plan(): late_out[:cut]]
    unnamed x20, local copies, waits for them, and re-layouts: 1.12 us -> 0.21 us
    ppermute x2 -> x3, starting transfers between devices: 2.86 us -> 3.64 us  [other_half(): return lax.ppermute(x, ('section', 'dp'), pairs)]
    pallas_call x28 -> x27, Pallas kernels: 10.8 us -> 10.7 us  [call(): pl.pallas_call(functools.partial(kernel, **static), out_shape=out, in_spe...]
  transfers between devices with their start and end apart: 16 -> 17, of which waited for: 6 -> 6; matrix products, arithmetic and copies ran while one was open for 2% -> 2% of each run, Pallas kernels for 3% -> 3%
where the time goes in v15:
time: 77 us; the launch traced here: 76.6 us
  waiting for transfers between devices  41.8 us (54%)
  starting transfers between devices  21.8 us (28%)
  Pallas kernels  10.7 us (14%)
  local copies, waits for them, and re-layouts  1.45 us (2%)
    ppermute x8, waiting for transfers between devices, send(): return lax.ppermute(x, 'section', [(start, end)])  17.5 us
    ppermute x3, waiting for transfers between devices, other_half(): return lax.ppermute(x, ('section', 'dp'), pairs)  17.4 us
    pallas_call x27, Pallas kernels, call(): pl.pallas_call(functools.partial(kernel, **static), out_shape=out, in_spe...  10.7 us
    ppermute x3, starting transfers between devices, image_plan(): piece = lax.ppermute(piece, ('section', 'row'), pairs)  7.8 us
    ppermute x8, starting transfers between devices, send(): return lax.ppermute(x, 'section', [(start, end)])  6.2 us
    ppermute x3, waiting for transfers between devices, image_plan(): lax.ppermute(piece, 'row', [(p, p ^ order[n]) for p in range(count)])  5.04 us
    ppermute x3, starting transfers between devices, image_plan(): lax.ppermute(piece, 'row', [(p, p ^ order[n]) for p in range(count)])  4.13 us
    ppermute x3, starting transfers between devices, other_half(): return lax.ppermute(x, ('section', 'dp'), pairs)  3.64 us
  transfers between devices with their start and end apart: 17, of which 6 were waited for; matrix products, arithmetic and copies ran while one was open for 2% of the time, Pallas kernels for 3%

profile of v15, /device:TPU:7, one launch (start us, length us, event | category | flops | bytes accessed | tf_op | source)
XLA Modules:
  0.0 76.6 jit_solution(10004559715835493640)
XLA Ops:
  0.1 0.8 %collective-permute-start.4 = (bf16[352,704]{1,0:T(8,128)(2,1)}, bf16[352,704]{1,0:T(8,128)(2,1)S(1)}, u32[]{:S(2)}, u32[]{:S(2)}) collective-permute-start(bf16[352,704]{1,0:T(8,128)(2,1)} %bitcast.25), channel_id=1, source_target_pairs={{0,1},{1,0},{16,17},{17,16},{2,3},{3,2},{18,19},{19,18},{4,5},{5,4... | collective-permute-start | bytes 1486856 | tf_op jit(solution)/shard_map/ppermute | solution.py:407
  0.9 1.2 %dynamic-slice_bitcast_fusion = (bf16[4,48,352]{2,1,0:T(8,128)(2,1)S(1)}, bf16[4,48,352]{2,1,0:T(8,128)(2,1)S(1)}, bf16[4,48,352]{2,1,0:T(8,128)(2,1)S(1)}, bf16[4,48,352]{2,1,0:T(8,128)(2,1)S(1)}) fusion(bf16[4,1,4,48,352]{4,3,2,1,0:T(8,128)(2,1)} %param.11, s32[]{:T(128)S(6)} %select_n.16, s32[]{:T(128)S(6)} %select_n.14, s32[]{:T(128)S(6)} %select_n.13, ...), kind=kLoop, calls=%fused_computation.1 | loop fusion | bytes 1081360 | tf_op jit(solution)/shard_map/squeeze | solution.py:399
  2.1 4.2 %collective-permute-start = (bf16[4,48,352]{2,1,0:T(8,128)(2,1)S(1)}, bf16[4,48,352]{2,1,0:T(8,128)(2,1)S(1)}, u32[]{:S(2)}, u32[]{:S(2)}) collective-permute-start(bf16[4,48,352]{2,1,0:T(8,128)(2,1)S(1)} %get-tuple-element.60), channel_id=1, source_target_pairs={{28,8},{30,10},{24,12},{26,14},{29,9},{31,11},{25,13},{27,15}} | collective-permute-start | bytes 405512 | tf_op jit(solution)/shard_map/ppermute | solution.py:402
  6.3 2.3 %collective-permute-start.1 = (bf16[4,48,352]{2,1,0:T(8,128)(2,1)S(1)}, bf16[4,48,352]{2,1,0:T(8,128)(2,1)S(1)}, u32[]{:S(2)}, u32[]{:S(2)}) collective-permute-start(bf16[4,48,352]{2,1,0:T(8,128)(2,1)S(1)} %get-tuple-element.62), channel_id=1, source_target_pairs={{30,8},{28,10},{26,12},{24,14},{31,9},{29,11},{27,13},{25,15}} | collective-permute-start | bytes 405512 | tf_op jit(solution)/shard_map/ppermute | solution.py:402
  8.6 1.3 %collective-permute-start.2 = (bf16[4,48,352]{2,1,0:T(8,128)(2,1)S(1)}, bf16[4,48,352]{2,1,0:T(8,128)(2,1)S(1)}, u32[]{:S(2)}, u32[]{:S(2)}) collective-permute-start(bf16[4,48,352]{2,1,0:T(8,128)(2,1)S(1)} %get-tuple-element.59), channel_id=1, source_target_pairs={{26,8},{24,10},{30,12},{28,14},{27,9},{25,11},{31,13},{29,15}} | collective-permute-start | bytes 405512 | tf_op jit(solution)/shard_map/ppermute | solution.py:402
  11.0 1.8 %collective-permute-done.2.refs_3_ = bf16[4,48,352]{2,1,0:T(8,128)(2,1)S(1)} collective-permute-done((bf16[4,48,352]{2,1,0:T(8,128)(2,1)S(1)}, bf16[4,48,352]{2,1,0:T(8,128)(2,1)S(1)}, u32[]{:S(2)}, u32[]{:S(2)}) %collective-permute-start.2) | collective-permute-done | bytes 135200 | tf_op jit(solution)/shard_map/ppermute | solution.py:402
  12.9 0.9 %collective-permute-start.5 = (bf16[2,16,48,352]{3,2,1,0:T(8,128)(2,1)S(1)}, bf16[2,16,48,352]{3,2,1,0:T(8,128)(2,1)S(1)}, u32[]{:S(2)}, u32[]{:S(2)}) collective-permute-start(bf16[2,16,48,352]{3,2,1,0:T(8,128)(2,1)S(1)} %last_piece.2), channel_id=1, source_target_pairs={{8,0},{9,1},{10,2},{11,3},{12,4},{13,5},{14,6},{15,7}} | collective-permute-start | bytes 3244040 | tf_op jit(solution)/shard_map/ppermute | solution.py:430
  13.9 0.7 collective-permute-start.6
  14.9 2.1 %collective-permute-start.8 = (bf16[704,704]{1,0:T(8,128)(2,1)S(1)}, bf16[704,704]{1,0:T(8,128)(2,1)S(1)}, u32[]{:S(2)}, u32[]{:S(2)}) collective-permute-start(bf16[704,704]{1,0:T(8,128)(2,1)S(1)} %maximum_maximum_fusion), channel_id=1, source_target_pairs={{8,9},{9,8},{24,25},{25,24},{10,11},{11,10},{26,27},{27,26},{12,13... | collective-permute-start | bytes 2973704 | tf_op jit(solution)/shard_map/ppermute | solution.py:407
  17.1 0.7 collective-permute-start.7
  17.9 17.4 %collective-permute-done.8.w_in.packed.in_b = bf16[704,704]{1,0:T(8,128)(2,1)S(1)} collective-permute-done((bf16[704,704]{1,0:T(8,128)(2,1)S(1)}, bf16[704,704]{1,0:T(8,128)(2,1)S(1)}, u32[]{:S(2)}, u32[]{:S(2)}) %collective-permute-start.8) | collective-permute-done | bytes 991264 | tf_op jit(solution)/shard_map/ppermute | solution.py:407
  35.4 0.7 collective-permute-start.9
  36.2 0.7 collective-permute-start.10
  36.9 0.7 collective-permute-start.11
  37.6 0.7 collective-permute-start.12
  38.6 1.3 %collective-permute-start.13 = (bf16[16,48,352]{2,1,0:T(8,128)(2,1)S(1)}, bf16[16,48,352]{2,1,0:T(8,128)(2,1)S(1)}, u32[]{:S(2)}, u32[]{:S(2)}) collective-permute-start(bf16[16,48,352]{2,1,0:T(8,128)(2,1)S(1)} %mlp.1.prev), channel_id=1, source_target_pairs={{16,24},{17,25},{18,26},{19,27},{20,28},{21,29},{22,30},{23,31}} | collective-permute-start | bytes 1622024 | tf_op jit(solution)/shard_map/ppermute | solution.py:430
  39.9 17.5 %collective-permute-done.13.x = bf16[16,48,352]{2,1,0:T(8,128)(2,1)S(1)} collective-permute-done((bf16[16,48,352]{2,1,0:T(8,128)(2,1)S(1)}, bf16[16,48,352]{2,1,0:T(8,128)(2,1)S(1)}, u32[]{:S(2)}, u32[]{:S(2)}) %collective-permute-start.13) | collective-permute-done | bytes 540704 | tf_op jit(solution)/shard_map/ppermute | solution.py:430
  57.4 7.0 %conv_up.1 = (bf16[768,704]{1,0:T(8,128)(2,1)S(1)}, bf16[768,704]{1,0:T(8,128)(2,1)S(1)}, f32[2,1,704]{2,1,0:T(1,128)S(1)}) custom-call(s32[1]{0:T(128)} %bitcast.1.section, bf16[16,48,352]{2,1,0:T(8,128)(2,1)S(1)} %collective-permute-done.13.x, f32[64,384]{1,0:T(8,128)S(1)} %get-tuple-element.32.cpar.refs_7_, bf16[352,704]{1,0:T(8,128)(2,1)S(1)} %bitcast.30, ...), custom_call_target="tpu_custom_call" | custom-call | flops 761266176 | bytes 2142724 | tf_op jit(solution)/shard_map/conv_up/pallas_call | solution.py:343
  64.9 2.7 %collective-permute-start.14 = (bf16[4,48,352]{2,1,0:T(8,128)(2,1)S(1)}, bf16[4,48,352]{2,1,0:T(8,128)(2,1)S(1)}, u32[]{:S(2)}, u32[]{:S(2)}) collective-permute-start(bf16[4,48,352]{2,1,0:T(8,128)(2,1)S(1)} %down_piece.13), channel_id=1, source_target_pairs={{0,4},{2,6},{4,0},{6,2},{1,5},{3,7},{5,1},{7,3},{8,12},{10,14},{12... | collective-permute-start | bytes 405512 | tf_op jit(solution)/shard_map/ppermute | solution.py:553
  68.2 1.3 %collective-permute-start.15 = (bf16[4,48,352]{2,1,0:T(8,128)(2,1)S(1)}, bf16[4,48,352]{2,1,0:T(8,128)(2,1)S(1)}, u32[]{:S(2)}, u32[]{:S(2)}) collective-permute-start(bf16[4,48,352]{2,1,0:T(8,128)(2,1)S(1)} %down_piece.14), channel_id=1, source_target_pairs={{0,6},{2,4},{4,2},{6,0},{1,7},{3,5},{5,3},{7,1},{8,14},{10,12},{12... | collective-permute-start | bytes 405512 | tf_op jit(solution)/shard_map/ppermute | solution.py:553
  70.6 1.2 %collective-permute-done.14.refs_1_ = bf16[4,48,352]{2,1,0:T(8,128)(2,1)S(1)} collective-permute-done((bf16[4,48,352]{2,1,0:T(8,128)(2,1)S(1)}, bf16[4,48,352]{2,1,0:T(8,128)(2,1)S(1)}, u32[]{:S(2)}, u32[]{:S(2)}) %collective-permute-start.14) | collective-permute-done | bytes 135200 | tf_op jit(solution)/shard_map/ppermute | solution.py:553
  71.8 2.4 %collective-permute-done.15.refs_2_ = bf16[4,48,352]{2,1,0:T(8,128)(2,1)S(1)} collective-permute-done((bf16[4,48,352]{2,1,0:T(8,128)(2,1)S(1)}, bf16[4,48,352]{2,1,0:T(8,128)(2,1)S(1)}, u32[]{:S(2)}, u32[]{:S(2)}) %collective-permute-start.15) | collective-permute-done | bytes 135200 | tf_op jit(solution)/shard_map/ppermute | solution.py:553
  74.2 1.4 %collective-permute-done.16.refs_3_ = bf16[4,48,352]{2,1,0:T(8,128)(2,1)S(1)} collective-permute-done((bf16[4,48,352]{2,1,0:T(8,128)(2,1)S(1)}, bf16[4,48,352]{2,1,0:T(8,128)(2,1)S(1)}, u32[]{:S(2)}, u32[]{:S(2)}) %collective-permute-start.16) | collective-permute-done | bytes 135200 | tf_op jit(solution)/shard_map/ppermute | solution.py:553
  75.6 0.8 %place.1 = bf16[1,4,1,4,48,352]{5,4,3,2,1,0:T(8,128)(2,1)} custom-call(s32[1]{0:T(128)} %bitcast.me, bf16[4,48,352]{2,1,0:T(8,128)(2,1)S(1)} %down_piece.12.refs_0_, bf16[4,48,352]{2,1,0:T(8,128)(2,1)S(1)} %collective-permute-done.14.refs_1_, bf16[4,48,352]{2,1,0:T(8,128)(2,1)S(1)} %collective-permute-done.15.refs_2_, ...), custom_call_target="tpu_custom_call" | custom-call | bytes 540676 | tf_op jit(solution)/shard_map/place/pallas_call | solution.py:343
  (60 shorter events, 4.1 us)
Async XLA Ops:
  0.0 9.9 %copy-start.5 = (bf16[1,1408]{1,0:T(2,128)(2,1)S(1)}, bf16[1,1408]{1,0:T(2,128)(2,1)}, u32[]{:S(2)}) copy-start(bf16[1,1408]{1,0:T(2,128)(2,1)} %refs_6_.1) | copy-start | bytes 8452
  0.0 10.0 %copy-start.4 = (bf16[1,1408]{1,0:T(2,128)(2,1)S(1)}, bf16[1,1408]{1,0:T(2,128)(2,1)}, u32[]{:S(2)}) copy-start(bf16[1,1408]{1,0:T(2,128)(2,1)} %refs_5_.1) | copy-start | bytes 8452
  0.0 10.0 %copy-start.3 = (bf16[1,1408]{1,0:T(2,128)(2,1)S(1)}, bf16[1,1408]{1,0:T(2,128)(2,1)}, u32[]{:S(2)}) copy-start(bf16[1,1408]{1,0:T(2,128)(2,1)} %refs_4_.1) | copy-start | bytes 8452
  0.0 10.0 %copy-start.8 = (bf16[1,352]{1,0:T(2,128)(2,1)S(1)}, bf16[1,352]{1,0:T(2,128)(2,1)}, u32[]{:S(2)}) copy-start(bf16[1,352]{1,0:T(2,128)(2,1)} %refs_2_.1) | copy-start | bytes 2116
  0.0 10.0 %copy-start.7 = (bf16[1,352]{1,0:T(2,128)(2,1)S(1)}, bf16[1,352]{1,0:T(2,128)(2,1)}, u32[]{:S(2)}) copy-start(bf16[1,352]{1,0:T(2,128)(2,1)} %refs_1_.1) | copy-start | bytes 2116
  0.0 10.0 %copy-start.6 = (bf16[1,352]{1,0:T(2,128)(2,1)S(1)}, bf16[1,352]{1,0:T(2,128)(2,1)}, u32[]{:S(2)}) copy-start(bf16[1,352]{1,0:T(2,128)(2,1)} %refs_0_.1) | copy-start | bytes 2116
  0.0 10.0 %copy-start.2 = (bf16[1,7,7,352]{3,2,1,0:T(8,128)(2,1)S(1)}, bf16[1,7,7,352]{3,2,1,0:T(8,128)(2,1)}, u32[]{:S(2)}) copy-start(bf16[1,7,7,352]{3,2,1,0:T(8,128)(2,1)} %kernel.1) | copy-start | bytes 103492
  0.1 12.8 %collective-permute-start.4 = (bf16[352,704]{1,0:T(8,128)(2,1)}, bf16[352,704]{1,0:T(8,128)(2,1)S(1)}, u32[]{:S(2)}, u32[]{:S(2)}) collective-permute-start(bf16[352,704]{1,0:T(8,128)(2,1)} %bitcast.25), channel_id=1, source_target_pairs={{0,1},{1,0},{16,17},{17,16},{2,3},{3,2},{18,19},{19,18},{4,5},{5,4... | collective-permute-start | bytes 1486856 | tf_op jit(solution)/shard_map/ppermute | solution.py:407
  2.1 8.9 %collective-permute-start = (bf16[4,48,352]{2,1,0:T(8,128)(2,1)S(1)}, bf16[4,48,352]{2,1,0:T(8,128)(2,1)S(1)}, u32[]{:S(2)}, u32[]{:S(2)}) collective-permute-start(bf16[4,48,352]{2,1,0:T(8,128)(2,1)S(1)} %get-tuple-element.60), channel_id=1, source_target_pairs={{28,8},{30,10},{24,12},{26,14},{29,9},{31,11},{25,13},{27,15}} | collective-permute-start | bytes 405512 | tf_op jit(solution)/shard_map/ppermute | solution.py:402
  6.3 4.7 %collective-permute-start.1 = (bf16[4,48,352]{2,1,0:T(8,128)(2,1)S(1)}, bf16[4,48,352]{2,1,0:T(8,128)(2,1)S(1)}, u32[]{:S(2)}, u32[]{:S(2)}) collective-permute-start(bf16[4,48,352]{2,1,0:T(8,128)(2,1)S(1)} %get-tuple-element.62), channel_id=1, source_target_pairs={{30,8},{28,10},{26,12},{24,14},{31,9},{29,11},{27,13},{25,15}} | collective-permute-start | bytes 405512 | tf_op jit(solution)/shard_map/ppermute | solution.py:402
  8.6 4.3 %collective-permute-start.2 = (bf16[4,48,352]{2,1,0:T(8,128)(2,1)S(1)}, bf16[4,48,352]{2,1,0:T(8,128)(2,1)S(1)}, u32[]{:S(2)}, u32[]{:S(2)}) collective-permute-start(bf16[4,48,352]{2,1,0:T(8,128)(2,1)S(1)} %get-tuple-element.59), channel_id=1, source_target_pairs={{26,8},{24,10},{30,12},{28,14},{27,9},{25,11},{31,13},{29,15}} | collective-permute-start | bytes 405512 | tf_op jit(solution)/shard_map/ppermute | solution.py:402
  10.3 0.7 collective-permute-start.3
  12.9 4.1 %collective-permute-start.5 = (bf16[2,16,48,352]{3,2,1,0:T(8,128)(2,1)S(1)}, bf16[2,16,48,352]{3,2,1,0:T(8,128)(2,1)S(1)}, u32[]{:S(2)}, u32[]{:S(2)}) collective-permute-start(bf16[2,16,48,352]{3,2,1,0:T(8,128)(2,1)S(1)} %last_piece.2), channel_id=1, source_target_pairs={{8,0},{9,1},{10,2},{11,3},{12,4},{13,5},{14,6},{15,7}} | collective-permute-start | bytes 3244040 | tf_op jit(solution)/shard_map/ppermute | solution.py:430
  13.9 3.2 %collective-permute-start.6 = (bf16[704,352]{1,0:T(8,128)(2,1)S(1)}, bf16[704,352]{1,0:T(8,128)(2,1)S(1)}, u32[]{:S(2)}, u32[]{:S(2)}) collective-permute-start(bf16[704,352]{1,0:T(8,128)(2,1)S(1)} %bitcast.13), channel_id=1, source_target_pairs={{0,1},{1,0},{16,17},{17,16},{2,3},{3,2},{18,19},{19,18},{4,5},{5,4... | collective-permute-start | bytes 1486856 | tf_op jit(solution)/shard_map/ppermute | solution.py:407
  14.9 20.3 %collective-permute-start.8 = (bf16[704,704]{1,0:T(8,128)(2,1)S(1)}, bf16[704,704]{1,0:T(8,128)(2,1)S(1)}, u32[]{:S(2)}, u32[]{:S(2)}) collective-permute-start(bf16[704,704]{1,0:T(8,128)(2,1)S(1)} %maximum_maximum_fusion), channel_id=1, source_target_pairs={{8,9},{9,8},{24,25},{25,24},{10,11},{11,10},{26,27},{27,26},{12,13... | collective-permute-start | bytes 2973704 | tf_op jit(solution)/shard_map/ppermute | solution.py:407
  17.1 0.7 collective-permute-start.7
  35.4 2.8 %collective-permute-start.9 = (bf16[4,48,352]{2,1,0:T(8,128)(2,1)S(1)}, bf16[4,48,352]{2,1,0:T(8,128)(2,1)S(1)}, u32[]{:S(2)}, u32[]{:S(2)}) collective-permute-start(bf16[4,48,352]{2,1,0:T(8,128)(2,1)S(1)} %down_piece.8.refs_0_), channel_id=1, source_target_pairs={{8,16},{9,17},{10,18},{11,19},{12,20},{13,21},{14,22},{15,23}} | collective-permute-start | bytes 405512 | tf_op jit(solution)/shard_map/ppermute | solution.py:430
  36.2 2.1 %collective-permute-start.10 = (bf16[4,48,352]{2,1,0:T(8,128)(2,1)S(1)}, bf16[4,48,352]{2,1,0:T(8,128)(2,1)S(1)}, u32[]{:S(2)}, u32[]{:S(2)}) collective-permute-start(bf16[4,48,352]{2,1,0:T(8,128)(2,1)S(1)} %down_piece.9.refs_1_), channel_id=1, source_target_pairs={{8,16},{9,17},{10,18},{11,19},{12,20},{13,21},{14,22},{15,23}} | collective-permute-start | bytes 405512 | tf_op jit(solution)/shard_map/ppermute | solution.py:430
  36.9 1.5 %collective-permute-start.11 = (bf16[4,48,352]{2,1,0:T(8,128)(2,1)S(1)}, bf16[4,48,352]{2,1,0:T(8,128)(2,1)S(1)}, u32[]{:S(2)}, u32[]{:S(2)}) collective-permute-start(bf16[4,48,352]{2,1,0:T(8,128)(2,1)S(1)} %down_piece.10.refs_2_), channel_id=1, source_target_pairs={{8,16},{9,17},{10,18},{11,19},{12,20},{13,21},{14,22},{15,23}} | collective-permute-start | bytes 405512 | tf_op jit(solution)/shard_map/ppermute | solution.py:430
  37.6 0.8 collective-permute-start.12
  38.6 18.8 %collective-permute-start.13 = (bf16[16,48,352]{2,1,0:T(8,128)(2,1)S(1)}, bf16[16,48,352]{2,1,0:T(8,128)(2,1)S(1)}, u32[]{:S(2)}, u32[]{:S(2)}) collective-permute-start(bf16[16,48,352]{2,1,0:T(8,128)(2,1)S(1)} %mlp.1.prev), channel_id=1, source_target_pairs={{16,24},{17,25},{18,26},{19,27},{20,28},{21,29},{22,30},{23,31}} | collective-permute-start | bytes 1622024 | tf_op jit(solution)/shard_map/ppermute | solution.py:430
  64.9 6.8 %collective-permute-start.14 = (bf16[4,48,352]{2,1,0:T(8,128)(2,1)S(1)}, bf16[4,48,352]{2,1,0:T(8,128)(2,1)S(1)}, u32[]{:S(2)}, u32[]{:S(2)}) collective-permute-start(bf16[4,48,352]{2,1,0:T(8,128)(2,1)S(1)} %down_piece.13), channel_id=1, source_target_pairs={{0,4},{2,6},{4,0},{6,2},{1,5},{3,7},{5,1},{7,3},{8,12},{10,14},{12... | collective-permute-start | bytes 405512 | tf_op jit(solution)/shard_map/ppermute | solution.py:553
  68.2 6.1 %collective-permute-start.15 = (bf16[4,48,352]{2,1,0:T(8,128)(2,1)S(1)}, bf16[4,48,352]{2,1,0:T(8,128)(2,1)S(1)}, u32[]{:S(2)}, u32[]{:S(2)}) collective-permute-start(bf16[4,48,352]{2,1,0:T(8,128)(2,1)S(1)} %down_piece.14), channel_id=1, source_target_pairs={{0,6},{2,4},{4,2},{6,0},{1,7},{3,5},{5,3},{7,1},{8,14},{10,12},{12... | collective-permute-start | bytes 405512 | tf_op jit(solution)/shard_map/ppermute | solution.py:553
  70.0 5.6 %collective-permute-start.16 = (bf16[4,48,352]{2,1,0:T(8,128)(2,1)S(1)}, bf16[4,48,352]{2,1,0:T(8,128)(2,1)S(1)}, u32[]{:S(2)}, u32[]{:S(2)}) collective-permute-start(bf16[4,48,352]{2,1,0:T(8,128)(2,1)S(1)} %down_piece.15), channel_id=1, source_target_pairs={{0,2},{2,0},{4,6},{6,4},{1,3},{3,1},{5,7},{7,5},{8,10},{10,8},{12,... | collective-permute-start | bytes 405512 | tf_op jit(solution)/shard_map/ppermute | solution.py:553
  (3 other events, 12.8 us)

commit v16 on v15

--- a/solution.py
+++ b/solution.py
@@ -385,7 +385,7 @@
     lanes = -(-channels // LANES) * LANES
     half = proj_in.shape[2]
     span = depth_kernel.shape[1]
-    order = (0, 2, 3, 1)
+    order = (0, 2, 1, 3)
     bf16 = jnp.bfloat16
     whole = shape(height, width, channels, dtype=bf16)
     piece_shape = shape(rows, width, channels, dtype=bf16)

time: 77 us -> 77.7 us (level)
    ppermute x3, waiting for transfers between devices: 17.4 us -> 18.2 us  [other_half(): return lax.ppermute(x, ('section', 'dp'), pairs)]
    ppermute x3, waiting for transfers between devices: 1.85 us -> 1.01 us  [image_plan(): piece = lax.ppermute(piece, ('section', 'row'), pairs)]
  transfers between devices with their start and end apart: 17 -> 17, of which waited for: 6 -> 6; matrix products, arithmetic and copies ran while one was open for 2% -> 2% of each run, Pallas kernels for 3% -> 2%
where the time goes in v16:
time: 77.7 us; the launch traced here: 77.3 us
  waiting for transfers between devices  41.8 us (54%)
  starting transfers between devices  22.4 us (29%)
  Pallas kernels  10.7 us (14%)
  local copies, waits for them, and re-layouts  1.45 us (2%)
    ppermute x3, waiting for transfers between devices, other_half(): return lax.ppermute(x, ('section', 'dp'), pairs)  18.2 us
    ppermute x8, waiting for transfers between devices, send(): return lax.ppermute(x, 'section', [(start, end)])  17.3 us
    pallas_call x27, Pallas kernels, call(): pl.pallas_call(functools.partial(kernel, **static), out_shape=out, in_spe...  10.7 us
    ppermute x3, starting transfers between devices, image_plan(): piece = lax.ppermute(piece, ('section', 'row'), pairs)  7.79 us
    ppermute x8, starting transfers between devices, send(): return lax.ppermute(x, 'section', [(start, end)])  6.2 us
    ppermute x3, waiting for transfers between devices, image_plan(): lax.ppermute(piece, 'row', [(p, p ^ order[n]) for p in range(count)])  5.27 us
    ppermute x3, starting transfers between devices, image_plan(): lax.ppermute(piece, 'row', [(p, p ^ order[n]) for p in range(count)])  4.75 us
    ppermute x3, starting transfers between devices, other_half(): return lax.ppermute(x, ('section', 'dp'), pairs)  3.64 us
  transfers between devices with their start and end apart: 17, of which 6 were waited for; matrix products, arithmetic and copies ran while one was open for 2% of the time, Pallas kernels for 2%

profile of v16, /device:TPU:7, one launch (start us, length us, event | category | flops | bytes accessed | tf_op | source)
XLA Modules:
  0.0 77.3 jit_solution(6293524260422123742)
XLA Ops:
  0.1 0.8 %collective-permute-start.4 = (bf16[352,704]{1,0:T(8,128)(2,1)}, bf16[352,704]{1,0:T(8,128)(2,1)S(1)}, u32[]{:S(2)}, u32[]{:S(2)}) collective-permute-start(bf16[352,704]{1,0:T(8,128)(2,1)} %bitcast.25), channel_id=1, source_target_pairs={{0,1},{1,0},{16,17},{17,16},{2,3},{3,2},{18,19},{19,18},{4,5},{5,4... | collective-permute-start | bytes 1486856 | tf_op jit(solution)/shard_map/ppermute | solution.py:407
  0.9 1.2 %dynamic-slice_bitcast_fusion = (bf16[4,48,352]{2,1,0:T(8,128)(2,1)S(1)}, bf16[4,48,352]{2,1,0:T(8,128)(2,1)S(1)}, bf16[4,48,352]{2,1,0:T(8,128)(2,1)S(1)}, bf16[4,48,352]{2,1,0:T(8,128)(2,1)S(1)}) fusion(bf16[4,1,4,48,352]{4,3,2,1,0:T(8,128)(2,1)} %param.11, s32[]{:T(128)S(6)} %select_n.16, s32[]{:T(128)S(6)} %select_n.14, s32[]{:T(128)S(6)} %select_n.13, ...), kind=kLoop, calls=%fused_computation.1 | loop fusion | bytes 1081360 | tf_op jit(solution)/shard_map/squeeze | solution.py:399
  2.1 4.2 %collective-permute-start = (bf16[4,48,352]{2,1,0:T(8,128)(2,1)S(1)}, bf16[4,48,352]{2,1,0:T(8,128)(2,1)S(1)}, u32[]{:S(2)}, u32[]{:S(2)}) collective-permute-start(bf16[4,48,352]{2,1,0:T(8,128)(2,1)S(1)} %get-tuple-element.60), channel_id=1, source_target_pairs={{28,8},{30,10},{24,12},{26,14},{29,9},{31,11},{25,13},{27,15}} | collective-permute-start | bytes 405512 | tf_op jit(solution)/shard_map/ppermute | solution.py:402
  6.3 1.3 %collective-permute-start.1 = (bf16[4,48,352]{2,1,0:T(8,128)(2,1)S(1)}, bf16[4,48,352]{2,1,0:T(8,128)(2,1)S(1)}, u32[]{:S(2)}, u32[]{:S(2)}) collective-permute-start(bf16[4,48,352]{2,1,0:T(8,128)(2,1)S(1)} %get-tuple-element.62), channel_id=1, source_target_pairs={{26,8},{24,10},{30,12},{28,14},{27,9},{25,11},{31,13},{29,15}} | collective-permute-start | bytes 405512 | tf_op jit(solution)/shard_map/ppermute | solution.py:402
  7.6 2.3 %collective-permute-start.2 = (bf16[4,48,352]{2,1,0:T(8,128)(2,1)S(1)}, bf16[4,48,352]{2,1,0:T(8,128)(2,1)S(1)}, u32[]{:S(2)}, u32[]{:S(2)}) collective-permute-start(bf16[4,48,352]{2,1,0:T(8,128)(2,1)S(1)} %get-tuple-element.59), channel_id=1, source_target_pairs={{30,8},{28,10},{26,12},{24,14},{31,9},{29,11},{27,13},{25,15}} | collective-permute-start | bytes 405512 | tf_op jit(solution)/shard_map/ppermute | solution.py:402
  10.3 0.7 collective-permute-start.3
  11.0 1.0 %collective-permute-done.2.refs_3_ = bf16[4,48,352]{2,1,0:T(8,128)(2,1)S(1)} collective-permute-done((bf16[4,48,352]{2,1,0:T(8,128)(2,1)S(1)}, bf16[4,48,352]{2,1,0:T(8,128)(2,1)S(1)}, u32[]{:S(2)}, u32[]{:S(2)}) %collective-permute-start.2) | collective-permute-done | bytes 135200 | tf_op jit(solution)/shard_map/ppermute | solution.py:402
  12.0 0.9 %collective-permute-start.5 = (bf16[2,16,48,352]{3,2,1,0:T(8,128)(2,1)S(1)}, bf16[2,16,48,352]{3,2,1,0:T(8,128)(2,1)S(1)}, u32[]{:S(2)}, u32[]{:S(2)}) collective-permute-start(bf16[2,16,48,352]{3,2,1,0:T(8,128)(2,1)S(1)} %last_piece.2), channel_id=1, source_target_pairs={{8,0},{9,1},{10,2},{11,3},{12,4},{13,5},{14,6},{15,7}} | collective-permute-start | bytes 3244040 | tf_op jit(solution)/shard_map/ppermute | solution.py:430
  13.1 0.7 collective-permute-start.6
  14.0 2.1 %collective-permute-start.8 = (bf16[704,704]{1,0:T(8,128)(2,1)S(1)}, bf16[704,704]{1,0:T(8,128)(2,1)S(1)}, u32[]{:S(2)}, u32[]{:S(2)}) collective-permute-start(bf16[704,704]{1,0:T(8,128)(2,1)S(1)} %maximum_maximum_fusion), channel_id=1, source_target_pairs={{8,9},{9,8},{24,25},{25,24},{10,11},{11,10},{26,27},{27,26},{12,13... | collective-permute-start | bytes 2973704 | tf_op jit(solution)/shard_map/ppermute | solution.py:407
  16.3 0.7 collective-permute-start.7
  17.0 18.2 %collective-permute-done.8.w_in.packed.in_b = bf16[704,704]{1,0:T(8,128)(2,1)S(1)} collective-permute-done((bf16[704,704]{1,0:T(8,128)(2,1)S(1)}, bf16[704,704]{1,0:T(8,128)(2,1)S(1)}, u32[]{:S(2)}, u32[]{:S(2)}) %collective-permute-start.8) | collective-permute-done | bytes 991264 | tf_op jit(solution)/shard_map/ppermute | solution.py:407
  35.4 0.7 collective-permute-start.9
  36.2 0.7 collective-permute-start.10
  36.9 0.7 collective-permute-start.11
  37.6 0.7 collective-permute-start.12
  38.6 1.3 %collective-permute-start.13 = (bf16[16,48,352]{2,1,0:T(8,128)(2,1)S(1)}, bf16[16,48,352]{2,1,0:T(8,128)(2,1)S(1)}, u32[]{:S(2)}, u32[]{:S(2)}) collective-permute-start(bf16[16,48,352]{2,1,0:T(8,128)(2,1)S(1)} %mlp.1.prev), channel_id=1, source_target_pairs={{16,24},{17,25},{18,26},{19,27},{20,28},{21,29},{22,30},{23,31}} | collective-permute-start | bytes 1622024 | tf_op jit(solution)/shard_map/ppermute | solution.py:430
  39.9 17.3 %collective-permute-done.13.x = bf16[16,48,352]{2,1,0:T(8,128)(2,1)S(1)} collective-permute-done((bf16[16,48,352]{2,1,0:T(8,128)(2,1)S(1)}, bf16[16,48,352]{2,1,0:T(8,128)(2,1)S(1)}, u32[]{:S(2)}, u32[]{:S(2)}) %collective-permute-start.13) | collective-permute-done | bytes 540704 | tf_op jit(solution)/shard_map/ppermute | solution.py:430
  57.2 7.0 %conv_up.1 = (bf16[768,704]{1,0:T(8,128)(2,1)S(1)}, bf16[768,704]{1,0:T(8,128)(2,1)S(1)}, f32[2,1,704]{2,1,0:T(1,128)S(1)}) custom-call(s32[1]{0:T(128)} %bitcast.1.section, bf16[16,48,352]{2,1,0:T(8,128)(2,1)S(1)} %collective-permute-done.13.x, f32[64,384]{1,0:T(8,128)S(1)} %get-tuple-element.32.cpar.refs_7_, bf16[352,704]{1,0:T(8,128)(2,1)S(1)} %bitcast.30, ...), custom_call_target="tpu_custom_call" | custom-call | flops 761266176 | bytes 2142724 | tf_op jit(solution)/shard_map/conv_up/pallas_call | solution.py:343
  64.7 2.5 %collective-permute-start.14 = (bf16[4,48,352]{2,1,0:T(8,128)(2,1)S(1)}, bf16[4,48,352]{2,1,0:T(8,128)(2,1)S(1)}, u32[]{:S(2)}, u32[]{:S(2)}) collective-permute-start(bf16[4,48,352]{2,1,0:T(8,128)(2,1)S(1)} %down_piece.13), channel_id=1, source_target_pairs={{0,4},{2,6},{4,0},{6,2},{1,5},{3,7},{5,1},{7,3},{8,12},{10,14},{12... | collective-permute-start | bytes 405512 | tf_op jit(solution)/shard_map/ppermute | solution.py:553
  67.7 2.2 %collective-permute-start.15 = (bf16[4,48,352]{2,1,0:T(8,128)(2,1)S(1)}, bf16[4,48,352]{2,1,0:T(8,128)(2,1)S(1)}, u32[]{:S(2)}, u32[]{:S(2)}) collective-permute-start(bf16[4,48,352]{2,1,0:T(8,128)(2,1)S(1)} %down_piece.14), channel_id=1, source_target_pairs={{0,2},{2,0},{4,6},{6,4},{1,3},{3,1},{5,7},{7,5},{8,10},{10,8},{12,... | collective-permute-start | bytes 405512 | tf_op jit(solution)/shard_map/ppermute | solution.py:553
  71.0 1.2 %collective-permute-done.14.refs_1_ = bf16[4,48,352]{2,1,0:T(8,128)(2,1)S(1)} collective-permute-done((bf16[4,48,352]{2,1,0:T(8,128)(2,1)S(1)}, bf16[4,48,352]{2,1,0:T(8,128)(2,1)S(1)}, u32[]{:S(2)}, u32[]{:S(2)}) %collective-permute-start.14) | collective-permute-done | bytes 135200 | tf_op jit(solution)/shard_map/ppermute | solution.py:553
  72.9 3.4 %collective-permute-done.16.refs_3_ = bf16[4,48,352]{2,1,0:T(8,128)(2,1)S(1)} collective-permute-done((bf16[4,48,352]{2,1,0:T(8,128)(2,1)S(1)}, bf16[4,48,352]{2,1,0:T(8,128)(2,1)S(1)}, u32[]{:S(2)}, u32[]{:S(2)}) %collective-permute-start.16) | collective-permute-done | bytes 135200 | tf_op jit(solution)/shard_map/ppermute | solution.py:553
  76.3 0.8 %place.1 = bf16[1,4,1,4,48,352]{5,4,3,2,1,0:T(8,128)(2,1)} custom-call(s32[1]{0:T(128)} %bitcast.me, bf16[4,48,352]{2,1,0:T(8,128)(2,1)S(1)} %down_piece.12.refs_0_, bf16[4,48,352]{2,1,0:T(8,128)(2,1)S(1)} %collective-permute-done.14.refs_1_, bf16[4,48,352]{2,1,0:T(8,128)(2,1)S(1)} %collective-permute-done.15.refs_2_, ...), custom_call_target="tpu_custom_call" | custom-call | bytes 540676 | tf_op jit(solution)/shard_map/place/pallas_call | solution.py:343
  (60 shorter events, 4.0 us)
Async XLA Ops:
  0.0 9.9 %copy-start.5 = (bf16[1,1408]{1,0:T(2,128)(2,1)S(1)}, bf16[1,1408]{1,0:T(2,128)(2,1)}, u32[]{:S(2)}) copy-start(bf16[1,1408]{1,0:T(2,128)(2,1)} %refs_6_.1) | copy-start | bytes 8452
  0.0 9.9 %copy-start.4 = (bf16[1,1408]{1,0:T(2,128)(2,1)S(1)}, bf16[1,1408]{1,0:T(2,128)(2,1)}, u32[]{:S(2)}) copy-start(bf16[1,1408]{1,0:T(2,128)(2,1)} %refs_5_.1) | copy-start | bytes 8452
  0.0 10.0 %copy-start.3 = (bf16[1,1408]{1,0:T(2,128)(2,1)S(1)}, bf16[1,1408]{1,0:T(2,128)(2,1)}, u32[]{:S(2)}) copy-start(bf16[1,1408]{1,0:T(2,128)(2,1)} %refs_4_.1) | copy-start | bytes 8452
  0.0 10.0 %copy-start.8 = (bf16[1,352]{1,0:T(2,128)(2,1)S(1)}, bf16[1,352]{1,0:T(2,128)(2,1)}, u32[]{:S(2)}) copy-start(bf16[1,352]{1,0:T(2,128)(2,1)} %refs_2_.1) | copy-start | bytes 2116
  0.0 10.0 %copy-start.7 = (bf16[1,352]{1,0:T(2,128)(2,1)S(1)}, bf16[1,352]{1,0:T(2,128)(2,1)}, u32[]{:S(2)}) copy-start(bf16[1,352]{1,0:T(2,128)(2,1)} %refs_1_.1) | copy-start | bytes 2116
  0.0 10.0 %copy-start.6 = (bf16[1,352]{1,0:T(2,128)(2,1)S(1)}, bf16[1,352]{1,0:T(2,128)(2,1)}, u32[]{:S(2)}) copy-start(bf16[1,352]{1,0:T(2,128)(2,1)} %refs_0_.1) | copy-start | bytes 2116
  0.0 10.0 %copy-start.2 = (bf16[1,7,7,352]{3,2,1,0:T(8,128)(2,1)S(1)}, bf16[1,7,7,352]{3,2,1,0:T(8,128)(2,1)}, u32[]{:S(2)}) copy-start(bf16[1,7,7,352]{3,2,1,0:T(8,128)(2,1)} %kernel.1) | copy-start | bytes 103492
  0.1 12.0 %collective-permute-start.4 = (bf16[352,704]{1,0:T(8,128)(2,1)}, bf16[352,704]{1,0:T(8,128)(2,1)S(1)}, u32[]{:S(2)}, u32[]{:S(2)}) collective-permute-start(bf16[352,704]{1,0:T(8,128)(2,1)} %bitcast.25), channel_id=1, source_target_pairs={{0,1},{1,0},{16,17},{17,16},{2,3},{3,2},{18,19},{19,18},{4,5},{5,4... | collective-permute-start | bytes 1486856 | tf_op jit(solution)/shard_map/ppermute | solution.py:407
  2.1 8.9 %collective-permute-start = (bf16[4,48,352]{2,1,0:T(8,128)(2,1)S(1)}, bf16[4,48,352]{2,1,0:T(8,128)(2,1)S(1)}, u32[]{:S(2)}, u32[]{:S(2)}) collective-permute-start(bf16[4,48,352]{2,1,0:T(8,128)(2,1)S(1)} %get-tuple-element.60), channel_id=1, source_target_pairs={{28,8},{30,10},{24,12},{26,14},{29,9},{31,11},{25,13},{27,15}} | collective-permute-start | bytes 405512 | tf_op jit(solution)/shard_map/ppermute | solution.py:402
  6.3 4.7 %collective-permute-start.1 = (bf16[4,48,352]{2,1,0:T(8,128)(2,1)S(1)}, bf16[4,48,352]{2,1,0:T(8,128)(2,1)S(1)}, u32[]{:S(2)}, u32[]{:S(2)}) collective-permute-start(bf16[4,48,352]{2,1,0:T(8,128)(2,1)S(1)} %get-tuple-element.62), channel_id=1, source_target_pairs={{26,8},{24,10},{30,12},{28,14},{27,9},{25,11},{31,13},{29,15}} | collective-permute-start | bytes 405512 | tf_op jit(solution)/shard_map/ppermute | solution.py:402
  7.6 4.4 %collective-permute-start.2 = (bf16[4,48,352]{2,1,0:T(8,128)(2,1)S(1)}, bf16[4,48,352]{2,1,0:T(8,128)(2,1)S(1)}, u32[]{:S(2)}, u32[]{:S(2)}) collective-permute-start(bf16[4,48,352]{2,1,0:T(8,128)(2,1)S(1)} %get-tuple-element.59), channel_id=1, source_target_pairs={{30,8},{28,10},{26,12},{24,14},{31,9},{29,11},{27,13},{25,15}} | collective-permute-start | bytes 405512 | tf_op jit(solution)/shard_map/ppermute | solution.py:402
  10.3 0.7 collective-permute-start.3
  12.0 4.2 %collective-permute-start.5 = (bf16[2,16,48,352]{3,2,1,0:T(8,128)(2,1)S(1)}, bf16[2,16,48,352]{3,2,1,0:T(8,128)(2,1)S(1)}, u32[]{:S(2)}, u32[]{:S(2)}) collective-permute-start(bf16[2,16,48,352]{3,2,1,0:T(8,128)(2,1)S(1)} %last_piece.2), channel_id=1, source_target_pairs={{8,0},{9,1},{10,2},{11,3},{12,4},{13,5},{14,6},{15,7}} | collective-permute-start | bytes 3244040 | tf_op jit(solution)/shard_map/ppermute | solution.py:430
  13.1 3.2 %collective-permute-start.6 = (bf16[704,352]{1,0:T(8,128)(2,1)S(1)}, bf16[704,352]{1,0:T(8,128)(2,1)S(1)}, u32[]{:S(2)}, u32[]{:S(2)}) collective-permute-start(bf16[704,352]{1,0:T(8,128)(2,1)S(1)} %bitcast.13), channel_id=1, source_target_pairs={{0,1},{1,0},{16,17},{17,16},{2,3},{3,2},{18,19},{19,18},{4,5},{5,4... | collective-permute-start | bytes 1486856 | tf_op jit(solution)/shard_map/ppermute | solution.py:407
  14.0 21.2 %collective-permute-start.8 = (bf16[704,704]{1,0:T(8,128)(2,1)S(1)}, bf16[704,704]{1,0:T(8,128)(2,1)S(1)}, u32[]{:S(2)}, u32[]{:S(2)}) collective-permute-start(bf16[704,704]{1,0:T(8,128)(2,1)S(1)} %maximum_maximum_fusion), channel_id=1, source_target_pairs={{8,9},{9,8},{24,25},{25,24},{10,11},{11,10},{26,27},{27,26},{12,13... | collective-permute-start | bytes 2973704 | tf_op jit(solution)/shard_map/ppermute | solution.py:407
  16.3 0.7 collective-permute-start.7
  35.4 2.8 %collective-permute-start.9 = (bf16[4,48,352]{2,1,0:T(8,128)(2,1)S(1)}, bf16[4,48,352]{2,1,0:T(8,128)(2,1)S(1)}, u32[]{:S(2)}, u32[]{:S(2)}) collective-permute-start(bf16[4,48,352]{2,1,0:T(8,128)(2,1)S(1)} %down_piece.8.refs_0_), channel_id=1, source_target_pairs={{8,16},{9,17},{10,18},{11,19},{12,20},{13,21},{14,22},{15,23}} | collective-permute-start | bytes 405512 | tf_op jit(solution)/shard_map/ppermute | solution.py:430
  36.2 2.1 %collective-permute-start.10 = (bf16[4,48,352]{2,1,0:T(8,128)(2,1)S(1)}, bf16[4,48,352]{2,1,0:T(8,128)(2,1)S(1)}, u32[]{:S(2)}, u32[]{:S(2)}) collective-permute-start(bf16[4,48,352]{2,1,0:T(8,128)(2,1)S(1)} %down_piece.9.refs_1_), channel_id=1, source_target_pairs={{8,16},{9,17},{10,18},{11,19},{12,20},{13,21},{14,22},{15,23}} | collective-permute-start | bytes 405512 | tf_op jit(solution)/shard_map/ppermute | solution.py:430
  36.9 1.5 %collective-permute-start.11 = (bf16[4,48,352]{2,1,0:T(8,128)(2,1)S(1)}, bf16[4,48,352]{2,1,0:T(8,128)(2,1)S(1)}, u32[]{:S(2)}, u32[]{:S(2)}) collective-permute-start(bf16[4,48,352]{2,1,0:T(8,128)(2,1)S(1)} %down_piece.10.refs_2_), channel_id=1, source_target_pairs={{8,16},{9,17},{10,18},{11,19},{12,20},{13,21},{14,22},{15,23}} | collective-permute-start | bytes 405512 | tf_op jit(solution)/shard_map/ppermute | solution.py:430
  37.6 0.8 collective-permute-start.12
  38.6 18.6 %collective-permute-start.13 = (bf16[16,48,352]{2,1,0:T(8,128)(2,1)S(1)}, bf16[16,48,352]{2,1,0:T(8,128)(2,1)S(1)}, u32[]{:S(2)}, u32[]{:S(2)}) collective-permute-start(bf16[16,48,352]{2,1,0:T(8,128)(2,1)S(1)} %mlp.1.prev), channel_id=1, source_target_pairs={{16,24},{17,25},{18,26},{19,27},{20,28},{21,29},{22,30},{23,31}} | collective-permute-start | bytes 1622024 | tf_op jit(solution)/shard_map/ppermute | solution.py:430
  64.7 7.5 %collective-permute-start.14 = (bf16[4,48,352]{2,1,0:T(8,128)(2,1)S(1)}, bf16[4,48,352]{2,1,0:T(8,128)(2,1)S(1)}, u32[]{:S(2)}, u32[]{:S(2)}) collective-permute-start(bf16[4,48,352]{2,1,0:T(8,128)(2,1)S(1)} %down_piece.13), channel_id=1, source_target_pairs={{0,4},{2,6},{4,0},{6,2},{1,5},{3,7},{5,1},{7,3},{8,12},{10,14},{12... | collective-permute-start | bytes 405512 | tf_op jit(solution)/shard_map/ppermute | solution.py:553
  67.7 5.1 %collective-permute-start.15 = (bf16[4,48,352]{2,1,0:T(8,128)(2,1)S(1)}, bf16[4,48,352]{2,1,0:T(8,128)(2,1)S(1)}, u32[]{:S(2)}, u32[]{:S(2)}) collective-permute-start(bf16[4,48,352]{2,1,0:T(8,128)(2,1)S(1)} %down_piece.14), channel_id=1, source_target_pairs={{0,2},{2,0},{4,6},{6,4},{1,3},{3,1},{5,7},{7,5},{8,10},{10,8},{12,... | collective-permute-start | bytes 405512 | tf_op jit(solution)/shard_map/ppermute | solution.py:553
  70.4 5.9 %collective-permute-start.16 = (bf16[4,48,352]{2,1,0:T(8,128)(2,1)S(1)}, bf16[4,48,352]{2,1,0:T(8,128)(2,1)S(1)}, u32[]{:S(2)}, u32[]{:S(2)}) collective-permute-start(bf16[4,48,352]{2,1,0:T(8,128)(2,1)S(1)} %down_piece.15), channel_id=1, source_target_pairs={{0,6},{2,4},{4,2},{6,0},{1,7},{3,5},{5,3},{7,1},{8,14},{10,12},{12... | collective-permute-start | bytes 405512 | tf_op jit(solution)/shard_map/ppermute | solution.py:553
  (3 other events, 12.8 us)

commit v17 on v15

--- a/solution.py
+++ b/solution.py
@@ -13,7 +13,7 @@
 VMEM_BYTES = 20 * 1024 * 1024
 REACH = 3
 CHUNK = 4
-NORM_ROWS = 8
+NORM_ROWS = 16
 IN_ORDER = (0, 1, 2, 3)
 VECTORS = 56
 
@@ -71,7 +71,7 @@
                 cq[h, q, :, at] = acc[h]
             return carry
 
-        return lax.fori_loop(0, stride, column, carry)
+        return lax.fori_loop(0, stride, column, carry, unroll=2)
 
     lax.fori_loop(0, lanes // LANES, group, 0)
 

time: 77 us -> 76.4 us (level)
  no operation moved by 1% of the time
where the time goes in v17:
time: 76.4 us; the launch traced here: 76 us
  waiting for transfers between devices  41.1 us (54%)
  starting transfers between devices  21.8 us (29%)
  Pallas kernels  10.7 us (14%)
  local copies, waits for them, and re-layouts  1.45 us (2%)
    ppermute x3, waiting for transfers between devices, other_half(): return lax.ppermute(x, ('section', 'dp'), pairs)  17.4 us
    ppermute x8, waiting for transfers between devices, send(): return lax.ppermute(x, 'section', [(start, end)])  16.9 us
    pallas_call x27, Pallas kernels, call(): pl.pallas_call(functools.partial(kernel, **static), out_shape=out, in_spe...  10.7 us
    ppermute x3, starting transfers between devices, image_plan(): piece = lax.ppermute(piece, ('section', 'row'), pairs)  7.8 us
    ppermute x8, starting transfers between devices, send(): return lax.ppermute(x, 'section', [(start, end)])  6.2 us
    ppermute x3, waiting for transfers between devices, image_plan(): lax.ppermute(piece, 'row', [(p, p ^ order[n]) for p in range(count)])  5.05 us
    ppermute x3, starting transfers between devices, image_plan(): lax.ppermute(piece, 'row', [(p, p ^ order[n]) for p in range(count)])  4.18 us
    ppermute x3, starting transfers between devices, other_half(): return lax.ppermute(x, ('section', 'dp'), pairs)  3.64 us
  transfers between devices with their start and end apart: 17, of which 6 were waited for; matrix products, arithmetic and copies ran while one was open for 2% of the time, Pallas kernels for 3%

profile of v17, /device:TPU:7, one launch (start us, length us, event | category | flops | bytes accessed | tf_op | source)
XLA Modules:
  0.0 76.0 jit_solution(14933235086905404170)
XLA Ops:
  0.1 0.8 %collective-permute-start.4 = (bf16[352,704]{1,0:T(8,128)(2,1)}, bf16[352,704]{1,0:T(8,128)(2,1)S(1)}, u32[]{:S(2)}, u32[]{:S(2)}) collective-permute-start(bf16[352,704]{1,0:T(8,128)(2,1)} %bitcast.25), channel_id=1, source_target_pairs={{0,1},{1,0},{16,17},{17,16},{2,3},{3,2},{18,19},{19,18},{4,5},{5,4... | collective-permute-start | bytes 1486856 | tf_op jit(solution)/shard_map/ppermute | solution.py:407
  0.9 1.2 %dynamic-slice_bitcast_fusion = (bf16[4,48,352]{2,1,0:T(8,128)(2,1)S(1)}, bf16[4,48,352]{2,1,0:T(8,128)(2,1)S(1)}, bf16[4,48,352]{2,1,0:T(8,128)(2,1)S(1)}, bf16[4,48,352]{2,1,0:T(8,128)(2,1)S(1)}) fusion(bf16[4,1,4,48,352]{4,3,2,1,0:T(8,128)(2,1)} %param.11, s32[]{:T(128)S(6)} %select_n.16, s32[]{:T(128)S(6)} %select_n.14, s32[]{:T(128)S(6)} %select_n.13, ...), kind=kLoop, calls=%fused_computation.1 | loop fusion | bytes 1081360 | tf_op jit(solution)/shard_map/squeeze | solution.py:399
  2.1 4.2 %collective-permute-start = (bf16[4,48,352]{2,1,0:T(8,128)(2,1)S(1)}, bf16[4,48,352]{2,1,0:T(8,128)(2,1)S(1)}, u32[]{:S(2)}, u32[]{:S(2)}) collective-permute-start(bf16[4,48,352]{2,1,0:T(8,128)(2,1)S(1)} %get-tuple-element.60), channel_id=1, source_target_pairs={{28,8},{30,10},{24,12},{26,14},{29,9},{31,11},{25,13},{27,15}} | collective-permute-start | bytes 405512 | tf_op jit(solution)/shard_map/ppermute | solution.py:402
  6.3 2.3 %collective-permute-start.1 = (bf16[4,48,352]{2,1,0:T(8,128)(2,1)S(1)}, bf16[4,48,352]{2,1,0:T(8,128)(2,1)S(1)}, u32[]{:S(2)}, u32[]{:S(2)}) collective-permute-start(bf16[4,48,352]{2,1,0:T(8,128)(2,1)S(1)} %get-tuple-element.62), channel_id=1, source_target_pairs={{30,8},{28,10},{26,12},{24,14},{31,9},{29,11},{27,13},{25,15}} | collective-permute-start | bytes 405512 | tf_op jit(solution)/shard_map/ppermute | solution.py:402
  8.6 1.3 %collective-permute-start.2 = (bf16[4,48,352]{2,1,0:T(8,128)(2,1)S(1)}, bf16[4,48,352]{2,1,0:T(8,128)(2,1)S(1)}, u32[]{:S(2)}, u32[]{:S(2)}) collective-permute-start(bf16[4,48,352]{2,1,0:T(8,128)(2,1)S(1)} %get-tuple-element.59), channel_id=1, source_target_pairs={{26,8},{24,10},{30,12},{28,14},{27,9},{25,11},{31,13},{29,15}} | collective-permute-start | bytes 405512 | tf_op jit(solution)/shard_map/ppermute | solution.py:402
  11.0 1.8 %collective-permute-done.2.refs_3_ = bf16[4,48,352]{2,1,0:T(8,128)(2,1)S(1)} collective-permute-done((bf16[4,48,352]{2,1,0:T(8,128)(2,1)S(1)}, bf16[4,48,352]{2,1,0:T(8,128)(2,1)S(1)}, u32[]{:S(2)}, u32[]{:S(2)}) %collective-permute-start.2) | collective-permute-done | bytes 135200 | tf_op jit(solution)/shard_map/ppermute | solution.py:402
  12.9 0.9 %collective-permute-start.5 = (bf16[2,16,48,352]{3,2,1,0:T(8,128)(2,1)S(1)}, bf16[2,16,48,352]{3,2,1,0:T(8,128)(2,1)S(1)}, u32[]{:S(2)}, u32[]{:S(2)}) collective-permute-start(bf16[2,16,48,352]{3,2,1,0:T(8,128)(2,1)S(1)} %last_piece.2), channel_id=1, source_target_pairs={{8,0},{9,1},{10,2},{11,3},{12,4},{13,5},{14,6},{15,7}} | collective-permute-start | bytes 3244040 | tf_op jit(solution)/shard_map/ppermute | solution.py:430
  13.9 0.7 collective-permute-start.6
  14.9 2.1 %collective-permute-start.8 = (bf16[704,704]{1,0:T(8,128)(2,1)S(1)}, bf16[704,704]{1,0:T(8,128)(2,1)S(1)}, u32[]{:S(2)}, u32[]{:S(2)}) collective-permute-start(bf16[704,704]{1,0:T(8,128)(2,1)S(1)} %maximum_maximum_fusion), channel_id=1, source_target_pairs={{8,9},{9,8},{24,25},{25,24},{10,11},{11,10},{26,27},{27,26},{12,13... | collective-permute-start | bytes 2973704 | tf_op jit(solution)/shard_map/ppermute | solution.py:407
  17.1 0.7 collective-permute-start.7
  17.9 17.4 %collective-permute-done.8.w_in.packed.in_b = bf16[704,704]{1,0:T(8,128)(2,1)S(1)} collective-permute-done((bf16[704,704]{1,0:T(8,128)(2,1)S(1)}, bf16[704,704]{1,0:T(8,128)(2,1)S(1)}, u32[]{:S(2)}, u32[]{:S(2)}) %collective-permute-start.8) | collective-permute-done | bytes 991264 | tf_op jit(solution)/shard_map/ppermute | solution.py:407
  35.4 0.7 collective-permute-start.9
  36.2 0.7 collective-permute-start.10
  36.9 0.7 collective-permute-start.11
  37.6 0.7 collective-permute-start.12
  38.6 1.3 %collective-permute-start.13 = (bf16[16,48,352]{2,1,0:T(8,128)(2,1)S(1)}, bf16[16,48,352]{2,1,0:T(8,128)(2,1)S(1)}, u32[]{:S(2)}, u32[]{:S(2)}) collective-permute-start(bf16[16,48,352]{2,1,0:T(8,128)(2,1)S(1)} %mlp.1.prev), channel_id=1, source_target_pairs={{16,24},{17,25},{18,26},{19,27},{20,28},{21,29},{22,30},{23,31}} | collective-permute-start | bytes 1622024 | tf_op jit(solution)/shard_map/ppermute | solution.py:430
  39.9 16.9 %collective-permute-done.13.x = bf16[16,48,352]{2,1,0:T(8,128)(2,1)S(1)} collective-permute-done((bf16[16,48,352]{2,1,0:T(8,128)(2,1)S(1)}, bf16[16,48,352]{2,1,0:T(8,128)(2,1)S(1)}, u32[]{:S(2)}, u32[]{:S(2)}) %collective-permute-start.13) | collective-permute-done | bytes 540704 | tf_op jit(solution)/shard_map/ppermute | solution.py:430
  56.8 7.0 %conv_up.1 = (bf16[768,704]{1,0:T(8,128)(2,1)S(1)}, bf16[768,704]{1,0:T(8,128)(2,1)S(1)}, f32[2,1,704]{2,1,0:T(1,128)S(1)}) custom-call(s32[1]{0:T(128)} %bitcast.1.section, bf16[16,48,352]{2,1,0:T(8,128)(2,1)S(1)} %collective-permute-done.13.x, f32[64,384]{1,0:T(8,128)S(1)} %get-tuple-element.32.cpar.refs_7_, bf16[352,704]{1,0:T(8,128)(2,1)S(1)} %bitcast.30, ...), custom_call_target="tpu_custom_call" | custom-call | flops 761266176 | bytes 2142724 | tf_op jit(solution)/shard_map/conv_up/pallas_call | solution.py:343
  64.3 2.8 %collective-permute-start.14 = (bf16[4,48,352]{2,1,0:T(8,128)(2,1)S(1)}, bf16[4,48,352]{2,1,0:T(8,128)(2,1)S(1)}, u32[]{:S(2)}, u32[]{:S(2)}) collective-permute-start(bf16[4,48,352]{2,1,0:T(8,128)(2,1)S(1)} %down_piece.13), channel_id=1, source_target_pairs={{0,4},{2,6},{4,0},{6,2},{1,5},{3,7},{5,1},{7,3},{8,12},{10,14},{12... | collective-permute-start | bytes 405512 | tf_op jit(solution)/shard_map/ppermute | solution.py:553
  67.6 1.3 %collective-permute-start.15 = (bf16[4,48,352]{2,1,0:T(8,128)(2,1)S(1)}, bf16[4,48,352]{2,1,0:T(8,128)(2,1)S(1)}, u32[]{:S(2)}, u32[]{:S(2)}) collective-permute-start(bf16[4,48,352]{2,1,0:T(8,128)(2,1)S(1)} %down_piece.14), channel_id=1, source_target_pairs={{0,6},{2,4},{4,2},{6,0},{1,7},{3,5},{5,3},{7,1},{8,14},{10,12},{12... | collective-permute-start | bytes 405512 | tf_op jit(solution)/shard_map/ppermute | solution.py:553
  70.0 1.2 %collective-permute-done.14.refs_1_ = bf16[4,48,352]{2,1,0:T(8,128)(2,1)S(1)} collective-permute-done((bf16[4,48,352]{2,1,0:T(8,128)(2,1)S(1)}, bf16[4,48,352]{2,1,0:T(8,128)(2,1)S(1)}, u32[]{:S(2)}, u32[]{:S(2)}) %collective-permute-start.14) | collective-permute-done | bytes 135200 | tf_op jit(solution)/shard_map/ppermute | solution.py:553
  71.2 2.4 %collective-permute-done.15.refs_2_ = bf16[4,48,352]{2,1,0:T(8,128)(2,1)S(1)} collective-permute-done((bf16[4,48,352]{2,1,0:T(8,128)(2,1)S(1)}, bf16[4,48,352]{2,1,0:T(8,128)(2,1)S(1)}, u32[]{:S(2)}, u32[]{:S(2)}) %collective-permute-start.15) | collective-permute-done | bytes 135200 | tf_op jit(solution)/shard_map/ppermute | solution.py:553
  73.6 1.4 %collective-permute-done.16.refs_3_ = bf16[4,48,352]{2,1,0:T(8,128)(2,1)S(1)} collective-permute-done((bf16[4,48,352]{2,1,0:T(8,128)(2,1)S(1)}, bf16[4,48,352]{2,1,0:T(8,128)(2,1)S(1)}, u32[]{:S(2)}, u32[]{:S(2)}) %collective-permute-start.16) | collective-permute-done | bytes 135200 | tf_op jit(solution)/shard_map/ppermute | solution.py:553
  75.0 0.8 %place.1 = bf16[1,4,1,4,48,352]{5,4,3,2,1,0:T(8,128)(2,1)} custom-call(s32[1]{0:T(128)} %bitcast.me, bf16[4,48,352]{2,1,0:T(8,128)(2,1)S(1)} %down_piece.12.refs_0_, bf16[4,48,352]{2,1,0:T(8,128)(2,1)S(1)} %collective-permute-done.14.refs_1_, bf16[4,48,352]{2,1,0:T(8,128)(2,1)S(1)} %collective-permute-done.15.refs_2_, ...), custom_call_target="tpu_custom_call" | custom-call | bytes 540676 | tf_op jit(solution)/shard_map/place/pallas_call | solution.py:343
  (60 shorter events, 4.0 us)
Async XLA Ops:
  0.0 9.9 %copy-start.5 = (bf16[1,1408]{1,0:T(2,128)(2,1)S(1)}, bf16[1,1408]{1,0:T(2,128)(2,1)}, u32[]{:S(2)}) copy-start(bf16[1,1408]{1,0:T(2,128)(2,1)} %refs_6_.1) | copy-start | bytes 8452
  0.0 10.0 %copy-start.4 = (bf16[1,1408]{1,0:T(2,128)(2,1)S(1)}, bf16[1,1408]{1,0:T(2,128)(2,1)}, u32[]{:S(2)}) copy-start(bf16[1,1408]{1,0:T(2,128)(2,1)} %refs_5_.1) | copy-start | bytes 8452
  0.0 10.0 %copy-start.3 = (bf16[1,1408]{1,0:T(2,128)(2,1)S(1)}, bf16[1,1408]{1,0:T(2,128)(2,1)}, u32[]{:S(2)}) copy-start(bf16[1,1408]{1,0:T(2,128)(2,1)} %refs_4_.1) | copy-start | bytes 8452
  0.0 10.0 %copy-start.8 = (bf16[1,352]{1,0:T(2,128)(2,1)S(1)}, bf16[1,352]{1,0:T(2,128)(2,1)}, u32[]{:S(2)}) copy-start(bf16[1,352]{1,0:T(2,128)(2,1)} %refs_2_.1) | copy-start | bytes 2116
  0.0 10.0 %copy-start.7 = (bf16[1,352]{1,0:T(2,128)(2,1)S(1)}, bf16[1,352]{1,0:T(2,128)(2,1)}, u32[]{:S(2)}) copy-start(bf16[1,352]{1,0:T(2,128)(2,1)} %refs_1_.1) | copy-start | bytes 2116
  0.0 10.0 %copy-start.6 = (bf16[1,352]{1,0:T(2,128)(2,1)S(1)}, bf16[1,352]{1,0:T(2,128)(2,1)}, u32[]{:S(2)}) copy-start(bf16[1,352]{1,0:T(2,128)(2,1)} %refs_0_.1) | copy-start | bytes 2116
  0.0 10.0 %copy-start.2 = (bf16[1,7,7,352]{3,2,1,0:T(8,128)(2,1)S(1)}, bf16[1,7,7,352]{3,2,1,0:T(8,128)(2,1)}, u32[]{:S(2)}) copy-start(bf16[1,7,7,352]{3,2,1,0:T(8,128)(2,1)} %kernel.1) | copy-start | bytes 103492
  0.1 12.8 %collective-permute-start.4 = (bf16[352,704]{1,0:T(8,128)(2,1)}, bf16[352,704]{1,0:T(8,128)(2,1)S(1)}, u32[]{:S(2)}, u32[]{:S(2)}) collective-permute-start(bf16[352,704]{1,0:T(8,128)(2,1)} %bitcast.25), channel_id=1, source_target_pairs={{0,1},{1,0},{16,17},{17,16},{2,3},{3,2},{18,19},{19,18},{4,5},{5,4... | collective-permute-start | bytes 1486856 | tf_op jit(solution)/shard_map/ppermute | solution.py:407
  2.1 8.9 %collective-permute-start = (bf16[4,48,352]{2,1,0:T(8,128)(2,1)S(1)}, bf16[4,48,352]{2,1,0:T(8,128)(2,1)S(1)}, u32[]{:S(2)}, u32[]{:S(2)}) collective-permute-start(bf16[4,48,352]{2,1,0:T(8,128)(2,1)S(1)} %get-tuple-element.60), channel_id=1, source_target_pairs={{28,8},{30,10},{24,12},{26,14},{29,9},{31,11},{25,13},{27,15}} | collective-permute-start | bytes 405512 | tf_op jit(solution)/shard_map/ppermute | solution.py:402
  6.3 4.7 %collective-permute-start.1 = (bf16[4,48,352]{2,1,0:T(8,128)(2,1)S(1)}, bf16[4,48,352]{2,1,0:T(8,128)(2,1)S(1)}, u32[]{:S(2)}, u32[]{:S(2)}) collective-permute-start(bf16[4,48,352]{2,1,0:T(8,128)(2,1)S(1)} %get-tuple-element.62), channel_id=1, source_target_pairs={{30,8},{28,10},{26,12},{24,14},{31,9},{29,11},{27,13},{25,15}} | collective-permute-start | bytes 405512 | tf_op jit(solution)/shard_map/ppermute | solution.py:402
  8.6 4.3 %collective-permute-start.2 = (bf16[4,48,352]{2,1,0:T(8,128)(2,1)S(1)}, bf16[4,48,352]{2,1,0:T(8,128)(2,1)S(1)}, u32[]{:S(2)}, u32[]{:S(2)}) collective-permute-start(bf16[4,48,352]{2,1,0:T(8,128)(2,1)S(1)} %get-tuple-element.59), channel_id=1, source_target_pairs={{26,8},{24,10},{30,12},{28,14},{27,9},{25,11},{31,13},{29,15}} | collective-permute-start | bytes 405512 | tf_op jit(solution)/shard_map/ppermute | solution.py:402
  10.3 0.7 collective-permute-start.3
  12.9 4.1 %collective-permute-start.5 = (bf16[2,16,48,352]{3,2,1,0:T(8,128)(2,1)S(1)}, bf16[2,16,48,352]{3,2,1,0:T(8,128)(2,1)S(1)}, u32[]{:S(2)}, u32[]{:S(2)}) collective-permute-start(bf16[2,16,48,352]{3,2,1,0:T(8,128)(2,1)S(1)} %last_piece.2), channel_id=1, source_target_pairs={{8,0},{9,1},{10,2},{11,3},{12,4},{13,5},{14,6},{15,7}} | collective-permute-start | bytes 3244040 | tf_op jit(solution)/shard_map/ppermute | solution.py:430
  13.9 3.2 %collective-permute-start.6 = (bf16[704,352]{1,0:T(8,128)(2,1)S(1)}, bf16[704,352]{1,0:T(8,128)(2,1)S(1)}, u32[]{:S(2)}, u32[]{:S(2)}) collective-permute-start(bf16[704,352]{1,0:T(8,128)(2,1)S(1)} %bitcast.13), channel_id=1, source_target_pairs={{0,1},{1,0},{16,17},{17,16},{2,3},{3,2},{18,19},{19,18},{4,5},{5,4... | collective-permute-start | bytes 1486856 | tf_op jit(solution)/shard_map/ppermute | solution.py:407
  14.9 20.3 %collective-permute-start.8 = (bf16[704,704]{1,0:T(8,128)(2,1)S(1)}, bf16[704,704]{1,0:T(8,128)(2,1)S(1)}, u32[]{:S(2)}, u32[]{:S(2)}) collective-permute-start(bf16[704,704]{1,0:T(8,128)(2,1)S(1)} %maximum_maximum_fusion), channel_id=1, source_target_pairs={{8,9},{9,8},{24,25},{25,24},{10,11},{11,10},{26,27},{27,26},{12,13... | collective-permute-start | bytes 2973704 | tf_op jit(solution)/shard_map/ppermute | solution.py:407
  17.1 0.7 collective-permute-start.7
  35.4 2.8 %collective-permute-start.9 = (bf16[4,48,352]{2,1,0:T(8,128)(2,1)S(1)}, bf16[4,48,352]{2,1,0:T(8,128)(2,1)S(1)}, u32[]{:S(2)}, u32[]{:S(2)}) collective-permute-start(bf16[4,48,352]{2,1,0:T(8,128)(2,1)S(1)} %down_piece.8.refs_0_), channel_id=1, source_target_pairs={{8,16},{9,17},{10,18},{11,19},{12,20},{13,21},{14,22},{15,23}} | collective-permute-start | bytes 405512 | tf_op jit(solution)/shard_map/ppermute | solution.py:430
  36.2 2.1 %collective-permute-start.10 = (bf16[4,48,352]{2,1,0:T(8,128)(2,1)S(1)}, bf16[4,48,352]{2,1,0:T(8,128)(2,1)S(1)}, u32[]{:S(2)}, u32[]{:S(2)}) collective-permute-start(bf16[4,48,352]{2,1,0:T(8,128)(2,1)S(1)} %down_piece.9.refs_1_), channel_id=1, source_target_pairs={{8,16},{9,17},{10,18},{11,19},{12,20},{13,21},{14,22},{15,23}} | collective-permute-start | bytes 405512 | tf_op jit(solution)/shard_map/ppermute | solution.py:430
  36.9 1.5 %collective-permute-start.11 = (bf16[4,48,352]{2,1,0:T(8,128)(2,1)S(1)}, bf16[4,48,352]{2,1,0:T(8,128)(2,1)S(1)}, u32[]{:S(2)}, u32[]{:S(2)}) collective-permute-start(bf16[4,48,352]{2,1,0:T(8,128)(2,1)S(1)} %down_piece.10.refs_2_), channel_id=1, source_target_pairs={{8,16},{9,17},{10,18},{11,19},{12,20},{13,21},{14,22},{15,23}} | collective-permute-start | bytes 405512 | tf_op jit(solution)/shard_map/ppermute | solution.py:430
  37.6 0.8 %collective-permute-start.12 = (bf16[4,48,352]{2,1,0:T(8,128)(2,1)S(1)}, bf16[4,48,352]{2,1,0:T(8,128)(2,1)S(1)}, u32[]{:S(2)}, u32[]{:S(2)}) collective-permute-start(bf16[4,48,352]{2,1,0:T(8,128)(2,1)S(1)} %down_piece.11.refs_3_), channel_id=1, source_target_pairs={{8,16},{9,17},{10,18},{11,19},{12,20},{13,21},{14,22},{15,23}} | collective-permute-start | bytes 405512 | tf_op jit(solution)/shard_map/ppermute | solution.py:430
  38.6 18.2 %collective-permute-start.13 = (bf16[16,48,352]{2,1,0:T(8,128)(2,1)S(1)}, bf16[16,48,352]{2,1,0:T(8,128)(2,1)S(1)}, u32[]{:S(2)}, u32[]{:S(2)}) collective-permute-start(bf16[16,48,352]{2,1,0:T(8,128)(2,1)S(1)} %mlp.1.prev), channel_id=1, source_target_pairs={{16,24},{17,25},{18,26},{19,27},{20,28},{21,29},{22,30},{23,31}} | collective-permute-start | bytes 1622024 | tf_op jit(solution)/shard_map/ppermute | solution.py:430
  64.3 6.9 %collective-permute-start.14 = (bf16[4,48,352]{2,1,0:T(8,128)(2,1)S(1)}, bf16[4,48,352]{2,1,0:T(8,128)(2,1)S(1)}, u32[]{:S(2)}, u32[]{:S(2)}) collective-permute-start(bf16[4,48,352]{2,1,0:T(8,128)(2,1)S(1)} %down_piece.13), channel_id=1, source_target_pairs={{0,4},{2,6},{4,0},{6,2},{1,5},{3,7},{5,1},{7,3},{8,12},{10,14},{12... | collective-permute-start | bytes 405512 | tf_op jit(solution)/shard_map/ppermute | solution.py:553
  67.6 6.1 %collective-permute-start.15 = (bf16[4,48,352]{2,1,0:T(8,128)(2,1)S(1)}, bf16[4,48,352]{2,1,0:T(8,128)(2,1)S(1)}, u32[]{:S(2)}, u32[]{:S(2)}) collective-permute-start(bf16[4,48,352]{2,1,0:T(8,128)(2,1)S(1)} %down_piece.14), channel_id=1, source_target_pairs={{0,6},{2,4},{4,2},{6,0},{1,7},{3,5},{5,3},{7,1},{8,14},{10,12},{12... | collective-permute-start | bytes 405512 | tf_op jit(solution)/shard_map/ppermute | solution.py:553
  69.4 5.6 %collective-permute-start.16 = (bf16[4,48,352]{2,1,0:T(8,128)(2,1)S(1)}, bf16[4,48,352]{2,1,0:T(8,128)(2,1)S(1)}, u32[]{:S(2)}, u32[]{:S(2)}) collective-permute-start(bf16[4,48,352]{2,1,0:T(8,128)(2,1)S(1)} %down_piece.15), channel_id=1, source_target_pairs={{0,2},{2,0},{4,6},{6,4},{1,3},{3,1},{5,7},{7,5},{8,10},{10,8},{12,... | collective-permute-start | bytes 405512 | tf_op jit(solution)/shard_map/ppermute | solution.py:553
  (3 other events, 12.8 us)

commit v18 on v17

--- a/solution.py
+++ b/solution.py
@@ -23,9 +23,14 @@
     stride = reach_cols - 2 * REACH
     width = stride * blocks
     groups = lanes // LANES
-    xp[...] = jnp.zeros(xp.shape, jnp.float32)
-
     unroll = min(height, NORM_ROWS)
+    border = jnp.zeros((unroll * groups, 8, LANES), jnp.float32)
+    xp[0 : unroll * groups, 0:8, :] = border
+    xp[0 : unroll * groups, 8 + width : 16 + width, :] = border
+    if lanes > channels:
+        for k in range(unroll):
+            last = k * groups + groups - 1
+            xp[last, 8 : 8 + width, :] = jnp.zeros((width, LANES), jnp.float32)
 
     def rows(n, carry):
         for k in range(unroll):

time: 76.4 us -> 76.3 us (level)
  no operation moved by 1% of the time
where the time goes in v18:
time: 76.3 us; the launch traced here: 75.9 us
  waiting for transfers between devices  41 us (54%)
  starting transfers between devices  21.8 us (29%)
  Pallas kernels  10.7 us (14%)
  local copies, waits for them, and re-layouts  1.45 us (2%)
    ppermute x3, waiting for transfers between devices, other_half(): return lax.ppermute(x, ('section', 'dp'), pairs)  17.4 us
    ppermute x8, waiting for transfers between devices, send(): return lax.ppermute(x, 'section', [(start, end)])  16.8 us
    pallas_call x27, Pallas kernels, call(): pl.pallas_call(functools.partial(kernel, **static), out_shape=out, in_spe...  10.7 us
    ppermute x3, starting transfers between devices, image_plan(): piece = lax.ppermute(piece, ('section', 'row'), pairs)  7.8 us
    ppermute x8, starting transfers between devices, send(): return lax.ppermute(x, 'section', [(start, end)])  6.2 us
    ppermute x3, waiting for transfers between devices, image_plan(): lax.ppermute(piece, 'row', [(p, p ^ order[n]) for p in range(count)])  5.05 us
    ppermute x3, starting transfers between devices, image_plan(): lax.ppermute(piece, 'row', [(p, p ^ order[n]) for p in range(count)])  4.18 us
    ppermute x3, starting transfers between devices, other_half(): return lax.ppermute(x, ('section', 'dp'), pairs)  3.64 us
  transfers between devices with their start and end apart: 17, of which 6 were waited for; matrix products, arithmetic and copies ran while one was open for 2% of the time, Pallas kernels for 3%

profile of v18, /device:TPU:7, one launch (start us, length us, event | category | flops | bytes accessed | tf_op | source)
XLA Modules:
  0.0 75.9 jit_solution(14737005204840609882)
XLA Ops:
  0.1 0.8 %collective-permute-start.4 = (bf16[352,704]{1,0:T(8,128)(2,1)}, bf16[352,704]{1,0:T(8,128)(2,1)S(1)}, u32[]{:S(2)}, u32[]{:S(2)}) collective-permute-start(bf16[352,704]{1,0:T(8,128)(2,1)} %bitcast.25), channel_id=1, source_target_pairs={{0,1},{1,0},{16,17},{17,16},{2,3},{3,2},{18,19},{19,18},{4,5},{5,4... | collective-permute-start | bytes 1486856 | tf_op jit(solution)/shard_map/ppermute | solution.py:412
  0.9 1.2 %dynamic-slice_bitcast_fusion = (bf16[4,48,352]{2,1,0:T(8,128)(2,1)S(1)}, bf16[4,48,352]{2,1,0:T(8,128)(2,1)S(1)}, bf16[4,48,352]{2,1,0:T(8,128)(2,1)S(1)}, bf16[4,48,352]{2,1,0:T(8,128)(2,1)S(1)}) fusion(bf16[4,1,4,48,352]{4,3,2,1,0:T(8,128)(2,1)} %param.11, s32[]{:T(128)S(6)} %select_n.16, s32[]{:T(128)S(6)} %select_n.14, s32[]{:T(128)S(6)} %select_n.13, ...), kind=kLoop, calls=%fused_computation.1 | loop fusion | bytes 1081360 | tf_op jit(solution)/shard_map/squeeze | solution.py:404
  2.1 4.2 %collective-permute-start = (bf16[4,48,352]{2,1,0:T(8,128)(2,1)S(1)}, bf16[4,48,352]{2,1,0:T(8,128)(2,1)S(1)}, u32[]{:S(2)}, u32[]{:S(2)}) collective-permute-start(bf16[4,48,352]{2,1,0:T(8,128)(2,1)S(1)} %get-tuple-element.60), channel_id=1, source_target_pairs={{28,8},{30,10},{24,12},{26,14},{29,9},{31,11},{25,13},{27,15}} | collective-permute-start | bytes 405512 | tf_op jit(solution)/shard_map/ppermute | solution.py:407
  6.3 2.3 %collective-permute-start.1 = (bf16[4,48,352]{2,1,0:T(8,128)(2,1)S(1)}, bf16[4,48,352]{2,1,0:T(8,128)(2,1)S(1)}, u32[]{:S(2)}, u32[]{:S(2)}) collective-permute-start(bf16[4,48,352]{2,1,0:T(8,128)(2,1)S(1)} %get-tuple-element.62), channel_id=1, source_target_pairs={{30,8},{28,10},{26,12},{24,14},{31,9},{29,11},{27,13},{25,15}} | collective-permute-start | bytes 405512 | tf_op jit(solution)/shard_map/ppermute | solution.py:407
  8.6 1.3 %collective-permute-start.2 = (bf16[4,48,352]{2,1,0:T(8,128)(2,1)S(1)}, bf16[4,48,352]{2,1,0:T(8,128)(2,1)S(1)}, u32[]{:S(2)}, u32[]{:S(2)}) collective-permute-start(bf16[4,48,352]{2,1,0:T(8,128)(2,1)S(1)} %get-tuple-element.59), channel_id=1, source_target_pairs={{26,8},{24,10},{30,12},{28,14},{27,9},{25,11},{31,13},{29,15}} | collective-permute-start | bytes 405512 | tf_op jit(solution)/shard_map/ppermute | solution.py:407
  11.0 1.8 %collective-permute-done.2.refs_3_ = bf16[4,48,352]{2,1,0:T(8,128)(2,1)S(1)} collective-permute-done((bf16[4,48,352]{2,1,0:T(8,128)(2,1)S(1)}, bf16[4,48,352]{2,1,0:T(8,128)(2,1)S(1)}, u32[]{:S(2)}, u32[]{:S(2)}) %collective-permute-start.2) | collective-permute-done | bytes 135200 | tf_op jit(solution)/shard_map/ppermute | solution.py:407
  12.9 0.9 %collective-permute-start.5 = (bf16[2,16,48,352]{3,2,1,0:T(8,128)(2,1)S(1)}, bf16[2,16,48,352]{3,2,1,0:T(8,128)(2,1)S(1)}, u32[]{:S(2)}, u32[]{:S(2)}) collective-permute-start(bf16[2,16,48,352]{3,2,1,0:T(8,128)(2,1)S(1)} %last_piece.2), channel_id=1, source_target_pairs={{8,0},{9,1},{10,2},{11,3},{12,4},{13,5},{14,6},{15,7}} | collective-permute-start | bytes 3244040 | tf_op jit(solution)/shard_map/ppermute | solution.py:435
  13.9 0.7 collective-permute-start.6
  14.9 2.1 %collective-permute-start.8 = (bf16[704,704]{1,0:T(8,128)(2,1)S(1)}, bf16[704,704]{1,0:T(8,128)(2,1)S(1)}, u32[]{:S(2)}, u32[]{:S(2)}) collective-permute-start(bf16[704,704]{1,0:T(8,128)(2,1)S(1)} %maximum_maximum_fusion), channel_id=1, source_target_pairs={{8,9},{9,8},{24,25},{25,24},{10,11},{11,10},{26,27},{27,26},{12,13... | collective-permute-start | bytes 2973704 | tf_op jit(solution)/shard_map/ppermute | solution.py:412
  17.1 0.7 collective-permute-start.7
  17.9 17.4 %collective-permute-done.8.w_in.packed.in_b = bf16[704,704]{1,0:T(8,128)(2,1)S(1)} collective-permute-done((bf16[704,704]{1,0:T(8,128)(2,1)S(1)}, bf16[704,704]{1,0:T(8,128)(2,1)S(1)}, u32[]{:S(2)}, u32[]{:S(2)}) %collective-permute-start.8) | collective-permute-done | bytes 991264 | tf_op jit(solution)/shard_map/ppermute | solution.py:412
  35.4 0.7 collective-permute-start.9
  36.2 0.7 collective-permute-start.10
  36.9 0.7 collective-permute-start.11
  37.6 0.7 collective-permute-start.12
  38.6 1.3 %collective-permute-start.13 = (bf16[16,48,352]{2,1,0:T(8,128)(2,1)S(1)}, bf16[16,48,352]{2,1,0:T(8,128)(2,1)S(1)}, u32[]{:S(2)}, u32[]{:S(2)}) collective-permute-start(bf16[16,48,352]{2,1,0:T(8,128)(2,1)S(1)} %mlp.1.prev), channel_id=1, source_target_pairs={{16,24},{17,25},{18,26},{19,27},{20,28},{21,29},{22,30},{23,31}} | collective-permute-start | bytes 1622024 | tf_op jit(solution)/shard_map/ppermute | solution.py:435
  39.9 16.8 %collective-permute-done.13.x = bf16[16,48,352]{2,1,0:T(8,128)(2,1)S(1)} collective-permute-done((bf16[16,48,352]{2,1,0:T(8,128)(2,1)S(1)}, bf16[16,48,352]{2,1,0:T(8,128)(2,1)S(1)}, u32[]{:S(2)}, u32[]{:S(2)}) %collective-permute-start.13) | collective-permute-done | bytes 540704 | tf_op jit(solution)/shard_map/ppermute | solution.py:435
  56.6 7.0 %conv_up.1 = (bf16[768,704]{1,0:T(8,128)(2,1)S(1)}, bf16[768,704]{1,0:T(8,128)(2,1)S(1)}, f32[2,1,704]{2,1,0:T(1,128)S(1)}) custom-call(s32[1]{0:T(128)} %bitcast.1.section, bf16[16,48,352]{2,1,0:T(8,128)(2,1)S(1)} %collective-permute-done.13.x, f32[64,384]{1,0:T(8,128)S(1)} %get-tuple-element.32.cpar.refs_7_, bf16[352,704]{1,0:T(8,128)(2,1)S(1)} %bitcast.30, ...), custom_call_target="tpu_custom_call" | custom-call | flops 761266176 | bytes 2142724 | tf_op jit(solution)/shard_map/conv_up/pallas_call | solution.py:348
  64.2 2.8 %collective-permute-start.14 = (bf16[4,48,352]{2,1,0:T(8,128)(2,1)S(1)}, bf16[4,48,352]{2,1,0:T(8,128)(2,1)S(1)}, u32[]{:S(2)}, u32[]{:S(2)}) collective-permute-start(bf16[4,48,352]{2,1,0:T(8,128)(2,1)S(1)} %down_piece.13), channel_id=1, source_target_pairs={{0,4},{2,6},{4,0},{6,2},{1,5},{3,7},{5,1},{7,3},{8,12},{10,14},{12... | collective-permute-start | bytes 405512 | tf_op jit(solution)/shard_map/ppermute | solution.py:558
  67.5 1.3 %collective-permute-start.15 = (bf16[4,48,352]{2,1,0:T(8,128)(2,1)S(1)}, bf16[4,48,352]{2,1,0:T(8,128)(2,1)S(1)}, u32[]{:S(2)}, u32[]{:S(2)}) collective-permute-start(bf16[4,48,352]{2,1,0:T(8,128)(2,1)S(1)} %down_piece.14), channel_id=1, source_target_pairs={{0,6},{2,4},{4,2},{6,0},{1,7},{3,5},{5,3},{7,1},{8,14},{10,12},{12... | collective-permute-start | bytes 405512 | tf_op jit(solution)/shard_map/ppermute | solution.py:558
  69.9 1.2 %collective-permute-done.14.refs_1_ = bf16[4,48,352]{2,1,0:T(8,128)(2,1)S(1)} collective-permute-done((bf16[4,48,352]{2,1,0:T(8,128)(2,1)S(1)}, bf16[4,48,352]{2,1,0:T(8,128)(2,1)S(1)}, u32[]{:S(2)}, u32[]{:S(2)}) %collective-permute-start.14) | collective-permute-done | bytes 135200 | tf_op jit(solution)/shard_map/ppermute | solution.py:558
  71.1 2.4 %collective-permute-done.15.refs_2_ = bf16[4,48,352]{2,1,0:T(8,128)(2,1)S(1)} collective-permute-done((bf16[4,48,352]{2,1,0:T(8,128)(2,1)S(1)}, bf16[4,48,352]{2,1,0:T(8,128)(2,1)S(1)}, u32[]{:S(2)}, u32[]{:S(2)}) %collective-permute-start.15) | collective-permute-done | bytes 135200 | tf_op jit(solution)/shard_map/ppermute | solution.py:558
  73.5 1.4 %collective-permute-done.16.refs_3_ = bf16[4,48,352]{2,1,0:T(8,128)(2,1)S(1)} collective-permute-done((bf16[4,48,352]{2,1,0:T(8,128)(2,1)S(1)}, bf16[4,48,352]{2,1,0:T(8,128)(2,1)S(1)}, u32[]{:S(2)}, u32[]{:S(2)}) %collective-permute-start.16) | collective-permute-done | bytes 135200 | tf_op jit(solution)/shard_map/ppermute | solution.py:558
  74.9 0.8 %place.1 = bf16[1,4,1,4,48,352]{5,4,3,2,1,0:T(8,128)(2,1)} custom-call(s32[1]{0:T(128)} %bitcast.me, bf16[4,48,352]{2,1,0:T(8,128)(2,1)S(1)} %down_piece.12.refs_0_, bf16[4,48,352]{2,1,0:T(8,128)(2,1)S(1)} %collective-permute-done.14.refs_1_, bf16[4,48,352]{2,1,0:T(8,128)(2,1)S(1)} %collective-permute-done.15.refs_2_, ...), custom_call_target="tpu_custom_call" | custom-call | bytes 540676 | tf_op jit(solution)/shard_map/place/pallas_call | solution.py:348
  (60 shorter events, 4.1 us)
Async XLA Ops:
  0.0 9.9 %copy-start.5 = (bf16[1,1408]{1,0:T(2,128)(2,1)S(1)}, bf16[1,1408]{1,0:T(2,128)(2,1)}, u32[]{:S(2)}) copy-start(bf16[1,1408]{1,0:T(2,128)(2,1)} %refs_6_.1) | copy-start | bytes 8452
  0.0 10.0 %copy-start.4 = (bf16[1,1408]{1,0:T(2,128)(2,1)S(1)}, bf16[1,1408]{1,0:T(2,128)(2,1)}, u32[]{:S(2)}) copy-start(bf16[1,1408]{1,0:T(2,128)(2,1)} %refs_5_.1) | copy-start | bytes 8452
  0.0 10.0 %copy-start.3 = (bf16[1,1408]{1,0:T(2,128)(2,1)S(1)}, bf16[1,1408]{1,0:T(2,128)(2,1)}, u32[]{:S(2)}) copy-start(bf16[1,1408]{1,0:T(2,128)(2,1)} %refs_4_.1) | copy-start | bytes 8452
  0.0 10.0 %copy-start.8 = (bf16[1,352]{1,0:T(2,128)(2,1)S(1)}, bf16[1,352]{1,0:T(2,128)(2,1)}, u32[]{:S(2)}) copy-start(bf16[1,352]{1,0:T(2,128)(2,1)} %refs_2_.1) | copy-start | bytes 2116
  0.0 10.0 %copy-start.7 = (bf16[1,352]{1,0:T(2,128)(2,1)S(1)}, bf16[1,352]{1,0:T(2,128)(2,1)}, u32[]{:S(2)}) copy-start(bf16[1,352]{1,0:T(2,128)(2,1)} %refs_1_.1) | copy-start | bytes 2116
  0.0 10.0 %copy-start.6 = (bf16[1,352]{1,0:T(2,128)(2,1)S(1)}, bf16[1,352]{1,0:T(2,128)(2,1)}, u32[]{:S(2)}) copy-start(bf16[1,352]{1,0:T(2,128)(2,1)} %refs_0_.1) | copy-start | bytes 2116
  0.0 10.0 %copy-start.2 = (bf16[1,7,7,352]{3,2,1,0:T(8,128)(2,1)S(1)}, bf16[1,7,7,352]{3,2,1,0:T(8,128)(2,1)}, u32[]{:S(2)}) copy-start(bf16[1,7,7,352]{3,2,1,0:T(8,128)(2,1)} %kernel.1) | copy-start | bytes 103492
  0.1 12.8 %collective-permute-start.4 = (bf16[352,704]{1,0:T(8,128)(2,1)}, bf16[352,704]{1,0:T(8,128)(2,1)S(1)}, u32[]{:S(2)}, u32[]{:S(2)}) collective-permute-start(bf16[352,704]{1,0:T(8,128)(2,1)} %bitcast.25), channel_id=1, source_target_pairs={{0,1},{1,0},{16,17},{17,16},{2,3},{3,2},{18,19},{19,18},{4,5},{5,4... | collective-permute-start | bytes 1486856 | tf_op jit(solution)/shard_map/ppermute | solution.py:412
  2.1 8.9 %collective-permute-start = (bf16[4,48,352]{2,1,0:T(8,128)(2,1)S(1)}, bf16[4,48,352]{2,1,0:T(8,128)(2,1)S(1)}, u32[]{:S(2)}, u32[]{:S(2)}) collective-permute-start(bf16[4,48,352]{2,1,0:T(8,128)(2,1)S(1)} %get-tuple-element.60), channel_id=1, source_target_pairs={{28,8},{30,10},{24,12},{26,14},{29,9},{31,11},{25,13},{27,15}} | collective-permute-start | bytes 405512 | tf_op jit(solution)/shard_map/ppermute | solution.py:407
  6.3 4.7 %collective-permute-start.1 = (bf16[4,48,352]{2,1,0:T(8,128)(2,1)S(1)}, bf16[4,48,352]{2,1,0:T(8,128)(2,1)S(1)}, u32[]{:S(2)}, u32[]{:S(2)}) collective-permute-start(bf16[4,48,352]{2,1,0:T(8,128)(2,1)S(1)} %get-tuple-element.62), channel_id=1, source_target_pairs={{30,8},{28,10},{26,12},{24,14},{31,9},{29,11},{27,13},{25,15}} | collective-permute-start | bytes 405512 | tf_op jit(solution)/shard_map/ppermute | solution.py:407
  8.6 4.3 %collective-permute-start.2 = (bf16[4,48,352]{2,1,0:T(8,128)(2,1)S(1)}, bf16[4,48,352]{2,1,0:T(8,128)(2,1)S(1)}, u32[]{:S(2)}, u32[]{:S(2)}) collective-permute-start(bf16[4,48,352]{2,1,0:T(8,128)(2,1)S(1)} %get-tuple-element.59), channel_id=1, source_target_pairs={{26,8},{24,10},{30,12},{28,14},{27,9},{25,11},{31,13},{29,15}} | collective-permute-start | bytes 405512 | tf_op jit(solution)/shard_map/ppermute | solution.py:407
  10.3 0.7 collective-permute-start.3
  12.9 4.1 %collective-permute-start.5 = (bf16[2,16,48,352]{3,2,1,0:T(8,128)(2,1)S(1)}, bf16[2,16,48,352]{3,2,1,0:T(8,128)(2,1)S(1)}, u32[]{:S(2)}, u32[]{:S(2)}) collective-permute-start(bf16[2,16,48,352]{3,2,1,0:T(8,128)(2,1)S(1)} %last_piece.2), channel_id=1, source_target_pairs={{8,0},{9,1},{10,2},{11,3},{12,4},{13,5},{14,6},{15,7}} | collective-permute-start | bytes 3244040 | tf_op jit(solution)/shard_map/ppermute | solution.py:435
  13.9 3.2 %collective-permute-start.6 = (bf16[704,352]{1,0:T(8,128)(2,1)S(1)}, bf16[704,352]{1,0:T(8,128)(2,1)S(1)}, u32[]{:S(2)}, u32[]{:S(2)}) collective-permute-start(bf16[704,352]{1,0:T(8,128)(2,1)S(1)} %bitcast.13), channel_id=1, source_target_pairs={{0,1},{1,0},{16,17},{17,16},{2,3},{3,2},{18,19},{19,18},{4,5},{5,4... | collective-permute-start | bytes 1486856 | tf_op jit(solution)/shard_map/ppermute | solution.py:412
  14.9 20.3 %collective-permute-start.8 = (bf16[704,704]{1,0:T(8,128)(2,1)S(1)}, bf16[704,704]{1,0:T(8,128)(2,1)S(1)}, u32[]{:S(2)}, u32[]{:S(2)}) collective-permute-start(bf16[704,704]{1,0:T(8,128)(2,1)S(1)} %maximum_maximum_fusion), channel_id=1, source_target_pairs={{8,9},{9,8},{24,25},{25,24},{10,11},{11,10},{26,27},{27,26},{12,13... | collective-permute-start | bytes 2973704 | tf_op jit(solution)/shard_map/ppermute | solution.py:412
  17.1 0.7 collective-permute-start.7
  35.4 2.8 %collective-permute-start.9 = (bf16[4,48,352]{2,1,0:T(8,128)(2,1)S(1)}, bf16[4,48,352]{2,1,0:T(8,128)(2,1)S(1)}, u32[]{:S(2)}, u32[]{:S(2)}) collective-permute-start(bf16[4,48,352]{2,1,0:T(8,128)(2,1)S(1)} %down_piece.8.refs_0_), channel_id=1, source_target_pairs={{8,16},{9,17},{10,18},{11,19},{12,20},{13,21},{14,22},{15,23}} | collective-permute-start | bytes 405512 | tf_op jit(solution)/shard_map/ppermute | solution.py:435
  36.2 2.1 %collective-permute-start.10 = (bf16[4,48,352]{2,1,0:T(8,128)(2,1)S(1)}, bf16[4,48,352]{2,1,0:T(8,128)(2,1)S(1)}, u32[]{:S(2)}, u32[]{:S(2)}) collective-permute-start(bf16[4,48,352]{2,1,0:T(8,128)(2,1)S(1)} %down_piece.9.refs_1_), channel_id=1, source_target_pairs={{8,16},{9,17},{10,18},{11,19},{12,20},{13,21},{14,22},{15,23}} | collective-permute-start | bytes 405512 | tf_op jit(solution)/shard_map/ppermute | solution.py:435
  36.9 1.5 %collective-permute-start.11 = (bf16[4,48,352]{2,1,0:T(8,128)(2,1)S(1)}, bf16[4,48,352]{2,1,0:T(8,128)(2,1)S(1)}, u32[]{:S(2)}, u32[]{:S(2)}) collective-permute-start(bf16[4,48,352]{2,1,0:T(8,128)(2,1)S(1)} %down_piece.10.refs_2_), channel_id=1, source_target_pairs={{8,16},{9,17},{10,18},{11,19},{12,20},{13,21},{14,22},{15,23}} | collective-permute-start | bytes 405512 | tf_op jit(solution)/shard_map/ppermute | solution.py:435
  37.6 0.8 %collective-permute-start.12 = (bf16[4,48,352]{2,1,0:T(8,128)(2,1)S(1)}, bf16[4,48,352]{2,1,0:T(8,128)(2,1)S(1)}, u32[]{:S(2)}, u32[]{:S(2)}) collective-permute-start(bf16[4,48,352]{2,1,0:T(8,128)(2,1)S(1)} %down_piece.11.refs_3_), channel_id=1, source_target_pairs={{8,16},{9,17},{10,18},{11,19},{12,20},{13,21},{14,22},{15,23}} | collective-permute-start | bytes 405512 | tf_op jit(solution)/shard_map/ppermute | solution.py:435
  38.6 18.1 %collective-permute-start.13 = (bf16[16,48,352]{2,1,0:T(8,128)(2,1)S(1)}, bf16[16,48,352]{2,1,0:T(8,128)(2,1)S(1)}, u32[]{:S(2)}, u32[]{:S(2)}) collective-permute-start(bf16[16,48,352]{2,1,0:T(8,128)(2,1)S(1)} %mlp.1.prev), channel_id=1, source_target_pairs={{16,24},{17,25},{18,26},{19,27},{20,28},{21,29},{22,30},{23,31}} | collective-permute-start | bytes 1622024 | tf_op jit(solution)/shard_map/ppermute | solution.py:435
  64.2 6.9 %collective-permute-start.14 = (bf16[4,48,352]{2,1,0:T(8,128)(2,1)S(1)}, bf16[4,48,352]{2,1,0:T(8,128)(2,1)S(1)}, u32[]{:S(2)}, u32[]{:S(2)}) collective-permute-start(bf16[4,48,352]{2,1,0:T(8,128)(2,1)S(1)} %down_piece.13), channel_id=1, source_target_pairs={{0,4},{2,6},{4,0},{6,2},{1,5},{3,7},{5,1},{7,3},{8,12},{10,14},{12... | collective-permute-start | bytes 405512 | tf_op jit(solution)/shard_map/ppermute | solution.py:558
  67.5 6.1 %collective-permute-start.15 = (bf16[4,48,352]{2,1,0:T(8,128)(2,1)S(1)}, bf16[4,48,352]{2,1,0:T(8,128)(2,1)S(1)}, u32[]{:S(2)}, u32[]{:S(2)}) collective-permute-start(bf16[4,48,352]{2,1,0:T(8,128)(2,1)S(1)} %down_piece.14), channel_id=1, source_target_pairs={{0,6},{2,4},{4,2},{6,0},{1,7},{3,5},{5,3},{7,1},{8,14},{10,12},{12... | collective-permute-start | bytes 405512 | tf_op jit(solution)/shard_map/ppermute | solution.py:558
  69.3 5.6 %collective-permute-start.16 = (bf16[4,48,352]{2,1,0:T(8,128)(2,1)S(1)}, bf16[4,48,352]{2,1,0:T(8,128)(2,1)S(1)}, u32[]{:S(2)}, u32[]{:S(2)}) collective-permute-start(bf16[4,48,352]{2,1,0:T(8,128)(2,1)S(1)} %down_piece.15), channel_id=1, source_target_pairs={{0,2},{2,0},{4,6},{6,4},{1,3},{3,1},{5,7},{7,5},{8,10},{10,8},{12,... | collective-permute-start | bytes 405512 | tf_op jit(solution)/shard_map/ppermute | solution.py:558
  (3 other events, 12.8 us)

commit v19 on v18

--- a/solution.py
+++ b/solution.py
@@ -185,24 +185,18 @@
 
 
 def prepare_kernel(part, kernel, *refs):
-    vectors, (cpar, fvec), (held, *staged), sems = refs[:7], refs[7:9], refs[9:-1], refs[-1]
-    moves = [(kernel, held), *zip(vectors, staged)]
-    copies = [pltpu.make_async_copy(a, b, sems.at[n]) for n, (a, b) in enumerate(moves)]
-    for copy in copies:
-        copy.start()
+    vectors, (cpar, fvec) = refs[:7], refs[7:]
     cpar[...] = jnp.zeros(cpar.shape, jnp.float32)
-    for copy in copies:
-        copy.wait()
     channels = kernel.shape[3]
     span = kernel.shape[1]
     half = fvec.shape[2]
     for i in range(span):
-        cpar[i * span : (i + 1) * span, 0:channels] = held[0, i].astype(jnp.float32)
+        cpar[i * span : (i + 1) * span, 0:channels] = kernel[0, i].astype(jnp.float32)
     for n in range(4):
-        cpar[VECTORS + n : VECTORS + n + 1, 0:channels] = staged[n][...].astype(jnp.float32)
+        cpar[VECTORS + n : VECTORS + n + 1, 0:channels] = vectors[n][...].astype(jnp.float32)
     first = part[0] == 0
     for n in range(3):
-        v = staged[4 + n][...].astype(jnp.float32)
+        v = vectors[4 + n][...].astype(jnp.float32)
         low, high = v[:, 0:half], v[:, half:]
         fvec[0, n : n + 1, :] = jnp.where(first, low, high)
         fvec[1, n : n + 1, :] = jnp.where(first, high, low)
@@ -426,9 +420,6 @@
         "prepare",
         (part, *held),
         (shape(VECTORS + 8, lanes), shape(2, 3, half)),
-        specs=[SMEM] + [HBM] * len(held),
-        scratch=[pltpu.VMEM(v.shape, v.dtype) for v in held]
-        + [pltpu.SemaphoreType.DMA((len(held),))],
     )
 
     def send(x, start, end):

time: 76.3 us -> 76.3 us (level)
  transfers between devices with their start and end apart: 17 -> 17, of which waited for: 6 -> 6; matrix products, arithmetic and copies ran while one was open for 2% -> 2% of each run, Pallas kernels for 3% -> 2%
where the time goes in v19:
time: 76.3 us; the launch traced here: 75.9 us
  waiting for transfers between devices  41.2 us (54%)
  starting transfers between devices  21.8 us (29%)
  Pallas kernels  10.5 us (14%)
  local copies, waits for them, and re-layouts  1.45 us (2%)
    ppermute x3, waiting for transfers between devices, other_half(): return lax.ppermute(x, ('section', 'dp'), pairs)  17.4 us
    ppermute x8, waiting for transfers between devices, send(): return lax.ppermute(x, 'section', [(start, end)])  16.8 us
    pallas_call x27, Pallas kernels, call(): pl.pallas_call(functools.partial(kernel, **static), out_shape=out, in_spe...  10.5 us
    ppermute x3, starting transfers between devices, image_plan(): piece = lax.ppermute(piece, ('section', 'row'), pairs)  7.8 us
    ppermute x8, starting transfers between devices, send(): return lax.ppermute(x, 'section', [(start, end)])  6.2 us
    ppermute x3, waiting for transfers between devices, image_plan(): lax.ppermute(piece, 'row', [(p, p ^ order[n]) for p in range(count)])  5.05 us
    ppermute x3, starting transfers between devices, image_plan(): lax.ppermute(piece, 'row', [(p, p ^ order[n]) for p in range(count)])  4.18 us
    ppermute x3, starting transfers between devices, other_half(): return lax.ppermute(x, ('section', 'dp'), pairs)  3.64 us
  transfers between devices with their start and end apart: 17, of which 6 were waited for; matrix products, arithmetic and copies ran while one was open for 2% of the time, Pallas kernels for 2%

profile of v19, /device:TPU:7, one launch (start us, length us, event | category | flops | bytes accessed | tf_op | source)
XLA Modules:
  0.0 75.9 jit_solution(15426779087417539305)
XLA Ops:
  0.1 0.8 %collective-permute-start.4 = (bf16[352,704]{1,0:T(8,128)(2,1)}, bf16[352,704]{1,0:T(8,128)(2,1)S(1)}, u32[]{:S(2)}, u32[]{:S(2)}) collective-permute-start(bf16[352,704]{1,0:T(8,128)(2,1)} %bitcast.25), channel_id=1, source_target_pairs={{0,1},{1,0},{16,17},{17,16},{2,3},{3,2},{18,19},{19,18},{4,5},{5,4... | collective-permute-start | bytes 1486856 | tf_op jit(solution)/shard_map/ppermute | solution.py:406
  0.9 1.2 %dynamic-slice_bitcast_fusion = (bf16[4,48,352]{2,1,0:T(8,128)(2,1)S(1)}, bf16[4,48,352]{2,1,0:T(8,128)(2,1)S(1)}, bf16[4,48,352]{2,1,0:T(8,128)(2,1)S(1)}, bf16[4,48,352]{2,1,0:T(8,128)(2,1)S(1)}) fusion(bf16[4,1,4,48,352]{4,3,2,1,0:T(8,128)(2,1)} %param.11, s32[]{:T(128)S(6)} %select_n.16, s32[]{:T(128)S(6)} %select_n.14, s32[]{:T(128)S(6)} %select_n.13, ...), kind=kLoop, calls=%fused_computation.1 | loop fusion | bytes 1081360 | tf_op jit(solution)/shard_map/squeeze | solution.py:398
  2.1 4.2 %collective-permute-start = (bf16[4,48,352]{2,1,0:T(8,128)(2,1)S(1)}, bf16[4,48,352]{2,1,0:T(8,128)(2,1)S(1)}, u32[]{:S(2)}, u32[]{:S(2)}) collective-permute-start(bf16[4,48,352]{2,1,0:T(8,128)(2,1)S(1)} %get-tuple-element.60), channel_id=1, source_target_pairs={{28,8},{30,10},{24,12},{26,14},{29,9},{31,11},{25,13},{27,15}} | collective-permute-start | bytes 405512 | tf_op jit(solution)/shard_map/ppermute | solution.py:401
  6.3 2.3 %collective-permute-start.1 = (bf16[4,48,352]{2,1,0:T(8,128)(2,1)S(1)}, bf16[4,48,352]{2,1,0:T(8,128)(2,1)S(1)}, u32[]{:S(2)}, u32[]{:S(2)}) collective-permute-start(bf16[4,48,352]{2,1,0:T(8,128)(2,1)S(1)} %get-tuple-element.62), channel_id=1, source_target_pairs={{30,8},{28,10},{26,12},{24,14},{31,9},{29,11},{27,13},{25,15}} | collective-permute-start | bytes 405512 | tf_op jit(solution)/shard_map/ppermute | solution.py:401
  8.6 1.3 %collective-permute-start.2 = (bf16[4,48,352]{2,1,0:T(8,128)(2,1)S(1)}, bf16[4,48,352]{2,1,0:T(8,128)(2,1)S(1)}, u32[]{:S(2)}, u32[]{:S(2)}) collective-permute-start(bf16[4,48,352]{2,1,0:T(8,128)(2,1)S(1)} %get-tuple-element.59), channel_id=1, source_target_pairs={{26,8},{24,10},{30,12},{28,14},{27,9},{25,11},{31,13},{29,15}} | collective-permute-start | bytes 405512 | tf_op jit(solution)/shard_map/ppermute | solution.py:401
  10.9 2.0 %collective-permute-done.2.refs_3_ = bf16[4,48,352]{2,1,0:T(8,128)(2,1)S(1)} collective-permute-done((bf16[4,48,352]{2,1,0:T(8,128)(2,1)S(1)}, bf16[4,48,352]{2,1,0:T(8,128)(2,1)S(1)}, u32[]{:S(2)}, u32[]{:S(2)}) %collective-permute-start.2) | collective-permute-done | bytes 135200 | tf_op jit(solution)/shard_map/ppermute | solution.py:401
  12.9 0.9 %collective-permute-start.5 = (bf16[2,16,48,352]{3,2,1,0:T(8,128)(2,1)S(1)}, bf16[2,16,48,352]{3,2,1,0:T(8,128)(2,1)S(1)}, u32[]{:S(2)}, u32[]{:S(2)}) collective-permute-start(bf16[2,16,48,352]{3,2,1,0:T(8,128)(2,1)S(1)} %last_piece.2), channel_id=1, source_target_pairs={{8,0},{9,1},{10,2},{11,3},{12,4},{13,5},{14,6},{15,7}} | collective-permute-start | bytes 3244040 | tf_op jit(solution)/shard_map/ppermute | solution.py:426
  13.9 0.7 collective-permute-start.6
  14.9 2.1 %collective-permute-start.8 = (bf16[704,704]{1,0:T(8,128)(2,1)S(1)}, bf16[704,704]{1,0:T(8,128)(2,1)S(1)}, u32[]{:S(2)}, u32[]{:S(2)}) collective-permute-start(bf16[704,704]{1,0:T(8,128)(2,1)S(1)} %maximum_maximum_fusion), channel_id=1, source_target_pairs={{8,9},{9,8},{24,25},{25,24},{10,11},{11,10},{26,27},{27,26},{12,13... | collective-permute-start | bytes 2973704 | tf_op jit(solution)/shard_map/ppermute | solution.py:406
  17.1 0.7 collective-permute-start.7
  17.9 17.4 %collective-permute-done.8.w_in.packed.in_b = bf16[704,704]{1,0:T(8,128)(2,1)S(1)} collective-permute-done((bf16[704,704]{1,0:T(8,128)(2,1)S(1)}, bf16[704,704]{1,0:T(8,128)(2,1)S(1)}, u32[]{:S(2)}, u32[]{:S(2)}) %collective-permute-start.8) | collective-permute-done | bytes 991264 | tf_op jit(solution)/shard_map/ppermute | solution.py:406
  35.4 0.7 collective-permute-start.9
  36.2 0.7 collective-permute-start.10
  36.9 0.7 collective-permute-start.11
  37.6 0.7 collective-permute-start.12
  38.6 1.3 %collective-permute-start.13 = (bf16[16,48,352]{2,1,0:T(8,128)(2,1)S(1)}, bf16[16,48,352]{2,1,0:T(8,128)(2,1)S(1)}, u32[]{:S(2)}, u32[]{:S(2)}) collective-permute-start(bf16[16,48,352]{2,1,0:T(8,128)(2,1)S(1)} %mlp.1.prev), channel_id=1, source_target_pairs={{16,24},{17,25},{18,26},{19,27},{20,28},{21,29},{22,30},{23,31}} | collective-permute-start | bytes 1622024 | tf_op jit(solution)/shard_map/ppermute | solution.py:426
  39.9 16.8 %collective-permute-done.13.x = bf16[16,48,352]{2,1,0:T(8,128)(2,1)S(1)} collective-permute-done((bf16[16,48,352]{2,1,0:T(8,128)(2,1)S(1)}, bf16[16,48,352]{2,1,0:T(8,128)(2,1)S(1)}, u32[]{:S(2)}, u32[]{:S(2)}) %collective-permute-start.13) | collective-permute-done | bytes 540704 | tf_op jit(solution)/shard_map/ppermute | solution.py:426
  56.6 7.0 %conv_up.1 = (bf16[768,704]{1,0:T(8,128)(2,1)S(1)}, bf16[768,704]{1,0:T(8,128)(2,1)S(1)}, f32[2,1,704]{2,1,0:T(1,128)S(1)}) custom-call(s32[1]{0:T(128)} %bitcast.1.section, bf16[16,48,352]{2,1,0:T(8,128)(2,1)S(1)} %collective-permute-done.13.x, f32[64,384]{1,0:T(8,128)S(1)} %get-tuple-element.32.cpar.refs_7_, bf16[352,704]{1,0:T(8,128)(2,1)S(1)} %bitcast.30, ...), custom_call_target="tpu_custom_call" | custom-call | flops 761266176 | bytes 2142724 | tf_op jit(solution)/shard_map/conv_up/pallas_call | solution.py:342
  64.2 2.8 %collective-permute-start.14 = (bf16[4,48,352]{2,1,0:T(8,128)(2,1)S(1)}, bf16[4,48,352]{2,1,0:T(8,128)(2,1)S(1)}, u32[]{:S(2)}, u32[]{:S(2)}) collective-permute-start(bf16[4,48,352]{2,1,0:T(8,128)(2,1)S(1)} %down_piece.13), channel_id=1, source_target_pairs={{0,4},{2,6},{4,0},{6,2},{1,5},{3,7},{5,1},{7,3},{8,12},{10,14},{12... | collective-permute-start | bytes 405512 | tf_op jit(solution)/shard_map/ppermute | solution.py:549
  67.5 1.3 %collective-permute-start.15 = (bf16[4,48,352]{2,1,0:T(8,128)(2,1)S(1)}, bf16[4,48,352]{2,1,0:T(8,128)(2,1)S(1)}, u32[]{:S(2)}, u32[]{:S(2)}) collective-permute-start(bf16[4,48,352]{2,1,0:T(8,128)(2,1)S(1)} %down_piece.14), channel_id=1, source_target_pairs={{0,6},{2,4},{4,2},{6,0},{1,7},{3,5},{5,3},{7,1},{8,14},{10,12},{12... | collective-permute-start | bytes 405512 | tf_op jit(solution)/shard_map/ppermute | solution.py:549
  69.9 1.2 %collective-permute-done.14.refs_1_ = bf16[4,48,352]{2,1,0:T(8,128)(2,1)S(1)} collective-permute-done((bf16[4,48,352]{2,1,0:T(8,128)(2,1)S(1)}, bf16[4,48,352]{2,1,0:T(8,128)(2,1)S(1)}, u32[]{:S(2)}, u32[]{:S(2)}) %collective-permute-start.14) | collective-permute-done | bytes 135200 | tf_op jit(solution)/shard_map/ppermute | solution.py:549
  71.1 2.4 %collective-permute-done.15.refs_2_ = bf16[4,48,352]{2,1,0:T(8,128)(2,1)S(1)} collective-permute-done((bf16[4,48,352]{2,1,0:T(8,128)(2,1)S(1)}, bf16[4,48,352]{2,1,0:T(8,128)(2,1)S(1)}, u32[]{:S(2)}, u32[]{:S(2)}) %collective-permute-start.15) | collective-permute-done | bytes 135200 | tf_op jit(solution)/shard_map/ppermute | solution.py:549
  73.5 1.4 %collective-permute-done.16.refs_3_ = bf16[4,48,352]{2,1,0:T(8,128)(2,1)S(1)} collective-permute-done((bf16[4,48,352]{2,1,0:T(8,128)(2,1)S(1)}, bf16[4,48,352]{2,1,0:T(8,128)(2,1)S(1)}, u32[]{:S(2)}, u32[]{:S(2)}) %collective-permute-start.16) | collective-permute-done | bytes 135200 | tf_op jit(solution)/shard_map/ppermute | solution.py:549
  74.9 0.8 %place.1 = bf16[1,4,1,4,48,352]{5,4,3,2,1,0:T(8,128)(2,1)} custom-call(s32[1]{0:T(128)} %bitcast.me, bf16[4,48,352]{2,1,0:T(8,128)(2,1)S(1)} %down_piece.12.refs_0_, bf16[4,48,352]{2,1,0:T(8,128)(2,1)S(1)} %collective-permute-done.14.refs_1_, bf16[4,48,352]{2,1,0:T(8,128)(2,1)S(1)} %collective-permute-done.15.refs_2_, ...), custom_call_target="tpu_custom_call" | custom-call | bytes 540676 | tf_op jit(solution)/shard_map/place/pallas_call | solution.py:342
  (60 shorter events, 3.9 us)
Async XLA Ops:
  0.0 9.9 %copy-start.5 = (bf16[1,1408]{1,0:T(2,128)(2,1)S(1)}, bf16[1,1408]{1,0:T(2,128)(2,1)}, u32[]{:S(2)}) copy-start(bf16[1,1408]{1,0:T(2,128)(2,1)} %refs_6_.1) | copy-start | bytes 8452
  0.0 10.0 %copy-start.4 = (bf16[1,1408]{1,0:T(2,128)(2,1)S(1)}, bf16[1,1408]{1,0:T(2,128)(2,1)}, u32[]{:S(2)}) copy-start(bf16[1,1408]{1,0:T(2,128)(2,1)} %refs_5_.1) | copy-start | bytes 8452
  0.0 10.0 %copy-start.3 = (bf16[1,1408]{1,0:T(2,128)(2,1)S(1)}, bf16[1,1408]{1,0:T(2,128)(2,1)}, u32[]{:S(2)}) copy-start(bf16[1,1408]{1,0:T(2,128)(2,1)} %refs_4_.1) | copy-start | bytes 8452
  0.0 10.0 %copy-start.8 = (bf16[1,352]{1,0:T(2,128)(2,1)S(1)}, bf16[1,352]{1,0:T(2,128)(2,1)}, u32[]{:S(2)}) copy-start(bf16[1,352]{1,0:T(2,128)(2,1)} %refs_2_.1) | copy-start | bytes 2116
  0.0 10.0 %copy-start.7 = (bf16[1,352]{1,0:T(2,128)(2,1)S(1)}, bf16[1,352]{1,0:T(2,128)(2,1)}, u32[]{:S(2)}) copy-start(bf16[1,352]{1,0:T(2,128)(2,1)} %refs_1_.1) | copy-start | bytes 2116
  0.0 10.0 %copy-start.6 = (bf16[1,352]{1,0:T(2,128)(2,1)S(1)}, bf16[1,352]{1,0:T(2,128)(2,1)}, u32[]{:S(2)}) copy-start(bf16[1,352]{1,0:T(2,128)(2,1)} %refs_0_.1) | copy-start | bytes 2116
  0.0 10.0 %copy-start.2 = (bf16[1,7,7,352]{3,2,1,0:T(8,128)(2,1)S(1)}, bf16[1,7,7,352]{3,2,1,0:T(8,128)(2,1)}, u32[]{:S(2)}) copy-start(bf16[1,7,7,352]{3,2,1,0:T(8,128)(2,1)} %kernel.1) | copy-start | bytes 103492
  0.1 12.8 %collective-permute-start.4 = (bf16[352,704]{1,0:T(8,128)(2,1)}, bf16[352,704]{1,0:T(8,128)(2,1)S(1)}, u32[]{:S(2)}, u32[]{:S(2)}) collective-permute-start(bf16[352,704]{1,0:T(8,128)(2,1)} %bitcast.25), channel_id=1, source_target_pairs={{0,1},{1,0},{16,17},{17,16},{2,3},{3,2},{18,19},{19,18},{4,5},{5,4... | collective-permute-start | bytes 1486856 | tf_op jit(solution)/shard_map/ppermute | solution.py:406
  2.1 8.7 %collective-permute-start = (bf16[4,48,352]{2,1,0:T(8,128)(2,1)S(1)}, bf16[4,48,352]{2,1,0:T(8,128)(2,1)S(1)}, u32[]{:S(2)}, u32[]{:S(2)}) collective-permute-start(bf16[4,48,352]{2,1,0:T(8,128)(2,1)S(1)} %get-tuple-element.60), channel_id=1, source_target_pairs={{28,8},{30,10},{24,12},{26,14},{29,9},{31,11},{25,13},{27,15}} | collective-permute-start | bytes 405512 | tf_op jit(solution)/shard_map/ppermute | solution.py:401
  6.3 4.5 %collective-permute-start.1 = (bf16[4,48,352]{2,1,0:T(8,128)(2,1)S(1)}, bf16[4,48,352]{2,1,0:T(8,128)(2,1)S(1)}, u32[]{:S(2)}, u32[]{:S(2)}) collective-permute-start(bf16[4,48,352]{2,1,0:T(8,128)(2,1)S(1)} %get-tuple-element.62), channel_id=1, source_target_pairs={{30,8},{28,10},{26,12},{24,14},{31,9},{29,11},{27,13},{25,15}} | collective-permute-start | bytes 405512 | tf_op jit(solution)/shard_map/ppermute | solution.py:401
  8.6 4.3 %collective-permute-start.2 = (bf16[4,48,352]{2,1,0:T(8,128)(2,1)S(1)}, bf16[4,48,352]{2,1,0:T(8,128)(2,1)S(1)}, u32[]{:S(2)}, u32[]{:S(2)}) collective-permute-start(bf16[4,48,352]{2,1,0:T(8,128)(2,1)S(1)} %get-tuple-element.59), channel_id=1, source_target_pairs={{26,8},{24,10},{30,12},{28,14},{27,9},{25,11},{31,13},{29,15}} | collective-permute-start | bytes 405512 | tf_op jit(solution)/shard_map/ppermute | solution.py:401
  10.1 0.7 collective-permute-start.3
  12.9 4.1 %collective-permute-start.5 = (bf16[2,16,48,352]{3,2,1,0:T(8,128)(2,1)S(1)}, bf16[2,16,48,352]{3,2,1,0:T(8,128)(2,1)S(1)}, u32[]{:S(2)}, u32[]{:S(2)}) collective-permute-start(bf16[2,16,48,352]{3,2,1,0:T(8,128)(2,1)S(1)} %last_piece.2), channel_id=1, source_target_pairs={{8,0},{9,1},{10,2},{11,3},{12,4},{13,5},{14,6},{15,7}} | collective-permute-start | bytes 3244040 | tf_op jit(solution)/shard_map/ppermute | solution.py:426
  13.9 3.2 %collective-permute-start.6 = (bf16[704,352]{1,0:T(8,128)(2,1)S(1)}, bf16[704,352]{1,0:T(8,128)(2,1)S(1)}, u32[]{:S(2)}, u32[]{:S(2)}) collective-permute-start(bf16[704,352]{1,0:T(8,128)(2,1)S(1)} %bitcast.13), channel_id=1, source_target_pairs={{0,1},{1,0},{16,17},{17,16},{2,3},{3,2},{18,19},{19,18},{4,5},{5,4... | collective-permute-start | bytes 1486856 | tf_op jit(solution)/shard_map/ppermute | solution.py:406
  14.9 20.3 %collective-permute-start.8 = (bf16[704,704]{1,0:T(8,128)(2,1)S(1)}, bf16[704,704]{1,0:T(8,128)(2,1)S(1)}, u32[]{:S(2)}, u32[]{:S(2)}) collective-permute-start(bf16[704,704]{1,0:T(8,128)(2,1)S(1)} %maximum_maximum_fusion), channel_id=1, source_target_pairs={{8,9},{9,8},{24,25},{25,24},{10,11},{11,10},{26,27},{27,26},{12,13... | collective-permute-start | bytes 2973704 | tf_op jit(solution)/shard_map/ppermute | solution.py:406
  17.1 0.7 collective-permute-start.7
  35.4 2.8 %collective-permute-start.9 = (bf16[4,48,352]{2,1,0:T(8,128)(2,1)S(1)}, bf16[4,48,352]{2,1,0:T(8,128)(2,1)S(1)}, u32[]{:S(2)}, u32[]{:S(2)}) collective-permute-start(bf16[4,48,352]{2,1,0:T(8,128)(2,1)S(1)} %down_piece.8.refs_0_), channel_id=1, source_target_pairs={{8,16},{9,17},{10,18},{11,19},{12,20},{13,21},{14,22},{15,23}} | collective-permute-start | bytes 405512 | tf_op jit(solution)/shard_map/ppermute | solution.py:426
  36.2 2.1 %collective-permute-start.10 = (bf16[4,48,352]{2,1,0:T(8,128)(2,1)S(1)}, bf16[4,48,352]{2,1,0:T(8,128)(2,1)S(1)}, u32[]{:S(2)}, u32[]{:S(2)}) collective-permute-start(bf16[4,48,352]{2,1,0:T(8,128)(2,1)S(1)} %down_piece.9.refs_1_), channel_id=1, source_target_pairs={{8,16},{9,17},{10,18},{11,19},{12,20},{13,21},{14,22},{15,23}} | collective-permute-start | bytes 405512 | tf_op jit(solution)/shard_map/ppermute | solution.py:426
  36.9 1.5 %collective-permute-start.11 = (bf16[4,48,352]{2,1,0:T(8,128)(2,1)S(1)}, bf16[4,48,352]{2,1,0:T(8,128)(2,1)S(1)}, u32[]{:S(2)}, u32[]{:S(2)}) collective-permute-start(bf16[4,48,352]{2,1,0:T(8,128)(2,1)S(1)} %down_piece.10.refs_2_), channel_id=1, source_target_pairs={{8,16},{9,17},{10,18},{11,19},{12,20},{13,21},{14,22},{15,23}} | collective-permute-start | bytes 405512 | tf_op jit(solution)/shard_map/ppermute | solution.py:426
  37.6 0.8 %collective-permute-start.12 = (bf16[4,48,352]{2,1,0:T(8,128)(2,1)S(1)}, bf16[4,48,352]{2,1,0:T(8,128)(2,1)S(1)}, u32[]{:S(2)}, u32[]{:S(2)}) collective-permute-start(bf16[4,48,352]{2,1,0:T(8,128)(2,1)S(1)} %down_piece.11.refs_3_), channel_id=1, source_target_pairs={{8,16},{9,17},{10,18},{11,19},{12,20},{13,21},{14,22},{15,23}} | collective-permute-start | bytes 405512 | tf_op jit(solution)/shard_map/ppermute | solution.py:426
  38.6 18.1 %collective-permute-start.13 = (bf16[16,48,352]{2,1,0:T(8,128)(2,1)S(1)}, bf16[16,48,352]{2,1,0:T(8,128)(2,1)S(1)}, u32[]{:S(2)}, u32[]{:S(2)}) collective-permute-start(bf16[16,48,352]{2,1,0:T(8,128)(2,1)S(1)} %mlp.1.prev), channel_id=1, source_target_pairs={{16,24},{17,25},{18,26},{19,27},{20,28},{21,29},{22,30},{23,31}} | collective-permute-start | bytes 1622024 | tf_op jit(solution)/shard_map/ppermute | solution.py:426
  64.2 6.9 %collective-permute-start.14 = (bf16[4,48,352]{2,1,0:T(8,128)(2,1)S(1)}, bf16[4,48,352]{2,1,0:T(8,128)(2,1)S(1)}, u32[]{:S(2)}, u32[]{:S(2)}) collective-permute-start(bf16[4,48,352]{2,1,0:T(8,128)(2,1)S(1)} %down_piece.13), channel_id=1, source_target_pairs={{0,4},{2,6},{4,0},{6,2},{1,5},{3,7},{5,1},{7,3},{8,12},{10,14},{12... | collective-permute-start | bytes 405512 | tf_op jit(solution)/shard_map/ppermute | solution.py:549
  67.5 6.1 %collective-permute-start.15 = (bf16[4,48,352]{2,1,0:T(8,128)(2,1)S(1)}, bf16[4,48,352]{2,1,0:T(8,128)(2,1)S(1)}, u32[]{:S(2)}, u32[]{:S(2)}) collective-permute-start(bf16[4,48,352]{2,1,0:T(8,128)(2,1)S(1)} %down_piece.14), channel_id=1, source_target_pairs={{0,6},{2,4},{4,2},{6,0},{1,7},{3,5},{5,3},{7,1},{8,14},{10,12},{12... | collective-permute-start | bytes 405512 | tf_op jit(solution)/shard_map/ppermute | solution.py:549
  69.3 5.6 %collective-permute-start.16 = (bf16[4,48,352]{2,1,0:T(8,128)(2,1)S(1)}, bf16[4,48,352]{2,1,0:T(8,128)(2,1)S(1)}, u32[]{:S(2)}, u32[]{:S(2)}) collective-permute-start(bf16[4,48,352]{2,1,0:T(8,128)(2,1)S(1)} %down_piece.15), channel_id=1, source_target_pairs={{0,2},{2,0},{4,6},{6,4},{1,3},{3,1},{5,7},{7,5},{8,10},{10,8},{12,... | collective-permute-start | bytes 405512 | tf_op jit(solution)/shard_map/ppermute | solution.py:549
  (3 other events, 12.8 us)
